TPU v7x, 32 devices: a whole 2x2x4 slice. The times are simulated.
32 devices in a mesh: groups: 2 (over y), mp: 8 (over z, x), batch: 2 (over core).
Axes of the slice: x: 2, y: 2, z: 4, core: 2. Of those that a mesh axis runs over, the one named last changes fastest.
Arguments:
- byte_ids: int32 [3, 1024], P(None, ('groups', 'batch')), parts along dimension 1, may hold values from 0 to 255
- h_start: bfloat16 [1024, 4096], P(('groups', 'batch'), 'mp'), parts along dimension 0, may hold values from -0.8984375 to 0.8984375
- c_start: float32 [1024, 4096], P(('groups', 'batch'), 'mp'), parts along dimension 0, may hold values from -4 to 4
- inter_weight: bfloat16 [4096, 4096], P('mp'), may hold values from -0.375 to 0.375
- inter_embed: bfloat16 [256, 4096], P(None, 'mp'), may hold values from -4 to 4
- gate_weight: bfloat16 [4096, 16384], P(None, 'mp'), may hold values from -0.1875 to 0.1875
- gate_embed: bfloat16 [256, 16384], P(None, 'mp'), may hold values from -3 to 3
- gate_bias: float32 [16384], P('mp'), may hold values from -3 to 3
Outputs:
- h_final: bfloat16 [1024, 4096], P(('groups', 'batch'), 'mp'), parts along dimension 0
- c_final: float32 [1024, 4096], P(('groups', 'batch'), 'mp'), parts along dimension 0
There are 2 independent parts, one for each index of `groups`. A program takes and returns all parts, laid end to end along the dimension named above; an argument that names none is the same for every part. Nothing has to cross between parts.
All inputs are finite; a program needn't handle non-finite values.
Results may differ from a plain program's by a relative error of at most 0.015.
Values may be sent and summed in bfloat16 or wider, within the bound.
No kernel may reach another device: no remote copies, remote signals or barrier semaphores. Data moves between devices by JAX's collectives and lax.ppermute only.
A program may use at most 128 MiB of HBM per device.

v0:
```python
import jax
import jax.numpy as jnp
from jax import lax
from jax.sharding import PartitionSpec as P


def local(
    byte_ids, h_start, c_start, inter_weight, inter_embed, gate_weight, gate_embed, gate_bias
):
    h_final = h_start
    c_final = c_start
    for step in range(byte_ids.shape[0]):
        rows_here = h_final.shape[0]
        onehot = (
            byte_ids[step][:, None] == jnp.arange(inter_embed.shape[0], dtype=jnp.int32)[None, :]
        ).astype(jnp.bfloat16)
        product = lax.dot_general(
            lax.all_gather(h_final, "mp", axis=1, tiled=True),
            inter_weight,
            (((1,), (1,)), ((), ())),
            preferred_element_type=jnp.float32,
        )
        lookup = jnp.dot(onehot, inter_embed, preferred_element_type=jnp.float32)
        inter_vals = (lookup * product).astype(jnp.bfloat16)
        gate_sums = jnp.dot(
            lax.all_gather(inter_vals, "mp", axis=1, tiled=True),
            gate_weight,
            preferred_element_type=jnp.float32,
        )
        gate_sums = (
            gate_sums
            + jnp.dot(onehot, gate_embed, preferred_element_type=jnp.float32)
            + gate_bias[None, :]
        )
        gate_sums = gate_sums.reshape(rows_here, gate_sums.shape[1] // 4, 4)
        in_gate = jax.nn.sigmoid(gate_sums[:, :, 0])
        forget = jax.nn.sigmoid(gate_sums[:, :, 1])
        out_gate = jax.nn.sigmoid(gate_sums[:, :, 2])
        update = jnp.tanh(gate_sums[:, :, 3])
        new_cell = forget * c_final + in_gate * update
        new_hidden = (out_gate * jnp.tanh(new_cell)).astype(jnp.bfloat16)
        h_final = new_hidden
        c_final = new_cell
    return (h_final, c_final)


def solution(mesh):
    in_specs = (
        P(None, ("groups", "batch")),
        P(("groups", "batch"), "mp"),
        P(("groups", "batch"), "mp"),
        P("mp", None),
        P(None, "mp"),
        P(None, "mp"),
        P(None, "mp"),
        P("mp"),
    )
    out_specs = (P(("groups", "batch"), "mp"), P(("groups", "batch"), "mp"))
    return jax.shard_map(local, mesh=mesh, in_specs=in_specs, out_specs=out_specs, check_vma=False)
```

profile of v0, /device:TPU:0, one launch (start us, length us, event | category | flops | bytes accessed | tf_op | source)
XLA Modules:
  0.0 379.5 jit_solution(11661832159043770891)
XLA Ops:
  7.2 0.0 all-gather.7.cloned.1.call-start
  7.2 0.7 all-gather.7.cloned.1.call-update
  7.9 0.0 all-gather.9.cloned.1.call-start
  8.0 0.8 fusion.70
  8.8 1.2 fusion.56
  10.0 53.9 %all-gather.7.cloned.1.call-done = bf16[256,4096]{1,0:T(8,128)(2,1)} async-done(((bf16[256,512]{1,0:T(8,128)(2,1)}), bf16[256,4096]{1,0:T(8,128)(2,1)}) %all-gather.7.cloned.1.call-update) | async-done | bytes 2097168 | tf_op jit(solution)/shard_map/all_gather | solution.py:18
  63.9 4.8 %fusion.3 = bf16[256,512]{1,0:T(8,128)(2,1)} fusion(f32[256,512]{1,0:T(8,128)S(1)} %fusion.56, bf16[256,4096]{1,0:T(8,128)(2,1)} %all-gather.7.cloned.1.call-done, bf16[512,4096]{1,0:T(8,128)(2,1)} %param.11), kind=kOutput, calls=%fused_computation.9 | convolution fusion | flops 1074003968 | bytes 7077888 | tf_op jit(solution)/shard_map/dot_general | solution.py:17
  68.7 0.0 all-gather.9.cloned.1.call-update
  68.7 0.0 all-gather.11.cloned.1.call-start
  68.8 1.0 copy.25
  69.8 48.4 %all-gather.9.cloned.1.call-done = bf16[256,4096]{1,0:T(8,128)(2,1)} async-done(((bf16[256,512]{1,0:T(8,128)(2,1)}), bf16[256,4096]{1,0:T(8,128)(2,1)}) %all-gather.9.cloned.1.call-update) | async-done | bytes 2097168 | tf_op jit(solution)/shard_map/all_gather | solution.py:26
  118.1 8.7 %fusion.71 = f32[256,2048]{1,0:T(8,128)S(1)} fusion(bf16[256,4096]{1,0:T(8,128)(2,1)} %all-gather.9.cloned.1.call-done, bf16[4096,2048]{1,0:T(8,128)(2,1)} %param.13), kind=kOutput, calls=%fused_computation.90 | convolution fusion | flops 4294967296 | bytes 20971520 | tf_op jit(solution)/shard_map/dot_general | solution.py:25
  126.9 0.5 fusion.2
  127.4 1.8 copy.22
  129.2 1.9 reshape.74
  131.1 1.1 fusion.69
  132.2 0.1 fusion.52
  132.3 0.9 fusion.6
  133.3 0.8 copy-done.1
  134.0 1.1 fusion.53
  135.2 0.0 all-gather.13.cloned.1.call-start
  135.2 0.3 fusion.57
  135.5 47.3 %all-gather.11.cloned.1.call-done = bf16[256,4096]{0,1:T(8,128)(2,1)} async-done(((bf16[256,512]{0,1:T(8,128)(2,1)}), bf16[256,4096]{0,1:T(8,128)(2,1)}) %all-gather.11.cloned.1.call-update) | async-done | bytes 2097168 | tf_op jit(solution)/shard_map/all_gather | solution.py:18
  182.8 4.8 %fusion.4 = bf16[256,512]{1,0:T(8,128)(2,1)} fusion(f32[256,512]{1,0:T(8,128)S(1)} %fusion.57, bf16[256,4096]{0,1:T(8,128)(2,1)} %all-gather.11.cloned.1.call-done, bf16[512,4096]{1,0:T(8,128)(2,1)} %param.11), kind=kOutput, calls=%fused_computation.10 | convolution fusion | flops 1074003968 | bytes 7077888 | tf_op jit(solution)/shard_map/dot_general | solution.py:17
  187.6 0.0 all-gather.13.cloned.1.call-update
  187.6 0.2 all-gather.15.cloned.1.call-start
  187.9 49.5 %all-gather.13.cloned.1.call-done = bf16[256,4096]{1,0:T(8,128)(2,1)} async-done(((bf16[256,512]{1,0:T(8,128)(2,1)}), bf16[256,4096]{1,0:T(8,128)(2,1)}) %all-gather.13.cloned.1.call-update) | async-done | bytes 2097168 | tf_op jit(solution)/shard_map/all_gather | solution.py:26
  237.4 8.7 %fusion.72 = f32[256,2048]{1,0:T(8,128)S(1)} fusion(bf16[256,4096]{1,0:T(8,128)(2,1)} %all-gather.13.cloned.1.call-done, bf16[4096,2048]{1,0:T(8,128)(2,1)} %param.13), kind=kOutput, calls=%fused_computation.91 | convolution fusion | flops 4294967296 | bytes 20971520 | tf_op jit(solution)/shard_map/dot_general | solution.py:25
  246.1 0.5 fusion.1
  246.6 1.8 copy.28
  248.4 1.9 reshape.75
  250.3 1.5 fusion.68
  251.9 1.6 fusion.54
  253.5 0.0 all-gather.15.cloned.1.call-update
  253.5 0.3 all-gather.17.cloned.1.call-start
  253.8 0.3 fusion.58
  254.0 47.1 %all-gather.15.cloned.1.call-done = bf16[256,4096]{0,1:T(8,128)(2,1)} async-done(((bf16[256,512]{0,1:T(8,128)(2,1)}), bf16[256,4096]{0,1:T(8,128)(2,1)}) %all-gather.15.cloned.1.call-update) | async-done | bytes 2097168 | tf_op jit(solution)/shard_map/all_gather | solution.py:18
  301.1 4.8 %fusion.5 = bf16[256,512]{1,0:T(8,128)(2,1)} fusion(f32[256,512]{1,0:T(8,128)S(1)} %fusion.58, bf16[256,4096]{0,1:T(8,128)(2,1)} %all-gather.15.cloned.1.call-done, bf16[512,4096]{1,0:T(8,128)(2,1)} %param.11), kind=kOutput, calls=%fused_computation.11 | convolution fusion | flops 1074003968 | bytes 7077888 | tf_op jit(solution)/shard_map/dot_general | solution.py:17
  305.9 0.0 all-gather.17.cloned.1.call-update
  306.0 49.7 %all-gather.17.cloned.1.call-done = bf16[256,4096]{1,0:T(8,128)(2,1)} async-done(((bf16[256,512]{1,0:T(8,128)(2,1)}), bf16[256,4096]{1,0:T(8,128)(2,1)}) %all-gather.17.cloned.1.call-update) | async-done | bytes 2097168 | tf_op jit(solution)/shard_map/all_gather | solution.py:26
  355.7 8.7 %fusion.73 = f32[256,2048]{1,0:T(8,128)S(1)} fusion(bf16[256,4096]{1,0:T(8,128)(2,1)} %all-gather.17.cloned.1.call-done, bf16[4096,2048]{1,0:T(8,128)(2,1)} %param.13), kind=kOutput, calls=%fused_computation.92 | convolution fusion | flops 4294967296 | bytes 20971520 | tf_op jit(solution)/shard_map/dot_general | solution.py:25
  364.4 0.5 fusion
  364.9 1.8 copy.33
  366.8 1.9 reshape.76
  368.6 1.6 fusion.67
  370.2 0.6 fusion.55
  370.8 1.0 copy.39
  371.8 0.8 copy.38
  (22 shorter events, 0.1 us)
Async XLA Ops:
  7.2 119.7 %copy-start = (bf16[256,2048]{1,0:T(8,128)(2,1)S(1)}, bf16[256,2048]{1,0:T(8,128)(2,1)}, u32[]{:S(2)}) copy-start(bf16[256,2048]{1,0:T(8,128)(2,1)} %param.14) | copy-start | bytes 3145732
  7.2 56.7 %all-gather.7.cloned.1.call-start = ((), (), s32[]{:S(2)}) async-start(), calls=%async_computation | async-start | bytes 2359296 | tf_op jit(solution)/shard_map/all_gather | solution.py:18
  7.9 110.2 %all-gather.9.cloned.1.call-start = ((), (), s32[]{:S(2)}) async-start(), calls=%async_computation.1 | async-start | bytes 2359296 | tf_op jit(solution)/shard_map/all_gather | solution.py:26
  10.0 58.8 %copy-start.9 = (f32[256,512]{1,0:T(8,128)S(1)}, f32[256,512]{1,0:T(8,128)}, u32[]{:S(2)}) copy-start(f32[256,512]{1,0:T(8,128)} %param.10) | copy-start | bytes 1572868
  68.7 114.1 %all-gather.11.cloned.1.call-start = ((), (), s32[]{:S(2)}) async-start(), calls=%async_computation.2 | async-start | bytes 2359296 | tf_op jit(solution)/shard_map/all_gather | solution.py:18
  69.8 57.1 %copy-start.10 = (f32[2048]{0:T(1024)S(1)}, f32[2048]{0:T(1024)}, u32[]{:S(2)}) copy-start(f32[2048]{0:T(1024)} %param.15) | copy-start | bytes 24580
  132.2 1.1 copy-start.5
  132.2 1.9 copy-start.3
  132.3 2.9 copy-start.7
  133.2 0.8 copy-start.1
  135.2 102.2 %all-gather.13.cloned.1.call-start = ((), (), s32[]{:S(2)}) async-start(), calls=%async_computation.3 | async-start | bytes 2359296 | tf_op jit(solution)/shard_map/all_gather | solution.py:26
  187.6 113.5 %all-gather.15.cloned.1.call-start = ((), (), s32[]{:S(2)}) async-start(), calls=%async_computation.4 | async-start | bytes 2359296 | tf_op jit(solution)/shard_map/all_gather | solution.py:18
  250.3 1.6 copy-start.2
  250.3 1.6 copy-start.4
  250.3 1.6 copy-start.6
  253.5 102.2 %all-gather.17.cloned.1.call-start = ((), (), s32[]{:S(2)}) async-start(), calls=%async_computation.5 | async-start | bytes 2359296 | tf_op jit(solution)/shard_map/all_gather | solution.py:26
  368.6 1.6 copy-start.8
Sparse Core Ops, SparseCore 0:
  10.1 53.7 all-gather.6
  68.8 49.2 all-gather.8
  135.3 47.4 all-gather.10
  187.8 49.5 all-gather.12
  253.6 47.4 all-gather.14
  306.1 49.5 all-gather.16
where the time goes:
time: 380 us; the launch traced here: 379 us
  waiting for transfers between devices  297 us (78%)
  matrix products  43.8 us (12%)
  local copies, waits for them, and re-layouts  19.8 us (5%)
  between operations  14.4 us (4%)
  other arithmetic  4.26 us (1%)
    all_gather x3, waiting for transfers between devices, local(): lax.all_gather(h_final, 'mp', axis=1, tiled=True)  148 us
    all_gather x3, waiting for transfers between devices, local(): lax.all_gather(inter_vals, 'mp', axis=1, tiled=True)  148 us
    dot_general x3, matrix products, local(): jnp.dot(lax.all_gather(inter_vals, 'mp', axis=1, tiled=True), gate_weight...  26.1 us
    dot_general x3, matrix products, local(): lax.dot_general(lax.all_gather(h_final, 'mp', axis=1, tiled=True), inter_...  14.5 us
  transfers between devices with their start and end apart: 6, of which 6 were waited for; matrix products, arithmetic and copies ran while one was open for 1% of the time, Pallas kernels for 0%

commit v1 on v0

v1 whole, which is shorter than its diff:
```python
import jax
import jax.numpy as jnp
from jax import lax
from jax.experimental import pallas as pl
from jax.experimental.pallas import tpu as pltpu
from jax.sharding import PartitionSpec as P

GATE_KINDS = 4
LANES = 128
MAX_RING = 8


def plain(
    byte_ids, h_start, c_start, inter_weight, inter_embed, gate_weight, gate_embed, gate_bias
):
    hidden = h_start
    cell = c_start
    for step in range(byte_ids.shape[0]):
        rows_here = hidden.shape[0]
        onehot = one_hot(byte_ids[step], inter_embed.shape[0])
        product = lax.dot_general(
            lax.all_gather(hidden, "mp", axis=1, tiled=True),
            inter_weight,
            (((1,), (1,)), ((), ())),
            preferred_element_type=jnp.float32,
        )
        lookup = jnp.dot(onehot, inter_embed, preferred_element_type=jnp.float32)
        inter_vals = (lookup * product).astype(jnp.bfloat16)
        gate_sums = jnp.dot(
            lax.all_gather(inter_vals, "mp", axis=1, tiled=True),
            gate_weight,
            preferred_element_type=jnp.float32,
        )
        gate_sums = (
            gate_sums
            + jnp.dot(onehot, gate_embed, preferred_element_type=jnp.float32)
            + gate_bias[None, :]
        )
        gate_sums = gate_sums.reshape(rows_here, gate_sums.shape[1] // GATE_KINDS, GATE_KINDS)
        hidden, cell = update_state([gate_sums[:, :, j] for j in range(GATE_KINDS)], cell)
    return hidden, cell


def one_hot(ids, vocab):
    return (ids[:, None] == jnp.arange(vocab, dtype=jnp.int32)[None, :]).astype(jnp.bfloat16)


def update_state(sums, cell):
    in_gate = jax.nn.sigmoid(sums[0])
    forget = jax.nn.sigmoid(sums[1])
    out_gate = jax.nn.sigmoid(sums[2])
    update = jnp.tanh(sums[3])
    cell = forget * cell + in_gate * update
    return (out_gate * jnp.tanh(cell)).astype(jnp.bfloat16), cell


def ring_of(devices):
    return list(range(0, devices, 2)) + list(range(devices - 1, 0, -2))


def ring_index(me, steps, devices):
    place = jnp.where(me % 2 == 0, me // 2, devices - 1 - me // 2)
    place = (place + steps + devices) % devices
    half = devices // 2
    return jnp.where(place < half, 2 * place, 2 * (devices - 1 - place) + 1)


def mix_into(mix_ref):
    group = mix_ref.shape[0]
    lanes = group // GATE_KINDS
    source = lax.broadcasted_iota(jnp.int32, (group, group), 0)
    target = lax.broadcasted_iota(jnp.int32, (group, group), 1)
    wanted = (target % lanes) * GATE_KINDS + target // lanes
    mix_ref[...] = (source == wanted).astype(jnp.float32).astype(jnp.bfloat16)


def sort_columns(block, mix, out_ref):
    group = mix.shape[0]
    lanes = group // GATE_KINDS
    units = out_ref.shape[1] // GATE_KINDS
    for g in range(units // lanes):
        mixed = jnp.dot(
            block[:, g * group : (g + 1) * group], mix, preferred_element_type=jnp.float32
        ).astype(out_ref.dtype)
        for j in range(GATE_KINDS):
            to = j * units + g * lanes
            out_ref[:, to : to + lanes] = mixed[:, j * lanes : (j + 1) * lanes]


def embed_kernel(embed_ref, bias_ref, out_ref, bias_out_ref, mix_ref):
    mix_into(mix_ref)
    sort_columns(embed_ref[...], mix_ref[...], out_ref)
    bias = jnp.broadcast_to(bias_ref[...], bias_out_ref.shape)
    high = bias.astype(jnp.bfloat16)
    left = bias - high.astype(jnp.float32)
    middle = left.astype(jnp.bfloat16)
    low = (left - middle.astype(jnp.float32)).astype(jnp.bfloat16)
    group = mix_ref.shape[0]
    lanes = group // GATE_KINDS
    units = out_ref.shape[1] // GATE_KINDS
    for g in range(units // lanes):
        here = slice(g * group, (g + 1) * group)
        mixed = [
            jnp.dot(term[:, here], mix_ref[...], preferred_element_type=jnp.float32)
            for term in (high, middle, low)
        ]
        mixed = (mixed[0] + mixed[1]) + mixed[2]
        for j in range(GATE_KINDS):
            to = j * units + g * lanes
            bias_out_ref[:, to : to + lanes] = mixed[:, j * lanes : (j + 1) * lanes]


def embed_by_gate(gate_embed, gate_bias):
    rows, columns = gate_embed.shape
    group = GATE_KINDS * LANES
    return pl.pallas_call(
        embed_kernel,
        out_shape=(
            jax.ShapeDtypeStruct((rows, columns), jnp.bfloat16),
            jax.ShapeDtypeStruct((8, columns), jnp.float32),
        ),
        scratch_shapes=[pltpu.VMEM((group, group), jnp.bfloat16)],
        compiler_params=pltpu.CompilerParams(vmem_limit_bytes=12 * 2**20),
        cost_estimate=pl.CostEstimate(
            flops=2 * rows * columns * group, bytes_accessed=4 * rows * columns, transcendentals=0
        ),
    )(gate_embed, gate_bias.reshape(1, columns))


def weight_kernel(me_ref, weight_ref, after_ref, out_ref, mix_ref):
    @pl.when(pl.program_id(0) == 0)
    def _():
        mix_into(mix_ref)

    sort_columns(weight_ref[...], mix_ref[...], out_ref)


def weight_by_gate(me, gate_weight, part, steps, devices, after):
    columns = gate_weight.shape[1]
    group = GATE_KINDS * LANES

    def block_at(i, me_ref):
        away = steps[0]
        for k in range(1, len(steps)):
            away = jnp.where(i == k, steps[k], away)
        return ring_index(me_ref[0], away, devices), 0

    return pl.pallas_call(
        weight_kernel,
        grid_spec=pltpu.PrefetchScalarGridSpec(
            num_scalar_prefetch=1,
            grid=(len(steps),),
            in_specs=[
                pl.BlockSpec((part, columns), block_at),
                pl.BlockSpec(memory_space=pl.ANY),
            ],
            out_specs=pl.BlockSpec((part, columns), lambda i, me_ref: (i, 0)),
            scratch_shapes=[pltpu.VMEM((group, group), jnp.bfloat16)],
        ),
        out_shape=jax.ShapeDtypeStruct((len(steps) * part, columns), jnp.bfloat16),
        compiler_params=pltpu.CompilerParams(vmem_limit_bytes=14 * 2**20),
        cost_estimate=pl.CostEstimate(
            flops=2 * len(steps) * part * columns * group,
            bytes_accessed=4 * len(steps) * part * columns,
            transcendentals=0,
        ),
    )(me, gate_weight, after)


def turn_kernel(me_ref, weight_ref, out_ref):
    out_ref[...] = weight_ref[...].T


def turned(me, inter_weight, part, away, devices):
    rows, columns = inter_weight.shape

    def block_at(i, me_ref):
        steps = jnp.where(i % 2 == 1, -((i + 1) // 2), i // 2)
        return 0, ring_index(me_ref[0], steps, devices)

    assert away == [(-((i + 1) // 2) if i % 2 else i // 2) % devices for i in range(devices)]
    return pl.pallas_call(
        turn_kernel,
        grid_spec=pltpu.PrefetchScalarGridSpec(
            num_scalar_prefetch=1,
            grid=(columns // part,),
            in_specs=[pl.BlockSpec((rows, part), block_at)],
            out_specs=pl.BlockSpec((part, rows), lambda i, me_ref: (i, 0)),
        ),
        out_shape=jax.ShapeDtypeStruct((columns, rows), jnp.bfloat16),
        compiler_params=pltpu.CompilerParams(vmem_limit_bytes=8 * 2**20),
        cost_estimate=pl.CostEstimate(
            flops=0, bytes_accessed=4 * rows * columns, transcendentals=0
        ),
    )(me, inter_weight)


def arrivals(block, ring, last):
    devices = len(ring)
    up = [(ring[i], ring[(i + 1) % devices]) for i in range(devices)]
    down = [(b, a) for a, b in up]
    groups = [[block]]
    below = above = block
    for _ in range(devices // 2 - 1):
        below = lax.ppermute(below, "mp", up)
        above = lax.ppermute(above, "mp", down)
        groups.append([below, above])
    if last == "up":
        farthest = lax.ppermute(below, "mp", up)
    elif last == "down":
        farthest = lax.ppermute(above, "mp", down)
    else:
        half = block.shape[0] // 2
        farthest = jnp.concatenate(
            [lax.ppermute(below[:half], "mp", up), lax.ppermute(above[half:], "mp", down)], 0
        )
    return groups + [[farthest]]


def dot32(a, b):
    return jnp.dot(a, b, preferred_element_type=jnp.float32)


def gathered_dot(arrived, weights, total=None):
    for k in range(len(weights) - 1):
        block = jnp.concatenate([jnp.concatenate(groups[k], 1) for groups in arrived], 0)
        term = dot32(block, weights[k])
        total = term if total is None else total + term
    rows = arrived[0][0][0].shape[0]
    return [
        total[c * rows : (c + 1) * rows] + dot32(groups[-1][0], weights[-1])
        for c, groups in enumerate(arrived)
    ]


def ringed(devices, chunks):
    ring = ring_of(devices)
    groups_away = [[0]] + [[-k, k] for k in range(1, devices // 2)] + [[devices // 2]]

    def local(
        byte_ids, h_start, c_start, inter_weight, inter_embed, gate_weight, gate_embed, gate_bias
    ):
        steps, streams = byte_ids.shape
        part = h_start.shape[1]
        rows = streams // chunks
        me = jnp.full((1,), lax.axis_index("mp"), jnp.int32)
        arrived = [arrivals(h_start, ring, "both")]
        weight_in = turned(
            me, inter_weight, part, [a % devices for g in groups_away for a in g], devices
        )
        ends = [0]
        for away in groups_away:
            ends.append(ends[-1] + len(away) * part)
        weights_in = [weight_in[ends[k] : ends[k + 1]] for k in range(len(groups_away))]
        embed, bias = embed_by_gate(gate_embed, gate_bias)
        weights_gate = [
            weight_by_gate(me, gate_weight, part, away, devices, arrived[0][min(k + 1, len(groups_away) - 1)][-1])
            for k, away in enumerate(groups_away)
        ]
        onehot = one_hot(byte_ids.reshape(-1), inter_embed.shape[0])
        lookup = dot32(onehot, inter_embed).astype(jnp.bfloat16)
        cells = [c_start[c * rows : (c + 1) * rows] for c in range(chunks)]
        ways = ["up" if c % 2 == 0 else "down" for c in range(chunks)] if chunks > 1 else ["both"]
        for step in range(steps):
            at = step * streams
            products = gathered_dot(arrived, weights_in)
            if len(products) < chunks:
                products = [products[0][c * rows : (c + 1) * rows] for c in range(chunks)]
            inters = [
                (lookup[at + c * rows : at + (c + 1) * rows].astype(jnp.float32) * product).astype(
                    jnp.bfloat16
                )
                for c, product in enumerate(products)
            ]
            arrived = [arrivals(inter, ring, way) for inter, way in zip(inters, ways)]
            sums = gathered_dot(arrived, weights_gate, dot32(onehot[at : at + streams], embed))
            hiddens = []
            for c in range(chunks):
                full = sums[c] + bias[:1]
                hidden, cells[c] = update_state(
                    [full[:, j * part : (j + 1) * part] for j in range(GATE_KINDS)], cells[c]
                )
                hiddens.append(hidden)
            if step + 1 < steps:
                arrived = [arrivals(hidden, ring, way) for hidden, way in zip(hiddens, ways)]
        return jnp.concatenate(hiddens, 0), jnp.concatenate(cells, 0)

    return local


def solution(mesh):
    in_specs = (
        P(None, ("groups", "batch")),
        P(("groups", "batch"), "mp"),
        P(("groups", "batch"), "mp"),
        P("mp", None),
        P(None, "mp"),
        P(None, "mp"),
        P(None, "mp"),
        P("mp"),
    )
    out_specs = (P(("groups", "batch"), "mp"), P(("groups", "batch"), "mp"))
    devices = mesh.shape["mp"]
    local = ringed(devices, 2) if 2 < devices <= MAX_RING else plain
    return jax.shard_map(local, mesh=mesh, in_specs=in_specs, out_specs=out_specs, check_vma=False)
```

time: 380 us -> 177 us (0.47)
  waiting for transfers between devices: 297 us -> 37.4 us
  starting transfers between devices: 0.64 us -> 80.9 us
  matrix products: 43.8 us -> 26.2 us
  Pallas kernels: 0 us -> 14.6 us
  between operations: 14.4 us -> 1.34 us
  local copies, waits for them, and re-layouts: 19.8 us -> 13.2 us
    all_gather x6 -> x0, waiting for transfers between devices: 296 us -> none  [the longest x3 148 us: local(): lax.all_gather(h_final, 'mp', axis=1, tiled=True)]
    ppermute x0 -> x78, starting transfers between devices: none -> 80.9 us  [the longest x33 35.9 us: arrivals(): below = lax.ppermute(below, 'mp', up)]
    ppermute x0 -> x78, waiting for transfers between devices: none -> 37.4 us  [the longest x33 17.7 us: arrivals(): below = lax.ppermute(below, 'mp', up)]
    dot_general x12 -> x39, matrix products: 43.8 us -> 26.2 us  [dot32(): return jnp.dot(a, b, preferred_element_type=jnp.float32)]
    pallas_call x0 -> x7, Pallas kernels: none -> 14.6 us  [the longest x5 10.7 us: weight_by_gate(): pl.pallas_call(weight_kernel, grid_spec=pltpu.PrefetchScalarGridSpec(num_...]
    unnamed x25 -> x35, local copies, waits for them, and re-layouts: 3.67 us -> 12.5 us
    reshape x3 -> x0, local copies, waits for them, and re-layouts: 5.58 us -> none  [local(): gate_sums = gate_sums.reshape(rows_here, gate_sums.shape[1] // 4, 4)]
    add x3 -> x0, local copies, waits for them, and re-layouts: 5.55 us -> none  [local(): gate_sums + jnp.dot(onehot, gate_embed, preferred_element_type=jnp.float32)]
  transfers between devices with their start and end apart: 6 -> 78, of which waited for: 6 -> 36; matrix products, arithmetic and copies ran while one was open for 1% -> 15% of each run, Pallas kernels for 0% -> 8%
where the time goes in v1:
time: 177 us
  starting transfers between devices  80.9 us (46%)
  waiting for transfers between devices  37.4 us (21%)
  matrix products  26.2 us (15%)
  Pallas kernels  14.6 us (8%)
  local copies, waits for them, and re-layouts  13.2 us (7%)
  other arithmetic  3.51 us (2%)
    ppermute x33, starting transfers between devices, arrivals(): below = lax.ppermute(below, 'mp', up)  35.9 us
    ppermute x33, starting transfers between devices, arrivals(): above = lax.ppermute(above, 'mp', down)  32.5 us
    dot_general x39, matrix products, dot32(): return jnp.dot(a, b, preferred_element_type=jnp.float32)  26.2 us
    ppermute x33, waiting for transfers between devices, arrivals(): below = lax.ppermute(below, 'mp', up)  17.7 us
    ppermute x33, waiting for transfers between devices, arrivals(): above = lax.ppermute(above, 'mp', down)  13.3 us
    unnamed x35, local copies, waits for them, and re-layouts  12.5 us
    pallas_call x5, Pallas kernels, weight_by_gate(): pl.pallas_call(weight_kernel, grid_spec=pltpu.PrefetchScalarGridSpec(num_...  10.7 us
    ppermute x5, starting transfers between devices, arrivals(): farthest = lax.ppermute(below, 'mp', up)  5.74 us
  transfers between devices with their start and end apart: 78, of which 36 were waited for; matrix products, arithmetic and copies ran while one was open for 15% of the time, Pallas kernels for 8%

profile of v1, /device:TPU:0, one launch (start us, length us, event | category | flops | bytes accessed | tf_op | source)
XLA Modules:
  0.0 177.1 jit_solution(11908980202451946271)
XLA Ops:
  0.6 3.0 %collective-permute-start.1 = (bf16[256,512]{1,0:T(8,128)(2,1)}, bf16[256,512]{1,0:T(8,128)(2,1)S(1)}, u32[]{:S(2)}, u32[]{:S(2)}) collective-permute-start(bf16[256,512]{1,0:T(8,128)(2,1)} %param.9), channel_id=1, source_target_pairs={{4,0},{8,4},{12,8},{14,12},{10,14},{6,10},{2,6},{0,2},{5,1},{9,5},... | collective-permute-start | bytes 786440 | tf_op jit(solution)/shard_map/ppermute | solution.py:206
  6.6 1.5 shard_map.95
  8.1 1.8 %fusion.256 = f32[256,2048]{1,0:T(8,128)} fusion(bf16[256,2048]{1,0:T(8,128)(2,1)S(1)} %get-tuple-element.4, pred[768,256]{1,0:T(32,128)(4,1)S(1)} %iota_compare_fusion), kind=kOutput, calls=%fused_computation.315 | convolution fusion | flops 268435456 | bytes 3211264 | tf_op jit(solution)/shard_map/dot_general | solution.py:221
  10.3 2.2 %copy-done.3 = bf16[512,4096]{1,0:T(8,128)(2,1)S(1)} copy-done((bf16[512,4096]{1,0:T(8,128)(2,1)S(1)}, bf16[512,4096]{1,0:T(8,128)(2,1)}, u32[]{:S(2)}) %copy-start.3) | copy-done | bytes 4194328
  12.5 2.3 %shard_map.96 = bf16[4096,512]{1,0:T(8,128)(2,1)S(1)} custom-call(s32[1]{0:T(128)} %bitcast.1.me_ref, bf16[512,4096]{1,0:T(8,128)(2,1)S(1)} %copy-done.3), custom_call_target="tpu_custom_call" | custom-call | bytes 8388608 | tf_op jit(solution)/shard_map/pallas_call | solution.py:182
  15.2 1.9 %collective-permute-start.3 = (bf16[256,512]{1,0:T(8,128)(2,1)S(1)}, bf16[256,512]{1,0:T(8,128)(2,1)S(1)}, u32[]{:S(2)}, u32[]{:S(2)}) collective-permute-start(bf16[256,512]{1,0:T(8,128)(2,1)S(1)} %collective-permute-done.1.after_ref), channel_id=1, source_target_pairs={{4,0},{8,4},{12,8},{14,12},{10,14},{6,10},{2,6},{0,2},{5,1},{9,5},... | collective-permute-start | bytes 786440 | tf_op jit(solution)/shard_map/ppermute | solution.py:206
  17.7 5.8 %copy-done.2 = bf16[4096,2048]{1,0:T(8,128)(2,1)S(1)} copy-done((bf16[4096,2048]{1,0:T(8,128)(2,1)S(1)}, bf16[4096,2048]{1,0:T(8,128)(2,1)}, u32[]{:S(2)}) %copy-start.2) | copy-done | bytes 16777240
  24.7 1.9 %collective-permute-start.5 = (bf16[256,512]{1,0:T(8,128)(2,1)S(1)}, bf16[256,512]{1,0:T(8,128)(2,1)S(1)}, u32[]{:S(2)}, u32[]{:S(2)}) collective-permute-start(bf16[256,512]{1,0:T(8,128)(2,1)S(1)} %collective-permute-done.3.after_ref), channel_id=1, source_target_pairs={{4,0},{8,4},{12,8},{14,12},{10,14},{6,10},{2,6},{0,2},{5,1},{9,5},... | collective-permute-start | bytes 786440 | tf_op jit(solution)/shard_map/ppermute | solution.py:206
  26.7 2.7 %shard_map.98 = bf16[1024,2048]{1,0:T(8,128)(2,1)S(1)} custom-call(s32[1]{0:T(128)} %bitcast.1.me_ref, bf16[4096,2048]{1,0:T(8,128)(2,1)S(1)} %copy-done.2, bf16[256,512]{1,0:T(8,128)(2,1)S(1)} %collective-permute-done.3.after_ref), custom_call_target="tpu_custom_call" | custom-call | flops 2147483648 | bytes 8388608 | tf_op jit(solution)/shard_map/pallas_call | solution.py:148
  30.1 1.9 %collective-permute-done.5.after_ref = bf16[256,512]{1,0:T(8,128)(2,1)S(1)} collective-permute-done((bf16[256,512]{1,0:T(8,128)(2,1)S(1)}, bf16[256,512]{1,0:T(8,128)(2,1)S(1)}, u32[]{:S(2)}, u32[]{:S(2)}) %collective-permute-start.5) | collective-permute-done | bytes 262176 | tf_op jit(solution)/shard_map/ppermute | solution.py:206
  32.0 1.6 collective-permute-start.7
  33.7 2.4 %collective-permute-done.4 = bf16[256,512]{1,0:T(8,128)(2,1)S(1)} collective-permute-done((bf16[256,512]{1,0:T(8,128)(2,1)S(1)}, bf16[256,512]{1,0:T(8,128)(2,1)S(1)}, u32[]{:S(2)}, u32[]{:S(2)}) %collective-permute-start.4) | collective-permute-done | bytes 262176 | tf_op jit(solution)/shard_map/ppermute | solution.py:205
  36.6 2.7 %shard_map.99 = bf16[1024,2048]{1,0:T(8,128)(2,1)S(1)} custom-call(s32[1]{0:T(128)} %bitcast.1.me_ref, bf16[4096,2048]{1,0:T(8,128)(2,1)S(1)} %copy-done.2, bf16[256,512]{1,0:T(8,128)(2,1)S(1)} %collective-permute-done.5.after_ref), custom_call_target="tpu_custom_call" | custom-call | flops 2147483648 | bytes 8388608 | tf_op jit(solution)/shard_map/pallas_call | solution.py:148
  39.4 1.8 %collective-permute-done.6 = bf16[128,512]{1,0:T(8,128)(2,1)S(1)} collective-permute-done((bf16[128,512]{1,0:T(8,128)(2,1)S(1)}, bf16[128,512]{1,0:T(8,128)(2,1)S(1)}, u32[]{:S(2)}, u32[]{:S(2)}) %collective-permute-start.6) | collective-permute-done | bytes 131104 | tf_op jit(solution)/shard_map/ppermute | solution.py:215
  46.9 3.3 %collective-permute-done.8 = bf16[128,512]{1,0:T(8,128)(2,1)S(1)} collective-permute-done((bf16[128,512]{1,0:T(8,128)(2,1)S(1)}, bf16[128,512]{1,0:T(8,128)(2,1)S(1)}, u32[]{:S(2)}, u32[]{:S(2)}) %collective-permute-start.8) | collective-permute-done | bytes 131104 | tf_op jit(solution)/shard_map/ppermute | solution.py:205
  50.2 1.4 collective-permute-start.12
  52.2 1.6 collective-permute-start.13
  54.3 2.7 %shard_map.100 = bf16[1024,2048]{1,0:T(8,128)(2,1)S(1)} custom-call(s32[1]{0:T(128)} %bitcast.1.me_ref, bf16[4096,2048]{1,0:T(8,128)(2,1)S(1)} %bitcast.40, bf16[256,512]{1,0:T(8,128)(2,1)S(1)} %constant_dynamic-update-slice_fusion.after_ref), custom_call_target="tpu_custom_call" | custom-call | flops 2147483648 | bytes 8388608 | tf_op jit(solution)/shard_map/pallas_call | solution.py:148
  57.0 2.0 %copy-done.6 = bf16[1024,2048]{1,0:T(8,128)(2,1)} copy-done((bf16[1024,2048]{1,0:T(8,128)(2,1)}, bf16[1024,2048]{1,0:T(8,128)(2,1)S(1)}, u32[]{:S(2)}) %copy-start.6) | copy-done | bytes 4194328
  60.3 1.5 collective-permute-start.16
  62.4 1.6 collective-permute-start.17
  64.5 1.4 convolution_add_fusion.8
  67.5 1.3 collective-permute-start.20
  71.1 1.4 fusion
  75.2 1.6 collective-permute-start.22
  77.3 1.6 collective-permute-start.24
  79.7 1.9 %collective-permute-done.22 = bf16[128,512]{1,0:T(8,128)(2,1)S(1)} collective-permute-done((bf16[128,512]{1,0:T(8,128)(2,1)S(1)}, bf16[128,512]{1,0:T(8,128)(2,1)S(1)}, u32[]{:S(2)}, u32[]{:S(2)}) %collective-permute-start.22) | collective-permute-done | bytes 131104 | tf_op jit(solution)/shard_map/ppermute | solution.py:205
  81.6 1.3 collective-permute-start.26
  89.0 1.7 collective-permute-done.28
  90.9 1.9 %collective-permute-start.33 = (bf16[128,512]{1,0:T(8,128)(2,1)S(1)}, bf16[128,512]{1,0:T(8,128)(2,1)S(1)}, u32[]{:S(2)}, u32[]{:S(2)}) collective-permute-start(bf16[128,512]{1,0:T(8,128)(2,1)S(1)} %collective-permute-done.29), channel_id=1, source_target_pairs={{4,0},{8,4},{12,8},{14,12},{10,14},{6,10},{2,6},{0,2},{5,1},{9,5},... | collective-permute-start | bytes 393224 | tf_op jit(solution)/shard_map/ppermute | solution.py:206
  94.2 2.4 %collective-permute-done.33 = bf16[128,512]{1,0:T(8,128)(2,1)S(1)} collective-permute-done((bf16[128,512]{1,0:T(8,128)(2,1)S(1)}, bf16[128,512]{1,0:T(8,128)(2,1)S(1)}, u32[]{:S(2)}, u32[]{:S(2)}) %collective-permute-start.33) | collective-permute-done | bytes 131104 | tf_op jit(solution)/shard_map/ppermute | solution.py:206
  96.7 1.8 %collective-permute-start.35 = (bf16[128,512]{1,0:T(8,128)(2,1)S(1)}, bf16[128,512]{1,0:T(8,128)(2,1)S(1)}, u32[]{:S(2)}, u32[]{:S(2)}) collective-permute-start(bf16[128,512]{1,0:T(8,128)(2,1)S(1)} %collective-permute-done.33), channel_id=1, source_target_pairs={{4,0},{8,4},{12,8},{14,12},{10,14},{6,10},{2,6},{0,2},{5,1},{9,5},... | collective-permute-start | bytes 393224 | tf_op jit(solution)/shard_map/ppermute | solution.py:211
  100.2 1.9 %collective-permute-start.37 = (bf16[128,512]{1,0:T(8,128)(2,1)S(1)}, bf16[128,512]{1,0:T(8,128)(2,1)S(1)}, u32[]{:S(2)}, u32[]{:S(2)}) collective-permute-start(bf16[128,512]{1,0:T(8,128)(2,1)S(1)} %fusion.17), channel_id=1, source_target_pairs={{4,0},{8,4},{12,8},{14,12},{10,14},{6,10},{2,6},{0,2},{5,1},{9,5},... | collective-permute-start | bytes 393224 | tf_op jit(solution)/shard_map/ppermute | solution.py:206
  102.9 1.3 collective-permute-start.38
  116.4 1.4 convolution_add_fusion.6
  119.1 2.9 %collective-permute-done.47 = bf16[128,512]{1,0:T(8,128)(2,1)S(1)} collective-permute-done((bf16[128,512]{1,0:T(8,128)(2,1)S(1)}, bf16[128,512]{1,0:T(8,128)(2,1)S(1)}, u32[]{:S(2)}, u32[]{:S(2)}) %collective-permute-start.47) | collective-permute-done | bytes 131104 | tf_op jit(solution)/shard_map/ppermute | solution.py:206
  122.9 1.3 fusion.93
  132.2 1.5 collective-permute-start.54
  145.5 2.4 %collective-permute-done.61 = bf16[128,512]{1,0:T(8,128)(2,1)S(1)} collective-permute-done((bf16[128,512]{1,0:T(8,128)(2,1)S(1)}, bf16[128,512]{1,0:T(8,128)(2,1)S(1)}, u32[]{:S(2)}, u32[]{:S(2)}) %collective-permute-start.61) | collective-permute-done | bytes 131104 | tf_op jit(solution)/shard_map/ppermute | solution.py:206
  153.1 1.8 %collective-permute-start.66 = (bf16[128,512]{1,0:T(8,128)(2,1)S(1)}, bf16[128,512]{1,0:T(8,128)(2,1)S(1)}, u32[]{:S(2)}, u32[]{:S(2)}) collective-permute-start(bf16[128,512]{1,0:T(8,128)(2,1)S(1)} %fusion.14), channel_id=1, source_target_pairs={{0,4},{4,8},{8,12},{12,14},{14,10},{10,6},{6,2},{2,0},{1,5},{5,9},... | collective-permute-start | bytes 393224 | tf_op jit(solution)/shard_map/ppermute | solution.py:205
  155.6 1.8 %collective-permute-start.68 = (bf16[128,512]{1,0:T(8,128)(2,1)S(1)}, bf16[128,512]{1,0:T(8,128)(2,1)S(1)}, u32[]{:S(2)}, u32[]{:S(2)}) collective-permute-start(bf16[128,512]{1,0:T(8,128)(2,1)S(1)} %collective-permute-done.64), channel_id=1, source_target_pairs={{0,4},{4,8},{8,12},{12,14},{14,10},{10,6},{6,2},{2,0},{1,5},{5,9},... | collective-permute-start | bytes 393224 | tf_op jit(solution)/shard_map/ppermute | solution.py:205
  158.1 1.7 collective-permute-start.70
  160.9 1.8 %collective-permute-start.72 = (bf16[128,512]{1,0:T(8,128)(2,1)S(1)}, bf16[128,512]{1,0:T(8,128)(2,1)S(1)}, u32[]{:S(2)}, u32[]{:S(2)}) collective-permute-start(bf16[128,512]{1,0:T(8,128)(2,1)S(1)} %collective-permute-done.68), channel_id=1, source_target_pairs={{0,4},{4,8},{8,12},{12,14},{14,10},{10,6},{6,2},{2,0},{1,5},{5,9},... | collective-permute-start | bytes 393224 | tf_op jit(solution)/shard_map/ppermute | solution.py:205
  163.1 1.7 collective-permute-start.74
  165.1 1.4 convolution_add_fusion.4
  166.5 1.8 %collective-permute-start.76 = (bf16[128,512]{1,0:T(8,128)(2,1)S(1)}, bf16[128,512]{1,0:T(8,128)(2,1)S(1)}, u32[]{:S(2)}, u32[]{:S(2)}) collective-permute-start(bf16[128,512]{1,0:T(8,128)(2,1)S(1)} %collective-permute-done.72), channel_id=1, source_target_pairs={{0,4},{4,8},{8,12},{12,14},{14,10},{10,6},{6,2},{2,0},{1,5},{5,9},... | collective-permute-start | bytes 393224 | tf_op jit(solution)/shard_map/ppermute | solution.py:209
  168.3 1.5 collective-permute-done.75
  171.3 1.4 fusion.2
  (204 shorter events, 82.0 us)
Async XLA Ops:
  0.6 14.5 %collective-permute-start.1 = (bf16[256,512]{1,0:T(8,128)(2,1)}, bf16[256,512]{1,0:T(8,128)(2,1)S(1)}, u32[]{:S(2)}, u32[]{:S(2)}) collective-permute-start(bf16[256,512]{1,0:T(8,128)(2,1)} %param.9), channel_id=1, source_target_pairs={{4,0},{8,4},{12,8},{14,12},{10,14},{6,10},{2,6},{0,2},{5,1},{9,5},... | collective-permute-start | bytes 786440 | tf_op jit(solution)/shard_map/ppermute | solution.py:206
  3.6 13.4 %collective-permute-start = (bf16[256,512]{1,0:T(8,128)(2,1)}, bf16[256,512]{1,0:T(8,128)(2,1)S(1)}, u32[]{:S(2)}, u32[]{:S(2)}) collective-permute-start(bf16[256,512]{1,0:T(8,128)(2,1)} %param.9), channel_id=1, source_target_pairs={{0,4},{4,8},{8,12},{12,14},{14,10},{10,6},{6,2},{2,0},{1,5},{5,9},... | collective-permute-start | bytes 786440 | tf_op jit(solution)/shard_map/ppermute | solution.py:205
  15.2 9.6 %collective-permute-start.3 = (bf16[256,512]{1,0:T(8,128)(2,1)S(1)}, bf16[256,512]{1,0:T(8,128)(2,1)S(1)}, u32[]{:S(2)}, u32[]{:S(2)}) collective-permute-start(bf16[256,512]{1,0:T(8,128)(2,1)S(1)} %collective-permute-done.1.after_ref), channel_id=1, source_target_pairs={{4,0},{8,4},{12,8},{14,12},{10,14},{6,10},{2,6},{0,2},{5,1},{9,5},... | collective-permute-start | bytes 786440 | tf_op jit(solution)/shard_map/ppermute | solution.py:206
  17.1 12.3 %collective-permute-start.2 = (bf16[256,512]{1,0:T(8,128)(2,1)S(1)}, bf16[256,512]{1,0:T(8,128)(2,1)S(1)}, u32[]{:S(2)}, u32[]{:S(2)}) collective-permute-start(bf16[256,512]{1,0:T(8,128)(2,1)S(1)} %collective-permute-done), channel_id=1, source_target_pairs={{0,4},{4,8},{8,12},{12,14},{14,10},{10,6},{6,2},{2,0},{1,5},{5,9},... | collective-permute-start | bytes 786440 | tf_op jit(solution)/shard_map/ppermute | solution.py:205
  24.7 7.3 %collective-permute-start.5 = (bf16[256,512]{1,0:T(8,128)(2,1)S(1)}, bf16[256,512]{1,0:T(8,128)(2,1)S(1)}, u32[]{:S(2)}, u32[]{:S(2)}) collective-permute-start(bf16[256,512]{1,0:T(8,128)(2,1)S(1)} %collective-permute-done.3.after_ref), channel_id=1, source_target_pairs={{4,0},{8,4},{12,8},{14,12},{10,14},{6,10},{2,6},{0,2},{5,1},{9,5},... | collective-permute-start | bytes 786440 | tf_op jit(solution)/shard_map/ppermute | solution.py:206
  29.4 6.7 %collective-permute-start.4 = (bf16[256,512]{1,0:T(8,128)(2,1)S(1)}, bf16[256,512]{1,0:T(8,128)(2,1)S(1)}, u32[]{:S(2)}, u32[]{:S(2)}) collective-permute-start(bf16[256,512]{1,0:T(8,128)(2,1)S(1)} %collective-permute-done.2), channel_id=1, source_target_pairs={{0,4},{4,8},{8,12},{12,14},{14,10},{10,6},{6,2},{2,0},{1,5},{5,9},... | collective-permute-start | bytes 786440 | tf_op jit(solution)/shard_map/ppermute | solution.py:205
  32.0 9.1 %collective-permute-start.7 = (bf16[128,512]{1,0:T(8,128)(2,1)S(1)}, bf16[128,512]{1,0:T(8,128)(2,1)S(1)}, u32[]{:S(2)}, u32[]{:S(2)}) collective-permute-start(bf16[128,512]{1,0:T(8,128)(2,1)S(1)} %slice.236), channel_id=1, source_target_pairs={{4,0},{8,4},{12,8},{14,12},{10,14},{6,10},{2,6},{0,2},{5,1},{9,5},... | collective-permute-start | bytes 393224 | tf_op jit(solution)/shard_map/ppermute | solution.py:215
  42.0 11.7 %collective-permute-start.10 = (bf16[128,512]{1,0:T(8,128)(2,1)S(1)}, bf16[128,512]{1,0:T(8,128)(2,1)S(1)}, u32[]{:S(2)}, u32[]{:S(2)}) collective-permute-start(bf16[128,512]{1,0:T(8,128)(2,1)S(1)} %get-tuple-element.19), channel_id=1, source_target_pairs={{0,4},{4,8},{8,12},{12,14},{14,10},{10,6},{6,2},{2,0},{1,5},{5,9},... | collective-permute-start | bytes 393224 | tf_op jit(solution)/shard_map/ppermute | solution.py:205
  43.3 8.3 %collective-permute-start.11 = (bf16[128,512]{1,0:T(8,128)(2,1)S(1)}, bf16[128,512]{1,0:T(8,128)(2,1)S(1)}, u32[]{:S(2)}, u32[]{:S(2)}) collective-permute-start(bf16[128,512]{1,0:T(8,128)(2,1)S(1)} %get-tuple-element.19), channel_id=1, source_target_pairs={{4,0},{8,4},{12,8},{14,12},{10,14},{6,10},{2,6},{0,2},{5,1},{9,5},... | collective-permute-start | bytes 393224 | tf_op jit(solution)/shard_map/ppermute | solution.py:206
  45.3 6.9 %collective-permute-start.9 = (bf16[128,512]{1,0:T(8,128)(2,1)S(1)}, bf16[128,512]{1,0:T(8,128)(2,1)S(1)}, u32[]{:S(2)}, u32[]{:S(2)}) collective-permute-start(bf16[128,512]{1,0:T(8,128)(2,1)S(1)} %get-tuple-element.18), channel_id=1, source_target_pairs={{4,0},{8,4},{12,8},{14,12},{10,14},{6,10},{2,6},{0,2},{5,1},{9,5},... | collective-permute-start | bytes 393224 | tf_op jit(solution)/shard_map/ppermute | solution.py:206
  50.2 10.1 %collective-permute-start.12 = (bf16[128,512]{1,0:T(8,128)(2,1)S(1)}, bf16[128,512]{1,0:T(8,128)(2,1)S(1)}, u32[]{:S(2)}, u32[]{:S(2)}) collective-permute-start(bf16[128,512]{1,0:T(8,128)(2,1)S(1)} %collective-permute-done.8), channel_id=1, source_target_pairs={{0,4},{4,8},{8,12},{12,14},{14,10},{10,6},{6,2},{2,0},{1,5},{5,9},... | collective-permute-start | bytes 393224 | tf_op jit(solution)/shard_map/ppermute | solution.py:205
  51.6 10.2 %collective-permute-start.15 = (bf16[128,512]{1,0:T(8,128)(2,1)S(1)}, bf16[128,512]{1,0:T(8,128)(2,1)S(1)}, u32[]{:S(2)}, u32[]{:S(2)}) collective-permute-start(bf16[128,512]{1,0:T(8,128)(2,1)S(1)} %collective-permute-done.11), channel_id=1, source_target_pairs={{4,0},{8,4},{12,8},{14,12},{10,14},{6,10},{2,6},{0,2},{5,1},{9,5},... | collective-permute-start | bytes 393224 | tf_op jit(solution)/shard_map/ppermute | solution.py:206
  52.2 10.2 %collective-permute-start.13 = (bf16[128,512]{1,0:T(8,128)(2,1)S(1)}, bf16[128,512]{1,0:T(8,128)(2,1)S(1)}, u32[]{:S(2)}, u32[]{:S(2)}) collective-permute-start(bf16[128,512]{1,0:T(8,128)(2,1)S(1)} %collective-permute-done.9), channel_id=1, source_target_pairs={{4,0},{8,4},{12,8},{14,12},{10,14},{6,10},{2,6},{0,2},{5,1},{9,5},... | collective-permute-start | bytes 393224 | tf_op jit(solution)/shard_map/ppermute | solution.py:206
  53.8 10.2 %collective-permute-start.14 = (bf16[128,512]{1,0:T(8,128)(2,1)S(1)}, bf16[128,512]{1,0:T(8,128)(2,1)S(1)}, u32[]{:S(2)}, u32[]{:S(2)}) collective-permute-start(bf16[128,512]{1,0:T(8,128)(2,1)S(1)} %collective-permute-done.10), channel_id=1, source_target_pairs={{0,4},{4,8},{8,12},{12,14},{14,10},{10,6},{6,2},{2,0},{1,5},{5,9},... | collective-permute-start | bytes 393224 | tf_op jit(solution)/shard_map/ppermute | solution.py:205
  60.3 7.2 %collective-permute-start.16 = (bf16[128,512]{1,0:T(8,128)(2,1)S(1)}, bf16[128,512]{1,0:T(8,128)(2,1)S(1)}, u32[]{:S(2)}, u32[]{:S(2)}) collective-permute-start(bf16[128,512]{1,0:T(8,128)(2,1)S(1)} %collective-permute-done.12), channel_id=1, source_target_pairs={{0,4},{4,8},{8,12},{12,14},{14,10},{10,6},{6,2},{2,0},{1,5},{5,9},... | collective-permute-start | bytes 393224 | tf_op jit(solution)/shard_map/ppermute | solution.py:205
  62.4 6.4 %collective-permute-start.17 = (bf16[128,512]{1,0:T(8,128)(2,1)S(1)}, bf16[128,512]{1,0:T(8,128)(2,1)S(1)}, u32[]{:S(2)}, u32[]{:S(2)}) collective-permute-start(bf16[128,512]{1,0:T(8,128)(2,1)S(1)} %collective-permute-done.13), channel_id=1, source_target_pairs={{4,0},{8,4},{12,8},{14,12},{10,14},{6,10},{2,6},{0,2},{5,1},{9,5},... | collective-permute-start | bytes 393224 | tf_op jit(solution)/shard_map/ppermute | solution.py:206
  66.8 6.4 %collective-permute-start.21 = (bf16[128,512]{1,0:T(8,128)(2,1)S(1)}, bf16[128,512]{1,0:T(8,128)(2,1)S(1)}, u32[]{:S(2)}, u32[]{:S(2)}) collective-permute-start(bf16[128,512]{1,0:T(8,128)(2,1)S(1)} %collective-permute-done.19), channel_id=1, source_target_pairs={{4,0},{8,4},{12,8},{14,12},{10,14},{6,10},{2,6},{0,2},{5,1},{9,5},... | collective-permute-start | bytes 393224 | tf_op jit(solution)/shard_map/ppermute | solution.py:211
  67.5 6.1 %collective-permute-start.20 = (bf16[128,512]{1,0:T(8,128)(2,1)S(1)}, bf16[128,512]{1,0:T(8,128)(2,1)S(1)}, u32[]{:S(2)}, u32[]{:S(2)}) collective-permute-start(bf16[128,512]{1,0:T(8,128)(2,1)S(1)} %collective-permute-done.16), channel_id=1, source_target_pairs={{0,4},{4,8},{8,12},{12,14},{14,10},{10,6},{6,2},{2,0},{1,5},{5,9},... | collective-permute-start | bytes 393224 | tf_op jit(solution)/shard_map/ppermute | solution.py:209
  75.2 6.4 %collective-permute-start.22 = (bf16[128,512]{1,0:T(8,128)(2,1)S(1)}, bf16[128,512]{1,0:T(8,128)(2,1)S(1)}, u32[]{:S(2)}, u32[]{:S(2)}) collective-permute-start(bf16[128,512]{1,0:T(8,128)(2,1)S(1)} %get-tuple-element.14), channel_id=1, source_target_pairs={{0,4},{4,8},{8,12},{12,14},{14,10},{10,6},{6,2},{2,0},{1,5},{5,9},... | collective-permute-start | bytes 393224 | tf_op jit(solution)/shard_map/ppermute | solution.py:205
  76.9 6.1 %collective-permute-start.23 = (bf16[128,512]{1,0:T(8,128)(2,1)S(1)}, bf16[128,512]{1,0:T(8,128)(2,1)S(1)}, u32[]{:S(2)}, u32[]{:S(2)}) collective-permute-start(bf16[128,512]{1,0:T(8,128)(2,1)S(1)} %get-tuple-element.14), channel_id=1, source_target_pairs={{4,0},{8,4},{12,8},{14,12},{10,14},{6,10},{2,6},{0,2},{5,1},{9,5},... | collective-permute-start | bytes 393224 | tf_op jit(solution)/shard_map/ppermute | solution.py:206
  77.3 7.1 %collective-permute-start.24 = (bf16[128,512]{1,0:T(8,128)(2,1)S(1)}, bf16[128,512]{1,0:T(8,128)(2,1)S(1)}, u32[]{:S(2)}, u32[]{:S(2)}) collective-permute-start(bf16[128,512]{1,0:T(8,128)(2,1)S(1)} %get-tuple-element.20), channel_id=1, source_target_pairs={{0,4},{4,8},{8,12},{12,14},{14,10},{10,6},{6,2},{2,0},{1,5},{5,9},... | collective-permute-start | bytes 393224 | tf_op jit(solution)/shard_map/ppermute | solution.py:205
  78.9 6.4 %collective-permute-start.25 = (bf16[128,512]{1,0:T(8,128)(2,1)S(1)}, bf16[128,512]{1,0:T(8,128)(2,1)S(1)}, u32[]{:S(2)}, u32[]{:S(2)}) collective-permute-start(bf16[128,512]{1,0:T(8,128)(2,1)S(1)} %get-tuple-element.20), channel_id=1, source_target_pairs={{4,0},{8,4},{12,8},{14,12},{10,14},{6,10},{2,6},{0,2},{5,1},{9,5},... | collective-permute-start | bytes 393224 | tf_op jit(solution)/shard_map/ppermute | solution.py:206
  84.4 6.3 %collective-permute-start.28 = (bf16[128,512]{1,0:T(8,128)(2,1)S(1)}, bf16[128,512]{1,0:T(8,128)(2,1)S(1)}, u32[]{:S(2)}, u32[]{:S(2)}) collective-permute-start(bf16[128,512]{1,0:T(8,128)(2,1)S(1)} %collective-permute-done.24), channel_id=1, source_target_pairs={{0,4},{4,8},{8,12},{12,14},{14,10},{10,6},{6,2},{2,0},{1,5},{5,9},... | collective-permute-start | bytes 393224 | tf_op jit(solution)/shard_map/ppermute | solution.py:205
  86.9 6.6 %collective-permute-start.30 = (bf16[128,512]{1,0:T(8,128)(2,1)S(1)}, bf16[128,512]{1,0:T(8,128)(2,1)S(1)}, u32[]{:S(2)}, u32[]{:S(2)}) collective-permute-start(bf16[128,512]{1,0:T(8,128)(2,1)S(1)} %collective-permute-done.26), channel_id=1, source_target_pairs={{0,4},{4,8},{8,12},{12,14},{14,10},{10,6},{6,2},{2,0},{1,5},{5,9},... | collective-permute-start | bytes 393224 | tf_op jit(solution)/shard_map/ppermute | solution.py:205
  88.1 10.4 %collective-permute-start.31 = (bf16[128,512]{1,0:T(8,128)(2,1)S(1)}, bf16[128,512]{1,0:T(8,128)(2,1)S(1)}, u32[]{:S(2)}, u32[]{:S(2)}) collective-permute-start(bf16[128,512]{1,0:T(8,128)(2,1)S(1)} %collective-permute-done.27), channel_id=1, source_target_pairs={{4,0},{8,4},{12,8},{14,12},{10,14},{6,10},{2,6},{0,2},{5,1},{9,5},... | collective-permute-start | bytes 393224 | tf_op jit(solution)/shard_map/ppermute | solution.py:206
  90.7 7.8 %collective-permute-start.32 = (bf16[128,512]{1,0:T(8,128)(2,1)S(1)}, bf16[128,512]{1,0:T(8,128)(2,1)S(1)}, u32[]{:S(2)}, u32[]{:S(2)}) collective-permute-start(bf16[128,512]{1,0:T(8,128)(2,1)S(1)} %collective-permute-done.28), channel_id=1, source_target_pairs={{0,4},{4,8},{8,12},{12,14},{14,10},{10,6},{6,2},{2,0},{1,5},{5,9},... | collective-permute-start | bytes 393224 | tf_op jit(solution)/shard_map/ppermute | solution.py:205
  93.5 6.3 %collective-permute-start.34 = (bf16[128,512]{1,0:T(8,128)(2,1)S(1)}, bf16[128,512]{1,0:T(8,128)(2,1)S(1)}, u32[]{:S(2)}, u32[]{:S(2)}) collective-permute-start(bf16[128,512]{1,0:T(8,128)(2,1)S(1)} %collective-permute-done.30), channel_id=1, source_target_pairs={{0,4},{4,8},{8,12},{12,14},{14,10},{10,6},{6,2},{2,0},{1,5},{5,9},... | collective-permute-start | bytes 393224 | tf_op jit(solution)/shard_map/ppermute | solution.py:209
  100.2 6.6 %collective-permute-start.37 = (bf16[128,512]{1,0:T(8,128)(2,1)S(1)}, bf16[128,512]{1,0:T(8,128)(2,1)S(1)}, u32[]{:S(2)}, u32[]{:S(2)}) collective-permute-start(bf16[128,512]{1,0:T(8,128)(2,1)S(1)} %fusion.17), channel_id=1, source_target_pairs={{4,0},{8,4},{12,8},{14,12},{10,14},{6,10},{2,6},{0,2},{5,1},{9,5},... | collective-permute-start | bytes 393224 | tf_op jit(solution)/shard_map/ppermute | solution.py:206
  107.9 6.4 %collective-permute-start.42 = (bf16[128,512]{1,0:T(8,128)(2,1)S(1)}, bf16[128,512]{1,0:T(8,128)(2,1)S(1)}, u32[]{:S(2)}, u32[]{:S(2)}) collective-permute-start(bf16[128,512]{1,0:T(8,128)(2,1)S(1)} %collective-permute-done.38), channel_id=1, source_target_pairs={{0,4},{4,8},{8,12},{12,14},{14,10},{10,6},{6,2},{2,0},{1,5},{5,9},... | collective-permute-start | bytes 393224 | tf_op jit(solution)/shard_map/ppermute | solution.py:205
  109.2 6.4 %collective-permute-start.43 = (bf16[128,512]{1,0:T(8,128)(2,1)S(1)}, bf16[128,512]{1,0:T(8,128)(2,1)S(1)}, u32[]{:S(2)}, u32[]{:S(2)}) collective-permute-start(bf16[128,512]{1,0:T(8,128)(2,1)S(1)} %collective-permute-done.39), channel_id=1, source_target_pairs={{4,0},{8,4},{12,8},{14,12},{10,14},{6,10},{2,6},{0,2},{5,1},{9,5},... | collective-permute-start | bytes 393224 | tf_op jit(solution)/shard_map/ppermute | solution.py:206
  111.3 6.5 %collective-permute-start.44 = (bf16[128,512]{1,0:T(8,128)(2,1)S(1)}, bf16[128,512]{1,0:T(8,128)(2,1)S(1)}, u32[]{:S(2)}, u32[]{:S(2)}) collective-permute-start(bf16[128,512]{1,0:T(8,128)(2,1)S(1)} %collective-permute-done.40), channel_id=1, source_target_pairs={{0,4},{4,8},{8,12},{12,14},{14,10},{10,6},{6,2},{2,0},{1,5},{5,9},... | collective-permute-start | bytes 393224 | tf_op jit(solution)/shard_map/ppermute | solution.py:205
  112.8 10.1 %collective-permute-start.45 = (bf16[128,512]{1,0:T(8,128)(2,1)S(1)}, bf16[128,512]{1,0:T(8,128)(2,1)S(1)}, u32[]{:S(2)}, u32[]{:S(2)}) collective-permute-start(bf16[128,512]{1,0:T(8,128)(2,1)S(1)} %collective-permute-done.41), channel_id=1, source_target_pairs={{4,0},{8,4},{12,8},{14,12},{10,14},{6,10},{2,6},{0,2},{5,1},{9,5},... | collective-permute-start | bytes 393224 | tf_op jit(solution)/shard_map/ppermute | solution.py:206
  114.3 8.5 %collective-permute-start.46 = (bf16[128,512]{1,0:T(8,128)(2,1)S(1)}, bf16[128,512]{1,0:T(8,128)(2,1)S(1)}, u32[]{:S(2)}, u32[]{:S(2)}) collective-permute-start(bf16[128,512]{1,0:T(8,128)(2,1)S(1)} %collective-permute-done.42), channel_id=1, source_target_pairs={{0,4},{4,8},{8,12},{12,14},{14,10},{10,6},{6,2},{2,0},{1,5},{5,9},... | collective-permute-start | bytes 393224 | tf_op jit(solution)/shard_map/ppermute | solution.py:205
  115.6 6.3 %collective-permute-start.47 = (bf16[128,512]{1,0:T(8,128)(2,1)S(1)}, bf16[128,512]{1,0:T(8,128)(2,1)S(1)}, u32[]{:S(2)}, u32[]{:S(2)}) collective-permute-start(bf16[128,512]{1,0:T(8,128)(2,1)S(1)} %collective-permute-done.43), channel_id=1, source_target_pairs={{4,0},{8,4},{12,8},{14,12},{10,14},{6,10},{2,6},{0,2},{5,1},{9,5},... | collective-permute-start | bytes 393224 | tf_op jit(solution)/shard_map/ppermute | solution.py:206
  117.8 7.7 %collective-permute-start.48 = (bf16[128,512]{1,0:T(8,128)(2,1)S(1)}, bf16[128,512]{1,0:T(8,128)(2,1)S(1)}, u32[]{:S(2)}, u32[]{:S(2)}) collective-permute-start(bf16[128,512]{1,0:T(8,128)(2,1)S(1)} %collective-permute-done.44), channel_id=1, source_target_pairs={{0,4},{4,8},{8,12},{12,14},{14,10},{10,6},{6,2},{2,0},{1,5},{5,9},... | collective-permute-start | bytes 393224 | tf_op jit(solution)/shard_map/ppermute | solution.py:209
  122.0 6.4 %collective-permute-start.49 = (bf16[128,512]{1,0:T(8,128)(2,1)S(1)}, bf16[128,512]{1,0:T(8,128)(2,1)S(1)}, u32[]{:S(2)}, u32[]{:S(2)}) collective-permute-start(bf16[128,512]{1,0:T(8,128)(2,1)S(1)} %collective-permute-done.47), channel_id=1, source_target_pairs={{4,0},{8,4},{12,8},{14,12},{10,14},{6,10},{2,6},{0,2},{5,1},{9,5},... | collective-permute-start | bytes 393224 | tf_op jit(solution)/shard_map/ppermute | solution.py:211
  127.4 6.2 %collective-permute-start.51 = (bf16[128,512]{1,0:T(8,128)(2,1)S(1)}, bf16[128,512]{1,0:T(8,128)(2,1)S(1)}, u32[]{:S(2)}, u32[]{:S(2)}) collective-permute-start(bf16[128,512]{1,0:T(8,128)(2,1)S(1)} %get-tuple-element.10), channel_id=1, source_target_pairs={{4,0},{8,4},{12,8},{14,12},{10,14},{6,10},{2,6},{0,2},{5,1},{9,5},... | collective-permute-start | bytes 393224 | tf_op jit(solution)/shard_map/ppermute | solution.py:206
  129.1 6.5 %collective-permute-start.52 = (bf16[128,512]{1,0:T(8,128)(2,1)S(1)}, bf16[128,512]{1,0:T(8,128)(2,1)S(1)}, u32[]{:S(2)}, u32[]{:S(2)}) collective-permute-start(bf16[128,512]{1,0:T(8,128)(2,1)S(1)} %get-tuple-element.12), channel_id=1, source_target_pairs={{0,4},{4,8},{8,12},{12,14},{14,10},{10,6},{6,2},{2,0},{1,5},{5,9},... | collective-permute-start | bytes 393224 | tf_op jit(solution)/shard_map/ppermute | solution.py:205
  130.3 6.3 %collective-permute-start.53 = (bf16[128,512]{1,0:T(8,128)(2,1)S(1)}, bf16[128,512]{1,0:T(8,128)(2,1)S(1)}, u32[]{:S(2)}, u32[]{:S(2)}) collective-permute-start(bf16[128,512]{1,0:T(8,128)(2,1)S(1)} %get-tuple-element.12), channel_id=1, source_target_pairs={{4,0},{8,4},{12,8},{14,12},{10,14},{6,10},{2,6},{0,2},{5,1},{9,5},... | collective-permute-start | bytes 393224 | tf_op jit(solution)/shard_map/ppermute | solution.py:206
  132.2 6.3 %collective-permute-start.54 = (bf16[128,512]{1,0:T(8,128)(2,1)S(1)}, bf16[128,512]{1,0:T(8,128)(2,1)S(1)}, u32[]{:S(2)}, u32[]{:S(2)}) collective-permute-start(bf16[128,512]{1,0:T(8,128)(2,1)S(1)} %collective-permute-done.50), channel_id=1, source_target_pairs={{0,4},{4,8},{8,12},{12,14},{14,10},{10,6},{6,2},{2,0},{1,5},{5,9},... | collective-permute-start | bytes 393224 | tf_op jit(solution)/shard_map/ppermute | solution.py:205
  136.5 6.3 %collective-permute-start.57 = (bf16[128,512]{1,0:T(8,128)(2,1)S(1)}, bf16[128,512]{1,0:T(8,128)(2,1)S(1)}, u32[]{:S(2)}, u32[]{:S(2)}) collective-permute-start(bf16[128,512]{1,0:T(8,128)(2,1)S(1)} %collective-permute-done.53), channel_id=1, source_target_pairs={{4,0},{8,4},{12,8},{14,12},{10,14},{6,10},{2,6},{0,2},{5,1},{9,5},... | collective-permute-start | bytes 393224 | tf_op jit(solution)/shard_map/ppermute | solution.py:206
  138.4 6.4 %collective-permute-start.58 = (bf16[128,512]{1,0:T(8,128)(2,1)S(1)}, bf16[128,512]{1,0:T(8,128)(2,1)S(1)}, u32[]{:S(2)}, u32[]{:S(2)}) collective-permute-start(bf16[128,512]{1,0:T(8,128)(2,1)S(1)} %collective-permute-done.54), channel_id=1, source_target_pairs={{0,4},{4,8},{8,12},{12,14},{14,10},{10,6},{6,2},{2,0},{1,5},{5,9},... | collective-permute-start | bytes 393224 | tf_op jit(solution)/shard_map/ppermute | solution.py:205
  139.5 9.3 %collective-permute-start.59 = (bf16[128,512]{1,0:T(8,128)(2,1)S(1)}, bf16[128,512]{1,0:T(8,128)(2,1)S(1)}, u32[]{:S(2)}, u32[]{:S(2)}) collective-permute-start(bf16[128,512]{1,0:T(8,128)(2,1)S(1)} %collective-permute-done.55), channel_id=1, source_target_pairs={{4,0},{8,4},{12,8},{14,12},{10,14},{6,10},{2,6},{0,2},{5,1},{9,5},... | collective-permute-start | bytes 393224 | tf_op jit(solution)/shard_map/ppermute | solution.py:206
  141.4 7.3 %collective-permute-start.60 = (bf16[128,512]{1,0:T(8,128)(2,1)S(1)}, bf16[128,512]{1,0:T(8,128)(2,1)S(1)}, u32[]{:S(2)}, u32[]{:S(2)}) collective-permute-start(bf16[128,512]{1,0:T(8,128)(2,1)S(1)} %collective-permute-done.56), channel_id=1, source_target_pairs={{0,4},{4,8},{8,12},{12,14},{14,10},{10,6},{6,2},{2,0},{1,5},{5,9},... | collective-permute-start | bytes 393224 | tf_op jit(solution)/shard_map/ppermute | solution.py:205
  151.0 6.4 %collective-permute-start.65 = (bf16[128,512]{1,0:T(8,128)(2,1)S(1)}, bf16[128,512]{1,0:T(8,128)(2,1)S(1)}, u32[]{:S(2)}, u32[]{:S(2)}) collective-permute-start(bf16[128,512]{1,0:T(8,128)(2,1)S(1)} %fusion.15), channel_id=1, source_target_pairs={{4,0},{8,4},{12,8},{14,12},{10,14},{6,10},{2,6},{0,2},{5,1},{9,5},... | collective-permute-start | bytes 393224 | tf_op jit(solution)/shard_map/ppermute | solution.py:206
  162.7 7.4 %collective-permute-start.73 = (bf16[128,512]{1,0:T(8,128)(2,1)S(1)}, bf16[128,512]{1,0:T(8,128)(2,1)S(1)}, u32[]{:S(2)}, u32[]{:S(2)}) collective-permute-start(bf16[128,512]{1,0:T(8,128)(2,1)S(1)} %collective-permute-done.69), channel_id=1, source_target_pairs={{4,0},{8,4},{12,8},{14,12},{10,14},{6,10},{2,6},{0,2},{5,1},{9,5},... | collective-permute-start | bytes 393224 | tf_op jit(solution)/shard_map/ppermute | solution.py:206
  163.1 7.0 %collective-permute-start.74 = (bf16[128,512]{1,0:T(8,128)(2,1)S(1)}, bf16[128,512]{1,0:T(8,128)(2,1)S(1)}, u32[]{:S(2)}, u32[]{:S(2)}) collective-permute-start(bf16[128,512]{1,0:T(8,128)(2,1)S(1)} %collective-permute-done.70), channel_id=1, source_target_pairs={{0,4},{4,8},{8,12},{12,14},{14,10},{10,6},{6,2},{2,0},{1,5},{5,9},... | collective-permute-start | bytes 393224 | tf_op jit(solution)/shard_map/ppermute | solution.py:205
  166.5 6.3 %collective-permute-start.76 = (bf16[128,512]{1,0:T(8,128)(2,1)S(1)}, bf16[128,512]{1,0:T(8,128)(2,1)S(1)}, u32[]{:S(2)}, u32[]{:S(2)}) collective-permute-start(bf16[128,512]{1,0:T(8,128)(2,1)S(1)} %collective-permute-done.72), channel_id=1, source_target_pairs={{0,4},{4,8},{8,12},{12,14},{14,10},{10,6},{6,2},{2,0},{1,5},{5,9},... | collective-permute-start | bytes 393224 | tf_op jit(solution)/shard_map/ppermute | solution.py:209
  (47 other events, 275.8 us)

commit v2 on v0

v2 whole, which is shorter than its diff:
```python
import math

import jax
import jax.numpy as jnp
from jax import lax
from jax.experimental import pallas as pl
from jax.experimental.pallas import tpu as pltpu
from jax.sharding import PartitionSpec as P

GATE_KINDS = 4
LANES = 128
MAX_RING = 8
SCRATCH = 16 * 2**20


def plain(
    byte_ids, h_start, c_start, inter_weight, inter_embed, gate_weight, gate_embed, gate_bias
):
    hidden = h_start
    cell = c_start
    for step in range(byte_ids.shape[0]):
        rows_here = hidden.shape[0]
        onehot = one_hot(byte_ids[step], inter_embed.shape[0])
        product = lax.dot_general(
            lax.all_gather(hidden, "mp", axis=1, tiled=True),
            inter_weight,
            (((1,), (1,)), ((), ())),
            preferred_element_type=jnp.float32,
        )
        lookup = jnp.dot(onehot, inter_embed, preferred_element_type=jnp.float32)
        inter_vals = (lookup * product).astype(jnp.bfloat16)
        gate_sums = jnp.dot(
            lax.all_gather(inter_vals, "mp", axis=1, tiled=True),
            gate_weight,
            preferred_element_type=jnp.float32,
        )
        gate_sums = (
            gate_sums
            + jnp.dot(onehot, gate_embed, preferred_element_type=jnp.float32)
            + gate_bias[None, :]
        )
        gate_sums = gate_sums.reshape(rows_here, gate_sums.shape[1] // GATE_KINDS, GATE_KINDS)
        hidden, cell = update_state([gate_sums[:, :, j] for j in range(GATE_KINDS)], cell)
    return hidden, cell


def one_hot(ids, vocab):
    return (ids[:, None] == jnp.arange(vocab, dtype=jnp.int32)[None, :]).astype(jnp.bfloat16)


def update_state(sums, cell):
    in_gate = jax.nn.sigmoid(sums[0])
    forget = jax.nn.sigmoid(sums[1])
    out_gate = jax.nn.sigmoid(sums[2])
    update = jnp.tanh(sums[3])
    cell = forget * cell + in_gate * update
    return (out_gate * jnp.tanh(cell)).astype(jnp.bfloat16), cell


def ring_of(devices):
    return list(range(0, devices, 2)) + list(range(devices - 1, 0, -2))


def ring_index(me, steps, devices):
    place = jnp.where(me % 2 == 0, me // 2, devices - 1 - me // 2)
    place = (place + steps + devices) % devices
    half = devices // 2
    return jnp.where(place < half, 2 * place, 2 * (devices - 1 - place) + 1)


def mix_matrix(group):
    lanes = group // GATE_KINDS
    source = jnp.arange(group, dtype=jnp.int32)[:, None]
    target = jnp.arange(group, dtype=jnp.int32)[None, :]
    wanted = (target % lanes) * GATE_KINDS + target // lanes
    return (source == wanted).astype(jnp.bfloat16)


def dot32(a, b):
    return jnp.dot(a, b, preferred_element_type=jnp.float32)


def dot32_turned(a, b):
    return lax.dot_general(a, b, (((1,), (1,)), ((), ())), preferred_element_type=jnp.float32)


def rows_of(refs):
    blocks = [ref[...] for ref in refs]
    return blocks[0] if len(blocks) == 1 else jnp.concatenate(blocks, 0)


class Gather:
    def __init__(self, me, weight, devices, part, turned):
        self.me, self.weight = me, weight
        self.devices, self.part, self.turned = devices, part, turned
        self.columns = weight.shape[0] if turned else weight.shape[1]

    def terms(self, me_ref, weight_ref, blocks, away, columns):
        total = None
        for block, steps in zip(blocks, away):
            start = pl.multiple_of(
                ring_index(me_ref[0], steps, self.devices) * self.part, self.part
            )
            if self.turned:
                term = dot32_turned(block, weight_ref[columns, pl.ds(start, self.part)])
            else:
                term = dot32(block, weight_ref[pl.ds(start, self.part), columns])
            total = term if total is None else total + term
        return total

    def tiles(self):
        width = min(self.columns, GATE_KINDS * LANES)
        return [slice(at, at + width) for at in range(0, self.columns, width)]

    def add(self, groups, away, total=None, first=None):
        chunks = len(groups[0])
        rows = sum(block.shape[0] for block in groups[0])
        extra = [] if total is None else [total]
        at = 0
        if first is not None:
            onehot, at, embed = first
            extra = [onehot, embed]

        def kernel(me_ref, weight_ref, *refs):
            extra_refs, refs, out_ref = refs[: len(extra)], refs[len(extra) : -1], refs[-1]
            blocks = [rows_of(refs[i * chunks : (i + 1) * chunks]) for i in range(len(away))]
            for columns in self.tiles():
                value = self.terms(me_ref, weight_ref, blocks, away, columns)
                if total is not None:
                    value = extra_refs[0][:, columns] + value
                if first is not None:
                    value = dot32(extra_refs[0][at : at + rows], extra_refs[1][:, columns]) + value
                out_ref[:, columns] = value

        return call(
            kernel,
            [self.me, self.weight, *extra, *[block for group in groups for block in group]],
            [jax.ShapeDtypeStruct((rows, self.columns), jnp.float32)],
            2 * rows * self.columns * self.part * len(away),
        )[0]


def call(kernel, operands, outs, flops):
    size = sum(math.prod(out.shape) * out.dtype.itemsize for out in outs)
    return pl.pallas_call(
        kernel,
        in_specs=[pl.BlockSpec(memory_space=pltpu.SMEM)]
        + [pl.BlockSpec(memory_space=pltpu.VMEM)] * (len(operands) - 1),
        out_specs=[pl.BlockSpec(memory_space=pltpu.VMEM)] * len(outs),
        out_shape=outs,
        compiler_params=pltpu.CompilerParams(vmem_limit_bytes=SCRATCH),
        cost_estimate=pl.CostEstimate(flops=flops, bytes_accessed=size, transcendentals=0),
    )(*operands)


def inter_of(gather, total, last, row, onehot, at, inter_embed, away):
    rows = last.shape[0]

    def kernel(me_ref, weight_ref, total_ref, last_ref, onehot_ref, embed_ref, out_ref):
        product = total_ref[row : row + rows] + gather.terms(
            me_ref, weight_ref, [last_ref[...]], [away], slice(None)
        )
        lookup = dot32(onehot_ref[at + row : at + row + rows], embed_ref[...])
        out_ref[...] = (lookup * product).astype(out_ref.dtype)

    return call(
        kernel,
        [gather.me, gather.weight, total, last, onehot, inter_embed],
        [jax.ShapeDtypeStruct((rows, gather.columns), jnp.bfloat16)],
        2 * rows * gather.columns * gather.part,
    )[0]


def state_of(gather, total, lasts, row, bias, cell, cell_row, mix, away):
    rows = sum(last.shape[0] for last in lasts)
    group = mix.shape[0]
    lanes = group // GATE_KINDS
    units = gather.columns // GATE_KINDS
    chunks = len(lasts)

    def kernel(me_ref, weight_ref, total_ref, bias_ref, cell_ref, mix_ref, *refs):
        last_refs, hidden_ref, cell_out_ref = refs[:chunks], refs[chunks], refs[chunks + 1]
        last = rows_of(last_refs)
        terms = []
        for columns in gather.tiles():
            full = total_ref[row : row + rows, columns] + gather.terms(
                me_ref, weight_ref, [last], [away], columns
            )
            full = full + bias_ref[:, columns]
            high = full.astype(jnp.bfloat16)
            terms += [high, (full - high.astype(jnp.float32)).astype(jnp.bfloat16)]
        mixed = dot32(jnp.concatenate(terms, 0), mix_ref[...])
        for g in range(len(terms) // 2):
            at = 2 * g * rows
            sums = mixed[at : at + rows] + mixed[at + rows : at + 2 * rows]
            here = slice(g * lanes, (g + 1) * lanes)
            hidden_ref[:, here], cell_out_ref[:, here] = update_state(
                [sums[:, j * lanes : (j + 1) * lanes] for j in range(GATE_KINDS)],
                cell_ref[cell_row : cell_row + rows, here],
            )

    return call(
        kernel,
        [gather.me, gather.weight, total, bias, cell, mix, *lasts],
        [
            jax.ShapeDtypeStruct((rows, units), jnp.bfloat16),
            jax.ShapeDtypeStruct((rows, units), jnp.float32),
        ],
        2 * rows * gather.columns * (gather.part + 2 * group),
    )


def arrivals(block, ring, last):
    devices = len(ring)
    up = [(ring[i], ring[(i + 1) % devices]) for i in range(devices)]
    down = [(b, a) for a, b in up]
    blocks = [block]
    below = above = block
    for _ in range(devices // 2 - 1):
        below = lax.ppermute(below, "mp", up)
        above = lax.ppermute(above, "mp", down)
        blocks += [below, above]
    if last == "up":
        farthest = [lax.ppermute(below, "mp", up)]
    elif last == "down":
        farthest = [lax.ppermute(above, "mp", down)]
    else:
        half = block.shape[0] // 2
        farthest = [
            lax.ppermute(below[:half], "mp", up),
            lax.ppermute(above[half:], "mp", down),
        ]
    return blocks, farthest


def ringed(devices, chunks, first_chunks):
    ring = ring_of(devices)
    away = [-((k + 1) // 2) if k % 2 else k // 2 for k in range(devices)]

    def local(
        byte_ids, h_start, c_start, inter_weight, inter_embed, gate_weight, gate_embed, gate_bias
    ):
        steps, streams = byte_ids.shape
        part = h_start.shape[1]
        me = jnp.full((1,), lax.axis_index("mp"), jnp.int32)
        to_inter = Gather(me, inter_weight, devices, part, True)
        to_gate = Gather(me, gate_weight, devices, part, False)
        mix = mix_matrix(GATE_KINDS * LANES)
        bias = gate_bias.reshape(1, -1)
        onehot = one_hot(byte_ids.reshape(-1), inter_embed.shape[0])

        def gathered(blocks, gather, first=None):
            ways = ["up" if c % 2 == 0 else "down" for c in range(len(blocks))]
            if len(blocks) == 1:
                ways = ["both"]
            arrived, farthest = zip(*[arrivals(b, ring, way) for b, way in zip(blocks, ways)])
            total = gather.add([[b[0] for b in arrived]], away[:1], first=first)
            for k in range(1, devices - 1, 2):
                total = gather.add(
                    [[b[k] for b in arrived], [b[k + 1] for b in arrived]],
                    away[k : k + 2],
                    total,
                )
            return total, [last for lasts in farthest for last in lasts]

        rows = streams // first_chunks
        hiddens = [h_start[c * rows : (c + 1) * rows] for c in range(first_chunks)]
        rows = streams // chunks
        cells = [(c_start, c * rows) for c in range(chunks)]
        for step in range(steps):
            at = step * streams
            total, lasts = gathered(hiddens, to_inter)
            inters = [
                inter_of(to_inter, total, last, c * rows, onehot, at, inter_embed, away[-1])
                for c, last in enumerate(lasts)
            ]
            total, lasts = gathered(inters, to_gate, (onehot, at, gate_embed))
            if step + 1 < steps:
                hiddens, updated = zip(
                    *[
                        state_of(to_gate, total, [last], c * rows, bias, *cells[c], mix, away[-1])
                        for c, last in enumerate(lasts)
                    ]
                )
                cells = [(cell, 0) for cell in updated]
            else:
                cell = cells[0][0]
                if cell.shape[0] < streams:
                    cell = jnp.concatenate([cell for cell, _ in cells], 0)
                return state_of(to_gate, total, lasts, 0, bias, cell, 0, mix, away[-1])

    return local


def solution(mesh):
    in_specs = (
        P(None, ("groups", "batch")),
        P(("groups", "batch"), "mp"),
        P(("groups", "batch"), "mp"),
        P("mp", None),
        P(None, "mp"),
        P(None, "mp"),
        P(None, "mp"),
        P("mp"),
    )
    out_specs = (P(("groups", "batch"), "mp"), P(("groups", "batch"), "mp"))
    devices = mesh.shape["mp"]
    local = ringed(devices, 2, 1) if 2 < devices <= MAX_RING else plain
    return jax.shard_map(local, mesh=mesh, in_specs=in_specs, out_specs=out_specs, check_vma=False)
```

time: 380 us -> 169 us (0.44)
  waiting for transfers between devices: 297 us -> 47.9 us
  starting transfers between devices: 0.64 us -> 85.1 us
  matrix products: 43.8 us -> 0 us
  Pallas kernels: 0 us -> 29 us
  local copies, waits for them, and re-layouts: 19.8 us -> 4.93 us
  between operations: 14.4 us -> 1.18 us
  other arithmetic: 4.26 us -> 0.34 us
    all_gather x6 -> x0, waiting for transfers between devices: 296 us -> none  [the longest x3 148 us: local(): lax.all_gather(h_final, 'mp', axis=1, tiled=True)]
    ppermute x0 -> x78, starting transfers between devices: none -> 85.1 us  [the longest x33 51.3 us: arrivals(): above = lax.ppermute(above, 'mp', down)]
    ppermute x0 -> x78, waiting for transfers between devices: none -> 47.9 us  [the longest x33 23.9 us: arrivals(): above = lax.ppermute(above, 'mp', down)]
    dot_general x12 -> x0, matrix products: 43.8 us -> none  [the longest x3 26.1 us: local(): jnp.dot(lax.all_gather(inter_vals, 'mp', axis=1, tiled=True), gate_weight...]
    pallas_call x0 -> x35, Pallas kernels: none -> 29 us  [call(): pl.pallas_call(kernel, in_specs=[pl.BlockSpec(memory_space=pltpu.SMEM)] +...]
    reshape x3 -> x0, local copies, waits for them, and re-layouts: 5.58 us -> none  [local(): gate_sums = gate_sums.reshape(rows_here, gate_sums.shape[1] // 4, 4)]
    add x3 -> x0, local copies, waits for them, and re-layouts: 5.55 us -> none  [local(): gate_sums + jnp.dot(onehot, gate_embed, preferred_element_type=jnp.float32)]
    slice x4 -> x2, local copies, waits for them, and re-layouts: 4.97 us -> 0.02 us  [the longest x1 0.01 us: arrivals(): above[half:]]
  transfers between devices with their start and end apart: 6 -> 78, of which waited for: 6 -> 32; matrix products, arithmetic and copies ran while one was open for 1% -> 1% of each run, Pallas kernels for 0% -> 16%
where the time goes in v2:
time: 169 us; the launch traced here: 168 us
  starting transfers between devices  85.1 us (50%)
  waiting for transfers between devices  47.9 us (28%)
  Pallas kernels  29 us (17%)
  local copies, waits for them, and re-layouts  4.93 us (3%)
    ppermute x33, starting transfers between devices, arrivals(): above = lax.ppermute(above, 'mp', down)  51.3 us
    pallas_call x35, Pallas kernels, call(): pl.pallas_call(kernel, in_specs=[pl.BlockSpec(memory_space=pltpu.SMEM)] +...  29 us
    ppermute x33, waiting for transfers between devices, arrivals(): above = lax.ppermute(above, 'mp', down)  23.9 us
    ppermute x33, starting transfers between devices, arrivals(): below = lax.ppermute(below, 'mp', up)  20.9 us
    ppermute x33, waiting for transfers between devices, arrivals(): below = lax.ppermute(below, 'mp', up)  17.6 us
    ppermute x5, starting transfers between devices, arrivals(): farthest = [lax.ppermute(above, 'mp', down)]  9.11 us
    unnamed x22, local copies, waits for them, and re-layouts  4.21 us
    ppermute x5, waiting for transfers between devices, arrivals(): farthest = [lax.ppermute(above, 'mp', down)]  4.21 us
  transfers between devices with their start and end apart: 78, of which 32 were waited for; matrix products, arithmetic and copies ran while one was open for 1% of the time, Pallas kernels for 16%

profile of v2, /device:TPU:0, one launch (start us, length us, event | category | flops | bytes accessed | tf_op | source)
XLA Modules:
  0.0 168.5 jit_solution(8828964845289789411)
XLA Ops:
  0.6 3.0 %collective-permute-start.1 = (bf16[256,512]{1,0:T(8,128)(2,1)}, bf16[256,512]{1,0:T(8,128)(2,1)S(1)}, u32[]{:S(2)}, u32[]{:S(2)}) collective-permute-start(bf16[256,512]{1,0:T(8,128)(2,1)} %refs_0_.1), channel_id=1, source_target_pairs={{4,0},{8,4},{12,8},{14,12},{10,14},{6,10},{2,6},{0,2},{5,1},{9,5},... | collective-permute-start | bytes 786440 | tf_op jit(solution)/shard_map/ppermute | solution.py:221
  3.8 6.5 %collective-permute-done.1.refs_2_ = bf16[256,512]{1,0:T(8,128)(2,1)S(1)} collective-permute-done((bf16[256,512]{1,0:T(8,128)(2,1)}, bf16[256,512]{1,0:T(8,128)(2,1)S(1)}, u32[]{:S(2)}, u32[]{:S(2)}) %collective-permute-start.1) | collective-permute-done | bytes 262176 | tf_op jit(solution)/shard_map/ppermute | solution.py:221
  10.2 1.7 collective-permute-start.3
  12.3 5.5 %collective-permute-done.3.refs_2_ = bf16[256,512]{1,0:T(8,128)(2,1)S(1)} collective-permute-done((bf16[256,512]{1,0:T(8,128)(2,1)S(1)}, bf16[256,512]{1,0:T(8,128)(2,1)S(1)}, u32[]{:S(2)}, u32[]{:S(2)}) %collective-permute-start.3) | collective-permute-done | bytes 262176 | tf_op jit(solution)/shard_map/ppermute | solution.py:221
  17.7 1.3 collective-permute-start.5
  20.4 3.8 %collective-permute-done.5.refs_2_ = bf16[256,512]{1,0:T(8,128)(2,1)S(1)} collective-permute-done((bf16[256,512]{1,0:T(8,128)(2,1)S(1)}, bf16[256,512]{1,0:T(8,128)(2,1)S(1)}, u32[]{:S(2)}, u32[]{:S(2)}) %collective-permute-start.5) | collective-permute-done | bytes 262176 | tf_op jit(solution)/shard_map/ppermute | solution.py:221
  24.3 1.6 collective-permute-start.7
  26.6 2.2 %copy-done = bf16[512,4096]{1,0:T(8,128)(2,1)S(1)} copy-done((bf16[512,4096]{1,0:T(8,128)(2,1)S(1)}, bf16[512,4096]{1,0:T(8,128)(2,1)}, u32[]{:S(2)}) %copy-start) | copy-done | bytes 4194328
  33.1 1.6 collective-permute-start.11
  35.5 1.7 collective-permute-start.8
  37.6 3.4 %collective-permute-done.9.refs_2_ = bf16[128,512]{1,0:T(8,128)(2,1)S(1)} collective-permute-done((bf16[128,512]{1,0:T(8,128)(2,1)S(1)}, bf16[128,512]{1,0:T(8,128)(2,1)S(1)}, u32[]{:S(2)}, u32[]{:S(2)}) %collective-permute-start.9) | collective-permute-done | bytes 131104 | tf_op jit(solution)/shard_map/ppermute | solution.py:220
  41.5 1.6 collective-permute-start.15
  43.8 1.3 collective-permute-start.14
  45.3 1.5 collective-permute-done.15.refs_4_
  46.7 1.9 %collective-permute-start.19 = (bf16[128,512]{1,0:T(8,128)(2,1)S(1)}, bf16[128,512]{1,0:T(8,128)(2,1)S(1)}, u32[]{:S(2)}, u32[]{:S(2)}) collective-permute-start(bf16[128,512]{1,0:T(8,128)(2,1)S(1)} %collective-permute-done.15.refs_4_), channel_id=1, source_target_pairs={{4,0},{8,4},{12,8},{14,12},{10,14},{6,10},{2,6},{0,2},{5,1},{9,5},... | collective-permute-start | bytes 393224 | tf_op jit(solution)/shard_map/ppermute | solution.py:221
  50.2 1.8 %collective-permute-start.17 = (bf16[128,512]{1,0:T(8,128)(2,1)S(1)}, bf16[128,512]{1,0:T(8,128)(2,1)S(1)}, u32[]{:S(2)}, u32[]{:S(2)}) collective-permute-start(bf16[128,512]{1,0:T(8,128)(2,1)S(1)} %collective-permute-done.13.refs_2_), channel_id=1, source_target_pairs={{0,4},{4,8},{8,12},{12,14},{14,10},{10,6},{6,2},{2,0},{1,5},{5,9},... | collective-permute-start | bytes 393224 | tf_op jit(solution)/shard_map/ppermute | solution.py:220
  53.5 2.0 %collective-permute-start.21 = (bf16[128,512]{1,0:T(8,128)(2,1)S(1)}, bf16[128,512]{1,0:T(8,128)(2,1)S(1)}, u32[]{:S(2)}, u32[]{:S(2)}) collective-permute-start(bf16[128,512]{1,0:T(8,128)(2,1)S(1)} %collective-permute-done.19.refs_4_), channel_id=1, source_target_pairs={{4,0},{8,4},{12,8},{14,12},{10,14},{6,10},{2,6},{0,2},{5,1},{9,5},... | collective-permute-start | bytes 393224 | tf_op jit(solution)/shard_map/ppermute | solution.py:226
  61.3 1.3 collective-permute-start.25
  65.3 1.3 collective-permute-start.24
  69.0 1.4 collective-permute-done.22.refs_1_
  70.8 1.3 collective-permute-done.23.refs_2_
  72.2 2.0 %collective-permute-start.28 = (bf16[128,512]{1,0:T(8,128)(2,1)S(1)}, bf16[128,512]{1,0:T(8,128)(2,1)S(1)}, u32[]{:S(2)}, u32[]{:S(2)}) collective-permute-start(bf16[128,512]{1,0:T(8,128)(2,1)S(1)} %collective-permute-done.24.refs_3_), channel_id=1, source_target_pairs={{4,0},{8,4},{12,8},{14,12},{10,14},{6,10},{2,6},{0,2},{5,1},{9,5},... | collective-permute-start | bytes 393224 | tf_op jit(solution)/shard_map/ppermute | solution.py:221
  74.2 2.0 %collective-permute-start.33 = (bf16[128,512]{1,0:T(8,128)(2,1)S(1)}, bf16[128,512]{1,0:T(8,128)(2,1)S(1)}, u32[]{:S(2)}, u32[]{:S(2)}) collective-permute-start(bf16[128,512]{1,0:T(8,128)(2,1)S(1)} %collective-permute-done.29.refs_4_), channel_id=1, source_target_pairs={{4,0},{8,4},{12,8},{14,12},{10,14},{6,10},{2,6},{0,2},{5,1},{9,5},... | collective-permute-start | bytes 393224 | tf_op jit(solution)/shard_map/ppermute | solution.py:221
  78.0 2.5 %collective-permute-start.32 = (bf16[128,512]{1,0:T(8,128)(2,1)S(1)}, bf16[128,512]{1,0:T(8,128)(2,1)S(1)}, u32[]{:S(2)}, u32[]{:S(2)}) collective-permute-start(bf16[128,512]{1,0:T(8,128)(2,1)S(1)} %collective-permute-done.28.refs_3_), channel_id=1, source_target_pairs={{4,0},{8,4},{12,8},{14,12},{10,14},{6,10},{2,6},{0,2},{5,1},{9,5},... | collective-permute-start | bytes 393224 | tf_op jit(solution)/shard_map/ppermute | solution.py:221
  80.8 2.5 %collective-permute-start.35 = (bf16[128,512]{1,0:T(8,128)(2,1)S(1)}, bf16[128,512]{1,0:T(8,128)(2,1)S(1)}, u32[]{:S(2)}, u32[]{:S(2)}) collective-permute-start(bf16[128,512]{1,0:T(8,128)(2,1)S(1)} %collective-permute-done.33.refs_4_), channel_id=1, source_target_pairs={{4,0},{8,4},{12,8},{14,12},{10,14},{6,10},{2,6},{0,2},{5,1},{9,5},... | collective-permute-start | bytes 393224 | tf_op jit(solution)/shard_map/ppermute | solution.py:226
  85.2 2.0 %collective-permute-done.35.last_ref = bf16[128,512]{1,0:T(8,128)(2,1)S(1)} collective-permute-done((bf16[128,512]{1,0:T(8,128)(2,1)S(1)}, bf16[128,512]{1,0:T(8,128)(2,1)S(1)}, u32[]{:S(2)}, u32[]{:S(2)}) %collective-permute-start.35) | collective-permute-done | bytes 131104 | tf_op jit(solution)/shard_map/ppermute | solution.py:226
  87.6 2.5 %collective-permute-start.39 = (bf16[128,512]{1,0:T(8,128)(2,1)S(1)}, bf16[128,512]{1,0:T(8,128)(2,1)S(1)}, u32[]{:S(2)}, u32[]{:S(2)}) collective-permute-start(bf16[128,512]{1,0:T(8,128)(2,1)S(1)} %shard_map.112.refs_3_), channel_id=1, source_target_pairs={{4,0},{8,4},{12,8},{14,12},{10,14},{6,10},{2,6},{0,2},{5,1},{9,5},... | collective-permute-start | bytes 393224 | tf_op jit(solution)/shard_map/ppermute | solution.py:221
  92.6 1.3 collective-permute-done.39.refs_4_
  94.0 2.1 %collective-permute-start.43 = (bf16[128,512]{1,0:T(8,128)(2,1)S(1)}, bf16[128,512]{1,0:T(8,128)(2,1)S(1)}, u32[]{:S(2)}, u32[]{:S(2)}) collective-permute-start(bf16[128,512]{1,0:T(8,128)(2,1)S(1)} %collective-permute-done.39.refs_4_), channel_id=1, source_target_pairs={{4,0},{8,4},{12,8},{14,12},{10,14},{6,10},{2,6},{0,2},{5,1},{9,5},... | collective-permute-start | bytes 393224 | tf_op jit(solution)/shard_map/ppermute | solution.py:221
  96.1 1.8 %collective-permute-done.36.refs_1_ = bf16[128,512]{1,0:T(8,128)(2,1)S(1)} collective-permute-done((bf16[128,512]{1,0:T(8,128)(2,1)S(1)}, bf16[128,512]{1,0:T(8,128)(2,1)S(1)}, u32[]{:S(2)}, u32[]{:S(2)}) %collective-permute-start.36) | collective-permute-done | bytes 131104 | tf_op jit(solution)/shard_map/ppermute | solution.py:220
  98.0 1.9 %collective-permute-start.42 = (bf16[128,512]{1,0:T(8,128)(2,1)S(1)}, bf16[128,512]{1,0:T(8,128)(2,1)S(1)}, u32[]{:S(2)}, u32[]{:S(2)}) collective-permute-start(bf16[128,512]{1,0:T(8,128)(2,1)S(1)} %collective-permute-done.38.refs_3_), channel_id=1, source_target_pairs={{4,0},{8,4},{12,8},{14,12},{10,14},{6,10},{2,6},{0,2},{5,1},{9,5},... | collective-permute-start | bytes 393224 | tf_op jit(solution)/shard_map/ppermute | solution.py:221
  100.0 2.5 %collective-permute-start.47 = (bf16[128,512]{1,0:T(8,128)(2,1)S(1)}, bf16[128,512]{1,0:T(8,128)(2,1)S(1)}, u32[]{:S(2)}, u32[]{:S(2)}) collective-permute-start(bf16[128,512]{1,0:T(8,128)(2,1)S(1)} %collective-permute-done.43.refs_4_), channel_id=1, source_target_pairs={{4,0},{8,4},{12,8},{14,12},{10,14},{6,10},{2,6},{0,2},{5,1},{9,5},... | collective-permute-start | bytes 393224 | tf_op jit(solution)/shard_map/ppermute | solution.py:221
  104.7 2.7 %collective-permute-start.46 = (bf16[128,512]{1,0:T(8,128)(2,1)S(1)}, bf16[128,512]{1,0:T(8,128)(2,1)S(1)}, u32[]{:S(2)}, u32[]{:S(2)}) collective-permute-start(bf16[128,512]{1,0:T(8,128)(2,1)S(1)} %collective-permute-done.42.refs_3_), channel_id=1, source_target_pairs={{4,0},{8,4},{12,8},{14,12},{10,14},{6,10},{2,6},{0,2},{5,1},{9,5},... | collective-permute-start | bytes 393224 | tf_op jit(solution)/shard_map/ppermute | solution.py:221
  108.6 2.1 %collective-permute-start.49 = (bf16[128,512]{1,0:T(8,128)(2,1)S(1)}, bf16[128,512]{1,0:T(8,128)(2,1)S(1)}, u32[]{:S(2)}, u32[]{:S(2)}) collective-permute-start(bf16[128,512]{1,0:T(8,128)(2,1)S(1)} %collective-permute-done.47.refs_4_), channel_id=1, source_target_pairs={{4,0},{8,4},{12,8},{14,12},{10,14},{6,10},{2,6},{0,2},{5,1},{9,5},... | collective-permute-start | bytes 393224 | tf_op jit(solution)/shard_map/ppermute | solution.py:226
  115.1 2.0 %collective-permute-start.53 = (bf16[128,512]{1,0:T(8,128)(2,1)S(1)}, bf16[128,512]{1,0:T(8,128)(2,1)S(1)}, u32[]{:S(2)}, u32[]{:S(2)}) collective-permute-start(bf16[128,512]{1,0:T(8,128)(2,1)S(1)} %get-tuple-element.15.refs_1_), channel_id=1, source_target_pairs={{4,0},{8,4},{12,8},{14,12},{10,14},{6,10},{2,6},{0,2},{5,1},{9,5},... | collective-permute-start | bytes 393224 | tf_op jit(solution)/shard_map/ppermute | solution.py:221
  120.2 2.0 %collective-permute-start.52 = (bf16[128,512]{1,0:T(8,128)(2,1)S(1)}, bf16[128,512]{1,0:T(8,128)(2,1)S(1)}, u32[]{:S(2)}, u32[]{:S(2)}) collective-permute-start(bf16[128,512]{1,0:T(8,128)(2,1)S(1)} %get-tuple-element.13.refs_0_), channel_id=1, source_target_pairs={{4,0},{8,4},{12,8},{14,12},{10,14},{6,10},{2,6},{0,2},{5,1},{9,5},... | collective-permute-start | bytes 393224 | tf_op jit(solution)/shard_map/ppermute | solution.py:221
  123.1 2.2 %collective-permute-done.50.refs_1_ = bf16[128,512]{1,0:T(8,128)(2,1)S(1)} collective-permute-done((bf16[128,512]{1,0:T(8,128)(2,1)S(1)}, bf16[128,512]{1,0:T(8,128)(2,1)S(1)}, u32[]{:S(2)}, u32[]{:S(2)}) %collective-permute-start.50) | collective-permute-done | bytes 131104 | tf_op jit(solution)/shard_map/ppermute | solution.py:220
  126.4 1.8 %collective-permute-done.51.refs_2_ = bf16[128,512]{1,0:T(8,128)(2,1)S(1)} collective-permute-done((bf16[128,512]{1,0:T(8,128)(2,1)S(1)}, bf16[128,512]{1,0:T(8,128)(2,1)S(1)}, u32[]{:S(2)}, u32[]{:S(2)}) %collective-permute-start.51) | collective-permute-done | bytes 131104 | tf_op jit(solution)/shard_map/ppermute | solution.py:220
  130.2 1.4 collective-permute-start.61
  132.3 1.4 collective-permute-done.55.refs_2_
  133.7 1.8 %collective-permute-start.59 = (bf16[128,512]{1,0:T(8,128)(2,1)S(1)}, bf16[128,512]{1,0:T(8,128)(2,1)S(1)}, u32[]{:S(2)}, u32[]{:S(2)}) collective-permute-start(bf16[128,512]{1,0:T(8,128)(2,1)S(1)} %collective-permute-done.55.refs_2_), channel_id=1, source_target_pairs={{0,4},{4,8},{8,12},{12,14},{14,10},{10,6},{6,2},{2,0},{1,5},{5,9},... | collective-permute-start | bytes 393224 | tf_op jit(solution)/shard_map/ppermute | solution.py:220
  142.6 1.4 collective-permute-start.67
  147.6 1.4 collective-permute-start.71
  151.4 1.4 collective-permute-start.70
  152.8 1.4 collective-permute-start.75
  159.3 1.4 collective-permute-start.77
  164.4 1.4 collective-permute-done.76.refs_0_
  165.7 2.8 %shard_map.129 = (bf16[256,512]{1,0:T(8,128)(2,1)}, f32[256,512]{1,0:T(8,128)}) custom-call(s32[1]{0:T(128)} %bitcast.me_ref, bf16[4096,2048]{1,0:T(8,128)(2,1)S(1)} %bitcast.3, f32[256,2048]{1,0:T(8,128)S(1)} %shard_map.128.total_ref, f32[1,2048]{1,0:T(1,128)S(1)} %bitcast.8, f32[256,512]{1,0:T(8,128)S(1)} %pad_maximum_fusion.cell_ref, ...), custom_call_target="tpu_custom_call" | custom-call | flops 1610612736 | bytes 786432 | tf_op jit(solution)/shard_map/pallas_call | solution.py:145
  (173 shorter events, 68.2 us)
Async XLA Ops:
  0.6 9.6 %collective-permute-start.1 = (bf16[256,512]{1,0:T(8,128)(2,1)}, bf16[256,512]{1,0:T(8,128)(2,1)S(1)}, u32[]{:S(2)}, u32[]{:S(2)}) collective-permute-start(bf16[256,512]{1,0:T(8,128)(2,1)} %refs_0_.1), channel_id=1, source_target_pairs={{4,0},{8,4},{12,8},{14,12},{10,14},{6,10},{2,6},{0,2},{5,1},{9,5},... | collective-permute-start | bytes 786440 | tf_op jit(solution)/shard_map/ppermute | solution.py:221
  3.6 8.3 %collective-permute-start = (bf16[256,512]{1,0:T(8,128)(2,1)}, bf16[256,512]{1,0:T(8,128)(2,1)S(1)}, u32[]{:S(2)}, u32[]{:S(2)}) collective-permute-start(bf16[256,512]{1,0:T(8,128)(2,1)} %refs_0_.1), channel_id=1, source_target_pairs={{0,4},{4,8},{8,12},{12,14},{14,10},{10,6},{6,2},{2,0},{1,5},{5,9},... | collective-permute-start | bytes 786440 | tf_op jit(solution)/shard_map/ppermute | solution.py:220
  10.2 7.5 %collective-permute-start.3 = (bf16[256,512]{1,0:T(8,128)(2,1)S(1)}, bf16[256,512]{1,0:T(8,128)(2,1)S(1)}, u32[]{:S(2)}, u32[]{:S(2)}) collective-permute-start(bf16[256,512]{1,0:T(8,128)(2,1)S(1)} %collective-permute-done.1.refs_2_), channel_id=1, source_target_pairs={{4,0},{8,4},{12,8},{14,12},{10,14},{6,10},{2,6},{0,2},{5,1},{9,5},... | collective-permute-start | bytes 786440 | tf_op jit(solution)/shard_map/ppermute | solution.py:221
  11.9 7.2 %collective-permute-start.2 = (bf16[256,512]{1,0:T(8,128)(2,1)S(1)}, bf16[256,512]{1,0:T(8,128)(2,1)S(1)}, u32[]{:S(2)}, u32[]{:S(2)}) collective-permute-start(bf16[256,512]{1,0:T(8,128)(2,1)S(1)} %collective-permute-done.refs_1_), channel_id=1, source_target_pairs={{0,4},{4,8},{8,12},{12,14},{14,10},{10,6},{6,2},{2,0},{1,5},{5,9},... | collective-permute-start | bytes 786440 | tf_op jit(solution)/shard_map/ppermute | solution.py:220
  17.7 6.6 %collective-permute-start.5 = (bf16[256,512]{1,0:T(8,128)(2,1)S(1)}, bf16[256,512]{1,0:T(8,128)(2,1)S(1)}, u32[]{:S(2)}, u32[]{:S(2)}) collective-permute-start(bf16[256,512]{1,0:T(8,128)(2,1)S(1)} %collective-permute-done.3.refs_2_), channel_id=1, source_target_pairs={{4,0},{8,4},{12,8},{14,12},{10,14},{6,10},{2,6},{0,2},{5,1},{9,5},... | collective-permute-start | bytes 786440 | tf_op jit(solution)/shard_map/ppermute | solution.py:221
  19.1 6.8 %collective-permute-start.4 = (bf16[256,512]{1,0:T(8,128)(2,1)S(1)}, bf16[256,512]{1,0:T(8,128)(2,1)S(1)}, u32[]{:S(2)}, u32[]{:S(2)}) collective-permute-start(bf16[256,512]{1,0:T(8,128)(2,1)S(1)} %collective-permute-done.2.refs_1_), channel_id=1, source_target_pairs={{0,4},{4,8},{8,12},{12,14},{14,10},{10,6},{6,2},{2,0},{1,5},{5,9},... | collective-permute-start | bytes 786440 | tf_op jit(solution)/shard_map/ppermute | solution.py:220
  24.3 7.4 %collective-permute-start.7 = (bf16[128,512]{1,0:T(8,128)(2,1)S(1)}, bf16[128,512]{1,0:T(8,128)(2,1)S(1)}, u32[]{:S(2)}, u32[]{:S(2)}) collective-permute-start(bf16[128,512]{1,0:T(8,128)(2,1)S(1)} %slice.9), channel_id=1, source_target_pairs={{4,0},{8,4},{12,8},{14,12},{10,14},{6,10},{2,6},{0,2},{5,1},{9,5},... | collective-permute-start | bytes 393224 | tf_op jit(solution)/shard_map/ppermute | solution.py:231
  25.9 9.3 %collective-permute-start.6 = (bf16[128,512]{1,0:T(8,128)(2,1)S(1)}, bf16[128,512]{1,0:T(8,128)(2,1)S(1)}, u32[]{:S(2)}, u32[]{:S(2)}) collective-permute-start(bf16[128,512]{1,0:T(8,128)(2,1)S(1)} %slice.8), channel_id=1, source_target_pairs={{0,4},{4,8},{8,12},{12,14},{14,10},{10,6},{6,2},{2,0},{1,5},{5,9},... | collective-permute-start | bytes 393224 | tf_op jit(solution)/shard_map/ppermute | solution.py:230
  33.1 8.4 %collective-permute-start.11 = (bf16[128,512]{1,0:T(8,128)(2,1)S(1)}, bf16[128,512]{1,0:T(8,128)(2,1)S(1)}, u32[]{:S(2)}, u32[]{:S(2)}) collective-permute-start(bf16[128,512]{1,0:T(8,128)(2,1)S(1)} %shard_map.100.refs_3_), channel_id=1, source_target_pairs={{4,0},{8,4},{12,8},{14,12},{10,14},{6,10},{2,6},{0,2},{5,1},{9,5},... | collective-permute-start | bytes 393224 | tf_op jit(solution)/shard_map/ppermute | solution.py:221
  34.7 6.4 %collective-permute-start.9 = (bf16[128,512]{1,0:T(8,128)(2,1)S(1)}, bf16[128,512]{1,0:T(8,128)(2,1)S(1)}, u32[]{:S(2)}, u32[]{:S(2)}) collective-permute-start(bf16[128,512]{1,0:T(8,128)(2,1)S(1)} %shard_map.100.refs_3_), channel_id=1, source_target_pairs={{0,4},{4,8},{8,12},{12,14},{14,10},{10,6},{6,2},{2,0},{1,5},{5,9},... | collective-permute-start | bytes 393224 | tf_op jit(solution)/shard_map/ppermute | solution.py:220
  35.5 7.6 %collective-permute-start.8 = (bf16[128,512]{1,0:T(8,128)(2,1)S(1)}, bf16[128,512]{1,0:T(8,128)(2,1)S(1)}, u32[]{:S(2)}, u32[]{:S(2)}) collective-permute-start(bf16[128,512]{1,0:T(8,128)(2,1)S(1)} %shard_map.99.refs_2_), channel_id=1, source_target_pairs={{0,4},{4,8},{8,12},{12,14},{14,10},{10,6},{6,2},{2,0},{1,5},{5,9},... | collective-permute-start | bytes 393224 | tf_op jit(solution)/shard_map/ppermute | solution.py:220
  37.2 6.6 %collective-permute-start.10 = (bf16[128,512]{1,0:T(8,128)(2,1)S(1)}, bf16[128,512]{1,0:T(8,128)(2,1)S(1)}, u32[]{:S(2)}, u32[]{:S(2)}) collective-permute-start(bf16[128,512]{1,0:T(8,128)(2,1)S(1)} %shard_map.99.refs_2_), channel_id=1, source_target_pairs={{4,0},{8,4},{12,8},{14,12},{10,14},{6,10},{2,6},{0,2},{5,1},{9,5},... | collective-permute-start | bytes 393224 | tf_op jit(solution)/shard_map/ppermute | solution.py:221
  41.1 9.2 %collective-permute-start.13 = (bf16[128,512]{1,0:T(8,128)(2,1)S(1)}, bf16[128,512]{1,0:T(8,128)(2,1)S(1)}, u32[]{:S(2)}, u32[]{:S(2)}) collective-permute-start(bf16[128,512]{1,0:T(8,128)(2,1)S(1)} %collective-permute-done.9.refs_2_), channel_id=1, source_target_pairs={{0,4},{4,8},{8,12},{12,14},{14,10},{10,6},{6,2},{2,0},{1,5},{5,9},... | collective-permute-start | bytes 393224 | tf_op jit(solution)/shard_map/ppermute | solution.py:220
  43.1 7.1 %collective-permute-start.12 = (bf16[128,512]{1,0:T(8,128)(2,1)S(1)}, bf16[128,512]{1,0:T(8,128)(2,1)S(1)}, u32[]{:S(2)}, u32[]{:S(2)}) collective-permute-start(bf16[128,512]{1,0:T(8,128)(2,1)S(1)} %collective-permute-done.8.refs_1_), channel_id=1, source_target_pairs={{0,4},{4,8},{8,12},{12,14},{14,10},{10,6},{6,2},{2,0},{1,5},{5,9},... | collective-permute-start | bytes 393224 | tf_op jit(solution)/shard_map/ppermute | solution.py:220
  43.8 8.2 %collective-permute-start.14 = (bf16[128,512]{1,0:T(8,128)(2,1)S(1)}, bf16[128,512]{1,0:T(8,128)(2,1)S(1)}, u32[]{:S(2)}, u32[]{:S(2)}) collective-permute-start(bf16[128,512]{1,0:T(8,128)(2,1)S(1)} %collective-permute-done.10.refs_3_), channel_id=1, source_target_pairs={{4,0},{8,4},{12,8},{14,12},{10,14},{6,10},{2,6},{0,2},{5,1},{9,5},... | collective-permute-start | bytes 393224 | tf_op jit(solution)/shard_map/ppermute | solution.py:221
  46.7 6.8 %collective-permute-start.19 = (bf16[128,512]{1,0:T(8,128)(2,1)S(1)}, bf16[128,512]{1,0:T(8,128)(2,1)S(1)}, u32[]{:S(2)}, u32[]{:S(2)}) collective-permute-start(bf16[128,512]{1,0:T(8,128)(2,1)S(1)} %collective-permute-done.15.refs_4_), channel_id=1, source_target_pairs={{4,0},{8,4},{12,8},{14,12},{10,14},{6,10},{2,6},{0,2},{5,1},{9,5},... | collective-permute-start | bytes 393224 | tf_op jit(solution)/shard_map/ppermute | solution.py:221
  50.2 6.7 %collective-permute-start.16 = (bf16[128,512]{1,0:T(8,128)(2,1)S(1)}, bf16[128,512]{1,0:T(8,128)(2,1)S(1)}, u32[]{:S(2)}, u32[]{:S(2)}) collective-permute-start(bf16[128,512]{1,0:T(8,128)(2,1)S(1)} %collective-permute-done.12.refs_1_), channel_id=1, source_target_pairs={{0,4},{4,8},{8,12},{12,14},{14,10},{10,6},{6,2},{2,0},{1,5},{5,9},... | collective-permute-start | bytes 393224 | tf_op jit(solution)/shard_map/ppermute | solution.py:220
  50.2 6.7 %collective-permute-start.17 = (bf16[128,512]{1,0:T(8,128)(2,1)S(1)}, bf16[128,512]{1,0:T(8,128)(2,1)S(1)}, u32[]{:S(2)}, u32[]{:S(2)}) collective-permute-start(bf16[128,512]{1,0:T(8,128)(2,1)S(1)} %collective-permute-done.13.refs_2_), channel_id=1, source_target_pairs={{0,4},{4,8},{8,12},{12,14},{14,10},{10,6},{6,2},{2,0},{1,5},{5,9},... | collective-permute-start | bytes 393224 | tf_op jit(solution)/shard_map/ppermute | solution.py:220
  53.5 6.6 %collective-permute-start.21 = (bf16[128,512]{1,0:T(8,128)(2,1)S(1)}, bf16[128,512]{1,0:T(8,128)(2,1)S(1)}, u32[]{:S(2)}, u32[]{:S(2)}) collective-permute-start(bf16[128,512]{1,0:T(8,128)(2,1)S(1)} %collective-permute-done.19.refs_4_), channel_id=1, source_target_pairs={{4,0},{8,4},{12,8},{14,12},{10,14},{6,10},{2,6},{0,2},{5,1},{9,5},... | collective-permute-start | bytes 393224 | tf_op jit(solution)/shard_map/ppermute | solution.py:226
  61.3 6.4 %collective-permute-start.25 = (bf16[128,512]{1,0:T(8,128)(2,1)S(1)}, bf16[128,512]{1,0:T(8,128)(2,1)S(1)}, u32[]{:S(2)}, u32[]{:S(2)}) collective-permute-start(bf16[128,512]{1,0:T(8,128)(2,1)S(1)} %get-tuple-element.11.refs_1_), channel_id=1, source_target_pairs={{4,0},{8,4},{12,8},{14,12},{10,14},{6,10},{2,6},{0,2},{5,1},{9,5},... | collective-permute-start | bytes 393224 | tf_op jit(solution)/shard_map/ppermute | solution.py:221
  63.7 6.6 %collective-permute-start.22 = (bf16[128,512]{1,0:T(8,128)(2,1)S(1)}, bf16[128,512]{1,0:T(8,128)(2,1)S(1)}, u32[]{:S(2)}, u32[]{:S(2)}) collective-permute-start(bf16[128,512]{1,0:T(8,128)(2,1)S(1)} %get-tuple-element.10.refs_0_), channel_id=1, source_target_pairs={{0,4},{4,8},{8,12},{12,14},{14,10},{10,6},{6,2},{2,0},{1,5},{5,9},... | collective-permute-start | bytes 393224 | tf_op jit(solution)/shard_map/ppermute | solution.py:220
  64.6 7.5 %collective-permute-start.23 = (bf16[128,512]{1,0:T(8,128)(2,1)S(1)}, bf16[128,512]{1,0:T(8,128)(2,1)S(1)}, u32[]{:S(2)}, u32[]{:S(2)}) collective-permute-start(bf16[128,512]{1,0:T(8,128)(2,1)S(1)} %get-tuple-element.11.refs_1_), channel_id=1, source_target_pairs={{0,4},{4,8},{8,12},{12,14},{14,10},{10,6},{6,2},{2,0},{1,5},{5,9},... | collective-permute-start | bytes 393224 | tf_op jit(solution)/shard_map/ppermute | solution.py:220
  65.3 6.9 %collective-permute-start.24 = (bf16[128,512]{1,0:T(8,128)(2,1)S(1)}, bf16[128,512]{1,0:T(8,128)(2,1)S(1)}, u32[]{:S(2)}, u32[]{:S(2)}) collective-permute-start(bf16[128,512]{1,0:T(8,128)(2,1)S(1)} %get-tuple-element.10.refs_0_), channel_id=1, source_target_pairs={{4,0},{8,4},{12,8},{14,12},{10,14},{6,10},{2,6},{0,2},{5,1},{9,5},... | collective-permute-start | bytes 393224 | tf_op jit(solution)/shard_map/ppermute | solution.py:221
  67.7 6.4 %collective-permute-start.29 = (bf16[128,512]{1,0:T(8,128)(2,1)S(1)}, bf16[128,512]{1,0:T(8,128)(2,1)S(1)}, u32[]{:S(2)}, u32[]{:S(2)}) collective-permute-start(bf16[128,512]{1,0:T(8,128)(2,1)S(1)} %collective-permute-done.25.refs_4_), channel_id=1, source_target_pairs={{4,0},{8,4},{12,8},{14,12},{10,14},{6,10},{2,6},{0,2},{5,1},{9,5},... | collective-permute-start | bytes 393224 | tf_op jit(solution)/shard_map/ppermute | solution.py:221
  74.2 6.7 %collective-permute-start.33 = (bf16[128,512]{1,0:T(8,128)(2,1)S(1)}, bf16[128,512]{1,0:T(8,128)(2,1)S(1)}, u32[]{:S(2)}, u32[]{:S(2)}) collective-permute-start(bf16[128,512]{1,0:T(8,128)(2,1)S(1)} %collective-permute-done.29.refs_4_), channel_id=1, source_target_pairs={{4,0},{8,4},{12,8},{14,12},{10,14},{6,10},{2,6},{0,2},{5,1},{9,5},... | collective-permute-start | bytes 393224 | tf_op jit(solution)/shard_map/ppermute | solution.py:221
  76.2 7.2 %collective-permute-start.30 = (bf16[128,512]{1,0:T(8,128)(2,1)S(1)}, bf16[128,512]{1,0:T(8,128)(2,1)S(1)}, u32[]{:S(2)}, u32[]{:S(2)}) collective-permute-start(bf16[128,512]{1,0:T(8,128)(2,1)S(1)} %collective-permute-done.26.refs_1_), channel_id=1, source_target_pairs={{0,4},{4,8},{8,12},{12,14},{14,10},{10,6},{6,2},{2,0},{1,5},{5,9},... | collective-permute-start | bytes 393224 | tf_op jit(solution)/shard_map/ppermute | solution.py:220
  77.1 7.6 %collective-permute-start.31 = (bf16[128,512]{1,0:T(8,128)(2,1)S(1)}, bf16[128,512]{1,0:T(8,128)(2,1)S(1)}, u32[]{:S(2)}, u32[]{:S(2)}) collective-permute-start(bf16[128,512]{1,0:T(8,128)(2,1)S(1)} %collective-permute-done.27.refs_2_), channel_id=1, source_target_pairs={{0,4},{4,8},{8,12},{12,14},{14,10},{10,6},{6,2},{2,0},{1,5},{5,9},... | collective-permute-start | bytes 393224 | tf_op jit(solution)/shard_map/ppermute | solution.py:220
  78.0 6.7 %collective-permute-start.32 = (bf16[128,512]{1,0:T(8,128)(2,1)S(1)}, bf16[128,512]{1,0:T(8,128)(2,1)S(1)}, u32[]{:S(2)}, u32[]{:S(2)}) collective-permute-start(bf16[128,512]{1,0:T(8,128)(2,1)S(1)} %collective-permute-done.28.refs_3_), channel_id=1, source_target_pairs={{4,0},{8,4},{12,8},{14,12},{10,14},{6,10},{2,6},{0,2},{5,1},{9,5},... | collective-permute-start | bytes 393224 | tf_op jit(solution)/shard_map/ppermute | solution.py:221
  83.3 6.8 %collective-permute-start.34 = (bf16[128,512]{1,0:T(8,128)(2,1)S(1)}, bf16[128,512]{1,0:T(8,128)(2,1)S(1)}, u32[]{:S(2)}, u32[]{:S(2)}) collective-permute-start(bf16[128,512]{1,0:T(8,128)(2,1)S(1)} %collective-permute-done.30.refs_1_), channel_id=1, source_target_pairs={{0,4},{4,8},{8,12},{12,14},{14,10},{10,6},{6,2},{2,0},{1,5},{5,9},... | collective-permute-start | bytes 393224 | tf_op jit(solution)/shard_map/ppermute | solution.py:224
  87.6 6.4 %collective-permute-start.39 = (bf16[128,512]{1,0:T(8,128)(2,1)S(1)}, bf16[128,512]{1,0:T(8,128)(2,1)S(1)}, u32[]{:S(2)}, u32[]{:S(2)}) collective-permute-start(bf16[128,512]{1,0:T(8,128)(2,1)S(1)} %shard_map.112.refs_3_), channel_id=1, source_target_pairs={{4,0},{8,4},{12,8},{14,12},{10,14},{6,10},{2,6},{0,2},{5,1},{9,5},... | collective-permute-start | bytes 393224 | tf_op jit(solution)/shard_map/ppermute | solution.py:221
  90.5 7.4 %collective-permute-start.36 = (bf16[128,512]{1,0:T(8,128)(2,1)S(1)}, bf16[128,512]{1,0:T(8,128)(2,1)S(1)}, u32[]{:S(2)}, u32[]{:S(2)}) collective-permute-start(bf16[128,512]{1,0:T(8,128)(2,1)S(1)} %shard_map.111.refs_2_), channel_id=1, source_target_pairs={{0,4},{4,8},{8,12},{12,14},{14,10},{10,6},{6,2},{2,0},{1,5},{5,9},... | collective-permute-start | bytes 393224 | tf_op jit(solution)/shard_map/ppermute | solution.py:220
  96.1 7.3 %collective-permute-start.41 = (bf16[128,512]{1,0:T(8,128)(2,1)S(1)}, bf16[128,512]{1,0:T(8,128)(2,1)S(1)}, u32[]{:S(2)}, u32[]{:S(2)}) collective-permute-start(bf16[128,512]{1,0:T(8,128)(2,1)S(1)} %collective-permute-done.37.refs_2_), channel_id=1, source_target_pairs={{0,4},{4,8},{8,12},{12,14},{14,10},{10,6},{6,2},{2,0},{1,5},{5,9},... | collective-permute-start | bytes 393224 | tf_op jit(solution)/shard_map/ppermute | solution.py:220
  97.9 6.5 %collective-permute-start.40 = (bf16[128,512]{1,0:T(8,128)(2,1)S(1)}, bf16[128,512]{1,0:T(8,128)(2,1)S(1)}, u32[]{:S(2)}, u32[]{:S(2)}) collective-permute-start(bf16[128,512]{1,0:T(8,128)(2,1)S(1)} %collective-permute-done.36.refs_1_), channel_id=1, source_target_pairs={{0,4},{4,8},{8,12},{12,14},{14,10},{10,6},{6,2},{2,0},{1,5},{5,9},... | collective-permute-start | bytes 393224 | tf_op jit(solution)/shard_map/ppermute | solution.py:220
  98.0 6.7 %collective-permute-start.42 = (bf16[128,512]{1,0:T(8,128)(2,1)S(1)}, bf16[128,512]{1,0:T(8,128)(2,1)S(1)}, u32[]{:S(2)}, u32[]{:S(2)}) collective-permute-start(bf16[128,512]{1,0:T(8,128)(2,1)S(1)} %collective-permute-done.38.refs_3_), channel_id=1, source_target_pairs={{4,0},{8,4},{12,8},{14,12},{10,14},{6,10},{2,6},{0,2},{5,1},{9,5},... | collective-permute-start | bytes 393224 | tf_op jit(solution)/shard_map/ppermute | solution.py:221
  100.0 8.7 %collective-permute-start.47 = (bf16[128,512]{1,0:T(8,128)(2,1)S(1)}, bf16[128,512]{1,0:T(8,128)(2,1)S(1)}, u32[]{:S(2)}, u32[]{:S(2)}) collective-permute-start(bf16[128,512]{1,0:T(8,128)(2,1)S(1)} %collective-permute-done.43.refs_4_), channel_id=1, source_target_pairs={{4,0},{8,4},{12,8},{14,12},{10,14},{6,10},{2,6},{0,2},{5,1},{9,5},... | collective-permute-start | bytes 393224 | tf_op jit(solution)/shard_map/ppermute | solution.py:221
  103.4 9.2 %collective-permute-start.45 = (bf16[128,512]{1,0:T(8,128)(2,1)S(1)}, bf16[128,512]{1,0:T(8,128)(2,1)S(1)}, u32[]{:S(2)}, u32[]{:S(2)}) collective-permute-start(bf16[128,512]{1,0:T(8,128)(2,1)S(1)} %collective-permute-done.41.refs_2_), channel_id=1, source_target_pairs={{0,4},{4,8},{8,12},{12,14},{14,10},{10,6},{6,2},{2,0},{1,5},{5,9},... | collective-permute-start | bytes 393224 | tf_op jit(solution)/shard_map/ppermute | solution.py:220
  104.4 8.2 %collective-permute-start.44 = (bf16[128,512]{1,0:T(8,128)(2,1)S(1)}, bf16[128,512]{1,0:T(8,128)(2,1)S(1)}, u32[]{:S(2)}, u32[]{:S(2)}) collective-permute-start(bf16[128,512]{1,0:T(8,128)(2,1)S(1)} %collective-permute-done.40.refs_1_), channel_id=1, source_target_pairs={{0,4},{4,8},{8,12},{12,14},{14,10},{10,6},{6,2},{2,0},{1,5},{5,9},... | collective-permute-start | bytes 393224 | tf_op jit(solution)/shard_map/ppermute | solution.py:220
  104.7 8.0 %collective-permute-start.46 = (bf16[128,512]{1,0:T(8,128)(2,1)S(1)}, bf16[128,512]{1,0:T(8,128)(2,1)S(1)}, u32[]{:S(2)}, u32[]{:S(2)}) collective-permute-start(bf16[128,512]{1,0:T(8,128)(2,1)S(1)} %collective-permute-done.42.refs_3_), channel_id=1, source_target_pairs={{4,0},{8,4},{12,8},{14,12},{10,14},{6,10},{2,6},{0,2},{5,1},{9,5},... | collective-permute-start | bytes 393224 | tf_op jit(solution)/shard_map/ppermute | solution.py:221
  115.1 7.1 %collective-permute-start.53 = (bf16[128,512]{1,0:T(8,128)(2,1)S(1)}, bf16[128,512]{1,0:T(8,128)(2,1)S(1)}, u32[]{:S(2)}, u32[]{:S(2)}) collective-permute-start(bf16[128,512]{1,0:T(8,128)(2,1)S(1)} %get-tuple-element.15.refs_1_), channel_id=1, source_target_pairs={{4,0},{8,4},{12,8},{14,12},{10,14},{6,10},{2,6},{0,2},{5,1},{9,5},... | collective-permute-start | bytes 393224 | tf_op jit(solution)/shard_map/ppermute | solution.py:221
  120.1 8.1 %collective-permute-start.51 = (bf16[128,512]{1,0:T(8,128)(2,1)S(1)}, bf16[128,512]{1,0:T(8,128)(2,1)S(1)}, u32[]{:S(2)}, u32[]{:S(2)}) collective-permute-start(bf16[128,512]{1,0:T(8,128)(2,1)S(1)} %get-tuple-element.15.refs_1_), channel_id=1, source_target_pairs={{0,4},{4,8},{8,12},{12,14},{14,10},{10,6},{6,2},{2,0},{1,5},{5,9},... | collective-permute-start | bytes 393224 | tf_op jit(solution)/shard_map/ppermute | solution.py:220
  120.2 9.0 %collective-permute-start.52 = (bf16[128,512]{1,0:T(8,128)(2,1)S(1)}, bf16[128,512]{1,0:T(8,128)(2,1)S(1)}, u32[]{:S(2)}, u32[]{:S(2)}) collective-permute-start(bf16[128,512]{1,0:T(8,128)(2,1)S(1)} %get-tuple-element.13.refs_0_), channel_id=1, source_target_pairs={{4,0},{8,4},{12,8},{14,12},{10,14},{6,10},{2,6},{0,2},{5,1},{9,5},... | collective-permute-start | bytes 393224 | tf_op jit(solution)/shard_map/ppermute | solution.py:221
  122.1 8.1 %collective-permute-start.57 = (bf16[128,512]{1,0:T(8,128)(2,1)S(1)}, bf16[128,512]{1,0:T(8,128)(2,1)S(1)}, u32[]{:S(2)}, u32[]{:S(2)}) collective-permute-start(bf16[128,512]{1,0:T(8,128)(2,1)S(1)} %collective-permute-done.53.refs_4_), channel_id=1, source_target_pairs={{4,0},{8,4},{12,8},{14,12},{10,14},{6,10},{2,6},{0,2},{5,1},{9,5},... | collective-permute-start | bytes 393224 | tf_op jit(solution)/shard_map/ppermute | solution.py:221
  130.2 7.0 %collective-permute-start.61 = (bf16[128,512]{1,0:T(8,128)(2,1)S(1)}, bf16[128,512]{1,0:T(8,128)(2,1)S(1)}, u32[]{:S(2)}, u32[]{:S(2)}) collective-permute-start(bf16[128,512]{1,0:T(8,128)(2,1)S(1)} %collective-permute-done.57.refs_4_), channel_id=1, source_target_pairs={{4,0},{8,4},{12,8},{14,12},{10,14},{6,10},{2,6},{0,2},{5,1},{9,5},... | collective-permute-start | bytes 393224 | tf_op jit(solution)/shard_map/ppermute | solution.py:221
  131.6 6.8 %collective-permute-start.58 = (bf16[128,512]{1,0:T(8,128)(2,1)S(1)}, bf16[128,512]{1,0:T(8,128)(2,1)S(1)}, u32[]{:S(2)}, u32[]{:S(2)}) collective-permute-start(bf16[128,512]{1,0:T(8,128)(2,1)S(1)} %collective-permute-done.54.refs_1_), channel_id=1, source_target_pairs={{0,4},{4,8},{8,12},{12,14},{14,10},{10,6},{6,2},{2,0},{1,5},{5,9},... | collective-permute-start | bytes 393224 | tf_op jit(solution)/shard_map/ppermute | solution.py:220
  133.7 6.9 %collective-permute-start.59 = (bf16[128,512]{1,0:T(8,128)(2,1)S(1)}, bf16[128,512]{1,0:T(8,128)(2,1)S(1)}, u32[]{:S(2)}, u32[]{:S(2)}) collective-permute-start(bf16[128,512]{1,0:T(8,128)(2,1)S(1)} %collective-permute-done.55.refs_2_), channel_id=1, source_target_pairs={{0,4},{4,8},{8,12},{12,14},{14,10},{10,6},{6,2},{2,0},{1,5},{5,9},... | collective-permute-start | bytes 393224 | tf_op jit(solution)/shard_map/ppermute | solution.py:220
  152.8 6.5 %collective-permute-start.75 = (bf16[128,512]{1,0:T(8,128)(2,1)S(1)}, bf16[128,512]{1,0:T(8,128)(2,1)S(1)}, u32[]{:S(2)}, u32[]{:S(2)}) collective-permute-start(bf16[128,512]{1,0:T(8,128)(2,1)S(1)} %collective-permute-done.71.refs_4_), channel_id=1, source_target_pairs={{4,0},{8,4},{12,8},{14,12},{10,14},{6,10},{2,6},{0,2},{5,1},{9,5},... | collective-permute-start | bytes 393224 | tf_op jit(solution)/shard_map/ppermute | solution.py:221
  154.3 6.4 %collective-permute-start.72 = (bf16[128,512]{1,0:T(8,128)(2,1)S(1)}, bf16[128,512]{1,0:T(8,128)(2,1)S(1)}, u32[]{:S(2)}, u32[]{:S(2)}) collective-permute-start(bf16[128,512]{1,0:T(8,128)(2,1)S(1)} %collective-permute-done.68.refs_1_), channel_id=1, source_target_pairs={{0,4},{4,8},{8,12},{12,14},{14,10},{10,6},{6,2},{2,0},{1,5},{5,9},... | collective-permute-start | bytes 393224 | tf_op jit(solution)/shard_map/ppermute | solution.py:220
  156.0 6.7 %collective-permute-start.73 = (bf16[128,512]{1,0:T(8,128)(2,1)S(1)}, bf16[128,512]{1,0:T(8,128)(2,1)S(1)}, u32[]{:S(2)}, u32[]{:S(2)}) collective-permute-start(bf16[128,512]{1,0:T(8,128)(2,1)S(1)} %collective-permute-done.69.refs_2_), channel_id=1, source_target_pairs={{0,4},{4,8},{8,12},{12,14},{14,10},{10,6},{6,2},{2,0},{1,5},{5,9},... | collective-permute-start | bytes 393224 | tf_op jit(solution)/shard_map/ppermute | solution.py:220
  (41 other events, 286.5 us)

commit v3 on v2

--- a/solution.py
+++ b/solution.py
@@ -45,7 +45,7 @@
 
 
 def one_hot(ids, vocab):
-    return (ids[:, None] == jnp.arange(vocab, dtype=jnp.int32)[None, :]).astype(jnp.bfloat16)
+    return (ids[..., None] == jnp.arange(vocab, dtype=jnp.int32)).astype(jnp.bfloat16)
 
 
 def update_state(sums, cell):
@@ -116,9 +116,8 @@
         chunks = len(groups[0])
         rows = sum(block.shape[0] for block in groups[0])
         extra = [] if total is None else [total]
-        at = 0
         if first is not None:
-            onehot, at, embed = first
+            onehot, step, embed = first
             extra = [onehot, embed]
 
         def kernel(me_ref, weight_ref, *refs):
@@ -129,7 +128,7 @@
                 if total is not None:
                     value = extra_refs[0][:, columns] + value
                 if first is not None:
-                    value = dot32(extra_refs[0][at : at + rows], extra_refs[1][:, columns]) + value
+                    value = dot32(extra_refs[0][step], extra_refs[1][:, columns]) + value
                 out_ref[:, columns] = value
 
         return call(
@@ -149,18 +148,18 @@
         out_specs=[pl.BlockSpec(memory_space=pltpu.VMEM)] * len(outs),
         out_shape=outs,
         compiler_params=pltpu.CompilerParams(vmem_limit_bytes=SCRATCH),
-        cost_estimate=pl.CostEstimate(flops=flops, bytes_accessed=size, transcendentals=0),
+        cost_estimate=pl.CostEstimate(flops=0, bytes_accessed=size, transcendentals=0),
     )(*operands)
 
 
-def inter_of(gather, total, last, row, onehot, at, inter_embed, away):
+def inter_of(gather, total, last, row, onehot, step, inter_embed, away):
     rows = last.shape[0]
 
     def kernel(me_ref, weight_ref, total_ref, last_ref, onehot_ref, embed_ref, out_ref):
         product = total_ref[row : row + rows] + gather.terms(
             me_ref, weight_ref, [last_ref[...]], [away], slice(None)
         )
-        lookup = dot32(onehot_ref[at + row : at + row + rows], embed_ref[...])
+        lookup = dot32(onehot_ref[step, row : row + rows], embed_ref[...])
         out_ref[...] = (lookup * product).astype(out_ref.dtype)
 
     return call(
@@ -210,31 +209,14 @@
     )
 
 
-def arrivals(block, ring, last):
-    devices = len(ring)
+def after(block, total):
+    return lax.optimization_barrier((block, total))[0]
+
+
+def ringed(devices, chunks, first_chunks):
+    ring = ring_of(devices)
     up = [(ring[i], ring[(i + 1) % devices]) for i in range(devices)]
     down = [(b, a) for a, b in up]
-    blocks = [block]
-    below = above = block
-    for _ in range(devices // 2 - 1):
-        below = lax.ppermute(below, "mp", up)
-        above = lax.ppermute(above, "mp", down)
-        blocks += [below, above]
-    if last == "up":
-        farthest = [lax.ppermute(below, "mp", up)]
-    elif last == "down":
-        farthest = [lax.ppermute(above, "mp", down)]
-    else:
-        half = block.shape[0] // 2
-        farthest = [
-            lax.ppermute(below[:half], "mp", up),
-            lax.ppermute(above[half:], "mp", down),
-        ]
-    return blocks, farthest
-
-
-def ringed(devices, chunks, first_chunks):
-    ring = ring_of(devices)
     away = [-((k + 1) // 2) if k % 2 else k // 2 for k in range(devices)]
 
     def local(
@@ -247,34 +229,45 @@
         to_gate = Gather(me, gate_weight, devices, part, False)
         mix = mix_matrix(GATE_KINDS * LANES)
         bias = gate_bias.reshape(1, -1)
-        onehot = one_hot(byte_ids.reshape(-1), inter_embed.shape[0])
+        onehot = one_hot(byte_ids, inter_embed.shape[0])
 
         def gathered(blocks, gather, first=None):
-            ways = ["up" if c % 2 == 0 else "down" for c in range(len(blocks))]
-            if len(blocks) == 1:
-                ways = ["both"]
-            arrived, farthest = zip(*[arrivals(b, ring, way) for b, way in zip(blocks, ways)])
-            total = gather.add([[b[0] for b in arrived]], away[:1], first=first)
+            count = len(blocks)
+            total = gather.add([blocks], away[:1], first=first)
+            below = [lax.ppermute(block, "mp", up) for block in blocks]
+            above = [lax.ppermute(block, "mp", down) for block in blocks]
             for k in range(1, devices - 1, 2):
-                total = gather.add(
-                    [[b[k] for b in arrived], [b[k + 1] for b in arrived]],
-                    away[k : k + 2],
-                    total,
-                )
-            return total, [last for lasts in farthest for last in lasts]
+                ready = total
+                total = gather.add([below, above], away[k : k + 2], total)
+                if k + 2 < devices - 1:
+                    below = [lax.ppermute(after(block, ready), "mp", up) for block in below]
+                    above = [lax.ppermute(after(block, ready), "mp", down) for block in above]
+            if count == 1:
+                half = blocks[0].shape[0] // 2
+                lasts = [
+                    lax.ppermute(after(below[0][:half], ready), "mp", up),
+                    lax.ppermute(after(above[0][half:], ready), "mp", down),
+                ]
+            else:
+                lasts = [
+                    lax.ppermute(after(above[c], ready), "mp", down)
+                    if c % 2
+                    else lax.ppermute(after(below[c], ready), "mp", up)
+                    for c in range(count)
+                ]
+            return total, lasts
 
         rows = streams // first_chunks
         hiddens = [h_start[c * rows : (c + 1) * rows] for c in range(first_chunks)]
         rows = streams // chunks
         cells = [(c_start, c * rows) for c in range(chunks)]
         for step in range(steps):
-            at = step * streams
             total, lasts = gathered(hiddens, to_inter)
             inters = [
-                inter_of(to_inter, total, last, c * rows, onehot, at, inter_embed, away[-1])
+                inter_of(to_inter, total, last, c * rows, onehot, step, inter_embed, away[-1])
                 for c, last in enumerate(lasts)
             ]
-            total, lasts = gathered(inters, to_gate, (onehot, at, gate_embed))
+            total, lasts = gathered(inters, to_gate, (onehot, step, gate_embed))
             if step + 1 < steps:
                 hiddens, updated = zip(
                     *[
@@ -305,5 +298,5 @@
     )
     out_specs = (P(("groups", "batch"), "mp"), P(("groups", "batch"), "mp"))
     devices = mesh.shape["mp"]
-    local = ringed(devices, 2, 1) if 2 < devices <= MAX_RING else plain
+    local = ringed(devices, 2, 2) if 2 < devices <= MAX_RING else plain
     return jax.shard_map(local, mesh=mesh, in_specs=in_specs, out_specs=out_specs, check_vma=False)

time: 169 us -> 155 us (0.917)
  waiting for transfers between devices: 47.9 us -> 29.9 us
  starting transfers between devices: 85.1 us -> 91.6 us
    ppermute x78 -> x84, waiting for transfers between devices: 47.9 us -> 29.9 us  [the longest x24 10.4 us: gathered(): above = [lax.ppermute(after(block, ready), 'mp', down) for block in above]]
    ppermute x78 -> x84, starting transfers between devices: 85.1 us -> 91.6 us  [the longest x24 41.3 us: gathered(): below = [lax.ppermute(after(block, ready), 'mp', up) for block in below]]
    unnamed x22, local copies, waits for them, and re-layouts: 4.21 us -> 2.25 us
  transfers between devices with their start and end apart: 78 -> 84, of which waited for: 32 -> 38; matrix products, arithmetic and copies ran while one was open for 1% -> 0% of each run, Pallas kernels for 16% -> 17%
where the time goes in v3:
time: 155 us
  starting transfers between devices  91.6 us (59%)
  waiting for transfers between devices  29.9 us (19%)
  Pallas kernels  28.8 us (19%)
  local copies, waits for them, and re-layouts  3.24 us (2%)
    ppermute x24, starting transfers between devices, gathered(): below = [lax.ppermute(after(block, ready), 'mp', up) for block in below]  41.3 us
    pallas_call x35, Pallas kernels, call(): pl.pallas_call(kernel, in_specs=[pl.BlockSpec(memory_space=pltpu.SMEM)] +...  28.8 us
    ppermute x12, starting transfers between devices, gathered(): below = [lax.ppermute(block, 'mp', up) for block in blocks]  21.2 us
    ppermute x24, waiting for transfers between devices, gathered(): above = [lax.ppermute(after(block, ready), 'mp', down) for block in above]  10.4 us
    ppermute x6, starting transfers between devices, gathered(): lax.ppermute(after(below[c], ready), 'mp', up)  10.3 us
    ppermute x24, starting transfers between devices, gathered(): above = [lax.ppermute(after(block, ready), 'mp', down) for block in above]  10.2 us
    ppermute x24, waiting for transfers between devices, gathered(): below = [lax.ppermute(after(block, ready), 'mp', up) for block in below]  7.7 us
    ppermute x12, starting transfers between devices, gathered(): above = [lax.ppermute(block, 'mp', down) for block in blocks]  6.12 us
  transfers between devices with their start and end apart: 84, of which 38 were waited for; matrix products, arithmetic and copies ran while one was open for 0% of the time, Pallas kernels for 17%

profile of v3, /device:TPU:0, one launch (start us, length us, event | category | flops | bytes accessed | tf_op | source)
XLA Modules:
  0.0 155.0 jit_solution(13736810278891198042)
XLA Ops:
  1.6 3.1 %collective-permute-start = (bf16[128,512]{1,0:T(8,128)(2,1)S(1)}, bf16[128,512]{1,0:T(8,128)(2,1)S(1)}, u32[]{:S(2)}, u32[]{:S(2)}) collective-permute-start(bf16[128,512]{1,0:T(8,128)(2,1)S(1)} %get-tuple-element.139.refs_0_), channel_id=1, source_target_pairs={{0,4},{4,8},{8,12},{12,14},{14,10},{10,6},{6,2},{2,0},{1,5},{5,9},... | collective-permute-start | bytes 393224 | tf_op jit(solution)/shard_map/ppermute | solution.py:237
  4.7 2.0 %collective-permute-start.1 = (bf16[128,512]{1,0:T(8,128)(2,1)S(1)}, bf16[128,512]{1,0:T(8,128)(2,1)S(1)}, u32[]{:S(2)}, u32[]{:S(2)}) collective-permute-start(bf16[128,512]{1,0:T(8,128)(2,1)S(1)} %get-tuple-element.138.refs_1_), channel_id=1, source_target_pairs={{0,4},{4,8},{8,12},{12,14},{14,10},{10,6},{6,2},{2,0},{1,5},{5,9},... | collective-permute-start | bytes 393224 | tf_op jit(solution)/shard_map/ppermute | solution.py:237
  6.7 2.2 %copy-done = bf16[512,4096]{1,0:T(8,128)(2,1)S(1)} copy-done((bf16[512,4096]{1,0:T(8,128)(2,1)S(1)}, bf16[512,4096]{1,0:T(8,128)(2,1)}, u32[]{:S(2)}) %copy-start) | copy-done | bytes 4194328
  9.3 2.1 %collective-permute-start.4 = (bf16[128,512]{1,0:T(8,128)(2,1)S(1)}, bf16[128,512]{1,0:T(8,128)(2,1)S(1)}, u32[]{:S(2)}, u32[]{:S(2)}) collective-permute-start(bf16[128,512]{1,0:T(8,128)(2,1)S(1)} %collective-permute-done.refs_1_), channel_id=1, source_target_pairs={{0,4},{4,8},{8,12},{12,14},{14,10},{10,6},{6,2},{2,0},{1,5},{5,9},... | collective-permute-start | bytes 393224 | tf_op jit(solution)/shard_map/ppermute | solution.py:243
  11.4 2.0 %collective-permute-start.5 = (bf16[128,512]{1,0:T(8,128)(2,1)S(1)}, bf16[128,512]{1,0:T(8,128)(2,1)S(1)}, u32[]{:S(2)}, u32[]{:S(2)}) collective-permute-start(bf16[128,512]{1,0:T(8,128)(2,1)S(1)} %collective-permute-done.1.refs_2_), channel_id=1, source_target_pairs={{0,4},{4,8},{8,12},{12,14},{14,10},{10,6},{6,2},{2,0},{1,5},{5,9},... | collective-permute-start | bytes 393224 | tf_op jit(solution)/shard_map/ppermute | solution.py:243
  13.9 1.8 %collective-permute-done.4.refs_1_ = bf16[128,512]{1,0:T(8,128)(2,1)S(1)} collective-permute-done((bf16[128,512]{1,0:T(8,128)(2,1)S(1)}, bf16[128,512]{1,0:T(8,128)(2,1)S(1)}, u32[]{:S(2)}, u32[]{:S(2)}) %collective-permute-start.4) | collective-permute-done | bytes 131104 | tf_op jit(solution)/shard_map/ppermute | solution.py:243
  15.7 1.7 %collective-permute-start.8 = (bf16[128,512]{1,0:T(8,128)(2,1)S(1)}, bf16[128,512]{1,0:T(8,128)(2,1)S(1)}, u32[]{:S(2)}, u32[]{:S(2)}) collective-permute-start(bf16[128,512]{1,0:T(8,128)(2,1)S(1)} %collective-permute-done.4.refs_1_), channel_id=1, source_target_pairs={{0,4},{4,8},{8,12},{12,14},{14,10},{10,6},{6,2},{2,0},{1,5},{5,9},... | collective-permute-start | bytes 393224 | tf_op jit(solution)/shard_map/ppermute | solution.py:243
  18.5 1.7 %collective-permute-start.9 = (bf16[128,512]{1,0:T(8,128)(2,1)S(1)}, bf16[128,512]{1,0:T(8,128)(2,1)S(1)}, u32[]{:S(2)}, u32[]{:S(2)}) collective-permute-start(bf16[128,512]{1,0:T(8,128)(2,1)S(1)} %collective-permute-done.5.refs_2_), channel_id=1, source_target_pairs={{0,4},{4,8},{8,12},{12,14},{14,10},{10,6},{6,2},{2,0},{1,5},{5,9},... | collective-permute-start | bytes 393224 | tf_op jit(solution)/shard_map/ppermute | solution.py:243
  21.4 1.7 %collective-permute-start.12 = (bf16[128,512]{1,0:T(8,128)(2,1)S(1)}, bf16[128,512]{1,0:T(8,128)(2,1)S(1)}, u32[]{:S(2)}, u32[]{:S(2)}) collective-permute-start(bf16[128,512]{1,0:T(8,128)(2,1)S(1)} %collective-permute-done.8.refs_1_), channel_id=1, source_target_pairs={{0,4},{4,8},{8,12},{12,14},{14,10},{10,6},{6,2},{2,0},{1,5},{5,9},... | collective-permute-start | bytes 393224 | tf_op jit(solution)/shard_map/ppermute | solution.py:255
  26.7 2.1 %collective-permute-start.14 = (bf16[128,512]{1,0:T(8,128)(2,1)S(1)}, bf16[128,512]{1,0:T(8,128)(2,1)S(1)}, u32[]{:S(2)}, u32[]{:S(2)}) collective-permute-start(bf16[128,512]{1,0:T(8,128)(2,1)S(1)} %shard_map.99.refs_2_), channel_id=1, source_target_pairs={{0,4},{4,8},{8,12},{12,14},{14,10},{10,6},{6,2},{2,0},{1,5},{5,9},... | collective-permute-start | bytes 393224 | tf_op jit(solution)/shard_map/ppermute | solution.py:237
  33.9 1.3 collective-permute-start.18
  36.7 1.3 collective-permute-start.19
  40.0 1.4 collective-permute-start.22
  50.3 2.2 %collective-permute-done.26.refs_0_ = bf16[128,512]{1,0:T(8,128)(2,1)S(1)} collective-permute-done((bf16[128,512]{1,0:T(8,128)(2,1)S(1)}, bf16[128,512]{1,0:T(8,128)(2,1)S(1)}, u32[]{:S(2)}, u32[]{:S(2)}) %collective-permute-start.26) | collective-permute-done | bytes 131104 | tf_op jit(solution)/shard_map/ppermute | solution.py:255
  55.4 1.6 %collective-permute-start.31 = (bf16[128,512]{1,0:T(8,128)(2,1)S(1)}, bf16[128,512]{1,0:T(8,128)(2,1)S(1)}, u32[]{:S(2)}, u32[]{:S(2)}) collective-permute-start(bf16[128,512]{1,0:T(8,128)(2,1)S(1)} %get-tuple-element.91.refs_1_), channel_id=1, source_target_pairs={{4,0},{8,4},{12,8},{14,12},{10,14},{6,10},{2,6},{0,2},{5,1},{9,5},... | collective-permute-start | bytes 393224 | tf_op jit(solution)/shard_map/ppermute | solution.py:238
  57.6 1.5 collective-permute-start.30
  60.4 1.3 collective-permute-done.31.refs_4_
  61.8 1.4 collective-permute-start.35
  65.8 1.5 collective-permute-start.36
  70.1 1.3 collective-permute-start.38
  72.0 1.4 collective-permute-start.40
  78.6 1.6 %collective-permute-start.42 = (bf16[128,512]{1,0:T(8,128)(2,1)S(1)}, bf16[128,512]{1,0:T(8,128)(2,1)S(1)}, u32[]{:S(2)}, u32[]{:S(2)}) collective-permute-start(bf16[128,512]{1,0:T(8,128)(2,1)S(1)} %shard_map.111.refs_2_), channel_id=1, source_target_pairs={{0,4},{4,8},{8,12},{12,14},{14,10},{10,6},{6,2},{2,0},{1,5},{5,9},... | collective-permute-start | bytes 393224 | tf_op jit(solution)/shard_map/ppermute | solution.py:237
  81.1 1.5 collective-permute-start.43
  84.1 1.6 %collective-permute-start.46 = (bf16[128,512]{1,0:T(8,128)(2,1)S(1)}, bf16[128,512]{1,0:T(8,128)(2,1)S(1)}, u32[]{:S(2)}, u32[]{:S(2)}) collective-permute-start(bf16[128,512]{1,0:T(8,128)(2,1)S(1)} %collective-permute-done.42.refs_1_), channel_id=1, source_target_pairs={{0,4},{4,8},{8,12},{12,14},{14,10},{10,6},{6,2},{2,0},{1,5},{5,9},... | collective-permute-start | bytes 393224 | tf_op jit(solution)/shard_map/ppermute | solution.py:243
  86.4 2.1 %collective-permute-start.47 = (bf16[128,512]{1,0:T(8,128)(2,1)S(1)}, bf16[128,512]{1,0:T(8,128)(2,1)S(1)}, u32[]{:S(2)}, u32[]{:S(2)}) collective-permute-start(bf16[128,512]{1,0:T(8,128)(2,1)S(1)} %collective-permute-done.43.refs_2_), channel_id=1, source_target_pairs={{0,4},{4,8},{8,12},{12,14},{14,10},{10,6},{6,2},{2,0},{1,5},{5,9},... | collective-permute-start | bytes 393224 | tf_op jit(solution)/shard_map/ppermute | solution.py:243
  90.1 1.8 %collective-permute-start.50 = (bf16[128,512]{1,0:T(8,128)(2,1)S(1)}, bf16[128,512]{1,0:T(8,128)(2,1)S(1)}, u32[]{:S(2)}, u32[]{:S(2)}) collective-permute-start(bf16[128,512]{1,0:T(8,128)(2,1)S(1)} %collective-permute-done.46.refs_1_), channel_id=1, source_target_pairs={{0,4},{4,8},{8,12},{12,14},{14,10},{10,6},{6,2},{2,0},{1,5},{5,9},... | collective-permute-start | bytes 393224 | tf_op jit(solution)/shard_map/ppermute | solution.py:243
  92.4 2.5 %collective-permute-start.51 = (bf16[128,512]{1,0:T(8,128)(2,1)S(1)}, bf16[128,512]{1,0:T(8,128)(2,1)S(1)}, u32[]{:S(2)}, u32[]{:S(2)}) collective-permute-start(bf16[128,512]{1,0:T(8,128)(2,1)S(1)} %collective-permute-done.47.refs_2_), channel_id=1, source_target_pairs={{0,4},{4,8},{8,12},{12,14},{14,10},{10,6},{6,2},{2,0},{1,5},{5,9},... | collective-permute-start | bytes 393224 | tf_op jit(solution)/shard_map/ppermute | solution.py:243
  96.5 1.7 %collective-permute-start.54 = (bf16[128,512]{1,0:T(8,128)(2,1)S(1)}, bf16[128,512]{1,0:T(8,128)(2,1)S(1)}, u32[]{:S(2)}, u32[]{:S(2)}) collective-permute-start(bf16[128,512]{1,0:T(8,128)(2,1)S(1)} %collective-permute-done.50.refs_1_), channel_id=1, source_target_pairs={{0,4},{4,8},{8,12},{12,14},{14,10},{10,6},{6,2},{2,0},{1,5},{5,9},... | collective-permute-start | bytes 393224 | tf_op jit(solution)/shard_map/ppermute | solution.py:255
  99.3 1.9 %collective-permute-done.52.refs_3_ = bf16[128,512]{1,0:T(8,128)(2,1)S(1)} collective-permute-done((bf16[128,512]{1,0:T(8,128)(2,1)S(1)}, bf16[128,512]{1,0:T(8,128)(2,1)S(1)}, u32[]{:S(2)}, u32[]{:S(2)}) %collective-permute-start.52) | collective-permute-done | bytes 131104 | tf_op jit(solution)/shard_map/ppermute | solution.py:244
  103.6 1.8 %collective-permute-start.56 = (bf16[128,512]{1,0:T(8,128)(2,1)S(1)}, bf16[128,512]{1,0:T(8,128)(2,1)S(1)}, u32[]{:S(2)}, u32[]{:S(2)}) collective-permute-start(bf16[128,512]{1,0:T(8,128)(2,1)S(1)} %get-tuple-element.112.refs_0_), channel_id=1, source_target_pairs={{0,4},{4,8},{8,12},{12,14},{14,10},{10,6},{6,2},{2,0},{1,5},{5,9},... | collective-permute-start | bytes 393224 | tf_op jit(solution)/shard_map/ppermute | solution.py:237
  106.8 2.0 %collective-permute-start.57 = (bf16[128,512]{1,0:T(8,128)(2,1)S(1)}, bf16[128,512]{1,0:T(8,128)(2,1)S(1)}, u32[]{:S(2)}, u32[]{:S(2)}) collective-permute-start(bf16[128,512]{1,0:T(8,128)(2,1)S(1)} %get-tuple-element.115.refs_1_), channel_id=1, source_target_pairs={{0,4},{4,8},{8,12},{12,14},{14,10},{10,6},{6,2},{2,0},{1,5},{5,9},... | collective-permute-start | bytes 393224 | tf_op jit(solution)/shard_map/ppermute | solution.py:237
  109.2 2.1 %collective-permute-start.60 = (bf16[128,512]{1,0:T(8,128)(2,1)S(1)}, bf16[128,512]{1,0:T(8,128)(2,1)S(1)}, u32[]{:S(2)}, u32[]{:S(2)}) collective-permute-start(bf16[128,512]{1,0:T(8,128)(2,1)S(1)} %collective-permute-done.56.refs_1_), channel_id=1, source_target_pairs={{0,4},{4,8},{8,12},{12,14},{14,10},{10,6},{6,2},{2,0},{1,5},{5,9},... | collective-permute-start | bytes 393224 | tf_op jit(solution)/shard_map/ppermute | solution.py:243
  111.8 1.3 collective-permute-done.57.refs_2_
  113.1 2.1 %collective-permute-start.61 = (bf16[128,512]{1,0:T(8,128)(2,1)S(1)}, bf16[128,512]{1,0:T(8,128)(2,1)S(1)}, u32[]{:S(2)}, u32[]{:S(2)}) collective-permute-start(bf16[128,512]{1,0:T(8,128)(2,1)S(1)} %collective-permute-done.57.refs_2_), channel_id=1, source_target_pairs={{0,4},{4,8},{8,12},{12,14},{14,10},{10,6},{6,2},{2,0},{1,5},{5,9},... | collective-permute-start | bytes 393224 | tf_op jit(solution)/shard_map/ppermute | solution.py:243
  115.9 2.1 %collective-permute-start.64 = (bf16[128,512]{1,0:T(8,128)(2,1)S(1)}, bf16[128,512]{1,0:T(8,128)(2,1)S(1)}, u32[]{:S(2)}, u32[]{:S(2)}) collective-permute-start(bf16[128,512]{1,0:T(8,128)(2,1)S(1)} %collective-permute-done.60.refs_1_), channel_id=1, source_target_pairs={{0,4},{4,8},{8,12},{12,14},{14,10},{10,6},{6,2},{2,0},{1,5},{5,9},... | collective-permute-start | bytes 393224 | tf_op jit(solution)/shard_map/ppermute | solution.py:243
  118.8 2.4 %collective-permute-start.65 = (bf16[128,512]{1,0:T(8,128)(2,1)S(1)}, bf16[128,512]{1,0:T(8,128)(2,1)S(1)}, u32[]{:S(2)}, u32[]{:S(2)}) collective-permute-start(bf16[128,512]{1,0:T(8,128)(2,1)S(1)} %collective-permute-done.61.refs_2_), channel_id=1, source_target_pairs={{0,4},{4,8},{8,12},{12,14},{14,10},{10,6},{6,2},{2,0},{1,5},{5,9},... | collective-permute-start | bytes 393224 | tf_op jit(solution)/shard_map/ppermute | solution.py:243
  121.9 2.3 %collective-permute-start.68 = (bf16[128,512]{1,0:T(8,128)(2,1)S(1)}, bf16[128,512]{1,0:T(8,128)(2,1)S(1)}, u32[]{:S(2)}, u32[]{:S(2)}) collective-permute-start(bf16[128,512]{1,0:T(8,128)(2,1)S(1)} %collective-permute-done.64.refs_1_), channel_id=1, source_target_pairs={{0,4},{4,8},{8,12},{12,14},{14,10},{10,6},{6,2},{2,0},{1,5},{5,9},... | collective-permute-start | bytes 393224 | tf_op jit(solution)/shard_map/ppermute | solution.py:255
  125.3 2.2 %collective-permute-done.66.refs_3_ = bf16[128,512]{1,0:T(8,128)(2,1)S(1)} collective-permute-done((bf16[128,512]{1,0:T(8,128)(2,1)S(1)}, bf16[128,512]{1,0:T(8,128)(2,1)S(1)}, u32[]{:S(2)}, u32[]{:S(2)}) %collective-permute-start.66) | collective-permute-done | bytes 131104 | tf_op jit(solution)/shard_map/ppermute | solution.py:244
  128.5 2.5 %collective-permute-start.70 = (bf16[128,512]{1,0:T(8,128)(2,1)S(1)}, bf16[128,512]{1,0:T(8,128)(2,1)S(1)}, u32[]{:S(2)}, u32[]{:S(2)}) collective-permute-start(bf16[128,512]{1,0:T(8,128)(2,1)S(1)} %shard_map.123.refs_2_), channel_id=1, source_target_pairs={{0,4},{4,8},{8,12},{12,14},{14,10},{10,6},{6,2},{2,0},{1,5},{5,9},... | collective-permute-start | bytes 393224 | tf_op jit(solution)/shard_map/ppermute | solution.py:237
  131.3 2.1 %collective-permute-start.71 = (bf16[128,512]{1,0:T(8,128)(2,1)S(1)}, bf16[128,512]{1,0:T(8,128)(2,1)S(1)}, u32[]{:S(2)}, u32[]{:S(2)}) collective-permute-start(bf16[128,512]{1,0:T(8,128)(2,1)S(1)} %shard_map.124.refs_3_), channel_id=1, source_target_pairs={{0,4},{4,8},{8,12},{12,14},{14,10},{10,6},{6,2},{2,0},{1,5},{5,9},... | collective-permute-start | bytes 393224 | tf_op jit(solution)/shard_map/ppermute | solution.py:237
  134.4 2.1 %collective-permute-start.74 = (bf16[128,512]{1,0:T(8,128)(2,1)S(1)}, bf16[128,512]{1,0:T(8,128)(2,1)S(1)}, u32[]{:S(2)}, u32[]{:S(2)}) collective-permute-start(bf16[128,512]{1,0:T(8,128)(2,1)S(1)} %collective-permute-done.70.refs_1_), channel_id=1, source_target_pairs={{0,4},{4,8},{8,12},{12,14},{14,10},{10,6},{6,2},{2,0},{1,5},{5,9},... | collective-permute-start | bytes 393224 | tf_op jit(solution)/shard_map/ppermute | solution.py:243
  136.5 2.0 %collective-permute-start.75 = (bf16[128,512]{1,0:T(8,128)(2,1)S(1)}, bf16[128,512]{1,0:T(8,128)(2,1)S(1)}, u32[]{:S(2)}, u32[]{:S(2)}) collective-permute-start(bf16[128,512]{1,0:T(8,128)(2,1)S(1)} %collective-permute-done.71.refs_2_), channel_id=1, source_target_pairs={{0,4},{4,8},{8,12},{12,14},{14,10},{10,6},{6,2},{2,0},{1,5},{5,9},... | collective-permute-start | bytes 393224 | tf_op jit(solution)/shard_map/ppermute | solution.py:243
  139.9 2.0 %collective-permute-start.78 = (bf16[128,512]{1,0:T(8,128)(2,1)S(1)}, bf16[128,512]{1,0:T(8,128)(2,1)S(1)}, u32[]{:S(2)}, u32[]{:S(2)}) collective-permute-start(bf16[128,512]{1,0:T(8,128)(2,1)S(1)} %collective-permute-done.74.refs_1_), channel_id=1, source_target_pairs={{0,4},{4,8},{8,12},{12,14},{14,10},{10,6},{6,2},{2,0},{1,5},{5,9},... | collective-permute-start | bytes 393224 | tf_op jit(solution)/shard_map/ppermute | solution.py:243
  142.0 2.0 %collective-permute-start.79 = (bf16[128,512]{1,0:T(8,128)(2,1)S(1)}, bf16[128,512]{1,0:T(8,128)(2,1)S(1)}, u32[]{:S(2)}, u32[]{:S(2)}) collective-permute-start(bf16[128,512]{1,0:T(8,128)(2,1)S(1)} %collective-permute-done.75.refs_2_), channel_id=1, source_target_pairs={{0,4},{4,8},{8,12},{12,14},{14,10},{10,6},{6,2},{2,0},{1,5},{5,9},... | collective-permute-start | bytes 393224 | tf_op jit(solution)/shard_map/ppermute | solution.py:243
  145.3 2.0 %collective-permute-start.82 = (bf16[128,512]{1,0:T(8,128)(2,1)S(1)}, bf16[128,512]{1,0:T(8,128)(2,1)S(1)}, u32[]{:S(2)}, u32[]{:S(2)}) collective-permute-start(bf16[128,512]{1,0:T(8,128)(2,1)S(1)} %collective-permute-done.78.refs_1_), channel_id=1, source_target_pairs={{0,4},{4,8},{8,12},{12,14},{14,10},{10,6},{6,2},{2,0},{1,5},{5,9},... | collective-permute-start | bytes 393224 | tf_op jit(solution)/shard_map/ppermute | solution.py:255
  147.4 1.5 collective-permute-done.80.refs_3_
  150.3 2.0 %collective-permute-done.83.refs_1_ = bf16[128,512]{1,0:T(8,128)(2,1)S(1)} collective-permute-done((bf16[128,512]{1,0:T(8,128)(2,1)S(1)}, bf16[128,512]{1,0:T(8,128)(2,1)S(1)}, u32[]{:S(2)}, u32[]{:S(2)}) %collective-permute-start.83) | collective-permute-done | bytes 131104 | tf_op jit(solution)/shard_map/ppermute | solution.py:253
  152.2 2.8 %shard_map.129 = (bf16[256,512]{1,0:T(8,128)(2,1)}, f32[256,512]{1,0:T(8,128)}) custom-call(s32[1]{0:T(128)} %bitcast.me_ref, bf16[4096,2048]{1,0:T(8,128)(2,1)S(1)} %bitcast.3, f32[256,2048]{1,0:T(8,128)S(1)} %shard_map.128.total_ref, f32[1,2048]{1,0:T(1,128)S(1)} %bitcast.8, f32[256,512]{1,0:T(8,128)S(1)} %pad_maximum_fusion.cell_ref, ...), custom_call_target="tpu_custom_call" | custom-call | bytes 786432 | tf_op jit(solution)/shard_map/pallas_call | solution.py:144
  (183 shorter events, 63.3 us)
Async XLA Ops:
  1.6 7.7 %collective-permute-start = (bf16[128,512]{1,0:T(8,128)(2,1)S(1)}, bf16[128,512]{1,0:T(8,128)(2,1)S(1)}, u32[]{:S(2)}, u32[]{:S(2)}) collective-permute-start(bf16[128,512]{1,0:T(8,128)(2,1)S(1)} %get-tuple-element.139.refs_0_), channel_id=1, source_target_pairs={{0,4},{4,8},{8,12},{12,14},{14,10},{10,6},{6,2},{2,0},{1,5},{5,9},... | collective-permute-start | bytes 393224 | tf_op jit(solution)/shard_map/ppermute | solution.py:237
  4.7 6.7 %collective-permute-start.3 = (bf16[128,512]{1,0:T(8,128)(2,1)S(1)}, bf16[128,512]{1,0:T(8,128)(2,1)S(1)}, u32[]{:S(2)}, u32[]{:S(2)}) collective-permute-start(bf16[128,512]{1,0:T(8,128)(2,1)S(1)} %get-tuple-element.138.refs_1_), channel_id=1, source_target_pairs={{4,0},{8,4},{12,8},{14,12},{10,14},{6,10},{2,6},{0,2},{5,1},{9,5},... | collective-permute-start | bytes 393224 | tf_op jit(solution)/shard_map/ppermute | solution.py:238
  4.7 6.7 %collective-permute-start.1 = (bf16[128,512]{1,0:T(8,128)(2,1)S(1)}, bf16[128,512]{1,0:T(8,128)(2,1)S(1)}, u32[]{:S(2)}, u32[]{:S(2)}) collective-permute-start(bf16[128,512]{1,0:T(8,128)(2,1)S(1)} %get-tuple-element.138.refs_1_), channel_id=1, source_target_pairs={{0,4},{4,8},{8,12},{12,14},{14,10},{10,6},{6,2},{2,0},{1,5},{5,9},... | collective-permute-start | bytes 393224 | tf_op jit(solution)/shard_map/ppermute | solution.py:237
  6.7 6.7 %collective-permute-start.2 = (bf16[128,512]{1,0:T(8,128)(2,1)S(1)}, bf16[128,512]{1,0:T(8,128)(2,1)S(1)}, u32[]{:S(2)}, u32[]{:S(2)}) collective-permute-start(bf16[128,512]{1,0:T(8,128)(2,1)S(1)} %get-tuple-element.139.refs_0_), channel_id=1, source_target_pairs={{4,0},{8,4},{12,8},{14,12},{10,14},{6,10},{2,6},{0,2},{5,1},{9,5},... | collective-permute-start | bytes 393224 | tf_op jit(solution)/shard_map/ppermute | solution.py:238
  9.3 6.4 %collective-permute-start.4 = (bf16[128,512]{1,0:T(8,128)(2,1)S(1)}, bf16[128,512]{1,0:T(8,128)(2,1)S(1)}, u32[]{:S(2)}, u32[]{:S(2)}) collective-permute-start(bf16[128,512]{1,0:T(8,128)(2,1)S(1)} %collective-permute-done.refs_1_), channel_id=1, source_target_pairs={{0,4},{4,8},{8,12},{12,14},{14,10},{10,6},{6,2},{2,0},{1,5},{5,9},... | collective-permute-start | bytes 393224 | tf_op jit(solution)/shard_map/ppermute | solution.py:243
  11.4 6.0 %collective-permute-start.7 = (bf16[128,512]{1,0:T(8,128)(2,1)S(1)}, bf16[128,512]{1,0:T(8,128)(2,1)S(1)}, u32[]{:S(2)}, u32[]{:S(2)}) collective-permute-start(bf16[128,512]{1,0:T(8,128)(2,1)S(1)} %collective-permute-done.3.refs_4_), channel_id=1, source_target_pairs={{4,0},{8,4},{12,8},{14,12},{10,14},{6,10},{2,6},{0,2},{5,1},{9,5},... | collective-permute-start | bytes 393224 | tf_op jit(solution)/shard_map/ppermute | solution.py:244
  11.4 7.1 %collective-permute-start.5 = (bf16[128,512]{1,0:T(8,128)(2,1)S(1)}, bf16[128,512]{1,0:T(8,128)(2,1)S(1)}, u32[]{:S(2)}, u32[]{:S(2)}) collective-permute-start(bf16[128,512]{1,0:T(8,128)(2,1)S(1)} %collective-permute-done.1.refs_2_), channel_id=1, source_target_pairs={{0,4},{4,8},{8,12},{12,14},{14,10},{10,6},{6,2},{2,0},{1,5},{5,9},... | collective-permute-start | bytes 393224 | tf_op jit(solution)/shard_map/ppermute | solution.py:243
  13.4 6.8 %collective-permute-start.6 = (bf16[128,512]{1,0:T(8,128)(2,1)S(1)}, bf16[128,512]{1,0:T(8,128)(2,1)S(1)}, u32[]{:S(2)}, u32[]{:S(2)}) collective-permute-start(bf16[128,512]{1,0:T(8,128)(2,1)S(1)} %collective-permute-done.2.refs_3_), channel_id=1, source_target_pairs={{4,0},{8,4},{12,8},{14,12},{10,14},{6,10},{2,6},{0,2},{5,1},{9,5},... | collective-permute-start | bytes 393224 | tf_op jit(solution)/shard_map/ppermute | solution.py:244
  26.7 7.2 %collective-permute-start.14 = (bf16[128,512]{1,0:T(8,128)(2,1)S(1)}, bf16[128,512]{1,0:T(8,128)(2,1)S(1)}, u32[]{:S(2)}, u32[]{:S(2)}) collective-permute-start(bf16[128,512]{1,0:T(8,128)(2,1)S(1)} %shard_map.99.refs_2_), channel_id=1, source_target_pairs={{0,4},{4,8},{8,12},{12,14},{14,10},{10,6},{6,2},{2,0},{1,5},{5,9},... | collective-permute-start | bytes 393224 | tf_op jit(solution)/shard_map/ppermute | solution.py:237
  29.2 6.4 %collective-permute-start.17 = (bf16[128,512]{1,0:T(8,128)(2,1)S(1)}, bf16[128,512]{1,0:T(8,128)(2,1)S(1)}, u32[]{:S(2)}, u32[]{:S(2)}) collective-permute-start(bf16[128,512]{1,0:T(8,128)(2,1)S(1)} %shard_map.100.refs_3_), channel_id=1, source_target_pairs={{4,0},{8,4},{12,8},{14,12},{10,14},{6,10},{2,6},{0,2},{5,1},{9,5},... | collective-permute-start | bytes 393224 | tf_op jit(solution)/shard_map/ppermute | solution.py:238
  30.1 6.6 %collective-permute-start.15 = (bf16[128,512]{1,0:T(8,128)(2,1)S(1)}, bf16[128,512]{1,0:T(8,128)(2,1)S(1)}, u32[]{:S(2)}, u32[]{:S(2)}) collective-permute-start(bf16[128,512]{1,0:T(8,128)(2,1)S(1)} %shard_map.100.refs_3_), channel_id=1, source_target_pairs={{0,4},{4,8},{8,12},{12,14},{14,10},{10,6},{6,2},{2,0},{1,5},{5,9},... | collective-permute-start | bytes 393224 | tf_op jit(solution)/shard_map/ppermute | solution.py:237
  31.3 6.7 %collective-permute-start.16 = (bf16[128,512]{1,0:T(8,128)(2,1)S(1)}, bf16[128,512]{1,0:T(8,128)(2,1)S(1)}, u32[]{:S(2)}, u32[]{:S(2)}) collective-permute-start(bf16[128,512]{1,0:T(8,128)(2,1)S(1)} %shard_map.99.refs_2_), channel_id=1, source_target_pairs={{4,0},{8,4},{12,8},{14,12},{10,14},{6,10},{2,6},{0,2},{5,1},{9,5},... | collective-permute-start | bytes 393224 | tf_op jit(solution)/shard_map/ppermute | solution.py:238
  33.9 6.1 %collective-permute-start.18 = (bf16[128,512]{1,0:T(8,128)(2,1)S(1)}, bf16[128,512]{1,0:T(8,128)(2,1)S(1)}, u32[]{:S(2)}, u32[]{:S(2)}) collective-permute-start(bf16[128,512]{1,0:T(8,128)(2,1)S(1)} %collective-permute-done.14.refs_1_), channel_id=1, source_target_pairs={{0,4},{4,8},{8,12},{12,14},{14,10},{10,6},{6,2},{2,0},{1,5},{5,9},... | collective-permute-start | bytes 393224 | tf_op jit(solution)/shard_map/ppermute | solution.py:243
  38.0 6.1 %collective-permute-start.20 = (bf16[128,512]{1,0:T(8,128)(2,1)S(1)}, bf16[128,512]{1,0:T(8,128)(2,1)S(1)}, u32[]{:S(2)}, u32[]{:S(2)}) collective-permute-start(bf16[128,512]{1,0:T(8,128)(2,1)S(1)} %collective-permute-done.16.refs_3_), channel_id=1, source_target_pairs={{4,0},{8,4},{12,8},{14,12},{10,14},{6,10},{2,6},{0,2},{5,1},{9,5},... | collective-permute-start | bytes 393224 | tf_op jit(solution)/shard_map/ppermute | solution.py:244
  40.0 6.3 %collective-permute-start.22 = (bf16[128,512]{1,0:T(8,128)(2,1)S(1)}, bf16[128,512]{1,0:T(8,128)(2,1)S(1)}, u32[]{:S(2)}, u32[]{:S(2)}) collective-permute-start(bf16[128,512]{1,0:T(8,128)(2,1)S(1)} %collective-permute-done.18.refs_1_), channel_id=1, source_target_pairs={{0,4},{4,8},{8,12},{12,14},{14,10},{10,6},{6,2},{2,0},{1,5},{5,9},... | collective-permute-start | bytes 393224 | tf_op jit(solution)/shard_map/ppermute | solution.py:243
  41.4 6.1 %collective-permute-start.25 = (bf16[128,512]{1,0:T(8,128)(2,1)S(1)}, bf16[128,512]{1,0:T(8,128)(2,1)S(1)}, u32[]{:S(2)}, u32[]{:S(2)}) collective-permute-start(bf16[128,512]{1,0:T(8,128)(2,1)S(1)} %collective-permute-done.21.refs_4_), channel_id=1, source_target_pairs={{4,0},{8,4},{12,8},{14,12},{10,14},{6,10},{2,6},{0,2},{5,1},{9,5},... | collective-permute-start | bytes 393224 | tf_op jit(solution)/shard_map/ppermute | solution.py:244
  42.5 6.1 %collective-permute-start.23 = (bf16[128,512]{1,0:T(8,128)(2,1)S(1)}, bf16[128,512]{1,0:T(8,128)(2,1)S(1)}, u32[]{:S(2)}, u32[]{:S(2)}) collective-permute-start(bf16[128,512]{1,0:T(8,128)(2,1)S(1)} %collective-permute-done.19.refs_2_), channel_id=1, source_target_pairs={{0,4},{4,8},{8,12},{12,14},{14,10},{10,6},{6,2},{2,0},{1,5},{5,9},... | collective-permute-start | bytes 393224 | tf_op jit(solution)/shard_map/ppermute | solution.py:243
  46.3 6.2 %collective-permute-start.26 = (bf16[128,512]{1,0:T(8,128)(2,1)S(1)}, bf16[128,512]{1,0:T(8,128)(2,1)S(1)}, u32[]{:S(2)}, u32[]{:S(2)}) collective-permute-start(bf16[128,512]{1,0:T(8,128)(2,1)S(1)} %collective-permute-done.22.refs_1_), channel_id=1, source_target_pairs={{0,4},{4,8},{8,12},{12,14},{14,10},{10,6},{6,2},{2,0},{1,5},{5,9},... | collective-permute-start | bytes 393224 | tf_op jit(solution)/shard_map/ppermute | solution.py:255
  47.5 6.9 %collective-permute-start.27 = (bf16[128,512]{1,0:T(8,128)(2,1)S(1)}, bf16[128,512]{1,0:T(8,128)(2,1)S(1)}, u32[]{:S(2)}, u32[]{:S(2)}) collective-permute-start(bf16[128,512]{1,0:T(8,128)(2,1)S(1)} %collective-permute-done.25.refs_4_), channel_id=1, source_target_pairs={{4,0},{8,4},{12,8},{14,12},{10,14},{6,10},{2,6},{0,2},{5,1},{9,5},... | collective-permute-start | bytes 393224 | tf_op jit(solution)/shard_map/ppermute | solution.py:253
  53.7 6.2 %collective-permute-start.28 = (bf16[128,512]{1,0:T(8,128)(2,1)S(1)}, bf16[128,512]{1,0:T(8,128)(2,1)S(1)}, u32[]{:S(2)}, u32[]{:S(2)}) collective-permute-start(bf16[128,512]{1,0:T(8,128)(2,1)S(1)} %get-tuple-element.89.refs_0_), channel_id=1, source_target_pairs={{0,4},{4,8},{8,12},{12,14},{14,10},{10,6},{6,2},{2,0},{1,5},{5,9},... | collective-permute-start | bytes 393224 | tf_op jit(solution)/shard_map/ppermute | solution.py:237
  55.4 6.3 %collective-permute-start.31 = (bf16[128,512]{1,0:T(8,128)(2,1)S(1)}, bf16[128,512]{1,0:T(8,128)(2,1)S(1)}, u32[]{:S(2)}, u32[]{:S(2)}) collective-permute-start(bf16[128,512]{1,0:T(8,128)(2,1)S(1)} %get-tuple-element.91.refs_1_), channel_id=1, source_target_pairs={{4,0},{8,4},{12,8},{14,12},{10,14},{6,10},{2,6},{0,2},{5,1},{9,5},... | collective-permute-start | bytes 393224 | tf_op jit(solution)/shard_map/ppermute | solution.py:238
  57.0 6.2 %collective-permute-start.29 = (bf16[128,512]{1,0:T(8,128)(2,1)S(1)}, bf16[128,512]{1,0:T(8,128)(2,1)S(1)}, u32[]{:S(2)}, u32[]{:S(2)}) collective-permute-start(bf16[128,512]{1,0:T(8,128)(2,1)S(1)} %get-tuple-element.91.refs_1_), channel_id=1, source_target_pairs={{0,4},{4,8},{8,12},{12,14},{14,10},{10,6},{6,2},{2,0},{1,5},{5,9},... | collective-permute-start | bytes 393224 | tf_op jit(solution)/shard_map/ppermute | solution.py:237
  57.6 7.0 %collective-permute-start.30 = (bf16[128,512]{1,0:T(8,128)(2,1)S(1)}, bf16[128,512]{1,0:T(8,128)(2,1)S(1)}, u32[]{:S(2)}, u32[]{:S(2)}) collective-permute-start(bf16[128,512]{1,0:T(8,128)(2,1)S(1)} %get-tuple-element.89.refs_0_), channel_id=1, source_target_pairs={{4,0},{8,4},{12,8},{14,12},{10,14},{6,10},{2,6},{0,2},{5,1},{9,5},... | collective-permute-start | bytes 393224 | tf_op jit(solution)/shard_map/ppermute | solution.py:238
  65.8 6.3 %collective-permute-start.36 = (bf16[128,512]{1,0:T(8,128)(2,1)S(1)}, bf16[128,512]{1,0:T(8,128)(2,1)S(1)}, u32[]{:S(2)}, u32[]{:S(2)}) collective-permute-start(bf16[128,512]{1,0:T(8,128)(2,1)S(1)} %collective-permute-done.32.refs_1_), channel_id=1, source_target_pairs={{0,4},{4,8},{8,12},{12,14},{14,10},{10,6},{6,2},{2,0},{1,5},{5,9},... | collective-permute-start | bytes 393224 | tf_op jit(solution)/shard_map/ppermute | solution.py:243
  67.2 6.4 %collective-permute-start.39 = (bf16[128,512]{1,0:T(8,128)(2,1)S(1)}, bf16[128,512]{1,0:T(8,128)(2,1)S(1)}, u32[]{:S(2)}, u32[]{:S(2)}) collective-permute-start(bf16[128,512]{1,0:T(8,128)(2,1)S(1)} %collective-permute-done.35.refs_4_), channel_id=1, source_target_pairs={{4,0},{8,4},{12,8},{14,12},{10,14},{6,10},{2,6},{0,2},{5,1},{9,5},... | collective-permute-start | bytes 393224 | tf_op jit(solution)/shard_map/ppermute | solution.py:244
  68.2 7.5 %collective-permute-start.37 = (bf16[128,512]{1,0:T(8,128)(2,1)S(1)}, bf16[128,512]{1,0:T(8,128)(2,1)S(1)}, u32[]{:S(2)}, u32[]{:S(2)}) collective-permute-start(bf16[128,512]{1,0:T(8,128)(2,1)S(1)} %collective-permute-done.33.refs_2_), channel_id=1, source_target_pairs={{0,4},{4,8},{8,12},{12,14},{14,10},{10,6},{6,2},{2,0},{1,5},{5,9},... | collective-permute-start | bytes 393224 | tf_op jit(solution)/shard_map/ppermute | solution.py:243
  70.1 6.7 %collective-permute-start.38 = (bf16[128,512]{1,0:T(8,128)(2,1)S(1)}, bf16[128,512]{1,0:T(8,128)(2,1)S(1)}, u32[]{:S(2)}, u32[]{:S(2)}) collective-permute-start(bf16[128,512]{1,0:T(8,128)(2,1)S(1)} %collective-permute-done.34.refs_3_), channel_id=1, source_target_pairs={{4,0},{8,4},{12,8},{14,12},{10,14},{6,10},{2,6},{0,2},{5,1},{9,5},... | collective-permute-start | bytes 393224 | tf_op jit(solution)/shard_map/ppermute | solution.py:244
  72.0 6.2 %collective-permute-start.40 = (bf16[128,512]{1,0:T(8,128)(2,1)S(1)}, bf16[128,512]{1,0:T(8,128)(2,1)S(1)}, u32[]{:S(2)}, u32[]{:S(2)}) collective-permute-start(bf16[128,512]{1,0:T(8,128)(2,1)S(1)} %collective-permute-done.36.refs_1_), channel_id=1, source_target_pairs={{0,4},{4,8},{8,12},{12,14},{14,10},{10,6},{6,2},{2,0},{1,5},{5,9},... | collective-permute-start | bytes 393224 | tf_op jit(solution)/shard_map/ppermute | solution.py:255
  73.7 6.5 %collective-permute-start.41 = (bf16[128,512]{1,0:T(8,128)(2,1)S(1)}, bf16[128,512]{1,0:T(8,128)(2,1)S(1)}, u32[]{:S(2)}, u32[]{:S(2)}) collective-permute-start(bf16[128,512]{1,0:T(8,128)(2,1)S(1)} %collective-permute-done.39.refs_4_), channel_id=1, source_target_pairs={{4,0},{8,4},{12,8},{14,12},{10,14},{6,10},{2,6},{0,2},{5,1},{9,5},... | collective-permute-start | bytes 393224 | tf_op jit(solution)/shard_map/ppermute | solution.py:253
  84.1 6.0 %collective-permute-start.46 = (bf16[128,512]{1,0:T(8,128)(2,1)S(1)}, bf16[128,512]{1,0:T(8,128)(2,1)S(1)}, u32[]{:S(2)}, u32[]{:S(2)}) collective-permute-start(bf16[128,512]{1,0:T(8,128)(2,1)S(1)} %collective-permute-done.42.refs_1_), channel_id=1, source_target_pairs={{0,4},{4,8},{8,12},{12,14},{14,10},{10,6},{6,2},{2,0},{1,5},{5,9},... | collective-permute-start | bytes 393224 | tf_op jit(solution)/shard_map/ppermute | solution.py:243
  85.7 6.2 %collective-permute-start.49 = (bf16[128,512]{1,0:T(8,128)(2,1)S(1)}, bf16[128,512]{1,0:T(8,128)(2,1)S(1)}, u32[]{:S(2)}, u32[]{:S(2)}) collective-permute-start(bf16[128,512]{1,0:T(8,128)(2,1)S(1)} %collective-permute-done.45.refs_4_), channel_id=1, source_target_pairs={{4,0},{8,4},{12,8},{14,12},{10,14},{6,10},{2,6},{0,2},{5,1},{9,5},... | collective-permute-start | bytes 393224 | tf_op jit(solution)/shard_map/ppermute | solution.py:244
  86.4 6.0 %collective-permute-start.47 = (bf16[128,512]{1,0:T(8,128)(2,1)S(1)}, bf16[128,512]{1,0:T(8,128)(2,1)S(1)}, u32[]{:S(2)}, u32[]{:S(2)}) collective-permute-start(bf16[128,512]{1,0:T(8,128)(2,1)S(1)} %collective-permute-done.43.refs_2_), channel_id=1, source_target_pairs={{0,4},{4,8},{8,12},{12,14},{14,10},{10,6},{6,2},{2,0},{1,5},{5,9},... | collective-permute-start | bytes 393224 | tf_op jit(solution)/shard_map/ppermute | solution.py:243
  88.5 6.4 %collective-permute-start.48 = (bf16[128,512]{1,0:T(8,128)(2,1)S(1)}, bf16[128,512]{1,0:T(8,128)(2,1)S(1)}, u32[]{:S(2)}, u32[]{:S(2)}) collective-permute-start(bf16[128,512]{1,0:T(8,128)(2,1)S(1)} %collective-permute-done.44.refs_3_), channel_id=1, source_target_pairs={{4,0},{8,4},{12,8},{14,12},{10,14},{6,10},{2,6},{0,2},{5,1},{9,5},... | collective-permute-start | bytes 393224 | tf_op jit(solution)/shard_map/ppermute | solution.py:244
  90.1 6.4 %collective-permute-start.50 = (bf16[128,512]{1,0:T(8,128)(2,1)S(1)}, bf16[128,512]{1,0:T(8,128)(2,1)S(1)}, u32[]{:S(2)}, u32[]{:S(2)}) collective-permute-start(bf16[128,512]{1,0:T(8,128)(2,1)S(1)} %collective-permute-done.46.refs_1_), channel_id=1, source_target_pairs={{0,4},{4,8},{8,12},{12,14},{14,10},{10,6},{6,2},{2,0},{1,5},{5,9},... | collective-permute-start | bytes 393224 | tf_op jit(solution)/shard_map/ppermute | solution.py:243
  91.9 6.4 %collective-permute-start.53 = (bf16[128,512]{1,0:T(8,128)(2,1)S(1)}, bf16[128,512]{1,0:T(8,128)(2,1)S(1)}, u32[]{:S(2)}, u32[]{:S(2)}) collective-permute-start(bf16[128,512]{1,0:T(8,128)(2,1)S(1)} %collective-permute-done.49.refs_4_), channel_id=1, source_target_pairs={{4,0},{8,4},{12,8},{14,12},{10,14},{6,10},{2,6},{0,2},{5,1},{9,5},... | collective-permute-start | bytes 393224 | tf_op jit(solution)/shard_map/ppermute | solution.py:244
  92.4 6.9 %collective-permute-start.51 = (bf16[128,512]{1,0:T(8,128)(2,1)S(1)}, bf16[128,512]{1,0:T(8,128)(2,1)S(1)}, u32[]{:S(2)}, u32[]{:S(2)}) collective-permute-start(bf16[128,512]{1,0:T(8,128)(2,1)S(1)} %collective-permute-done.47.refs_2_), channel_id=1, source_target_pairs={{0,4},{4,8},{8,12},{12,14},{14,10},{10,6},{6,2},{2,0},{1,5},{5,9},... | collective-permute-start | bytes 393224 | tf_op jit(solution)/shard_map/ppermute | solution.py:243
  94.9 6.3 %collective-permute-start.52 = (bf16[128,512]{1,0:T(8,128)(2,1)S(1)}, bf16[128,512]{1,0:T(8,128)(2,1)S(1)}, u32[]{:S(2)}, u32[]{:S(2)}) collective-permute-start(bf16[128,512]{1,0:T(8,128)(2,1)S(1)} %collective-permute-done.48.refs_3_), channel_id=1, source_target_pairs={{4,0},{8,4},{12,8},{14,12},{10,14},{6,10},{2,6},{0,2},{5,1},{9,5},... | collective-permute-start | bytes 393224 | tf_op jit(solution)/shard_map/ppermute | solution.py:244
  98.2 7.2 %collective-permute-start.55 = (bf16[128,512]{1,0:T(8,128)(2,1)S(1)}, bf16[128,512]{1,0:T(8,128)(2,1)S(1)}, u32[]{:S(2)}, u32[]{:S(2)}) collective-permute-start(bf16[128,512]{1,0:T(8,128)(2,1)S(1)} %collective-permute-done.53.refs_4_), channel_id=1, source_target_pairs={{4,0},{8,4},{12,8},{14,12},{10,14},{6,10},{2,6},{0,2},{5,1},{9,5},... | collective-permute-start | bytes 393224 | tf_op jit(solution)/shard_map/ppermute | solution.py:253
  106.8 6.3 %collective-permute-start.57 = (bf16[128,512]{1,0:T(8,128)(2,1)S(1)}, bf16[128,512]{1,0:T(8,128)(2,1)S(1)}, u32[]{:S(2)}, u32[]{:S(2)}) collective-permute-start(bf16[128,512]{1,0:T(8,128)(2,1)S(1)} %get-tuple-element.115.refs_1_), channel_id=1, source_target_pairs={{0,4},{4,8},{8,12},{12,14},{14,10},{10,6},{6,2},{2,0},{1,5},{5,9},... | collective-permute-start | bytes 393224 | tf_op jit(solution)/shard_map/ppermute | solution.py:237
  108.9 6.3 %collective-permute-start.58 = (bf16[128,512]{1,0:T(8,128)(2,1)S(1)}, bf16[128,512]{1,0:T(8,128)(2,1)S(1)}, u32[]{:S(2)}, u32[]{:S(2)}) collective-permute-start(bf16[128,512]{1,0:T(8,128)(2,1)S(1)} %get-tuple-element.112.refs_0_), channel_id=1, source_target_pairs={{4,0},{8,4},{12,8},{14,12},{10,14},{6,10},{2,6},{0,2},{5,1},{9,5},... | collective-permute-start | bytes 393224 | tf_op jit(solution)/shard_map/ppermute | solution.py:238
  109.2 6.7 %collective-permute-start.60 = (bf16[128,512]{1,0:T(8,128)(2,1)S(1)}, bf16[128,512]{1,0:T(8,128)(2,1)S(1)}, u32[]{:S(2)}, u32[]{:S(2)}) collective-permute-start(bf16[128,512]{1,0:T(8,128)(2,1)S(1)} %collective-permute-done.56.refs_1_), channel_id=1, source_target_pairs={{0,4},{4,8},{8,12},{12,14},{14,10},{10,6},{6,2},{2,0},{1,5},{5,9},... | collective-permute-start | bytes 393224 | tf_op jit(solution)/shard_map/ppermute | solution.py:243
  111.7 6.3 %collective-permute-start.63 = (bf16[128,512]{1,0:T(8,128)(2,1)S(1)}, bf16[128,512]{1,0:T(8,128)(2,1)S(1)}, u32[]{:S(2)}, u32[]{:S(2)}) collective-permute-start(bf16[128,512]{1,0:T(8,128)(2,1)S(1)} %collective-permute-done.59.refs_4_), channel_id=1, source_target_pairs={{4,0},{8,4},{12,8},{14,12},{10,14},{6,10},{2,6},{0,2},{5,1},{9,5},... | collective-permute-start | bytes 393224 | tf_op jit(solution)/shard_map/ppermute | solution.py:244
  115.2 6.2 %collective-permute-start.62 = (bf16[128,512]{1,0:T(8,128)(2,1)S(1)}, bf16[128,512]{1,0:T(8,128)(2,1)S(1)}, u32[]{:S(2)}, u32[]{:S(2)}) collective-permute-start(bf16[128,512]{1,0:T(8,128)(2,1)S(1)} %collective-permute-done.58.refs_3_), channel_id=1, source_target_pairs={{4,0},{8,4},{12,8},{14,12},{10,14},{6,10},{2,6},{0,2},{5,1},{9,5},... | collective-permute-start | bytes 393224 | tf_op jit(solution)/shard_map/ppermute | solution.py:244
  118.0 6.6 %collective-permute-start.67 = (bf16[128,512]{1,0:T(8,128)(2,1)S(1)}, bf16[128,512]{1,0:T(8,128)(2,1)S(1)}, u32[]{:S(2)}, u32[]{:S(2)}) collective-permute-start(bf16[128,512]{1,0:T(8,128)(2,1)S(1)} %collective-permute-done.63.refs_4_), channel_id=1, source_target_pairs={{4,0},{8,4},{12,8},{14,12},{10,14},{6,10},{2,6},{0,2},{5,1},{9,5},... | collective-permute-start | bytes 393224 | tf_op jit(solution)/shard_map/ppermute | solution.py:244
  118.8 6.4 %collective-permute-start.65 = (bf16[128,512]{1,0:T(8,128)(2,1)S(1)}, bf16[128,512]{1,0:T(8,128)(2,1)S(1)}, u32[]{:S(2)}, u32[]{:S(2)}) collective-permute-start(bf16[128,512]{1,0:T(8,128)(2,1)S(1)} %collective-permute-done.61.refs_2_), channel_id=1, source_target_pairs={{0,4},{4,8},{8,12},{12,14},{14,10},{10,6},{6,2},{2,0},{1,5},{5,9},... | collective-permute-start | bytes 393224 | tf_op jit(solution)/shard_map/ppermute | solution.py:243
  121.5 6.0 %collective-permute-start.66 = (bf16[128,512]{1,0:T(8,128)(2,1)S(1)}, bf16[128,512]{1,0:T(8,128)(2,1)S(1)}, u32[]{:S(2)}, u32[]{:S(2)}) collective-permute-start(bf16[128,512]{1,0:T(8,128)(2,1)S(1)} %collective-permute-done.62.refs_3_), channel_id=1, source_target_pairs={{4,0},{8,4},{12,8},{14,12},{10,14},{6,10},{2,6},{0,2},{5,1},{9,5},... | collective-permute-start | bytes 393224 | tf_op jit(solution)/shard_map/ppermute | solution.py:244
  121.9 6.2 %collective-permute-start.68 = (bf16[128,512]{1,0:T(8,128)(2,1)S(1)}, bf16[128,512]{1,0:T(8,128)(2,1)S(1)}, u32[]{:S(2)}, u32[]{:S(2)}) collective-permute-start(bf16[128,512]{1,0:T(8,128)(2,1)S(1)} %collective-permute-done.64.refs_1_), channel_id=1, source_target_pairs={{0,4},{4,8},{8,12},{12,14},{14,10},{10,6},{6,2},{2,0},{1,5},{5,9},... | collective-permute-start | bytes 393224 | tf_op jit(solution)/shard_map/ppermute | solution.py:255
  124.6 6.3 %collective-permute-start.69 = (bf16[128,512]{1,0:T(8,128)(2,1)S(1)}, bf16[128,512]{1,0:T(8,128)(2,1)S(1)}, u32[]{:S(2)}, u32[]{:S(2)}) collective-permute-start(bf16[128,512]{1,0:T(8,128)(2,1)S(1)} %collective-permute-done.67.refs_4_), channel_id=1, source_target_pairs={{4,0},{8,4},{12,8},{14,12},{10,14},{6,10},{2,6},{0,2},{5,1},{9,5},... | collective-permute-start | bytes 393224 | tf_op jit(solution)/shard_map/ppermute | solution.py:253
  (47 other events, 289.1 us)

commit v4 on v3

--- a/solution.py
+++ b/solution.py
@@ -1,5 +1,3 @@
-import math
-
 import jax
 import jax.numpy as jnp
 from jax import lax
@@ -135,27 +133,25 @@
             kernel,
             [self.me, self.weight, *extra, *[block for group in groups for block in group]],
             [jax.ShapeDtypeStruct((rows, self.columns), jnp.float32)],
-            2 * rows * self.columns * self.part * len(away),
         )[0]
 
 
-def call(kernel, operands, outs, flops):
-    size = sum(math.prod(out.shape) * out.dtype.itemsize for out in outs)
+def call(kernel, operands, outs, space=pltpu.VMEM, scratch=()):
     return pl.pallas_call(
         kernel,
         in_specs=[pl.BlockSpec(memory_space=pltpu.SMEM)]
         + [pl.BlockSpec(memory_space=pltpu.VMEM)] * (len(operands) - 1),
-        out_specs=[pl.BlockSpec(memory_space=pltpu.VMEM)] * len(outs),
+        out_specs=[pl.BlockSpec(memory_space=space)] * len(outs),
         out_shape=outs,
+        scratch_shapes=list(scratch),
         compiler_params=pltpu.CompilerParams(vmem_limit_bytes=SCRATCH),
-        cost_estimate=pl.CostEstimate(flops=0, bytes_accessed=size, transcendentals=0),
     )(*operands)
 
 
 def inter_of(gather, total, last, row, onehot, step, inter_embed, away):
     rows = last.shape[0]
 
-    def kernel(me_ref, weight_ref, total_ref, last_ref, onehot_ref, embed_ref, out_ref):
+    def kernel(me_ref, weight_ref, total_ref, onehot_ref, embed_ref, last_ref, out_ref):
         product = total_ref[row : row + rows] + gather.terms(
             me_ref, weight_ref, [last_ref[...]], [away], slice(None)
         )
@@ -164,26 +160,38 @@
 
     return call(
         kernel,
-        [gather.me, gather.weight, total, last, onehot, inter_embed],
+        [gather.me, gather.weight, total, onehot, inter_embed, last],
         [jax.ShapeDtypeStruct((rows, gather.columns), jnp.bfloat16)],
-        2 * rows * gather.columns * gather.part,
     )[0]
 
 
-def state_of(gather, total, lasts, row, bias, cell, cell_row, mix, away):
-    rows = sum(last.shape[0] for last in lasts)
+def state_of(gather, total, last, row, bias, cell, cell_row, mix, away, done=None):
+    rows = last.shape[0]
     group = mix.shape[0]
     lanes = group // GATE_KINDS
     units = gather.columns // GATE_KINDS
-    chunks = len(lasts)
-
-    def kernel(me_ref, weight_ref, total_ref, bias_ref, cell_ref, mix_ref, *refs):
-        last_refs, hidden_ref, cell_out_ref = refs[:chunks], refs[chunks], refs[chunks + 1]
-        last = rows_of(last_refs)
+    ends = done is not None
+    before = [array for pair in done for array in pair] if ends else []
+
+    def kernel(me_ref, weight_ref, total_ref, bias_ref, cell_ref, mix_ref, last_ref, *refs):
+        before_refs, refs = refs[: len(before)], refs[len(before) :]
+        hidden_ref, cell_new_ref = refs[2:4] if ends else refs
+        copies = []
+
+        def send(sources, at):
+            for source, target in zip(sources, refs):
+                copy = pltpu.make_async_copy(
+                    source, target.at[pl.ds(at, rows)], refs[4].at[len(copies)]
+                )
+                copy.start()
+                copies.append(copy)
+
+        for c in range(len(before) // 2):
+            send(before_refs[2 * c : 2 * c + 2], c * rows)
         terms = []
         for columns in gather.tiles():
             full = total_ref[row : row + rows, columns] + gather.terms(
-                me_ref, weight_ref, [last], [away], columns
+                me_ref, weight_ref, [last_ref[...]], [away], columns
             )
             full = full + bias_ref[:, columns]
             high = full.astype(jnp.bfloat16)
@@ -193,19 +201,28 @@
             at = 2 * g * rows
             sums = mixed[at : at + rows] + mixed[at + rows : at + 2 * rows]
             here = slice(g * lanes, (g + 1) * lanes)
-            hidden_ref[:, here], cell_out_ref[:, here] = update_state(
+            hidden_ref[:, here], cell_new_ref[:, here] = update_state(
                 [sums[:, j * lanes : (j + 1) * lanes] for j in range(GATE_KINDS)],
                 cell_ref[cell_row : cell_row + rows, here],
             )
-
+        if ends:
+            send((hidden_ref, cell_new_ref), row)
+        for copy in copies:
+            copy.wait()
+
+    operands = [gather.me, gather.weight, total, bias, cell, mix, last, *before]
+    kinds = (jnp.bfloat16, jnp.float32)
+    high = total.shape[0] if ends else rows
+    shapes = [jax.ShapeDtypeStruct((high, units), kind) for kind in kinds]
+    if not ends:
+        return call(kernel, operands, shapes)
     return call(
         kernel,
-        [gather.me, gather.weight, total, bias, cell, mix, *lasts],
-        [
-            jax.ShapeDtypeStruct((rows, units), jnp.bfloat16),
-            jax.ShapeDtypeStruct((rows, units), jnp.float32),
-        ],
-        2 * rows * gather.columns * (gather.part + 2 * group),
+        operands,
+        shapes,
+        pl.ANY,
+        [pltpu.VMEM((rows, units), kind) for kind in kinds]
+        + [pltpu.SemaphoreType.DMA((len(before) + 2,))],
     )
 
 
@@ -213,7 +230,7 @@
     return lax.optimization_barrier((block, total))[0]
 
 
-def ringed(devices, chunks, first_chunks):
+def ringed(devices, chunks):
     ring = ring_of(devices)
     up = [(ring[i], ring[(i + 1) % devices]) for i in range(devices)]
     down = [(b, a) for a, b in up]
@@ -224,6 +241,17 @@
     ):
         steps, streams = byte_ids.shape
         part = h_start.shape[1]
+        if part % LANES or streams % (16 * chunks):
+            return plain(
+                byte_ids,
+                h_start,
+                c_start,
+                inter_weight,
+                inter_embed,
+                gate_weight,
+                gate_embed,
+                gate_bias,
+            )
         me = jnp.full((1,), lax.axis_index("mp"), jnp.int32)
         to_inter = Gather(me, inter_weight, devices, part, True)
         to_gate = Gather(me, gate_weight, devices, part, False)
@@ -231,35 +259,32 @@
         bias = gate_bias.reshape(1, -1)
         onehot = one_hot(byte_ids, inter_embed.shape[0])
 
+        def cut(array):
+            rows = streams // chunks
+            return [array[c * rows : (c + 1) * rows] for c in range(chunks)]
+
         def gathered(blocks, gather, first=None):
-            count = len(blocks)
             total = gather.add([blocks], away[:1], first=first)
             below = [lax.ppermute(block, "mp", up) for block in blocks]
             above = [lax.ppermute(block, "mp", down) for block in blocks]
+            if len(blocks) == 1:
+                below, above = cut(below[0]), cut(above[0])
             for k in range(1, devices - 1, 2):
                 ready = total
                 total = gather.add([below, above], away[k : k + 2], total)
                 if k + 2 < devices - 1:
                     below = [lax.ppermute(after(block, ready), "mp", up) for block in below]
                     above = [lax.ppermute(after(block, ready), "mp", down) for block in above]
-            if count == 1:
-                half = blocks[0].shape[0] // 2
-                lasts = [
-                    lax.ppermute(after(below[0][:half], ready), "mp", up),
-                    lax.ppermute(after(above[0][half:], ready), "mp", down),
-                ]
-            else:
-                lasts = [
-                    lax.ppermute(after(above[c], ready), "mp", down)
-                    if c % 2
-                    else lax.ppermute(after(below[c], ready), "mp", up)
-                    for c in range(count)
-                ]
+            lasts = [
+                lax.ppermute(above[c], "mp", down)
+                if c % 2
+                else lax.ppermute(below[c], "mp", up)
+                for c in range(chunks)
+            ]
             return total, lasts
 
-        rows = streams // first_chunks
-        hiddens = [h_start[c * rows : (c + 1) * rows] for c in range(first_chunks)]
         rows = streams // chunks
+        hiddens = [h_start]
         cells = [(c_start, c * rows) for c in range(chunks)]
         for step in range(steps):
             total, lasts = gathered(hiddens, to_inter)
@@ -268,19 +293,15 @@
                 for c, last in enumerate(lasts)
             ]
             total, lasts = gathered(inters, to_gate, (onehot, step, gate_embed))
-            if step + 1 < steps:
-                hiddens, updated = zip(
-                    *[
-                        state_of(to_gate, total, [last], c * rows, bias, *cells[c], mix, away[-1])
-                        for c, last in enumerate(lasts)
-                    ]
+            updates = []
+            for c, last in enumerate(lasts):
+                done = updates if step + 1 == steps and c + 1 == chunks else None
+                updates.append(
+                    state_of(to_gate, total, last, c * rows, bias, *cells[c], mix, away[-1], done)
                 )
-                cells = [(cell, 0) for cell in updated]
-            else:
-                cell = cells[0][0]
-                if cell.shape[0] < streams:
-                    cell = jnp.concatenate([cell for cell, _ in cells], 0)
-                return state_of(to_gate, total, lasts, 0, bias, cell, 0, mix, away[-1])
+            hiddens = [hidden for hidden, _ in updates]
+            cells = [(cell, 0) for _, cell in updates]
+        return tuple(updates[-1])
 
     return local
 
@@ -298,5 +319,5 @@
     )
     out_specs = (P(("groups", "batch"), "mp"), P(("groups", "batch"), "mp"))
     devices = mesh.shape["mp"]
-    local = ringed(devices, 2, 2) if 2 < devices <= MAX_RING else plain
+    local = ringed(devices, 2) if 2 < devices <= MAX_RING else plain
     return jax.shard_map(local, mesh=mesh, in_specs=in_specs, out_specs=out_specs, check_vma=False)

time: 155 us -> 153 us (0.987)
  starting transfers between devices: 91.6 us -> 88.1 us
    ppermute x24, starting transfers between devices: 10.2 us -> 5.7 us  [gathered(): above = [lax.ppermute(after(block, ready), 'mp', down) for block in above]]
    ppermute x12, waiting for transfers between devices: 6 us -> 2 us  [the longest x6 1.56 us: gathered(): lax.ppermute(below[c], 'mp', up)]
    ppermute x24, starting transfers between devices: 41.3 us -> 44.7 us  [gathered(): below = [lax.ppermute(after(block, ready), 'mp', up) for block in below]]
    ppermute x12 -> x11, starting transfers between devices: 6.12 us -> 2.97 us  [gathered(): above = [lax.ppermute(block, 'mp', down) for block in blocks]]
    ppermute x12 -> x11, waiting for transfers between devices: 2.9 us -> 4.95 us  [gathered(): below = [lax.ppermute(block, 'mp', up) for block in blocks]]
    ppermute x24, waiting for transfers between devices: 7.7 us -> 9.74 us  [gathered(): below = [lax.ppermute(after(block, ready), 'mp', up) for block in below]]
    unnamed x22 -> x24, local copies, waits for them, and re-layouts: 2.25 us -> 3.19 us
    ppermute x12 -> x11, waiting for transfers between devices: 2.94 us -> 3.41 us  [gathered(): above = [lax.ppermute(block, 'mp', down) for block in blocks]]
  transfers between devices with their start and end apart: 84 -> 82, of which waited for: 38 -> 40; matrix products, arithmetic and copies ran while one was open for 0% -> 0% of each run, Pallas kernels for 17% -> 18%
where the time goes in v4:
time: 153 us
  starting transfers between devices  88.1 us (58%)
  waiting for transfers between devices  30.9 us (20%)
  Pallas kernels  29 us (19%)
  local copies, waits for them, and re-layouts  3.23 us (2%)
    ppermute x24, starting transfers between devices, gathered(): below = [lax.ppermute(after(block, ready), 'mp', up) for block in below]  44.7 us
    pallas_call x36, Pallas kernels, call(): pl.pallas_call(kernel, in_specs=[pl.BlockSpec(memory_space=pltpu.SMEM)] +...  29 us
    ppermute x11, starting transfers between devices, gathered(): below = [lax.ppermute(block, 'mp', up) for block in blocks]  21.4 us
    ppermute x6, starting transfers between devices, gathered(): lax.ppermute(below[c], 'mp', up)  11.7 us
    ppermute x24, waiting for transfers between devices, gathered(): above = [lax.ppermute(after(block, ready), 'mp', down) for block in above]  10.8 us
    ppermute x24, waiting for transfers between devices, gathered(): below = [lax.ppermute(after(block, ready), 'mp', up) for block in below]  9.74 us
    ppermute x24, starting transfers between devices, gathered(): above = [lax.ppermute(after(block, ready), 'mp', down) for block in above]  5.7 us
    ppermute x11, waiting for transfers between devices, gathered(): below = [lax.ppermute(block, 'mp', up) for block in blocks]  4.95 us
  transfers between devices with their start and end apart: 82, of which 40 were waited for; matrix products, arithmetic and copies ran while one was open for 0% of the time, Pallas kernels for 18%

profile of v4, /device:TPU:0, one launch (start us, length us, event | category | flops | bytes accessed | tf_op | source)
XLA Modules:
  0.0 153.0 jit_solution(16095422737295725985)
XLA Ops:
  0.6 3.1 %collective-permute-start = (bf16[256,512]{1,0:T(8,128)(2,1)}, bf16[256,512]{1,0:T(8,128)(2,1)S(1)}, u32[]{:S(2)}, u32[]{:S(2)}) collective-permute-start(bf16[256,512]{1,0:T(8,128)(2,1)} %refs_0_.1), channel_id=1, source_target_pairs={{0,4},{4,8},{8,12},{12,14},{14,10},{10,6},{6,2},{2,0},{1,5},{5,9},... | collective-permute-start | bytes 786440 | tf_op jit(solution)/shard_map/ppermute | solution.py:268
  3.7 2.2 %copy-done = bf16[512,4096]{1,0:T(8,128)(2,1)S(1)} copy-done((bf16[512,4096]{1,0:T(8,128)(2,1)S(1)}, bf16[512,4096]{1,0:T(8,128)(2,1)}, u32[]{:S(2)}) %copy-start) | copy-done | bytes 4194328
  7.2 2.9 %collective-permute-done = bf16[256,512]{1,0:T(8,128)(2,1)S(1)} collective-permute-done((bf16[256,512]{1,0:T(8,128)(2,1)}, bf16[256,512]{1,0:T(8,128)(2,1)S(1)}, u32[]{:S(2)}, u32[]{:S(2)}) %collective-permute-start) | collective-permute-done | bytes 262176 | tf_op jit(solution)/shard_map/ppermute | solution.py:268
  10.2 1.9 %collective-permute-start.2 = (bf16[128,512]{1,0:T(8,128)(2,1)S(1)}, bf16[128,512]{1,0:T(8,128)(2,1)S(1)}, u32[]{:S(2)}, u32[]{:S(2)}) collective-permute-start(bf16[128,512]{1,0:T(8,128)(2,1)S(1)} %get-tuple-element.60.refs_1_), channel_id=1, source_target_pairs={{0,4},{4,8},{8,12},{12,14},{14,10},{10,6},{6,2},{2,0},{1,5},{5,9},... | collective-permute-start | bytes 393224 | tf_op jit(solution)/shard_map/ppermute | solution.py:276
  12.8 1.9 %collective-permute-start.3 = (bf16[128,512]{1,0:T(8,128)(2,1)S(1)}, bf16[128,512]{1,0:T(8,128)(2,1)S(1)}, u32[]{:S(2)}, u32[]{:S(2)}) collective-permute-start(bf16[128,512]{1,0:T(8,128)(2,1)S(1)} %get-tuple-element.61.refs_2_), channel_id=1, source_target_pairs={{0,4},{4,8},{8,12},{12,14},{14,10},{10,6},{6,2},{2,0},{1,5},{5,9},... | collective-permute-start | bytes 393224 | tf_op jit(solution)/shard_map/ppermute | solution.py:276
  16.3 2.1 %collective-permute-start.6 = (bf16[128,512]{1,0:T(8,128)(2,1)S(1)}, bf16[128,512]{1,0:T(8,128)(2,1)S(1)}, u32[]{:S(2)}, u32[]{:S(2)}) collective-permute-start(bf16[128,512]{1,0:T(8,128)(2,1)S(1)} %collective-permute-done.2.refs_1_), channel_id=1, source_target_pairs={{0,4},{4,8},{8,12},{12,14},{14,10},{10,6},{6,2},{2,0},{1,5},{5,9},... | collective-permute-start | bytes 393224 | tf_op jit(solution)/shard_map/ppermute | solution.py:276
  19.3 1.9 %collective-permute-start.7 = (bf16[128,512]{1,0:T(8,128)(2,1)S(1)}, bf16[128,512]{1,0:T(8,128)(2,1)S(1)}, u32[]{:S(2)}, u32[]{:S(2)}) collective-permute-start(bf16[128,512]{1,0:T(8,128)(2,1)S(1)} %collective-permute-done.3.refs_2_), channel_id=1, source_target_pairs={{0,4},{4,8},{8,12},{12,14},{14,10},{10,6},{6,2},{2,0},{1,5},{5,9},... | collective-permute-start | bytes 393224 | tf_op jit(solution)/shard_map/ppermute | solution.py:276
  22.2 1.8 %collective-permute-start.10 = (bf16[128,512]{1,0:T(8,128)(2,1)S(1)}, bf16[128,512]{1,0:T(8,128)(2,1)S(1)}, u32[]{:S(2)}, u32[]{:S(2)}) collective-permute-start(bf16[128,512]{1,0:T(8,128)(2,1)S(1)} %collective-permute-done.6.refs_1_), channel_id=1, source_target_pairs={{0,4},{4,8},{8,12},{12,14},{14,10},{10,6},{6,2},{2,0},{1,5},{5,9},... | collective-permute-start | bytes 393224 | tf_op jit(solution)/shard_map/ppermute | solution.py:281
  25.1 1.5 %collective-permute-done.8.refs_3_ = bf16[128,512]{1,0:T(8,128)(2,1)S(1)} collective-permute-done((bf16[128,512]{1,0:T(8,128)(2,1)S(1)}, bf16[128,512]{1,0:T(8,128)(2,1)S(1)}, u32[]{:S(2)}, u32[]{:S(2)}) %collective-permute-start.8) | collective-permute-done | bytes 131104 | tf_op jit(solution)/shard_map/ppermute | solution.py:277
  27.6 1.9 %collective-permute-start.12 = (bf16[128,512]{1,0:T(8,128)(2,1)S(1)}, bf16[128,512]{1,0:T(8,128)(2,1)S(1)}, u32[]{:S(2)}, u32[]{:S(2)}) collective-permute-start(bf16[128,512]{1,0:T(8,128)(2,1)S(1)} %shard_map.99.refs_2_), channel_id=1, source_target_pairs={{0,4},{4,8},{8,12},{12,14},{14,10},{10,6},{6,2},{2,0},{1,5},{5,9},... | collective-permute-start | bytes 393224 | tf_op jit(solution)/shard_map/ppermute | solution.py:268
  30.1 1.8 %collective-permute-start.13 = (bf16[128,512]{1,0:T(8,128)(2,1)S(1)}, bf16[128,512]{1,0:T(8,128)(2,1)S(1)}, u32[]{:S(2)}, u32[]{:S(2)}) collective-permute-start(bf16[128,512]{1,0:T(8,128)(2,1)S(1)} %shard_map.100.refs_3_), channel_id=1, source_target_pairs={{0,4},{4,8},{8,12},{12,14},{14,10},{10,6},{6,2},{2,0},{1,5},{5,9},... | collective-permute-start | bytes 393224 | tf_op jit(solution)/shard_map/ppermute | solution.py:268
  33.2 2.0 %collective-permute-start.16 = (bf16[128,512]{1,0:T(8,128)(2,1)S(1)}, bf16[128,512]{1,0:T(8,128)(2,1)S(1)}, u32[]{:S(2)}, u32[]{:S(2)}) collective-permute-start(bf16[128,512]{1,0:T(8,128)(2,1)S(1)} %collective-permute-done.12.refs_1_), channel_id=1, source_target_pairs={{0,4},{4,8},{8,12},{12,14},{14,10},{10,6},{6,2},{2,0},{1,5},{5,9},... | collective-permute-start | bytes 393224 | tf_op jit(solution)/shard_map/ppermute | solution.py:276
  36.5 1.8 %collective-permute-start.17 = (bf16[128,512]{1,0:T(8,128)(2,1)S(1)}, bf16[128,512]{1,0:T(8,128)(2,1)S(1)}, u32[]{:S(2)}, u32[]{:S(2)}) collective-permute-start(bf16[128,512]{1,0:T(8,128)(2,1)S(1)} %collective-permute-done.13.refs_2_), channel_id=1, source_target_pairs={{0,4},{4,8},{8,12},{12,14},{14,10},{10,6},{6,2},{2,0},{1,5},{5,9},... | collective-permute-start | bytes 393224 | tf_op jit(solution)/shard_map/ppermute | solution.py:276
  40.3 2.0 %collective-permute-start.20 = (bf16[128,512]{1,0:T(8,128)(2,1)S(1)}, bf16[128,512]{1,0:T(8,128)(2,1)S(1)}, u32[]{:S(2)}, u32[]{:S(2)}) collective-permute-start(bf16[128,512]{1,0:T(8,128)(2,1)S(1)} %collective-permute-done.16.refs_1_), channel_id=1, source_target_pairs={{0,4},{4,8},{8,12},{12,14},{14,10},{10,6},{6,2},{2,0},{1,5},{5,9},... | collective-permute-start | bytes 393224 | tf_op jit(solution)/shard_map/ppermute | solution.py:276
  42.4 1.9 %collective-permute-start.21 = (bf16[128,512]{1,0:T(8,128)(2,1)S(1)}, bf16[128,512]{1,0:T(8,128)(2,1)S(1)}, u32[]{:S(2)}, u32[]{:S(2)}) collective-permute-start(bf16[128,512]{1,0:T(8,128)(2,1)S(1)} %collective-permute-done.17.refs_2_), channel_id=1, source_target_pairs={{0,4},{4,8},{8,12},{12,14},{14,10},{10,6},{6,2},{2,0},{1,5},{5,9},... | collective-permute-start | bytes 393224 | tf_op jit(solution)/shard_map/ppermute | solution.py:276
  45.4 2.0 %collective-permute-start.24 = (bf16[128,512]{1,0:T(8,128)(2,1)S(1)}, bf16[128,512]{1,0:T(8,128)(2,1)S(1)}, u32[]{:S(2)}, u32[]{:S(2)}) collective-permute-start(bf16[128,512]{1,0:T(8,128)(2,1)S(1)} %collective-permute-done.20.refs_1_), channel_id=1, source_target_pairs={{0,4},{4,8},{8,12},{12,14},{14,10},{10,6},{6,2},{2,0},{1,5},{5,9},... | collective-permute-start | bytes 393224 | tf_op jit(solution)/shard_map/ppermute | solution.py:281
  52.7 2.2 %collective-permute-start.26 = (bf16[128,512]{1,0:T(8,128)(2,1)S(1)}, bf16[128,512]{1,0:T(8,128)(2,1)S(1)}, u32[]{:S(2)}, u32[]{:S(2)}) collective-permute-start(bf16[128,512]{1,0:T(8,128)(2,1)S(1)} %get-tuple-element.76.refs_0_), channel_id=1, source_target_pairs={{0,4},{4,8},{8,12},{12,14},{14,10},{10,6},{6,2},{2,0},{1,5},{5,9},... | collective-permute-start | bytes 393224 | tf_op jit(solution)/shard_map/ppermute | solution.py:268
  56.1 2.0 %collective-permute-start.27 = (bf16[128,512]{1,0:T(8,128)(2,1)S(1)}, bf16[128,512]{1,0:T(8,128)(2,1)S(1)}, u32[]{:S(2)}, u32[]{:S(2)}) collective-permute-start(bf16[128,512]{1,0:T(8,128)(2,1)S(1)} %get-tuple-element.77.refs_1_), channel_id=1, source_target_pairs={{0,4},{4,8},{8,12},{12,14},{14,10},{10,6},{6,2},{2,0},{1,5},{5,9},... | collective-permute-start | bytes 393224 | tf_op jit(solution)/shard_map/ppermute | solution.py:268
  59.1 2.1 %collective-permute-start.30 = (bf16[128,512]{1,0:T(8,128)(2,1)S(1)}, bf16[128,512]{1,0:T(8,128)(2,1)S(1)}, u32[]{:S(2)}, u32[]{:S(2)}) collective-permute-start(bf16[128,512]{1,0:T(8,128)(2,1)S(1)} %collective-permute-done.26.refs_1_), channel_id=1, source_target_pairs={{0,4},{4,8},{8,12},{12,14},{14,10},{10,6},{6,2},{2,0},{1,5},{5,9},... | collective-permute-start | bytes 393224 | tf_op jit(solution)/shard_map/ppermute | solution.py:276
  62.0 2.1 %collective-permute-start.31 = (bf16[128,512]{1,0:T(8,128)(2,1)S(1)}, bf16[128,512]{1,0:T(8,128)(2,1)S(1)}, u32[]{:S(2)}, u32[]{:S(2)}) collective-permute-start(bf16[128,512]{1,0:T(8,128)(2,1)S(1)} %collective-permute-done.27.refs_2_), channel_id=1, source_target_pairs={{0,4},{4,8},{8,12},{12,14},{14,10},{10,6},{6,2},{2,0},{1,5},{5,9},... | collective-permute-start | bytes 393224 | tf_op jit(solution)/shard_map/ppermute | solution.py:276
  65.4 2.0 %collective-permute-start.34 = (bf16[128,512]{1,0:T(8,128)(2,1)S(1)}, bf16[128,512]{1,0:T(8,128)(2,1)S(1)}, u32[]{:S(2)}, u32[]{:S(2)}) collective-permute-start(bf16[128,512]{1,0:T(8,128)(2,1)S(1)} %collective-permute-done.30.refs_1_), channel_id=1, source_target_pairs={{0,4},{4,8},{8,12},{12,14},{14,10},{10,6},{6,2},{2,0},{1,5},{5,9},... | collective-permute-start | bytes 393224 | tf_op jit(solution)/shard_map/ppermute | solution.py:276
  67.6 2.0 %collective-permute-start.35 = (bf16[128,512]{1,0:T(8,128)(2,1)S(1)}, bf16[128,512]{1,0:T(8,128)(2,1)S(1)}, u32[]{:S(2)}, u32[]{:S(2)}) collective-permute-start(bf16[128,512]{1,0:T(8,128)(2,1)S(1)} %collective-permute-done.31.refs_2_), channel_id=1, source_target_pairs={{0,4},{4,8},{8,12},{12,14},{14,10},{10,6},{6,2},{2,0},{1,5},{5,9},... | collective-permute-start | bytes 393224 | tf_op jit(solution)/shard_map/ppermute | solution.py:276
  69.6 1.6 %collective-permute-done.34.refs_1_ = bf16[128,512]{1,0:T(8,128)(2,1)S(1)} collective-permute-done((bf16[128,512]{1,0:T(8,128)(2,1)S(1)}, bf16[128,512]{1,0:T(8,128)(2,1)S(1)}, u32[]{:S(2)}, u32[]{:S(2)}) %collective-permute-start.34) | collective-permute-done | bytes 131104 | tf_op jit(solution)/shard_map/ppermute | solution.py:276
  71.3 2.5 %collective-permute-start.38 = (bf16[128,512]{1,0:T(8,128)(2,1)S(1)}, bf16[128,512]{1,0:T(8,128)(2,1)S(1)}, u32[]{:S(2)}, u32[]{:S(2)}) collective-permute-start(bf16[128,512]{1,0:T(8,128)(2,1)S(1)} %collective-permute-done.34.refs_1_), channel_id=1, source_target_pairs={{0,4},{4,8},{8,12},{12,14},{14,10},{10,6},{6,2},{2,0},{1,5},{5,9},... | collective-permute-start | bytes 393224 | tf_op jit(solution)/shard_map/ppermute | solution.py:281
  74.3 2.3 %collective-permute-done.36.refs_3_ = bf16[128,512]{1,0:T(8,128)(2,1)S(1)} collective-permute-done((bf16[128,512]{1,0:T(8,128)(2,1)S(1)}, bf16[128,512]{1,0:T(8,128)(2,1)S(1)}, u32[]{:S(2)}, u32[]{:S(2)}) %collective-permute-start.36) | collective-permute-done | bytes 131104 | tf_op jit(solution)/shard_map/ppermute | solution.py:277
  77.7 2.3 %collective-permute-start.40 = (bf16[128,512]{1,0:T(8,128)(2,1)S(1)}, bf16[128,512]{1,0:T(8,128)(2,1)S(1)}, u32[]{:S(2)}, u32[]{:S(2)}) collective-permute-start(bf16[128,512]{1,0:T(8,128)(2,1)S(1)} %shard_map.111.refs_2_), channel_id=1, source_target_pairs={{0,4},{4,8},{8,12},{12,14},{14,10},{10,6},{6,2},{2,0},{1,5},{5,9},... | collective-permute-start | bytes 393224 | tf_op jit(solution)/shard_map/ppermute | solution.py:268
  80.5 1.9 %collective-permute-start.41 = (bf16[128,512]{1,0:T(8,128)(2,1)S(1)}, bf16[128,512]{1,0:T(8,128)(2,1)S(1)}, u32[]{:S(2)}, u32[]{:S(2)}) collective-permute-start(bf16[128,512]{1,0:T(8,128)(2,1)S(1)} %shard_map.112.refs_3_), channel_id=1, source_target_pairs={{0,4},{4,8},{8,12},{12,14},{14,10},{10,6},{6,2},{2,0},{1,5},{5,9},... | collective-permute-start | bytes 393224 | tf_op jit(solution)/shard_map/ppermute | solution.py:268
  84.0 2.3 %collective-permute-start.44 = (bf16[128,512]{1,0:T(8,128)(2,1)S(1)}, bf16[128,512]{1,0:T(8,128)(2,1)S(1)}, u32[]{:S(2)}, u32[]{:S(2)}) collective-permute-start(bf16[128,512]{1,0:T(8,128)(2,1)S(1)} %collective-permute-done.40.refs_1_), channel_id=1, source_target_pairs={{0,4},{4,8},{8,12},{12,14},{14,10},{10,6},{6,2},{2,0},{1,5},{5,9},... | collective-permute-start | bytes 393224 | tf_op jit(solution)/shard_map/ppermute | solution.py:276
  86.9 2.2 %collective-permute-start.45 = (bf16[128,512]{1,0:T(8,128)(2,1)S(1)}, bf16[128,512]{1,0:T(8,128)(2,1)S(1)}, u32[]{:S(2)}, u32[]{:S(2)}) collective-permute-start(bf16[128,512]{1,0:T(8,128)(2,1)S(1)} %collective-permute-done.41.refs_2_), channel_id=1, source_target_pairs={{0,4},{4,8},{8,12},{12,14},{14,10},{10,6},{6,2},{2,0},{1,5},{5,9},... | collective-permute-start | bytes 393224 | tf_op jit(solution)/shard_map/ppermute | solution.py:276
  90.4 2.0 %collective-permute-start.48 = (bf16[128,512]{1,0:T(8,128)(2,1)S(1)}, bf16[128,512]{1,0:T(8,128)(2,1)S(1)}, u32[]{:S(2)}, u32[]{:S(2)}) collective-permute-start(bf16[128,512]{1,0:T(8,128)(2,1)S(1)} %collective-permute-done.44.refs_1_), channel_id=1, source_target_pairs={{0,4},{4,8},{8,12},{12,14},{14,10},{10,6},{6,2},{2,0},{1,5},{5,9},... | collective-permute-start | bytes 393224 | tf_op jit(solution)/shard_map/ppermute | solution.py:276
  92.5 2.3 %collective-permute-start.49 = (bf16[128,512]{1,0:T(8,128)(2,1)S(1)}, bf16[128,512]{1,0:T(8,128)(2,1)S(1)}, u32[]{:S(2)}, u32[]{:S(2)}) collective-permute-start(bf16[128,512]{1,0:T(8,128)(2,1)S(1)} %collective-permute-done.45.refs_2_), channel_id=1, source_target_pairs={{0,4},{4,8},{8,12},{12,14},{14,10},{10,6},{6,2},{2,0},{1,5},{5,9},... | collective-permute-start | bytes 393224 | tf_op jit(solution)/shard_map/ppermute | solution.py:276
  94.8 1.8 %collective-permute-done.48.refs_1_ = bf16[128,512]{1,0:T(8,128)(2,1)S(1)} collective-permute-done((bf16[128,512]{1,0:T(8,128)(2,1)S(1)}, bf16[128,512]{1,0:T(8,128)(2,1)S(1)}, u32[]{:S(2)}, u32[]{:S(2)}) %collective-permute-start.48) | collective-permute-done | bytes 131104 | tf_op jit(solution)/shard_map/ppermute | solution.py:276
  96.5 2.3 %collective-permute-start.52 = (bf16[128,512]{1,0:T(8,128)(2,1)S(1)}, bf16[128,512]{1,0:T(8,128)(2,1)S(1)}, u32[]{:S(2)}, u32[]{:S(2)}) collective-permute-start(bf16[128,512]{1,0:T(8,128)(2,1)S(1)} %collective-permute-done.48.refs_1_), channel_id=1, source_target_pairs={{0,4},{4,8},{8,12},{12,14},{14,10},{10,6},{6,2},{2,0},{1,5},{5,9},... | collective-permute-start | bytes 393224 | tf_op jit(solution)/shard_map/ppermute | solution.py:281
  104.0 1.6 %collective-permute-start.54 = (bf16[128,512]{1,0:T(8,128)(2,1)S(1)}, bf16[128,512]{1,0:T(8,128)(2,1)S(1)}, u32[]{:S(2)}, u32[]{:S(2)}) collective-permute-start(bf16[128,512]{1,0:T(8,128)(2,1)S(1)} %get-tuple-element.95.refs_0_), channel_id=1, source_target_pairs={{0,4},{4,8},{8,12},{12,14},{14,10},{10,6},{6,2},{2,0},{1,5},{5,9},... | collective-permute-start | bytes 393224 | tf_op jit(solution)/shard_map/ppermute | solution.py:268
  107.3 1.6 %collective-permute-start.55 = (bf16[128,512]{1,0:T(8,128)(2,1)S(1)}, bf16[128,512]{1,0:T(8,128)(2,1)S(1)}, u32[]{:S(2)}, u32[]{:S(2)}) collective-permute-start(bf16[128,512]{1,0:T(8,128)(2,1)S(1)} %get-tuple-element.97.refs_1_), channel_id=1, source_target_pairs={{0,4},{4,8},{8,12},{12,14},{14,10},{10,6},{6,2},{2,0},{1,5},{5,9},... | collective-permute-start | bytes 393224 | tf_op jit(solution)/shard_map/ppermute | solution.py:268
  109.6 1.7 %collective-permute-start.58 = (bf16[128,512]{1,0:T(8,128)(2,1)S(1)}, bf16[128,512]{1,0:T(8,128)(2,1)S(1)}, u32[]{:S(2)}, u32[]{:S(2)}) collective-permute-start(bf16[128,512]{1,0:T(8,128)(2,1)S(1)} %collective-permute-done.54.refs_1_), channel_id=1, source_target_pairs={{0,4},{4,8},{8,12},{12,14},{14,10},{10,6},{6,2},{2,0},{1,5},{5,9},... | collective-permute-start | bytes 393224 | tf_op jit(solution)/shard_map/ppermute | solution.py:276
  116.1 1.5 %collective-permute-start.62 = (bf16[128,512]{1,0:T(8,128)(2,1)S(1)}, bf16[128,512]{1,0:T(8,128)(2,1)S(1)}, u32[]{:S(2)}, u32[]{:S(2)}) collective-permute-start(bf16[128,512]{1,0:T(8,128)(2,1)S(1)} %collective-permute-done.58.refs_1_), channel_id=1, source_target_pairs={{0,4},{4,8},{8,12},{12,14},{14,10},{10,6},{6,2},{2,0},{1,5},{5,9},... | collective-permute-start | bytes 393224 | tf_op jit(solution)/shard_map/ppermute | solution.py:276
  118.7 1.7 %collective-permute-start.63 = (bf16[128,512]{1,0:T(8,128)(2,1)S(1)}, bf16[128,512]{1,0:T(8,128)(2,1)S(1)}, u32[]{:S(2)}, u32[]{:S(2)}) collective-permute-start(bf16[128,512]{1,0:T(8,128)(2,1)S(1)} %collective-permute-done.59.refs_2_), channel_id=1, source_target_pairs={{0,4},{4,8},{8,12},{12,14},{14,10},{10,6},{6,2},{2,0},{1,5},{5,9},... | collective-permute-start | bytes 393224 | tf_op jit(solution)/shard_map/ppermute | solution.py:276
  122.3 1.7 %collective-permute-start.66 = (bf16[128,512]{1,0:T(8,128)(2,1)S(1)}, bf16[128,512]{1,0:T(8,128)(2,1)S(1)}, u32[]{:S(2)}, u32[]{:S(2)}) collective-permute-start(bf16[128,512]{1,0:T(8,128)(2,1)S(1)} %collective-permute-done.62.refs_1_), channel_id=1, source_target_pairs={{0,4},{4,8},{8,12},{12,14},{14,10},{10,6},{6,2},{2,0},{1,5},{5,9},... | collective-permute-start | bytes 393224 | tf_op jit(solution)/shard_map/ppermute | solution.py:281
  124.9 1.9 %collective-permute-done.64.refs_3_ = bf16[128,512]{1,0:T(8,128)(2,1)S(1)} collective-permute-done((bf16[128,512]{1,0:T(8,128)(2,1)S(1)}, bf16[128,512]{1,0:T(8,128)(2,1)S(1)}, u32[]{:S(2)}, u32[]{:S(2)}) %collective-permute-start.64) | collective-permute-done | bytes 131104 | tf_op jit(solution)/shard_map/ppermute | solution.py:277
  128.5 1.6 %collective-permute-start.68 = (bf16[128,512]{1,0:T(8,128)(2,1)S(1)}, bf16[128,512]{1,0:T(8,128)(2,1)S(1)}, u32[]{:S(2)}, u32[]{:S(2)}) collective-permute-start(bf16[128,512]{1,0:T(8,128)(2,1)S(1)} %shard_map.123.refs_2_), channel_id=1, source_target_pairs={{0,4},{4,8},{8,12},{12,14},{14,10},{10,6},{6,2},{2,0},{1,5},{5,9},... | collective-permute-start | bytes 393224 | tf_op jit(solution)/shard_map/ppermute | solution.py:268
  131.0 1.5 %collective-permute-start.69 = (bf16[128,512]{1,0:T(8,128)(2,1)S(1)}, bf16[128,512]{1,0:T(8,128)(2,1)S(1)}, u32[]{:S(2)}, u32[]{:S(2)}) collective-permute-start(bf16[128,512]{1,0:T(8,128)(2,1)S(1)} %shard_map.124.refs_3_), channel_id=1, source_target_pairs={{0,4},{4,8},{8,12},{12,14},{14,10},{10,6},{6,2},{2,0},{1,5},{5,9},... | collective-permute-start | bytes 393224 | tf_op jit(solution)/shard_map/ppermute | solution.py:268
  134.0 1.6 %collective-permute-start.72 = (bf16[128,512]{1,0:T(8,128)(2,1)S(1)}, bf16[128,512]{1,0:T(8,128)(2,1)S(1)}, u32[]{:S(2)}, u32[]{:S(2)}) collective-permute-start(bf16[128,512]{1,0:T(8,128)(2,1)S(1)} %collective-permute-done.68.refs_1_), channel_id=1, source_target_pairs={{0,4},{4,8},{8,12},{12,14},{14,10},{10,6},{6,2},{2,0},{1,5},{5,9},... | collective-permute-start | bytes 393224 | tf_op jit(solution)/shard_map/ppermute | solution.py:276
  136.1 1.5 %collective-permute-start.73 = (bf16[128,512]{1,0:T(8,128)(2,1)S(1)}, bf16[128,512]{1,0:T(8,128)(2,1)S(1)}, u32[]{:S(2)}, u32[]{:S(2)}) collective-permute-start(bf16[128,512]{1,0:T(8,128)(2,1)S(1)} %collective-permute-done.69.refs_2_), channel_id=1, source_target_pairs={{0,4},{4,8},{8,12},{12,14},{14,10},{10,6},{6,2},{2,0},{1,5},{5,9},... | collective-permute-start | bytes 393224 | tf_op jit(solution)/shard_map/ppermute | solution.py:276
  139.4 1.6 %collective-permute-start.76 = (bf16[128,512]{1,0:T(8,128)(2,1)S(1)}, bf16[128,512]{1,0:T(8,128)(2,1)S(1)}, u32[]{:S(2)}, u32[]{:S(2)}) collective-permute-start(bf16[128,512]{1,0:T(8,128)(2,1)S(1)} %collective-permute-done.72.refs_1_), channel_id=1, source_target_pairs={{0,4},{4,8},{8,12},{12,14},{14,10},{10,6},{6,2},{2,0},{1,5},{5,9},... | collective-permute-start | bytes 393224 | tf_op jit(solution)/shard_map/ppermute | solution.py:276
  141.4 1.5 %collective-permute-start.77 = (bf16[128,512]{1,0:T(8,128)(2,1)S(1)}, bf16[128,512]{1,0:T(8,128)(2,1)S(1)}, u32[]{:S(2)}, u32[]{:S(2)}) collective-permute-start(bf16[128,512]{1,0:T(8,128)(2,1)S(1)} %collective-permute-done.73.refs_2_), channel_id=1, source_target_pairs={{0,4},{4,8},{8,12},{12,14},{14,10},{10,6},{6,2},{2,0},{1,5},{5,9},... | collective-permute-start | bytes 393224 | tf_op jit(solution)/shard_map/ppermute | solution.py:276
  144.4 1.5 %collective-permute-start.81 = (bf16[128,512]{1,0:T(8,128)(2,1)S(1)}, bf16[128,512]{1,0:T(8,128)(2,1)S(1)}, u32[]{:S(2)}, u32[]{:S(2)}) collective-permute-start(bf16[128,512]{1,0:T(8,128)(2,1)S(1)} %collective-permute-done.76.refs_1_), channel_id=1, source_target_pairs={{0,4},{4,8},{8,12},{12,14},{14,10},{10,6},{6,2},{2,0},{1,5},{5,9},... | collective-permute-start | bytes 393224 | tf_op jit(solution)/shard_map/ppermute | solution.py:281
  150.9 1.9 %shard_map.130 = (bf16[256,512]{1,0:T(8,128)(2,1)}, f32[256,512]{1,0:T(8,128)}) custom-call(s32[1]{0:T(128)} %bitcast.me_ref, bf16[4096,2048]{1,0:T(8,128)(2,1)S(1)} %bitcast.3, f32[256,2048]{1,0:T(8,128)S(1)} %shard_map.128.total_ref, f32[1,2048]{1,0:T(1,128)S(1)} %bitcast.9, f32[128,512]{1,0:T(8,128)S(1)} %get-tuple-element.114.cell_ref, ...), custom_call_target="tpu_custom_call" | custom-call | tf_op jit(solution)/shard_map/pallas_call | solution.py:140
  (182 shorter events, 58.8 us)
Async XLA Ops:
  0.6 9.5 %collective-permute-start = (bf16[256,512]{1,0:T(8,128)(2,1)}, bf16[256,512]{1,0:T(8,128)(2,1)S(1)}, u32[]{:S(2)}, u32[]{:S(2)}) collective-permute-start(bf16[256,512]{1,0:T(8,128)(2,1)} %refs_0_.1), channel_id=1, source_target_pairs={{0,4},{4,8},{8,12},{12,14},{14,10},{10,6},{6,2},{2,0},{1,5},{5,9},... | collective-permute-start | bytes 786440 | tf_op jit(solution)/shard_map/ppermute | solution.py:268
  3.7 8.3 %collective-permute-start.1 = (bf16[256,512]{1,0:T(8,128)(2,1)}, bf16[256,512]{1,0:T(8,128)(2,1)S(1)}, u32[]{:S(2)}, u32[]{:S(2)}) collective-permute-start(bf16[256,512]{1,0:T(8,128)(2,1)} %refs_0_.1), channel_id=1, source_target_pairs={{4,0},{8,4},{12,8},{14,12},{10,14},{6,10},{2,6},{0,2},{5,1},{9,5},... | collective-permute-start | bytes 786440 | tf_op jit(solution)/shard_map/ppermute | solution.py:269
  10.2 6.1 %collective-permute-start.2 = (bf16[128,512]{1,0:T(8,128)(2,1)S(1)}, bf16[128,512]{1,0:T(8,128)(2,1)S(1)}, u32[]{:S(2)}, u32[]{:S(2)}) collective-permute-start(bf16[128,512]{1,0:T(8,128)(2,1)S(1)} %get-tuple-element.60.refs_1_), channel_id=1, source_target_pairs={{0,4},{4,8},{8,12},{12,14},{14,10},{10,6},{6,2},{2,0},{1,5},{5,9},... | collective-permute-start | bytes 393224 | tf_op jit(solution)/shard_map/ppermute | solution.py:276
  12.1 6.4 %collective-permute-start.5 = (bf16[128,512]{1,0:T(8,128)(2,1)S(1)}, bf16[128,512]{1,0:T(8,128)(2,1)S(1)}, u32[]{:S(2)}, u32[]{:S(2)}) collective-permute-start(bf16[128,512]{1,0:T(8,128)(2,1)S(1)} %get-tuple-element.63.refs_4_), channel_id=1, source_target_pairs={{4,0},{8,4},{12,8},{14,12},{10,14},{6,10},{2,6},{0,2},{5,1},{9,5},... | collective-permute-start | bytes 393224 | tf_op jit(solution)/shard_map/ppermute | solution.py:277
  12.8 6.5 %collective-permute-start.3 = (bf16[128,512]{1,0:T(8,128)(2,1)S(1)}, bf16[128,512]{1,0:T(8,128)(2,1)S(1)}, u32[]{:S(2)}, u32[]{:S(2)}) collective-permute-start(bf16[128,512]{1,0:T(8,128)(2,1)S(1)} %get-tuple-element.61.refs_2_), channel_id=1, source_target_pairs={{0,4},{4,8},{8,12},{12,14},{14,10},{10,6},{6,2},{2,0},{1,5},{5,9},... | collective-permute-start | bytes 393224 | tf_op jit(solution)/shard_map/ppermute | solution.py:276
  14.7 6.5 %collective-permute-start.4 = (bf16[128,512]{1,0:T(8,128)(2,1)S(1)}, bf16[128,512]{1,0:T(8,128)(2,1)S(1)}, u32[]{:S(2)}, u32[]{:S(2)}) collective-permute-start(bf16[128,512]{1,0:T(8,128)(2,1)S(1)} %get-tuple-element.62.refs_3_), channel_id=1, source_target_pairs={{4,0},{8,4},{12,8},{14,12},{10,14},{6,10},{2,6},{0,2},{5,1},{9,5},... | collective-permute-start | bytes 393224 | tf_op jit(solution)/shard_map/ppermute | solution.py:277
  16.3 6.0 %collective-permute-start.6 = (bf16[128,512]{1,0:T(8,128)(2,1)S(1)}, bf16[128,512]{1,0:T(8,128)(2,1)S(1)}, u32[]{:S(2)}, u32[]{:S(2)}) collective-permute-start(bf16[128,512]{1,0:T(8,128)(2,1)S(1)} %collective-permute-done.2.refs_1_), channel_id=1, source_target_pairs={{0,4},{4,8},{8,12},{12,14},{14,10},{10,6},{6,2},{2,0},{1,5},{5,9},... | collective-permute-start | bytes 393224 | tf_op jit(solution)/shard_map/ppermute | solution.py:276
  29.8 6.4 %collective-permute-start.15 = (bf16[128,512]{1,0:T(8,128)(2,1)S(1)}, bf16[128,512]{1,0:T(8,128)(2,1)S(1)}, u32[]{:S(2)}, u32[]{:S(2)}) collective-permute-start(bf16[128,512]{1,0:T(8,128)(2,1)S(1)} %shard_map.100.refs_3_), channel_id=1, source_target_pairs={{4,0},{8,4},{12,8},{14,12},{10,14},{6,10},{2,6},{0,2},{5,1},{9,5},... | collective-permute-start | bytes 393224 | tf_op jit(solution)/shard_map/ppermute | solution.py:269
  30.1 6.4 %collective-permute-start.13 = (bf16[128,512]{1,0:T(8,128)(2,1)S(1)}, bf16[128,512]{1,0:T(8,128)(2,1)S(1)}, u32[]{:S(2)}, u32[]{:S(2)}) collective-permute-start(bf16[128,512]{1,0:T(8,128)(2,1)S(1)} %shard_map.100.refs_3_), channel_id=1, source_target_pairs={{0,4},{4,8},{8,12},{12,14},{14,10},{10,6},{6,2},{2,0},{1,5},{5,9},... | collective-permute-start | bytes 393224 | tf_op jit(solution)/shard_map/ppermute | solution.py:268
  31.9 7.1 %collective-permute-start.14 = (bf16[128,512]{1,0:T(8,128)(2,1)S(1)}, bf16[128,512]{1,0:T(8,128)(2,1)S(1)}, u32[]{:S(2)}, u32[]{:S(2)}) collective-permute-start(bf16[128,512]{1,0:T(8,128)(2,1)S(1)} %shard_map.99.refs_2_), channel_id=1, source_target_pairs={{4,0},{8,4},{12,8},{14,12},{10,14},{6,10},{2,6},{0,2},{5,1},{9,5},... | collective-permute-start | bytes 393224 | tf_op jit(solution)/shard_map/ppermute | solution.py:269
  33.2 7.2 %collective-permute-start.16 = (bf16[128,512]{1,0:T(8,128)(2,1)S(1)}, bf16[128,512]{1,0:T(8,128)(2,1)S(1)}, u32[]{:S(2)}, u32[]{:S(2)}) collective-permute-start(bf16[128,512]{1,0:T(8,128)(2,1)S(1)} %collective-permute-done.12.refs_1_), channel_id=1, source_target_pairs={{0,4},{4,8},{8,12},{12,14},{14,10},{10,6},{6,2},{2,0},{1,5},{5,9},... | collective-permute-start | bytes 393224 | tf_op jit(solution)/shard_map/ppermute | solution.py:276
  36.2 6.2 %collective-permute-start.19 = (bf16[128,512]{1,0:T(8,128)(2,1)S(1)}, bf16[128,512]{1,0:T(8,128)(2,1)S(1)}, u32[]{:S(2)}, u32[]{:S(2)}) collective-permute-start(bf16[128,512]{1,0:T(8,128)(2,1)S(1)} %collective-permute-done.15.refs_4_), channel_id=1, source_target_pairs={{4,0},{8,4},{12,8},{14,12},{10,14},{6,10},{2,6},{0,2},{5,1},{9,5},... | collective-permute-start | bytes 393224 | tf_op jit(solution)/shard_map/ppermute | solution.py:277
  36.5 5.9 %collective-permute-start.17 = (bf16[128,512]{1,0:T(8,128)(2,1)S(1)}, bf16[128,512]{1,0:T(8,128)(2,1)S(1)}, u32[]{:S(2)}, u32[]{:S(2)}) collective-permute-start(bf16[128,512]{1,0:T(8,128)(2,1)S(1)} %collective-permute-done.13.refs_2_), channel_id=1, source_target_pairs={{0,4},{4,8},{8,12},{12,14},{14,10},{10,6},{6,2},{2,0},{1,5},{5,9},... | collective-permute-start | bytes 393224 | tf_op jit(solution)/shard_map/ppermute | solution.py:276
  39.0 6.3 %collective-permute-start.18 = (bf16[128,512]{1,0:T(8,128)(2,1)S(1)}, bf16[128,512]{1,0:T(8,128)(2,1)S(1)}, u32[]{:S(2)}, u32[]{:S(2)}) collective-permute-start(bf16[128,512]{1,0:T(8,128)(2,1)S(1)} %collective-permute-done.14.refs_3_), channel_id=1, source_target_pairs={{4,0},{8,4},{12,8},{14,12},{10,14},{6,10},{2,6},{0,2},{5,1},{9,5},... | collective-permute-start | bytes 393224 | tf_op jit(solution)/shard_map/ppermute | solution.py:277
  42.4 6.8 %collective-permute-start.21 = (bf16[128,512]{1,0:T(8,128)(2,1)S(1)}, bf16[128,512]{1,0:T(8,128)(2,1)S(1)}, u32[]{:S(2)}, u32[]{:S(2)}) collective-permute-start(bf16[128,512]{1,0:T(8,128)(2,1)S(1)} %collective-permute-done.17.refs_2_), channel_id=1, source_target_pairs={{0,4},{4,8},{8,12},{12,14},{14,10},{10,6},{6,2},{2,0},{1,5},{5,9},... | collective-permute-start | bytes 393224 | tf_op jit(solution)/shard_map/ppermute | solution.py:276
  45.4 6.2 %collective-permute-start.24 = (bf16[128,512]{1,0:T(8,128)(2,1)S(1)}, bf16[128,512]{1,0:T(8,128)(2,1)S(1)}, u32[]{:S(2)}, u32[]{:S(2)}) collective-permute-start(bf16[128,512]{1,0:T(8,128)(2,1)S(1)} %collective-permute-done.20.refs_1_), channel_id=1, source_target_pairs={{0,4},{4,8},{8,12},{12,14},{14,10},{10,6},{6,2},{2,0},{1,5},{5,9},... | collective-permute-start | bytes 393224 | tf_op jit(solution)/shard_map/ppermute | solution.py:281
  47.5 7.4 %collective-permute-start.25 = (bf16[128,512]{1,0:T(8,128)(2,1)S(1)}, bf16[128,512]{1,0:T(8,128)(2,1)S(1)}, u32[]{:S(2)}, u32[]{:S(2)}) collective-permute-start(bf16[128,512]{1,0:T(8,128)(2,1)S(1)} %collective-permute-done.23.refs_4_), channel_id=1, source_target_pairs={{4,0},{8,4},{12,8},{14,12},{10,14},{6,10},{2,6},{0,2},{5,1},{9,5},... | collective-permute-start | bytes 393224 | tf_op jit(solution)/shard_map/ppermute | solution.py:279
  52.7 6.4 %collective-permute-start.26 = (bf16[128,512]{1,0:T(8,128)(2,1)S(1)}, bf16[128,512]{1,0:T(8,128)(2,1)S(1)}, u32[]{:S(2)}, u32[]{:S(2)}) collective-permute-start(bf16[128,512]{1,0:T(8,128)(2,1)S(1)} %get-tuple-element.76.refs_0_), channel_id=1, source_target_pairs={{0,4},{4,8},{8,12},{12,14},{14,10},{10,6},{6,2},{2,0},{1,5},{5,9},... | collective-permute-start | bytes 393224 | tf_op jit(solution)/shard_map/ppermute | solution.py:268
  56.1 5.9 %collective-permute-start.27 = (bf16[128,512]{1,0:T(8,128)(2,1)S(1)}, bf16[128,512]{1,0:T(8,128)(2,1)S(1)}, u32[]{:S(2)}, u32[]{:S(2)}) collective-permute-start(bf16[128,512]{1,0:T(8,128)(2,1)S(1)} %get-tuple-element.77.refs_1_), channel_id=1, source_target_pairs={{0,4},{4,8},{8,12},{12,14},{14,10},{10,6},{6,2},{2,0},{1,5},{5,9},... | collective-permute-start | bytes 393224 | tf_op jit(solution)/shard_map/ppermute | solution.py:268
  58.1 6.4 %collective-permute-start.28 = (bf16[128,512]{1,0:T(8,128)(2,1)S(1)}, bf16[128,512]{1,0:T(8,128)(2,1)S(1)}, u32[]{:S(2)}, u32[]{:S(2)}) collective-permute-start(bf16[128,512]{1,0:T(8,128)(2,1)S(1)} %get-tuple-element.76.refs_0_), channel_id=1, source_target_pairs={{4,0},{8,4},{12,8},{14,12},{10,14},{6,10},{2,6},{0,2},{5,1},{9,5},... | collective-permute-start | bytes 393224 | tf_op jit(solution)/shard_map/ppermute | solution.py:269
  59.1 6.3 %collective-permute-start.30 = (bf16[128,512]{1,0:T(8,128)(2,1)S(1)}, bf16[128,512]{1,0:T(8,128)(2,1)S(1)}, u32[]{:S(2)}, u32[]{:S(2)}) collective-permute-start(bf16[128,512]{1,0:T(8,128)(2,1)S(1)} %collective-permute-done.26.refs_1_), channel_id=1, source_target_pairs={{0,4},{4,8},{8,12},{12,14},{14,10},{10,6},{6,2},{2,0},{1,5},{5,9},... | collective-permute-start | bytes 393224 | tf_op jit(solution)/shard_map/ppermute | solution.py:276
  61.7 5.9 %collective-permute-start.33 = (bf16[128,512]{1,0:T(8,128)(2,1)S(1)}, bf16[128,512]{1,0:T(8,128)(2,1)S(1)}, u32[]{:S(2)}, u32[]{:S(2)}) collective-permute-start(bf16[128,512]{1,0:T(8,128)(2,1)S(1)} %collective-permute-done.29.refs_4_), channel_id=1, source_target_pairs={{4,0},{8,4},{12,8},{14,12},{10,14},{6,10},{2,6},{0,2},{5,1},{9,5},... | collective-permute-start | bytes 393224 | tf_op jit(solution)/shard_map/ppermute | solution.py:277
  67.6 6.2 %collective-permute-start.37 = (bf16[128,512]{1,0:T(8,128)(2,1)S(1)}, bf16[128,512]{1,0:T(8,128)(2,1)S(1)}, u32[]{:S(2)}, u32[]{:S(2)}) collective-permute-start(bf16[128,512]{1,0:T(8,128)(2,1)S(1)} %collective-permute-done.33.refs_4_), channel_id=1, source_target_pairs={{4,0},{8,4},{12,8},{14,12},{10,14},{6,10},{2,6},{0,2},{5,1},{9,5},... | collective-permute-start | bytes 393224 | tf_op jit(solution)/shard_map/ppermute | solution.py:277
  67.6 6.7 %collective-permute-start.35 = (bf16[128,512]{1,0:T(8,128)(2,1)S(1)}, bf16[128,512]{1,0:T(8,128)(2,1)S(1)}, u32[]{:S(2)}, u32[]{:S(2)}) collective-permute-start(bf16[128,512]{1,0:T(8,128)(2,1)S(1)} %collective-permute-done.31.refs_2_), channel_id=1, source_target_pairs={{0,4},{4,8},{8,12},{12,14},{14,10},{10,6},{6,2},{2,0},{1,5},{5,9},... | collective-permute-start | bytes 393224 | tf_op jit(solution)/shard_map/ppermute | solution.py:276
  69.6 7.0 %collective-permute-start.36 = (bf16[128,512]{1,0:T(8,128)(2,1)S(1)}, bf16[128,512]{1,0:T(8,128)(2,1)S(1)}, u32[]{:S(2)}, u32[]{:S(2)}) collective-permute-start(bf16[128,512]{1,0:T(8,128)(2,1)S(1)} %collective-permute-done.32.refs_3_), channel_id=1, source_target_pairs={{4,0},{8,4},{12,8},{14,12},{10,14},{6,10},{2,6},{0,2},{5,1},{9,5},... | collective-permute-start | bytes 393224 | tf_op jit(solution)/shard_map/ppermute | solution.py:277
  71.3 6.1 %collective-permute-start.38 = (bf16[128,512]{1,0:T(8,128)(2,1)S(1)}, bf16[128,512]{1,0:T(8,128)(2,1)S(1)}, u32[]{:S(2)}, u32[]{:S(2)}) collective-permute-start(bf16[128,512]{1,0:T(8,128)(2,1)S(1)} %collective-permute-done.34.refs_1_), channel_id=1, source_target_pairs={{0,4},{4,8},{8,12},{12,14},{14,10},{10,6},{6,2},{2,0},{1,5},{5,9},... | collective-permute-start | bytes 393224 | tf_op jit(solution)/shard_map/ppermute | solution.py:281
  73.8 6.2 %collective-permute-start.39 = (bf16[128,512]{1,0:T(8,128)(2,1)S(1)}, bf16[128,512]{1,0:T(8,128)(2,1)S(1)}, u32[]{:S(2)}, u32[]{:S(2)}) collective-permute-start(bf16[128,512]{1,0:T(8,128)(2,1)S(1)} %collective-permute-done.37.refs_4_), channel_id=1, source_target_pairs={{4,0},{8,4},{12,8},{14,12},{10,14},{6,10},{2,6},{0,2},{5,1},{9,5},... | collective-permute-start | bytes 393224 | tf_op jit(solution)/shard_map/ppermute | solution.py:279
  77.7 6.4 %collective-permute-start.40 = (bf16[128,512]{1,0:T(8,128)(2,1)S(1)}, bf16[128,512]{1,0:T(8,128)(2,1)S(1)}, u32[]{:S(2)}, u32[]{:S(2)}) collective-permute-start(bf16[128,512]{1,0:T(8,128)(2,1)S(1)} %shard_map.111.refs_2_), channel_id=1, source_target_pairs={{0,4},{4,8},{8,12},{12,14},{14,10},{10,6},{6,2},{2,0},{1,5},{5,9},... | collective-permute-start | bytes 393224 | tf_op jit(solution)/shard_map/ppermute | solution.py:268
  80.3 6.2 %collective-permute-start.43 = (bf16[128,512]{1,0:T(8,128)(2,1)S(1)}, bf16[128,512]{1,0:T(8,128)(2,1)S(1)}, u32[]{:S(2)}, u32[]{:S(2)}) collective-permute-start(bf16[128,512]{1,0:T(8,128)(2,1)S(1)} %shard_map.112.refs_3_), channel_id=1, source_target_pairs={{4,0},{8,4},{12,8},{14,12},{10,14},{6,10},{2,6},{0,2},{5,1},{9,5},... | collective-permute-start | bytes 393224 | tf_op jit(solution)/shard_map/ppermute | solution.py:269
  80.5 6.4 %collective-permute-start.41 = (bf16[128,512]{1,0:T(8,128)(2,1)S(1)}, bf16[128,512]{1,0:T(8,128)(2,1)S(1)}, u32[]{:S(2)}, u32[]{:S(2)}) collective-permute-start(bf16[128,512]{1,0:T(8,128)(2,1)S(1)} %shard_map.112.refs_3_), channel_id=1, source_target_pairs={{0,4},{4,8},{8,12},{12,14},{14,10},{10,6},{6,2},{2,0},{1,5},{5,9},... | collective-permute-start | bytes 393224 | tf_op jit(solution)/shard_map/ppermute | solution.py:268
  82.4 6.7 %collective-permute-start.42 = (bf16[128,512]{1,0:T(8,128)(2,1)S(1)}, bf16[128,512]{1,0:T(8,128)(2,1)S(1)}, u32[]{:S(2)}, u32[]{:S(2)}) collective-permute-start(bf16[128,512]{1,0:T(8,128)(2,1)S(1)} %shard_map.111.refs_2_), channel_id=1, source_target_pairs={{4,0},{8,4},{12,8},{14,12},{10,14},{6,10},{2,6},{0,2},{5,1},{9,5},... | collective-permute-start | bytes 393224 | tf_op jit(solution)/shard_map/ppermute | solution.py:269
  84.0 6.4 %collective-permute-start.44 = (bf16[128,512]{1,0:T(8,128)(2,1)S(1)}, bf16[128,512]{1,0:T(8,128)(2,1)S(1)}, u32[]{:S(2)}, u32[]{:S(2)}) collective-permute-start(bf16[128,512]{1,0:T(8,128)(2,1)S(1)} %collective-permute-done.40.refs_1_), channel_id=1, source_target_pairs={{0,4},{4,8},{8,12},{12,14},{14,10},{10,6},{6,2},{2,0},{1,5},{5,9},... | collective-permute-start | bytes 393224 | tf_op jit(solution)/shard_map/ppermute | solution.py:276
  86.5 5.9 %collective-permute-start.47 = (bf16[128,512]{1,0:T(8,128)(2,1)S(1)}, bf16[128,512]{1,0:T(8,128)(2,1)S(1)}, u32[]{:S(2)}, u32[]{:S(2)}) collective-permute-start(bf16[128,512]{1,0:T(8,128)(2,1)S(1)} %collective-permute-done.43.refs_4_), channel_id=1, source_target_pairs={{4,0},{8,4},{12,8},{14,12},{10,14},{6,10},{2,6},{0,2},{5,1},{9,5},... | collective-permute-start | bytes 393224 | tf_op jit(solution)/shard_map/ppermute | solution.py:277
  90.4 6.1 %collective-permute-start.48 = (bf16[128,512]{1,0:T(8,128)(2,1)S(1)}, bf16[128,512]{1,0:T(8,128)(2,1)S(1)}, u32[]{:S(2)}, u32[]{:S(2)}) collective-permute-start(bf16[128,512]{1,0:T(8,128)(2,1)S(1)} %collective-permute-done.44.refs_1_), channel_id=1, source_target_pairs={{0,4},{4,8},{8,12},{12,14},{14,10},{10,6},{6,2},{2,0},{1,5},{5,9},... | collective-permute-start | bytes 393224 | tf_op jit(solution)/shard_map/ppermute | solution.py:276
  92.5 6.4 %collective-permute-start.51 = (bf16[128,512]{1,0:T(8,128)(2,1)S(1)}, bf16[128,512]{1,0:T(8,128)(2,1)S(1)}, u32[]{:S(2)}, u32[]{:S(2)}) collective-permute-start(bf16[128,512]{1,0:T(8,128)(2,1)S(1)} %collective-permute-done.47.refs_4_), channel_id=1, source_target_pairs={{4,0},{8,4},{12,8},{14,12},{10,14},{6,10},{2,6},{0,2},{5,1},{9,5},... | collective-permute-start | bytes 393224 | tf_op jit(solution)/shard_map/ppermute | solution.py:277
  92.5 7.6 %collective-permute-start.49 = (bf16[128,512]{1,0:T(8,128)(2,1)S(1)}, bf16[128,512]{1,0:T(8,128)(2,1)S(1)}, u32[]{:S(2)}, u32[]{:S(2)}) collective-permute-start(bf16[128,512]{1,0:T(8,128)(2,1)S(1)} %collective-permute-done.45.refs_2_), channel_id=1, source_target_pairs={{0,4},{4,8},{8,12},{12,14},{14,10},{10,6},{6,2},{2,0},{1,5},{5,9},... | collective-permute-start | bytes 393224 | tf_op jit(solution)/shard_map/ppermute | solution.py:276
  94.8 6.6 %collective-permute-start.50 = (bf16[128,512]{1,0:T(8,128)(2,1)S(1)}, bf16[128,512]{1,0:T(8,128)(2,1)S(1)}, u32[]{:S(2)}, u32[]{:S(2)}) collective-permute-start(bf16[128,512]{1,0:T(8,128)(2,1)S(1)} %collective-permute-done.46.refs_3_), channel_id=1, source_target_pairs={{4,0},{8,4},{12,8},{14,12},{10,14},{6,10},{2,6},{0,2},{5,1},{9,5},... | collective-permute-start | bytes 393224 | tf_op jit(solution)/shard_map/ppermute | solution.py:277
  96.5 6.4 %collective-permute-start.52 = (bf16[128,512]{1,0:T(8,128)(2,1)S(1)}, bf16[128,512]{1,0:T(8,128)(2,1)S(1)}, u32[]{:S(2)}, u32[]{:S(2)}) collective-permute-start(bf16[128,512]{1,0:T(8,128)(2,1)S(1)} %collective-permute-done.48.refs_1_), channel_id=1, source_target_pairs={{0,4},{4,8},{8,12},{12,14},{14,10},{10,6},{6,2},{2,0},{1,5},{5,9},... | collective-permute-start | bytes 393224 | tf_op jit(solution)/shard_map/ppermute | solution.py:281
  98.8 6.8 %collective-permute-start.53 = (bf16[128,512]{1,0:T(8,128)(2,1)S(1)}, bf16[128,512]{1,0:T(8,128)(2,1)S(1)}, u32[]{:S(2)}, u32[]{:S(2)}) collective-permute-start(bf16[128,512]{1,0:T(8,128)(2,1)S(1)} %collective-permute-done.51.refs_4_), channel_id=1, source_target_pairs={{4,0},{8,4},{12,8},{14,12},{10,14},{6,10},{2,6},{0,2},{5,1},{9,5},... | collective-permute-start | bytes 393224 | tf_op jit(solution)/shard_map/ppermute | solution.py:279
  109.6 6.4 %collective-permute-start.58 = (bf16[128,512]{1,0:T(8,128)(2,1)S(1)}, bf16[128,512]{1,0:T(8,128)(2,1)S(1)}, u32[]{:S(2)}, u32[]{:S(2)}) collective-permute-start(bf16[128,512]{1,0:T(8,128)(2,1)S(1)} %collective-permute-done.54.refs_1_), channel_id=1, source_target_pairs={{0,4},{4,8},{8,12},{12,14},{14,10},{10,6},{6,2},{2,0},{1,5},{5,9},... | collective-permute-start | bytes 393224 | tf_op jit(solution)/shard_map/ppermute | solution.py:276
  111.8 6.4 %collective-permute-start.61 = (bf16[128,512]{1,0:T(8,128)(2,1)S(1)}, bf16[128,512]{1,0:T(8,128)(2,1)S(1)}, u32[]{:S(2)}, u32[]{:S(2)}) collective-permute-start(bf16[128,512]{1,0:T(8,128)(2,1)S(1)} %collective-permute-done.57.refs_4_), channel_id=1, source_target_pairs={{4,0},{8,4},{12,8},{14,12},{10,14},{6,10},{2,6},{0,2},{5,1},{9,5},... | collective-permute-start | bytes 393224 | tf_op jit(solution)/shard_map/ppermute | solution.py:277
  112.6 6.2 %collective-permute-start.59 = (bf16[128,512]{1,0:T(8,128)(2,1)S(1)}, bf16[128,512]{1,0:T(8,128)(2,1)S(1)}, u32[]{:S(2)}, u32[]{:S(2)}) collective-permute-start(bf16[128,512]{1,0:T(8,128)(2,1)S(1)} %collective-permute-done.55.refs_2_), channel_id=1, source_target_pairs={{0,4},{4,8},{8,12},{12,14},{14,10},{10,6},{6,2},{2,0},{1,5},{5,9},... | collective-permute-start | bytes 393224 | tf_op jit(solution)/shard_map/ppermute | solution.py:276
  113.8 7.1 %collective-permute-start.60 = (bf16[128,512]{1,0:T(8,128)(2,1)S(1)}, bf16[128,512]{1,0:T(8,128)(2,1)S(1)}, u32[]{:S(2)}, u32[]{:S(2)}) collective-permute-start(bf16[128,512]{1,0:T(8,128)(2,1)S(1)} %collective-permute-done.56.refs_3_), channel_id=1, source_target_pairs={{4,0},{8,4},{12,8},{14,12},{10,14},{6,10},{2,6},{0,2},{5,1},{9,5},... | collective-permute-start | bytes 393224 | tf_op jit(solution)/shard_map/ppermute | solution.py:277
  116.1 6.2 %collective-permute-start.62 = (bf16[128,512]{1,0:T(8,128)(2,1)S(1)}, bf16[128,512]{1,0:T(8,128)(2,1)S(1)}, u32[]{:S(2)}, u32[]{:S(2)}) collective-permute-start(bf16[128,512]{1,0:T(8,128)(2,1)S(1)} %collective-permute-done.58.refs_1_), channel_id=1, source_target_pairs={{0,4},{4,8},{8,12},{12,14},{14,10},{10,6},{6,2},{2,0},{1,5},{5,9},... | collective-permute-start | bytes 393224 | tf_op jit(solution)/shard_map/ppermute | solution.py:276
  118.7 6.1 %collective-permute-start.63 = (bf16[128,512]{1,0:T(8,128)(2,1)S(1)}, bf16[128,512]{1,0:T(8,128)(2,1)S(1)}, u32[]{:S(2)}, u32[]{:S(2)}) collective-permute-start(bf16[128,512]{1,0:T(8,128)(2,1)S(1)} %collective-permute-done.59.refs_2_), channel_id=1, source_target_pairs={{0,4},{4,8},{8,12},{12,14},{14,10},{10,6},{6,2},{2,0},{1,5},{5,9},... | collective-permute-start | bytes 393224 | tf_op jit(solution)/shard_map/ppermute | solution.py:276
  121.0 5.8 %collective-permute-start.64 = (bf16[128,512]{1,0:T(8,128)(2,1)S(1)}, bf16[128,512]{1,0:T(8,128)(2,1)S(1)}, u32[]{:S(2)}, u32[]{:S(2)}) collective-permute-start(bf16[128,512]{1,0:T(8,128)(2,1)S(1)} %collective-permute-done.60.refs_3_), channel_id=1, source_target_pairs={{4,0},{8,4},{12,8},{14,12},{10,14},{6,10},{2,6},{0,2},{5,1},{9,5},... | collective-permute-start | bytes 393224 | tf_op jit(solution)/shard_map/ppermute | solution.py:277
  123.9 6.1 %collective-permute-start.67 = (bf16[128,512]{1,0:T(8,128)(2,1)S(1)}, bf16[128,512]{1,0:T(8,128)(2,1)S(1)}, u32[]{:S(2)}, u32[]{:S(2)}) collective-permute-start(bf16[128,512]{1,0:T(8,128)(2,1)S(1)} %collective-permute-done.65.refs_4_), channel_id=1, source_target_pairs={{4,0},{8,4},{12,8},{14,12},{10,14},{6,10},{2,6},{0,2},{5,1},{9,5},... | collective-permute-start | bytes 393224 | tf_op jit(solution)/shard_map/ppermute | solution.py:279
  141.4 6.2 %collective-permute-start.77 = (bf16[128,512]{1,0:T(8,128)(2,1)S(1)}, bf16[128,512]{1,0:T(8,128)(2,1)S(1)}, u32[]{:S(2)}, u32[]{:S(2)}) collective-permute-start(bf16[128,512]{1,0:T(8,128)(2,1)S(1)} %collective-permute-done.73.refs_2_), channel_id=1, source_target_pairs={{0,4},{4,8},{8,12},{12,14},{14,10},{10,6},{6,2},{2,0},{1,5},{5,9},... | collective-permute-start | bytes 393224 | tf_op jit(solution)/shard_map/ppermute | solution.py:276
  (46 other events, 268.7 us)

commit v5 on v4

--- a/solution.py
+++ b/solution.py
@@ -8,7 +8,7 @@
 GATE_KINDS = 4
 LANES = 128
 MAX_RING = 8
-SCRATCH = 16 * 2**20
+SCRATCH = 12 * 2**20
 
 
 def plain(
@@ -107,7 +107,7 @@
         return total
 
     def tiles(self):
-        width = min(self.columns, GATE_KINDS * LANES)
+        width = min(self.columns, (2 if self.turned else GATE_KINDS) * LANES)
         return [slice(at, at + width) for at in range(0, self.columns, width)]
 
     def add(self, groups, away, total=None, first=None):
@@ -273,8 +273,8 @@
                 ready = total
                 total = gather.add([below, above], away[k : k + 2], total)
                 if k + 2 < devices - 1:
+                    above = [lax.ppermute(after(block, ready), "mp", down) for block in above]
                     below = [lax.ppermute(after(block, ready), "mp", up) for block in below]
-                    above = [lax.ppermute(after(block, ready), "mp", down) for block in above]
             lasts = [
                 lax.ppermute(above[c], "mp", down)
                 if c % 2

time: 153 us -> 153 us (level)
  transfers between devices with their start and end apart: 82 -> 82, of which waited for: 40 -> 39; matrix products, arithmetic and copies ran while one was open for 0% -> 0% of each run, Pallas kernels for 18% -> 18%
where the time goes in v5:
time: 153 us
  starting transfers between devices  88.4 us (58%)
  waiting for transfers between devices  30.7 us (20%)
  Pallas kernels  29.1 us (19%)
  local copies, waits for them, and re-layouts  3.23 us (2%)
    ppermute x24, starting transfers between devices, gathered(): below = [lax.ppermute(after(block, ready), 'mp', up) for block in below]  45.9 us
    pallas_call x36, Pallas kernels, call(): pl.pallas_call(kernel, in_specs=[pl.BlockSpec(memory_space=pltpu.SMEM)] +...  29.1 us
    ppermute x11, starting transfers between devices, gathered(): below = [lax.ppermute(block, 'mp', up) for block in blocks]  22 us
    ppermute x6, starting transfers between devices, gathered(): lax.ppermute(below[c], 'mp', up)  12.2 us
    ppermute x24, waiting for transfers between devices, gathered(): above = [lax.ppermute(after(block, ready), 'mp', down) for block in above]  11.1 us
    ppermute x24, waiting for transfers between devices, gathered(): below = [lax.ppermute(after(block, ready), 'mp', up) for block in below]  9.62 us
    ppermute x11, waiting for transfers between devices, gathered(): below = [lax.ppermute(block, 'mp', up) for block in blocks]  4.88 us
    ppermute x24, starting transfers between devices, gathered(): above = [lax.ppermute(after(block, ready), 'mp', down) for block in above]  4.6 us
  transfers between devices with their start and end apart: 82, of which 39 were waited for; matrix products, arithmetic and copies ran while one was open for 0% of the time, Pallas kernels for 18%

profile of v5, /device:TPU:0, one launch (start us, length us, event | category | flops | bytes accessed | tf_op | source)
XLA Modules:
  0.0 153.0 jit_solution(3107665007721995120)
XLA Ops:
  0.6 3.1 %collective-permute-start = (bf16[256,512]{1,0:T(8,128)(2,1)}, bf16[256,512]{1,0:T(8,128)(2,1)S(1)}, u32[]{:S(2)}, u32[]{:S(2)}) collective-permute-start(bf16[256,512]{1,0:T(8,128)(2,1)} %refs_0_.1), channel_id=1, source_target_pairs={{0,4},{4,8},{8,12},{12,14},{14,10},{10,6},{6,2},{2,0},{1,5},{5,9},... | collective-permute-start | bytes 786440 | tf_op jit(solution)/shard_map/ppermute | solution.py:268
  3.7 2.2 %copy-done = bf16[512,4096]{1,0:T(8,128)(2,1)S(1)} copy-done((bf16[512,4096]{1,0:T(8,128)(2,1)S(1)}, bf16[512,4096]{1,0:T(8,128)(2,1)}, u32[]{:S(2)}) %copy-start) | copy-done | bytes 4194328
  7.2 2.9 %collective-permute-done = bf16[256,512]{1,0:T(8,128)(2,1)S(1)} collective-permute-done((bf16[256,512]{1,0:T(8,128)(2,1)}, bf16[256,512]{1,0:T(8,128)(2,1)S(1)}, u32[]{:S(2)}, u32[]{:S(2)}) %collective-permute-start) | collective-permute-done | bytes 262176 | tf_op jit(solution)/shard_map/ppermute | solution.py:268
  10.2 1.9 %collective-permute-start.2 = (bf16[128,512]{1,0:T(8,128)(2,1)S(1)}, bf16[128,512]{1,0:T(8,128)(2,1)S(1)}, u32[]{:S(2)}, u32[]{:S(2)}) collective-permute-start(bf16[128,512]{1,0:T(8,128)(2,1)S(1)} %get-tuple-element.60.refs_1_), channel_id=1, source_target_pairs={{0,4},{4,8},{8,12},{12,14},{14,10},{10,6},{6,2},{2,0},{1,5},{5,9},... | collective-permute-start | bytes 393224 | tf_op jit(solution)/shard_map/ppermute | solution.py:277
  12.8 1.9 %collective-permute-start.3 = (bf16[128,512]{1,0:T(8,128)(2,1)S(1)}, bf16[128,512]{1,0:T(8,128)(2,1)S(1)}, u32[]{:S(2)}, u32[]{:S(2)}) collective-permute-start(bf16[128,512]{1,0:T(8,128)(2,1)S(1)} %get-tuple-element.61.refs_2_), channel_id=1, source_target_pairs={{0,4},{4,8},{8,12},{12,14},{14,10},{10,6},{6,2},{2,0},{1,5},{5,9},... | collective-permute-start | bytes 393224 | tf_op jit(solution)/shard_map/ppermute | solution.py:277
  16.3 2.1 %collective-permute-start.6 = (bf16[128,512]{1,0:T(8,128)(2,1)S(1)}, bf16[128,512]{1,0:T(8,128)(2,1)S(1)}, u32[]{:S(2)}, u32[]{:S(2)}) collective-permute-start(bf16[128,512]{1,0:T(8,128)(2,1)S(1)} %collective-permute-done.2.refs_1_), channel_id=1, source_target_pairs={{0,4},{4,8},{8,12},{12,14},{14,10},{10,6},{6,2},{2,0},{1,5},{5,9},... | collective-permute-start | bytes 393224 | tf_op jit(solution)/shard_map/ppermute | solution.py:277
  19.3 1.9 %collective-permute-start.7 = (bf16[128,512]{1,0:T(8,128)(2,1)S(1)}, bf16[128,512]{1,0:T(8,128)(2,1)S(1)}, u32[]{:S(2)}, u32[]{:S(2)}) collective-permute-start(bf16[128,512]{1,0:T(8,128)(2,1)S(1)} %collective-permute-done.3.refs_2_), channel_id=1, source_target_pairs={{0,4},{4,8},{8,12},{12,14},{14,10},{10,6},{6,2},{2,0},{1,5},{5,9},... | collective-permute-start | bytes 393224 | tf_op jit(solution)/shard_map/ppermute | solution.py:277
  22.2 1.8 %collective-permute-start.10 = (bf16[128,512]{1,0:T(8,128)(2,1)S(1)}, bf16[128,512]{1,0:T(8,128)(2,1)S(1)}, u32[]{:S(2)}, u32[]{:S(2)}) collective-permute-start(bf16[128,512]{1,0:T(8,128)(2,1)S(1)} %collective-permute-done.6.refs_1_), channel_id=1, source_target_pairs={{0,4},{4,8},{8,12},{12,14},{14,10},{10,6},{6,2},{2,0},{1,5},{5,9},... | collective-permute-start | bytes 393224 | tf_op jit(solution)/shard_map/ppermute | solution.py:281
  25.1 1.5 collective-permute-done.8.refs_3_
  27.6 1.9 %collective-permute-start.12 = (bf16[128,512]{1,0:T(8,128)(2,1)S(1)}, bf16[128,512]{1,0:T(8,128)(2,1)S(1)}, u32[]{:S(2)}, u32[]{:S(2)}) collective-permute-start(bf16[128,512]{1,0:T(8,128)(2,1)S(1)} %shard_map.99.refs_2_), channel_id=1, source_target_pairs={{0,4},{4,8},{8,12},{12,14},{14,10},{10,6},{6,2},{2,0},{1,5},{5,9},... | collective-permute-start | bytes 393224 | tf_op jit(solution)/shard_map/ppermute | solution.py:268
  30.1 1.8 %collective-permute-start.13 = (bf16[128,512]{1,0:T(8,128)(2,1)S(1)}, bf16[128,512]{1,0:T(8,128)(2,1)S(1)}, u32[]{:S(2)}, u32[]{:S(2)}) collective-permute-start(bf16[128,512]{1,0:T(8,128)(2,1)S(1)} %shard_map.100.refs_3_), channel_id=1, source_target_pairs={{0,4},{4,8},{8,12},{12,14},{14,10},{10,6},{6,2},{2,0},{1,5},{5,9},... | collective-permute-start | bytes 393224 | tf_op jit(solution)/shard_map/ppermute | solution.py:268
  33.1 2.0 %collective-permute-start.16 = (bf16[128,512]{1,0:T(8,128)(2,1)S(1)}, bf16[128,512]{1,0:T(8,128)(2,1)S(1)}, u32[]{:S(2)}, u32[]{:S(2)}) collective-permute-start(bf16[128,512]{1,0:T(8,128)(2,1)S(1)} %collective-permute-done.12.refs_1_), channel_id=1, source_target_pairs={{0,4},{4,8},{8,12},{12,14},{14,10},{10,6},{6,2},{2,0},{1,5},{5,9},... | collective-permute-start | bytes 393224 | tf_op jit(solution)/shard_map/ppermute | solution.py:277
  36.5 1.8 %collective-permute-start.17 = (bf16[128,512]{1,0:T(8,128)(2,1)S(1)}, bf16[128,512]{1,0:T(8,128)(2,1)S(1)}, u32[]{:S(2)}, u32[]{:S(2)}) collective-permute-start(bf16[128,512]{1,0:T(8,128)(2,1)S(1)} %collective-permute-done.13.refs_2_), channel_id=1, source_target_pairs={{0,4},{4,8},{8,12},{12,14},{14,10},{10,6},{6,2},{2,0},{1,5},{5,9},... | collective-permute-start | bytes 393224 | tf_op jit(solution)/shard_map/ppermute | solution.py:277
  40.3 2.0 %collective-permute-start.20 = (bf16[128,512]{1,0:T(8,128)(2,1)S(1)}, bf16[128,512]{1,0:T(8,128)(2,1)S(1)}, u32[]{:S(2)}, u32[]{:S(2)}) collective-permute-start(bf16[128,512]{1,0:T(8,128)(2,1)S(1)} %collective-permute-done.16.refs_1_), channel_id=1, source_target_pairs={{0,4},{4,8},{8,12},{12,14},{14,10},{10,6},{6,2},{2,0},{1,5},{5,9},... | collective-permute-start | bytes 393224 | tf_op jit(solution)/shard_map/ppermute | solution.py:277
  42.4 1.9 %collective-permute-start.21 = (bf16[128,512]{1,0:T(8,128)(2,1)S(1)}, bf16[128,512]{1,0:T(8,128)(2,1)S(1)}, u32[]{:S(2)}, u32[]{:S(2)}) collective-permute-start(bf16[128,512]{1,0:T(8,128)(2,1)S(1)} %collective-permute-done.17.refs_2_), channel_id=1, source_target_pairs={{0,4},{4,8},{8,12},{12,14},{14,10},{10,6},{6,2},{2,0},{1,5},{5,9},... | collective-permute-start | bytes 393224 | tf_op jit(solution)/shard_map/ppermute | solution.py:277
  45.4 2.0 %collective-permute-start.24 = (bf16[128,512]{1,0:T(8,128)(2,1)S(1)}, bf16[128,512]{1,0:T(8,128)(2,1)S(1)}, u32[]{:S(2)}, u32[]{:S(2)}) collective-permute-start(bf16[128,512]{1,0:T(8,128)(2,1)S(1)} %collective-permute-done.20.refs_1_), channel_id=1, source_target_pairs={{0,4},{4,8},{8,12},{12,14},{14,10},{10,6},{6,2},{2,0},{1,5},{5,9},... | collective-permute-start | bytes 393224 | tf_op jit(solution)/shard_map/ppermute | solution.py:281
  52.7 2.2 %collective-permute-start.26 = (bf16[128,512]{1,0:T(8,128)(2,1)S(1)}, bf16[128,512]{1,0:T(8,128)(2,1)S(1)}, u32[]{:S(2)}, u32[]{:S(2)}) collective-permute-start(bf16[128,512]{1,0:T(8,128)(2,1)S(1)} %get-tuple-element.76.refs_0_), channel_id=1, source_target_pairs={{0,4},{4,8},{8,12},{12,14},{14,10},{10,6},{6,2},{2,0},{1,5},{5,9},... | collective-permute-start | bytes 393224 | tf_op jit(solution)/shard_map/ppermute | solution.py:268
  56.1 2.0 %collective-permute-start.27 = (bf16[128,512]{1,0:T(8,128)(2,1)S(1)}, bf16[128,512]{1,0:T(8,128)(2,1)S(1)}, u32[]{:S(2)}, u32[]{:S(2)}) collective-permute-start(bf16[128,512]{1,0:T(8,128)(2,1)S(1)} %get-tuple-element.77.refs_1_), channel_id=1, source_target_pairs={{0,4},{4,8},{8,12},{12,14},{14,10},{10,6},{6,2},{2,0},{1,5},{5,9},... | collective-permute-start | bytes 393224 | tf_op jit(solution)/shard_map/ppermute | solution.py:268
  59.1 2.1 %collective-permute-start.30 = (bf16[128,512]{1,0:T(8,128)(2,1)S(1)}, bf16[128,512]{1,0:T(8,128)(2,1)S(1)}, u32[]{:S(2)}, u32[]{:S(2)}) collective-permute-start(bf16[128,512]{1,0:T(8,128)(2,1)S(1)} %collective-permute-done.26.refs_1_), channel_id=1, source_target_pairs={{0,4},{4,8},{8,12},{12,14},{14,10},{10,6},{6,2},{2,0},{1,5},{5,9},... | collective-permute-start | bytes 393224 | tf_op jit(solution)/shard_map/ppermute | solution.py:277
  62.0 2.1 %collective-permute-start.31 = (bf16[128,512]{1,0:T(8,128)(2,1)S(1)}, bf16[128,512]{1,0:T(8,128)(2,1)S(1)}, u32[]{:S(2)}, u32[]{:S(2)}) collective-permute-start(bf16[128,512]{1,0:T(8,128)(2,1)S(1)} %collective-permute-done.27.refs_2_), channel_id=1, source_target_pairs={{0,4},{4,8},{8,12},{12,14},{14,10},{10,6},{6,2},{2,0},{1,5},{5,9},... | collective-permute-start | bytes 393224 | tf_op jit(solution)/shard_map/ppermute | solution.py:277
  65.4 2.0 %collective-permute-start.34 = (bf16[128,512]{1,0:T(8,128)(2,1)S(1)}, bf16[128,512]{1,0:T(8,128)(2,1)S(1)}, u32[]{:S(2)}, u32[]{:S(2)}) collective-permute-start(bf16[128,512]{1,0:T(8,128)(2,1)S(1)} %collective-permute-done.30.refs_1_), channel_id=1, source_target_pairs={{0,4},{4,8},{8,12},{12,14},{14,10},{10,6},{6,2},{2,0},{1,5},{5,9},... | collective-permute-start | bytes 393224 | tf_op jit(solution)/shard_map/ppermute | solution.py:277
  67.5 2.0 %collective-permute-start.35 = (bf16[128,512]{1,0:T(8,128)(2,1)S(1)}, bf16[128,512]{1,0:T(8,128)(2,1)S(1)}, u32[]{:S(2)}, u32[]{:S(2)}) collective-permute-start(bf16[128,512]{1,0:T(8,128)(2,1)S(1)} %collective-permute-done.31.refs_2_), channel_id=1, source_target_pairs={{0,4},{4,8},{8,12},{12,14},{14,10},{10,6},{6,2},{2,0},{1,5},{5,9},... | collective-permute-start | bytes 393224 | tf_op jit(solution)/shard_map/ppermute | solution.py:277
  69.6 1.6 %collective-permute-done.34.refs_1_ = bf16[128,512]{1,0:T(8,128)(2,1)S(1)} collective-permute-done((bf16[128,512]{1,0:T(8,128)(2,1)S(1)}, bf16[128,512]{1,0:T(8,128)(2,1)S(1)}, u32[]{:S(2)}, u32[]{:S(2)}) %collective-permute-start.34) | collective-permute-done | bytes 131104 | tf_op jit(solution)/shard_map/ppermute | solution.py:277
  71.2 2.5 %collective-permute-start.38 = (bf16[128,512]{1,0:T(8,128)(2,1)S(1)}, bf16[128,512]{1,0:T(8,128)(2,1)S(1)}, u32[]{:S(2)}, u32[]{:S(2)}) collective-permute-start(bf16[128,512]{1,0:T(8,128)(2,1)S(1)} %collective-permute-done.34.refs_1_), channel_id=1, source_target_pairs={{0,4},{4,8},{8,12},{12,14},{14,10},{10,6},{6,2},{2,0},{1,5},{5,9},... | collective-permute-start | bytes 393224 | tf_op jit(solution)/shard_map/ppermute | solution.py:281
  74.2 2.3 %collective-permute-done.36.refs_3_ = bf16[128,512]{1,0:T(8,128)(2,1)S(1)} collective-permute-done((bf16[128,512]{1,0:T(8,128)(2,1)S(1)}, bf16[128,512]{1,0:T(8,128)(2,1)S(1)}, u32[]{:S(2)}, u32[]{:S(2)}) %collective-permute-start.36) | collective-permute-done | bytes 131104 | tf_op jit(solution)/shard_map/ppermute | solution.py:276
  77.7 2.3 %collective-permute-start.40 = (bf16[128,512]{1,0:T(8,128)(2,1)S(1)}, bf16[128,512]{1,0:T(8,128)(2,1)S(1)}, u32[]{:S(2)}, u32[]{:S(2)}) collective-permute-start(bf16[128,512]{1,0:T(8,128)(2,1)S(1)} %shard_map.111.refs_2_), channel_id=1, source_target_pairs={{0,4},{4,8},{8,12},{12,14},{14,10},{10,6},{6,2},{2,0},{1,5},{5,9},... | collective-permute-start | bytes 393224 | tf_op jit(solution)/shard_map/ppermute | solution.py:268
  80.5 1.9 %collective-permute-start.41 = (bf16[128,512]{1,0:T(8,128)(2,1)S(1)}, bf16[128,512]{1,0:T(8,128)(2,1)S(1)}, u32[]{:S(2)}, u32[]{:S(2)}) collective-permute-start(bf16[128,512]{1,0:T(8,128)(2,1)S(1)} %shard_map.112.refs_3_), channel_id=1, source_target_pairs={{0,4},{4,8},{8,12},{12,14},{14,10},{10,6},{6,2},{2,0},{1,5},{5,9},... | collective-permute-start | bytes 393224 | tf_op jit(solution)/shard_map/ppermute | solution.py:268
  84.0 2.3 %collective-permute-start.44 = (bf16[128,512]{1,0:T(8,128)(2,1)S(1)}, bf16[128,512]{1,0:T(8,128)(2,1)S(1)}, u32[]{:S(2)}, u32[]{:S(2)}) collective-permute-start(bf16[128,512]{1,0:T(8,128)(2,1)S(1)} %collective-permute-done.40.refs_1_), channel_id=1, source_target_pairs={{0,4},{4,8},{8,12},{12,14},{14,10},{10,6},{6,2},{2,0},{1,5},{5,9},... | collective-permute-start | bytes 393224 | tf_op jit(solution)/shard_map/ppermute | solution.py:277
  86.9 2.2 %collective-permute-start.45 = (bf16[128,512]{1,0:T(8,128)(2,1)S(1)}, bf16[128,512]{1,0:T(8,128)(2,1)S(1)}, u32[]{:S(2)}, u32[]{:S(2)}) collective-permute-start(bf16[128,512]{1,0:T(8,128)(2,1)S(1)} %collective-permute-done.41.refs_2_), channel_id=1, source_target_pairs={{0,4},{4,8},{8,12},{12,14},{14,10},{10,6},{6,2},{2,0},{1,5},{5,9},... | collective-permute-start | bytes 393224 | tf_op jit(solution)/shard_map/ppermute | solution.py:277
  90.4 2.1 %collective-permute-start.48 = (bf16[128,512]{1,0:T(8,128)(2,1)S(1)}, bf16[128,512]{1,0:T(8,128)(2,1)S(1)}, u32[]{:S(2)}, u32[]{:S(2)}) collective-permute-start(bf16[128,512]{1,0:T(8,128)(2,1)S(1)} %collective-permute-done.44.refs_1_), channel_id=1, source_target_pairs={{0,4},{4,8},{8,12},{12,14},{14,10},{10,6},{6,2},{2,0},{1,5},{5,9},... | collective-permute-start | bytes 393224 | tf_op jit(solution)/shard_map/ppermute | solution.py:277
  92.5 2.3 %collective-permute-start.49 = (bf16[128,512]{1,0:T(8,128)(2,1)S(1)}, bf16[128,512]{1,0:T(8,128)(2,1)S(1)}, u32[]{:S(2)}, u32[]{:S(2)}) collective-permute-start(bf16[128,512]{1,0:T(8,128)(2,1)S(1)} %collective-permute-done.45.refs_2_), channel_id=1, source_target_pairs={{0,4},{4,8},{8,12},{12,14},{14,10},{10,6},{6,2},{2,0},{1,5},{5,9},... | collective-permute-start | bytes 393224 | tf_op jit(solution)/shard_map/ppermute | solution.py:277
  94.8 1.6 %collective-permute-done.48.refs_1_ = bf16[128,512]{1,0:T(8,128)(2,1)S(1)} collective-permute-done((bf16[128,512]{1,0:T(8,128)(2,1)S(1)}, bf16[128,512]{1,0:T(8,128)(2,1)S(1)}, u32[]{:S(2)}, u32[]{:S(2)}) %collective-permute-start.48) | collective-permute-done | bytes 131104 | tf_op jit(solution)/shard_map/ppermute | solution.py:277
  96.5 2.4 %collective-permute-start.52 = (bf16[128,512]{1,0:T(8,128)(2,1)S(1)}, bf16[128,512]{1,0:T(8,128)(2,1)S(1)}, u32[]{:S(2)}, u32[]{:S(2)}) collective-permute-start(bf16[128,512]{1,0:T(8,128)(2,1)S(1)} %collective-permute-done.48.refs_1_), channel_id=1, source_target_pairs={{0,4},{4,8},{8,12},{12,14},{14,10},{10,6},{6,2},{2,0},{1,5},{5,9},... | collective-permute-start | bytes 393224 | tf_op jit(solution)/shard_map/ppermute | solution.py:281
  103.9 1.7 %collective-permute-start.54 = (bf16[128,512]{1,0:T(8,128)(2,1)S(1)}, bf16[128,512]{1,0:T(8,128)(2,1)S(1)}, u32[]{:S(2)}, u32[]{:S(2)}) collective-permute-start(bf16[128,512]{1,0:T(8,128)(2,1)S(1)} %get-tuple-element.95.refs_0_), channel_id=1, source_target_pairs={{0,4},{4,8},{8,12},{12,14},{14,10},{10,6},{6,2},{2,0},{1,5},{5,9},... | collective-permute-start | bytes 393224 | tf_op jit(solution)/shard_map/ppermute | solution.py:268
  107.2 1.7 %collective-permute-start.55 = (bf16[128,512]{1,0:T(8,128)(2,1)S(1)}, bf16[128,512]{1,0:T(8,128)(2,1)S(1)}, u32[]{:S(2)}, u32[]{:S(2)}) collective-permute-start(bf16[128,512]{1,0:T(8,128)(2,1)S(1)} %get-tuple-element.97.refs_1_), channel_id=1, source_target_pairs={{0,4},{4,8},{8,12},{12,14},{14,10},{10,6},{6,2},{2,0},{1,5},{5,9},... | collective-permute-start | bytes 393224 | tf_op jit(solution)/shard_map/ppermute | solution.py:268
  109.6 1.8 %collective-permute-start.58 = (bf16[128,512]{1,0:T(8,128)(2,1)S(1)}, bf16[128,512]{1,0:T(8,128)(2,1)S(1)}, u32[]{:S(2)}, u32[]{:S(2)}) collective-permute-start(bf16[128,512]{1,0:T(8,128)(2,1)S(1)} %collective-permute-done.54.refs_1_), channel_id=1, source_target_pairs={{0,4},{4,8},{8,12},{12,14},{14,10},{10,6},{6,2},{2,0},{1,5},{5,9},... | collective-permute-start | bytes 393224 | tf_op jit(solution)/shard_map/ppermute | solution.py:277
  115.9 1.7 %collective-permute-start.62 = (bf16[128,512]{1,0:T(8,128)(2,1)S(1)}, bf16[128,512]{1,0:T(8,128)(2,1)S(1)}, u32[]{:S(2)}, u32[]{:S(2)}) collective-permute-start(bf16[128,512]{1,0:T(8,128)(2,1)S(1)} %collective-permute-done.58.refs_1_), channel_id=1, source_target_pairs={{0,4},{4,8},{8,12},{12,14},{14,10},{10,6},{6,2},{2,0},{1,5},{5,9},... | collective-permute-start | bytes 393224 | tf_op jit(solution)/shard_map/ppermute | solution.py:277
  118.7 1.7 %collective-permute-start.63 = (bf16[128,512]{1,0:T(8,128)(2,1)S(1)}, bf16[128,512]{1,0:T(8,128)(2,1)S(1)}, u32[]{:S(2)}, u32[]{:S(2)}) collective-permute-start(bf16[128,512]{1,0:T(8,128)(2,1)S(1)} %collective-permute-done.59.refs_2_), channel_id=1, source_target_pairs={{0,4},{4,8},{8,12},{12,14},{14,10},{10,6},{6,2},{2,0},{1,5},{5,9},... | collective-permute-start | bytes 393224 | tf_op jit(solution)/shard_map/ppermute | solution.py:277
  122.1 1.9 %collective-permute-start.66 = (bf16[128,512]{1,0:T(8,128)(2,1)S(1)}, bf16[128,512]{1,0:T(8,128)(2,1)S(1)}, u32[]{:S(2)}, u32[]{:S(2)}) collective-permute-start(bf16[128,512]{1,0:T(8,128)(2,1)S(1)} %collective-permute-done.62.refs_1_), channel_id=1, source_target_pairs={{0,4},{4,8},{8,12},{12,14},{14,10},{10,6},{6,2},{2,0},{1,5},{5,9},... | collective-permute-start | bytes 393224 | tf_op jit(solution)/shard_map/ppermute | solution.py:281
  124.7 2.1 %collective-permute-done.64.refs_3_ = bf16[128,512]{1,0:T(8,128)(2,1)S(1)} collective-permute-done((bf16[128,512]{1,0:T(8,128)(2,1)S(1)}, bf16[128,512]{1,0:T(8,128)(2,1)S(1)}, u32[]{:S(2)}, u32[]{:S(2)}) %collective-permute-start.64) | collective-permute-done | bytes 131104 | tf_op jit(solution)/shard_map/ppermute | solution.py:276
  128.3 1.8 %collective-permute-start.68 = (bf16[128,512]{1,0:T(8,128)(2,1)S(1)}, bf16[128,512]{1,0:T(8,128)(2,1)S(1)}, u32[]{:S(2)}, u32[]{:S(2)}) collective-permute-start(bf16[128,512]{1,0:T(8,128)(2,1)S(1)} %shard_map.123.refs_2_), channel_id=1, source_target_pairs={{0,4},{4,8},{8,12},{12,14},{14,10},{10,6},{6,2},{2,0},{1,5},{5,9},... | collective-permute-start | bytes 393224 | tf_op jit(solution)/shard_map/ppermute | solution.py:268
  130.9 1.6 %collective-permute-start.69 = (bf16[128,512]{1,0:T(8,128)(2,1)S(1)}, bf16[128,512]{1,0:T(8,128)(2,1)S(1)}, u32[]{:S(2)}, u32[]{:S(2)}) collective-permute-start(bf16[128,512]{1,0:T(8,128)(2,1)S(1)} %shard_map.124.refs_3_), channel_id=1, source_target_pairs={{0,4},{4,8},{8,12},{12,14},{14,10},{10,6},{6,2},{2,0},{1,5},{5,9},... | collective-permute-start | bytes 393224 | tf_op jit(solution)/shard_map/ppermute | solution.py:268
  133.9 1.7 %collective-permute-start.72 = (bf16[128,512]{1,0:T(8,128)(2,1)S(1)}, bf16[128,512]{1,0:T(8,128)(2,1)S(1)}, u32[]{:S(2)}, u32[]{:S(2)}) collective-permute-start(bf16[128,512]{1,0:T(8,128)(2,1)S(1)} %collective-permute-done.68.refs_1_), channel_id=1, source_target_pairs={{0,4},{4,8},{8,12},{12,14},{14,10},{10,6},{6,2},{2,0},{1,5},{5,9},... | collective-permute-start | bytes 393224 | tf_op jit(solution)/shard_map/ppermute | solution.py:277
  136.0 1.6 %collective-permute-start.73 = (bf16[128,512]{1,0:T(8,128)(2,1)S(1)}, bf16[128,512]{1,0:T(8,128)(2,1)S(1)}, u32[]{:S(2)}, u32[]{:S(2)}) collective-permute-start(bf16[128,512]{1,0:T(8,128)(2,1)S(1)} %collective-permute-done.69.refs_2_), channel_id=1, source_target_pairs={{0,4},{4,8},{8,12},{12,14},{14,10},{10,6},{6,2},{2,0},{1,5},{5,9},... | collective-permute-start | bytes 393224 | tf_op jit(solution)/shard_map/ppermute | solution.py:277
  139.3 1.7 %collective-permute-start.76 = (bf16[128,512]{1,0:T(8,128)(2,1)S(1)}, bf16[128,512]{1,0:T(8,128)(2,1)S(1)}, u32[]{:S(2)}, u32[]{:S(2)}) collective-permute-start(bf16[128,512]{1,0:T(8,128)(2,1)S(1)} %collective-permute-done.72.refs_1_), channel_id=1, source_target_pairs={{0,4},{4,8},{8,12},{12,14},{14,10},{10,6},{6,2},{2,0},{1,5},{5,9},... | collective-permute-start | bytes 393224 | tf_op jit(solution)/shard_map/ppermute | solution.py:277
  141.4 1.6 %collective-permute-start.77 = (bf16[128,512]{1,0:T(8,128)(2,1)S(1)}, bf16[128,512]{1,0:T(8,128)(2,1)S(1)}, u32[]{:S(2)}, u32[]{:S(2)}) collective-permute-start(bf16[128,512]{1,0:T(8,128)(2,1)S(1)} %collective-permute-done.73.refs_2_), channel_id=1, source_target_pairs={{0,4},{4,8},{8,12},{12,14},{14,10},{10,6},{6,2},{2,0},{1,5},{5,9},... | collective-permute-start | bytes 393224 | tf_op jit(solution)/shard_map/ppermute | solution.py:277
  144.3 1.6 %collective-permute-start.81 = (bf16[128,512]{1,0:T(8,128)(2,1)S(1)}, bf16[128,512]{1,0:T(8,128)(2,1)S(1)}, u32[]{:S(2)}, u32[]{:S(2)}) collective-permute-start(bf16[128,512]{1,0:T(8,128)(2,1)S(1)} %collective-permute-done.76.refs_1_), channel_id=1, source_target_pairs={{0,4},{4,8},{8,12},{12,14},{14,10},{10,6},{6,2},{2,0},{1,5},{5,9},... | collective-permute-start | bytes 393224 | tf_op jit(solution)/shard_map/ppermute | solution.py:281
  150.9 1.9 %shard_map.130 = (bf16[256,512]{1,0:T(8,128)(2,1)}, f32[256,512]{1,0:T(8,128)}) custom-call(s32[1]{0:T(128)} %bitcast.me_ref, bf16[4096,2048]{1,0:T(8,128)(2,1)S(1)} %bitcast.3, f32[256,2048]{1,0:T(8,128)S(1)} %shard_map.128.total_ref, f32[1,2048]{1,0:T(1,128)S(1)} %bitcast.9, f32[128,512]{1,0:T(8,128)S(1)} %get-tuple-element.114.cell_ref, ...), custom_call_target="tpu_custom_call" | custom-call | tf_op jit(solution)/shard_map/pallas_call | solution.py:140
  (182 shorter events, 56.8 us)
Async XLA Ops:
  0.6 9.5 %collective-permute-start = (bf16[256,512]{1,0:T(8,128)(2,1)}, bf16[256,512]{1,0:T(8,128)(2,1)S(1)}, u32[]{:S(2)}, u32[]{:S(2)}) collective-permute-start(bf16[256,512]{1,0:T(8,128)(2,1)} %refs_0_.1), channel_id=1, source_target_pairs={{0,4},{4,8},{8,12},{12,14},{14,10},{10,6},{6,2},{2,0},{1,5},{5,9},... | collective-permute-start | bytes 786440 | tf_op jit(solution)/shard_map/ppermute | solution.py:268
  3.7 8.3 %collective-permute-start.1 = (bf16[256,512]{1,0:T(8,128)(2,1)}, bf16[256,512]{1,0:T(8,128)(2,1)S(1)}, u32[]{:S(2)}, u32[]{:S(2)}) collective-permute-start(bf16[256,512]{1,0:T(8,128)(2,1)} %refs_0_.1), channel_id=1, source_target_pairs={{4,0},{8,4},{12,8},{14,12},{10,14},{6,10},{2,6},{0,2},{5,1},{9,5},... | collective-permute-start | bytes 786440 | tf_op jit(solution)/shard_map/ppermute | solution.py:269
  10.2 6.1 %collective-permute-start.2 = (bf16[128,512]{1,0:T(8,128)(2,1)S(1)}, bf16[128,512]{1,0:T(8,128)(2,1)S(1)}, u32[]{:S(2)}, u32[]{:S(2)}) collective-permute-start(bf16[128,512]{1,0:T(8,128)(2,1)S(1)} %get-tuple-element.60.refs_1_), channel_id=1, source_target_pairs={{0,4},{4,8},{8,12},{12,14},{14,10},{10,6},{6,2},{2,0},{1,5},{5,9},... | collective-permute-start | bytes 393224 | tf_op jit(solution)/shard_map/ppermute | solution.py:277
  12.1 6.4 %collective-permute-start.5 = (bf16[128,512]{1,0:T(8,128)(2,1)S(1)}, bf16[128,512]{1,0:T(8,128)(2,1)S(1)}, u32[]{:S(2)}, u32[]{:S(2)}) collective-permute-start(bf16[128,512]{1,0:T(8,128)(2,1)S(1)} %get-tuple-element.63.refs_4_), channel_id=1, source_target_pairs={{4,0},{8,4},{12,8},{14,12},{10,14},{6,10},{2,6},{0,2},{5,1},{9,5},... | collective-permute-start | bytes 393224 | tf_op jit(solution)/shard_map/ppermute | solution.py:276
  12.8 6.5 %collective-permute-start.3 = (bf16[128,512]{1,0:T(8,128)(2,1)S(1)}, bf16[128,512]{1,0:T(8,128)(2,1)S(1)}, u32[]{:S(2)}, u32[]{:S(2)}) collective-permute-start(bf16[128,512]{1,0:T(8,128)(2,1)S(1)} %get-tuple-element.61.refs_2_), channel_id=1, source_target_pairs={{0,4},{4,8},{8,12},{12,14},{14,10},{10,6},{6,2},{2,0},{1,5},{5,9},... | collective-permute-start | bytes 393224 | tf_op jit(solution)/shard_map/ppermute | solution.py:277
  14.7 6.5 %collective-permute-start.4 = (bf16[128,512]{1,0:T(8,128)(2,1)S(1)}, bf16[128,512]{1,0:T(8,128)(2,1)S(1)}, u32[]{:S(2)}, u32[]{:S(2)}) collective-permute-start(bf16[128,512]{1,0:T(8,128)(2,1)S(1)} %get-tuple-element.62.refs_3_), channel_id=1, source_target_pairs={{4,0},{8,4},{12,8},{14,12},{10,14},{6,10},{2,6},{0,2},{5,1},{9,5},... | collective-permute-start | bytes 393224 | tf_op jit(solution)/shard_map/ppermute | solution.py:276
  16.3 6.0 %collective-permute-start.6 = (bf16[128,512]{1,0:T(8,128)(2,1)S(1)}, bf16[128,512]{1,0:T(8,128)(2,1)S(1)}, u32[]{:S(2)}, u32[]{:S(2)}) collective-permute-start(bf16[128,512]{1,0:T(8,128)(2,1)S(1)} %collective-permute-done.2.refs_1_), channel_id=1, source_target_pairs={{0,4},{4,8},{8,12},{12,14},{14,10},{10,6},{6,2},{2,0},{1,5},{5,9},... | collective-permute-start | bytes 393224 | tf_op jit(solution)/shard_map/ppermute | solution.py:277
  29.8 6.4 %collective-permute-start.15 = (bf16[128,512]{1,0:T(8,128)(2,1)S(1)}, bf16[128,512]{1,0:T(8,128)(2,1)S(1)}, u32[]{:S(2)}, u32[]{:S(2)}) collective-permute-start(bf16[128,512]{1,0:T(8,128)(2,1)S(1)} %shard_map.100.refs_3_), channel_id=1, source_target_pairs={{4,0},{8,4},{12,8},{14,12},{10,14},{6,10},{2,6},{0,2},{5,1},{9,5},... | collective-permute-start | bytes 393224 | tf_op jit(solution)/shard_map/ppermute | solution.py:269
  30.1 6.4 %collective-permute-start.13 = (bf16[128,512]{1,0:T(8,128)(2,1)S(1)}, bf16[128,512]{1,0:T(8,128)(2,1)S(1)}, u32[]{:S(2)}, u32[]{:S(2)}) collective-permute-start(bf16[128,512]{1,0:T(8,128)(2,1)S(1)} %shard_map.100.refs_3_), channel_id=1, source_target_pairs={{0,4},{4,8},{8,12},{12,14},{14,10},{10,6},{6,2},{2,0},{1,5},{5,9},... | collective-permute-start | bytes 393224 | tf_op jit(solution)/shard_map/ppermute | solution.py:268
  31.9 7.1 %collective-permute-start.14 = (bf16[128,512]{1,0:T(8,128)(2,1)S(1)}, bf16[128,512]{1,0:T(8,128)(2,1)S(1)}, u32[]{:S(2)}, u32[]{:S(2)}) collective-permute-start(bf16[128,512]{1,0:T(8,128)(2,1)S(1)} %shard_map.99.refs_2_), channel_id=1, source_target_pairs={{4,0},{8,4},{12,8},{14,12},{10,14},{6,10},{2,6},{0,2},{5,1},{9,5},... | collective-permute-start | bytes 393224 | tf_op jit(solution)/shard_map/ppermute | solution.py:269
  33.1 7.2 %collective-permute-start.16 = (bf16[128,512]{1,0:T(8,128)(2,1)S(1)}, bf16[128,512]{1,0:T(8,128)(2,1)S(1)}, u32[]{:S(2)}, u32[]{:S(2)}) collective-permute-start(bf16[128,512]{1,0:T(8,128)(2,1)S(1)} %collective-permute-done.12.refs_1_), channel_id=1, source_target_pairs={{0,4},{4,8},{8,12},{12,14},{14,10},{10,6},{6,2},{2,0},{1,5},{5,9},... | collective-permute-start | bytes 393224 | tf_op jit(solution)/shard_map/ppermute | solution.py:277
  36.2 6.2 %collective-permute-start.19 = (bf16[128,512]{1,0:T(8,128)(2,1)S(1)}, bf16[128,512]{1,0:T(8,128)(2,1)S(1)}, u32[]{:S(2)}, u32[]{:S(2)}) collective-permute-start(bf16[128,512]{1,0:T(8,128)(2,1)S(1)} %collective-permute-done.15.refs_4_), channel_id=1, source_target_pairs={{4,0},{8,4},{12,8},{14,12},{10,14},{6,10},{2,6},{0,2},{5,1},{9,5},... | collective-permute-start | bytes 393224 | tf_op jit(solution)/shard_map/ppermute | solution.py:276
  36.5 5.9 %collective-permute-start.17 = (bf16[128,512]{1,0:T(8,128)(2,1)S(1)}, bf16[128,512]{1,0:T(8,128)(2,1)S(1)}, u32[]{:S(2)}, u32[]{:S(2)}) collective-permute-start(bf16[128,512]{1,0:T(8,128)(2,1)S(1)} %collective-permute-done.13.refs_2_), channel_id=1, source_target_pairs={{0,4},{4,8},{8,12},{12,14},{14,10},{10,6},{6,2},{2,0},{1,5},{5,9},... | collective-permute-start | bytes 393224 | tf_op jit(solution)/shard_map/ppermute | solution.py:277
  39.0 6.3 %collective-permute-start.18 = (bf16[128,512]{1,0:T(8,128)(2,1)S(1)}, bf16[128,512]{1,0:T(8,128)(2,1)S(1)}, u32[]{:S(2)}, u32[]{:S(2)}) collective-permute-start(bf16[128,512]{1,0:T(8,128)(2,1)S(1)} %collective-permute-done.14.refs_3_), channel_id=1, source_target_pairs={{4,0},{8,4},{12,8},{14,12},{10,14},{6,10},{2,6},{0,2},{5,1},{9,5},... | collective-permute-start | bytes 393224 | tf_op jit(solution)/shard_map/ppermute | solution.py:276
  42.4 6.8 %collective-permute-start.21 = (bf16[128,512]{1,0:T(8,128)(2,1)S(1)}, bf16[128,512]{1,0:T(8,128)(2,1)S(1)}, u32[]{:S(2)}, u32[]{:S(2)}) collective-permute-start(bf16[128,512]{1,0:T(8,128)(2,1)S(1)} %collective-permute-done.17.refs_2_), channel_id=1, source_target_pairs={{0,4},{4,8},{8,12},{12,14},{14,10},{10,6},{6,2},{2,0},{1,5},{5,9},... | collective-permute-start | bytes 393224 | tf_op jit(solution)/shard_map/ppermute | solution.py:277
  45.4 6.2 %collective-permute-start.24 = (bf16[128,512]{1,0:T(8,128)(2,1)S(1)}, bf16[128,512]{1,0:T(8,128)(2,1)S(1)}, u32[]{:S(2)}, u32[]{:S(2)}) collective-permute-start(bf16[128,512]{1,0:T(8,128)(2,1)S(1)} %collective-permute-done.20.refs_1_), channel_id=1, source_target_pairs={{0,4},{4,8},{8,12},{12,14},{14,10},{10,6},{6,2},{2,0},{1,5},{5,9},... | collective-permute-start | bytes 393224 | tf_op jit(solution)/shard_map/ppermute | solution.py:281
  47.5 7.4 %collective-permute-start.25 = (bf16[128,512]{1,0:T(8,128)(2,1)S(1)}, bf16[128,512]{1,0:T(8,128)(2,1)S(1)}, u32[]{:S(2)}, u32[]{:S(2)}) collective-permute-start(bf16[128,512]{1,0:T(8,128)(2,1)S(1)} %collective-permute-done.23.refs_4_), channel_id=1, source_target_pairs={{4,0},{8,4},{12,8},{14,12},{10,14},{6,10},{2,6},{0,2},{5,1},{9,5},... | collective-permute-start | bytes 393224 | tf_op jit(solution)/shard_map/ppermute | solution.py:279
  52.7 6.4 %collective-permute-start.26 = (bf16[128,512]{1,0:T(8,128)(2,1)S(1)}, bf16[128,512]{1,0:T(8,128)(2,1)S(1)}, u32[]{:S(2)}, u32[]{:S(2)}) collective-permute-start(bf16[128,512]{1,0:T(8,128)(2,1)S(1)} %get-tuple-element.76.refs_0_), channel_id=1, source_target_pairs={{0,4},{4,8},{8,12},{12,14},{14,10},{10,6},{6,2},{2,0},{1,5},{5,9},... | collective-permute-start | bytes 393224 | tf_op jit(solution)/shard_map/ppermute | solution.py:268
  56.1 5.9 %collective-permute-start.27 = (bf16[128,512]{1,0:T(8,128)(2,1)S(1)}, bf16[128,512]{1,0:T(8,128)(2,1)S(1)}, u32[]{:S(2)}, u32[]{:S(2)}) collective-permute-start(bf16[128,512]{1,0:T(8,128)(2,1)S(1)} %get-tuple-element.77.refs_1_), channel_id=1, source_target_pairs={{0,4},{4,8},{8,12},{12,14},{14,10},{10,6},{6,2},{2,0},{1,5},{5,9},... | collective-permute-start | bytes 393224 | tf_op jit(solution)/shard_map/ppermute | solution.py:268
  58.1 6.4 %collective-permute-start.28 = (bf16[128,512]{1,0:T(8,128)(2,1)S(1)}, bf16[128,512]{1,0:T(8,128)(2,1)S(1)}, u32[]{:S(2)}, u32[]{:S(2)}) collective-permute-start(bf16[128,512]{1,0:T(8,128)(2,1)S(1)} %get-tuple-element.76.refs_0_), channel_id=1, source_target_pairs={{4,0},{8,4},{12,8},{14,12},{10,14},{6,10},{2,6},{0,2},{5,1},{9,5},... | collective-permute-start | bytes 393224 | tf_op jit(solution)/shard_map/ppermute | solution.py:269
  59.1 6.3 %collective-permute-start.30 = (bf16[128,512]{1,0:T(8,128)(2,1)S(1)}, bf16[128,512]{1,0:T(8,128)(2,1)S(1)}, u32[]{:S(2)}, u32[]{:S(2)}) collective-permute-start(bf16[128,512]{1,0:T(8,128)(2,1)S(1)} %collective-permute-done.26.refs_1_), channel_id=1, source_target_pairs={{0,4},{4,8},{8,12},{12,14},{14,10},{10,6},{6,2},{2,0},{1,5},{5,9},... | collective-permute-start | bytes 393224 | tf_op jit(solution)/shard_map/ppermute | solution.py:277
  61.7 5.8 %collective-permute-start.33 = (bf16[128,512]{1,0:T(8,128)(2,1)S(1)}, bf16[128,512]{1,0:T(8,128)(2,1)S(1)}, u32[]{:S(2)}, u32[]{:S(2)}) collective-permute-start(bf16[128,512]{1,0:T(8,128)(2,1)S(1)} %collective-permute-done.29.refs_4_), channel_id=1, source_target_pairs={{4,0},{8,4},{12,8},{14,12},{10,14},{6,10},{2,6},{0,2},{5,1},{9,5},... | collective-permute-start | bytes 393224 | tf_op jit(solution)/shard_map/ppermute | solution.py:276
  67.5 6.2 %collective-permute-start.37 = (bf16[128,512]{1,0:T(8,128)(2,1)S(1)}, bf16[128,512]{1,0:T(8,128)(2,1)S(1)}, u32[]{:S(2)}, u32[]{:S(2)}) collective-permute-start(bf16[128,512]{1,0:T(8,128)(2,1)S(1)} %collective-permute-done.33.refs_4_), channel_id=1, source_target_pairs={{4,0},{8,4},{12,8},{14,12},{10,14},{6,10},{2,6},{0,2},{5,1},{9,5},... | collective-permute-start | bytes 393224 | tf_op jit(solution)/shard_map/ppermute | solution.py:276
  67.5 6.7 %collective-permute-start.35 = (bf16[128,512]{1,0:T(8,128)(2,1)S(1)}, bf16[128,512]{1,0:T(8,128)(2,1)S(1)}, u32[]{:S(2)}, u32[]{:S(2)}) collective-permute-start(bf16[128,512]{1,0:T(8,128)(2,1)S(1)} %collective-permute-done.31.refs_2_), channel_id=1, source_target_pairs={{0,4},{4,8},{8,12},{12,14},{14,10},{10,6},{6,2},{2,0},{1,5},{5,9},... | collective-permute-start | bytes 393224 | tf_op jit(solution)/shard_map/ppermute | solution.py:277
  69.6 7.0 %collective-permute-start.36 = (bf16[128,512]{1,0:T(8,128)(2,1)S(1)}, bf16[128,512]{1,0:T(8,128)(2,1)S(1)}, u32[]{:S(2)}, u32[]{:S(2)}) collective-permute-start(bf16[128,512]{1,0:T(8,128)(2,1)S(1)} %collective-permute-done.32.refs_3_), channel_id=1, source_target_pairs={{4,0},{8,4},{12,8},{14,12},{10,14},{6,10},{2,6},{0,2},{5,1},{9,5},... | collective-permute-start | bytes 393224 | tf_op jit(solution)/shard_map/ppermute | solution.py:276
  71.2 6.0 %collective-permute-start.38 = (bf16[128,512]{1,0:T(8,128)(2,1)S(1)}, bf16[128,512]{1,0:T(8,128)(2,1)S(1)}, u32[]{:S(2)}, u32[]{:S(2)}) collective-permute-start(bf16[128,512]{1,0:T(8,128)(2,1)S(1)} %collective-permute-done.34.refs_1_), channel_id=1, source_target_pairs={{0,4},{4,8},{8,12},{12,14},{14,10},{10,6},{6,2},{2,0},{1,5},{5,9},... | collective-permute-start | bytes 393224 | tf_op jit(solution)/shard_map/ppermute | solution.py:281
  73.7 6.2 %collective-permute-start.39 = (bf16[128,512]{1,0:T(8,128)(2,1)S(1)}, bf16[128,512]{1,0:T(8,128)(2,1)S(1)}, u32[]{:S(2)}, u32[]{:S(2)}) collective-permute-start(bf16[128,512]{1,0:T(8,128)(2,1)S(1)} %collective-permute-done.37.refs_4_), channel_id=1, source_target_pairs={{4,0},{8,4},{12,8},{14,12},{10,14},{6,10},{2,6},{0,2},{5,1},{9,5},... | collective-permute-start | bytes 393224 | tf_op jit(solution)/shard_map/ppermute | solution.py:279
  77.7 6.3 %collective-permute-start.40 = (bf16[128,512]{1,0:T(8,128)(2,1)S(1)}, bf16[128,512]{1,0:T(8,128)(2,1)S(1)}, u32[]{:S(2)}, u32[]{:S(2)}) collective-permute-start(bf16[128,512]{1,0:T(8,128)(2,1)S(1)} %shard_map.111.refs_2_), channel_id=1, source_target_pairs={{0,4},{4,8},{8,12},{12,14},{14,10},{10,6},{6,2},{2,0},{1,5},{5,9},... | collective-permute-start | bytes 393224 | tf_op jit(solution)/shard_map/ppermute | solution.py:268
  80.3 6.2 %collective-permute-start.43 = (bf16[128,512]{1,0:T(8,128)(2,1)S(1)}, bf16[128,512]{1,0:T(8,128)(2,1)S(1)}, u32[]{:S(2)}, u32[]{:S(2)}) collective-permute-start(bf16[128,512]{1,0:T(8,128)(2,1)S(1)} %shard_map.112.refs_3_), channel_id=1, source_target_pairs={{4,0},{8,4},{12,8},{14,12},{10,14},{6,10},{2,6},{0,2},{5,1},{9,5},... | collective-permute-start | bytes 393224 | tf_op jit(solution)/shard_map/ppermute | solution.py:269
  80.5 6.4 %collective-permute-start.41 = (bf16[128,512]{1,0:T(8,128)(2,1)S(1)}, bf16[128,512]{1,0:T(8,128)(2,1)S(1)}, u32[]{:S(2)}, u32[]{:S(2)}) collective-permute-start(bf16[128,512]{1,0:T(8,128)(2,1)S(1)} %shard_map.112.refs_3_), channel_id=1, source_target_pairs={{0,4},{4,8},{8,12},{12,14},{14,10},{10,6},{6,2},{2,0},{1,5},{5,9},... | collective-permute-start | bytes 393224 | tf_op jit(solution)/shard_map/ppermute | solution.py:268
  82.4 6.7 %collective-permute-start.42 = (bf16[128,512]{1,0:T(8,128)(2,1)S(1)}, bf16[128,512]{1,0:T(8,128)(2,1)S(1)}, u32[]{:S(2)}, u32[]{:S(2)}) collective-permute-start(bf16[128,512]{1,0:T(8,128)(2,1)S(1)} %shard_map.111.refs_2_), channel_id=1, source_target_pairs={{4,0},{8,4},{12,8},{14,12},{10,14},{6,10},{2,6},{0,2},{5,1},{9,5},... | collective-permute-start | bytes 393224 | tf_op jit(solution)/shard_map/ppermute | solution.py:269
  84.0 6.4 %collective-permute-start.44 = (bf16[128,512]{1,0:T(8,128)(2,1)S(1)}, bf16[128,512]{1,0:T(8,128)(2,1)S(1)}, u32[]{:S(2)}, u32[]{:S(2)}) collective-permute-start(bf16[128,512]{1,0:T(8,128)(2,1)S(1)} %collective-permute-done.40.refs_1_), channel_id=1, source_target_pairs={{0,4},{4,8},{8,12},{12,14},{14,10},{10,6},{6,2},{2,0},{1,5},{5,9},... | collective-permute-start | bytes 393224 | tf_op jit(solution)/shard_map/ppermute | solution.py:277
  86.5 6.0 %collective-permute-start.47 = (bf16[128,512]{1,0:T(8,128)(2,1)S(1)}, bf16[128,512]{1,0:T(8,128)(2,1)S(1)}, u32[]{:S(2)}, u32[]{:S(2)}) collective-permute-start(bf16[128,512]{1,0:T(8,128)(2,1)S(1)} %collective-permute-done.43.refs_4_), channel_id=1, source_target_pairs={{4,0},{8,4},{12,8},{14,12},{10,14},{6,10},{2,6},{0,2},{5,1},{9,5},... | collective-permute-start | bytes 393224 | tf_op jit(solution)/shard_map/ppermute | solution.py:276
  90.4 6.1 %collective-permute-start.48 = (bf16[128,512]{1,0:T(8,128)(2,1)S(1)}, bf16[128,512]{1,0:T(8,128)(2,1)S(1)}, u32[]{:S(2)}, u32[]{:S(2)}) collective-permute-start(bf16[128,512]{1,0:T(8,128)(2,1)S(1)} %collective-permute-done.44.refs_1_), channel_id=1, source_target_pairs={{0,4},{4,8},{8,12},{12,14},{14,10},{10,6},{6,2},{2,0},{1,5},{5,9},... | collective-permute-start | bytes 393224 | tf_op jit(solution)/shard_map/ppermute | solution.py:277
  92.5 6.4 %collective-permute-start.51 = (bf16[128,512]{1,0:T(8,128)(2,1)S(1)}, bf16[128,512]{1,0:T(8,128)(2,1)S(1)}, u32[]{:S(2)}, u32[]{:S(2)}) collective-permute-start(bf16[128,512]{1,0:T(8,128)(2,1)S(1)} %collective-permute-done.47.refs_4_), channel_id=1, source_target_pairs={{4,0},{8,4},{12,8},{14,12},{10,14},{6,10},{2,6},{0,2},{5,1},{9,5},... | collective-permute-start | bytes 393224 | tf_op jit(solution)/shard_map/ppermute | solution.py:276
  92.5 7.6 %collective-permute-start.49 = (bf16[128,512]{1,0:T(8,128)(2,1)S(1)}, bf16[128,512]{1,0:T(8,128)(2,1)S(1)}, u32[]{:S(2)}, u32[]{:S(2)}) collective-permute-start(bf16[128,512]{1,0:T(8,128)(2,1)S(1)} %collective-permute-done.45.refs_2_), channel_id=1, source_target_pairs={{0,4},{4,8},{8,12},{12,14},{14,10},{10,6},{6,2},{2,0},{1,5},{5,9},... | collective-permute-start | bytes 393224 | tf_op jit(solution)/shard_map/ppermute | solution.py:277
  94.8 6.6 %collective-permute-start.50 = (bf16[128,512]{1,0:T(8,128)(2,1)S(1)}, bf16[128,512]{1,0:T(8,128)(2,1)S(1)}, u32[]{:S(2)}, u32[]{:S(2)}) collective-permute-start(bf16[128,512]{1,0:T(8,128)(2,1)S(1)} %collective-permute-done.46.refs_3_), channel_id=1, source_target_pairs={{4,0},{8,4},{12,8},{14,12},{10,14},{6,10},{2,6},{0,2},{5,1},{9,5},... | collective-permute-start | bytes 393224 | tf_op jit(solution)/shard_map/ppermute | solution.py:276
  96.5 6.4 %collective-permute-start.52 = (bf16[128,512]{1,0:T(8,128)(2,1)S(1)}, bf16[128,512]{1,0:T(8,128)(2,1)S(1)}, u32[]{:S(2)}, u32[]{:S(2)}) collective-permute-start(bf16[128,512]{1,0:T(8,128)(2,1)S(1)} %collective-permute-done.48.refs_1_), channel_id=1, source_target_pairs={{0,4},{4,8},{8,12},{12,14},{14,10},{10,6},{6,2},{2,0},{1,5},{5,9},... | collective-permute-start | bytes 393224 | tf_op jit(solution)/shard_map/ppermute | solution.py:281
  98.8 6.8 %collective-permute-start.53 = (bf16[128,512]{1,0:T(8,128)(2,1)S(1)}, bf16[128,512]{1,0:T(8,128)(2,1)S(1)}, u32[]{:S(2)}, u32[]{:S(2)}) collective-permute-start(bf16[128,512]{1,0:T(8,128)(2,1)S(1)} %collective-permute-done.51.refs_4_), channel_id=1, source_target_pairs={{4,0},{8,4},{12,8},{14,12},{10,14},{6,10},{2,6},{0,2},{5,1},{9,5},... | collective-permute-start | bytes 393224 | tf_op jit(solution)/shard_map/ppermute | solution.py:279
  109.6 6.3 %collective-permute-start.58 = (bf16[128,512]{1,0:T(8,128)(2,1)S(1)}, bf16[128,512]{1,0:T(8,128)(2,1)S(1)}, u32[]{:S(2)}, u32[]{:S(2)}) collective-permute-start(bf16[128,512]{1,0:T(8,128)(2,1)S(1)} %collective-permute-done.54.refs_1_), channel_id=1, source_target_pairs={{0,4},{4,8},{8,12},{12,14},{14,10},{10,6},{6,2},{2,0},{1,5},{5,9},... | collective-permute-start | bytes 393224 | tf_op jit(solution)/shard_map/ppermute | solution.py:277
  111.8 6.4 %collective-permute-start.61 = (bf16[128,512]{1,0:T(8,128)(2,1)S(1)}, bf16[128,512]{1,0:T(8,128)(2,1)S(1)}, u32[]{:S(2)}, u32[]{:S(2)}) collective-permute-start(bf16[128,512]{1,0:T(8,128)(2,1)S(1)} %collective-permute-done.57.refs_4_), channel_id=1, source_target_pairs={{4,0},{8,4},{12,8},{14,12},{10,14},{6,10},{2,6},{0,2},{5,1},{9,5},... | collective-permute-start | bytes 393224 | tf_op jit(solution)/shard_map/ppermute | solution.py:276
  112.3 6.4 %collective-permute-start.59 = (bf16[128,512]{1,0:T(8,128)(2,1)S(1)}, bf16[128,512]{1,0:T(8,128)(2,1)S(1)}, u32[]{:S(2)}, u32[]{:S(2)}) collective-permute-start(bf16[128,512]{1,0:T(8,128)(2,1)S(1)} %collective-permute-done.55.refs_2_), channel_id=1, source_target_pairs={{0,4},{4,8},{8,12},{12,14},{14,10},{10,6},{6,2},{2,0},{1,5},{5,9},... | collective-permute-start | bytes 393224 | tf_op jit(solution)/shard_map/ppermute | solution.py:277
  113.8 7.1 %collective-permute-start.60 = (bf16[128,512]{1,0:T(8,128)(2,1)S(1)}, bf16[128,512]{1,0:T(8,128)(2,1)S(1)}, u32[]{:S(2)}, u32[]{:S(2)}) collective-permute-start(bf16[128,512]{1,0:T(8,128)(2,1)S(1)} %collective-permute-done.56.refs_3_), channel_id=1, source_target_pairs={{4,0},{8,4},{12,8},{14,12},{10,14},{6,10},{2,6},{0,2},{5,1},{9,5},... | collective-permute-start | bytes 393224 | tf_op jit(solution)/shard_map/ppermute | solution.py:276
  115.9 6.2 %collective-permute-start.62 = (bf16[128,512]{1,0:T(8,128)(2,1)S(1)}, bf16[128,512]{1,0:T(8,128)(2,1)S(1)}, u32[]{:S(2)}, u32[]{:S(2)}) collective-permute-start(bf16[128,512]{1,0:T(8,128)(2,1)S(1)} %collective-permute-done.58.refs_1_), channel_id=1, source_target_pairs={{0,4},{4,8},{8,12},{12,14},{14,10},{10,6},{6,2},{2,0},{1,5},{5,9},... | collective-permute-start | bytes 393224 | tf_op jit(solution)/shard_map/ppermute | solution.py:277
  118.7 6.0 %collective-permute-start.63 = (bf16[128,512]{1,0:T(8,128)(2,1)S(1)}, bf16[128,512]{1,0:T(8,128)(2,1)S(1)}, u32[]{:S(2)}, u32[]{:S(2)}) collective-permute-start(bf16[128,512]{1,0:T(8,128)(2,1)S(1)} %collective-permute-done.59.refs_2_), channel_id=1, source_target_pairs={{0,4},{4,8},{8,12},{12,14},{14,10},{10,6},{6,2},{2,0},{1,5},{5,9},... | collective-permute-start | bytes 393224 | tf_op jit(solution)/shard_map/ppermute | solution.py:277
  121.0 5.8 %collective-permute-start.64 = (bf16[128,512]{1,0:T(8,128)(2,1)S(1)}, bf16[128,512]{1,0:T(8,128)(2,1)S(1)}, u32[]{:S(2)}, u32[]{:S(2)}) collective-permute-start(bf16[128,512]{1,0:T(8,128)(2,1)S(1)} %collective-permute-done.60.refs_3_), channel_id=1, source_target_pairs={{4,0},{8,4},{12,8},{14,12},{10,14},{6,10},{2,6},{0,2},{5,1},{9,5},... | collective-permute-start | bytes 393224 | tf_op jit(solution)/shard_map/ppermute | solution.py:276
  123.9 6.1 %collective-permute-start.67 = (bf16[128,512]{1,0:T(8,128)(2,1)S(1)}, bf16[128,512]{1,0:T(8,128)(2,1)S(1)}, u32[]{:S(2)}, u32[]{:S(2)}) collective-permute-start(bf16[128,512]{1,0:T(8,128)(2,1)S(1)} %collective-permute-done.65.refs_4_), channel_id=1, source_target_pairs={{4,0},{8,4},{12,8},{14,12},{10,14},{6,10},{2,6},{0,2},{5,1},{9,5},... | collective-permute-start | bytes 393224 | tf_op jit(solution)/shard_map/ppermute | solution.py:279
  141.4 6.2 %collective-permute-start.77 = (bf16[128,512]{1,0:T(8,128)(2,1)S(1)}, bf16[128,512]{1,0:T(8,128)(2,1)S(1)}, u32[]{:S(2)}, u32[]{:S(2)}) collective-permute-start(bf16[128,512]{1,0:T(8,128)(2,1)S(1)} %collective-permute-done.73.refs_2_), channel_id=1, source_target_pairs={{0,4},{4,8},{8,12},{12,14},{14,10},{10,6},{6,2},{2,0},{1,5},{5,9},... | collective-permute-start | bytes 393224 | tf_op jit(solution)/shard_map/ppermute | solution.py:277
  (46 other events, 277.8 us)

commit v6 on v4

--- a/solution.py
+++ b/solution.py
@@ -106,8 +106,8 @@
             total = term if total is None else total + term
         return total
 
-    def tiles(self):
-        width = min(self.columns, GATE_KINDS * LANES)
+    def tiles(self, width=GATE_KINDS * LANES):
+        width = min(self.columns, width)
         return [slice(at, at + width) for at in range(0, self.columns, width)]
 
     def add(self, groups, away, total=None, first=None):
@@ -121,7 +121,7 @@
         def kernel(me_ref, weight_ref, *refs):
             extra_refs, refs, out_ref = refs[: len(extra)], refs[len(extra) : -1], refs[-1]
             blocks = [rows_of(refs[i * chunks : (i + 1) * chunks]) for i in range(len(away))]
-            for columns in self.tiles():
+            for columns in self.tiles(2 * LANES):
                 value = self.terms(me_ref, weight_ref, blocks, away, columns)
                 if total is not None:
                     value = extra_refs[0][:, columns] + value

time: 153 us -> 153 us (level)
  no operation moved by 1% of the time
where the time goes in v6:
time: 153 us
  starting transfers between devices  88.1 us (58%)
  waiting for transfers between devices  30.9 us (20%)
  Pallas kernels  29 us (19%)
  local copies, waits for them, and re-layouts  3.23 us (2%)
    ppermute x24, starting transfers between devices, gathered(): below = [lax.ppermute(after(block, ready), 'mp', up) for block in below]  44.7 us
    pallas_call x36, Pallas kernels, call(): pl.pallas_call(kernel, in_specs=[pl.BlockSpec(memory_space=pltpu.SMEM)] +...  29 us
    ppermute x11, starting transfers between devices, gathered(): below = [lax.ppermute(block, 'mp', up) for block in blocks]  21.4 us
    ppermute x6, starting transfers between devices, gathered(): lax.ppermute(below[c], 'mp', up)  11.7 us
    ppermute x24, waiting for transfers between devices, gathered(): above = [lax.ppermute(after(block, ready), 'mp', down) for block in above]  10.8 us
    ppermute x24, waiting for transfers between devices, gathered(): below = [lax.ppermute(after(block, ready), 'mp', up) for block in below]  9.74 us
    ppermute x24, starting transfers between devices, gathered(): above = [lax.ppermute(after(block, ready), 'mp', down) for block in above]  5.7 us
    ppermute x11, waiting for transfers between devices, gathered(): below = [lax.ppermute(block, 'mp', up) for block in blocks]  4.95 us
  transfers between devices with their start and end apart: 82, of which 40 were waited for; matrix products, arithmetic and copies ran while one was open for 0% of the time, Pallas kernels for 18%

profile of v6, /device:TPU:0, one launch (start us, length us, event | category | flops | bytes accessed | tf_op | source)
XLA Modules:
  0.0 153.0 jit_solution(5547483644334184592)
XLA Ops:
  0.6 3.1 %collective-permute-start = (bf16[256,512]{1,0:T(8,128)(2,1)}, bf16[256,512]{1,0:T(8,128)(2,1)S(1)}, u32[]{:S(2)}, u32[]{:S(2)}) collective-permute-start(bf16[256,512]{1,0:T(8,128)(2,1)} %refs_0_.1), channel_id=1, source_target_pairs={{0,4},{4,8},{8,12},{12,14},{14,10},{10,6},{6,2},{2,0},{1,5},{5,9},... | collective-permute-start | bytes 786440 | tf_op jit(solution)/shard_map/ppermute | solution.py:268
  3.7 2.2 %copy-done = bf16[512,4096]{1,0:T(8,128)(2,1)S(1)} copy-done((bf16[512,4096]{1,0:T(8,128)(2,1)S(1)}, bf16[512,4096]{1,0:T(8,128)(2,1)}, u32[]{:S(2)}) %copy-start) | copy-done | bytes 4194328
  7.2 2.9 %collective-permute-done = bf16[256,512]{1,0:T(8,128)(2,1)S(1)} collective-permute-done((bf16[256,512]{1,0:T(8,128)(2,1)}, bf16[256,512]{1,0:T(8,128)(2,1)S(1)}, u32[]{:S(2)}, u32[]{:S(2)}) %collective-permute-start) | collective-permute-done | bytes 262176 | tf_op jit(solution)/shard_map/ppermute | solution.py:268
  10.2 1.9 %collective-permute-start.2 = (bf16[128,512]{1,0:T(8,128)(2,1)S(1)}, bf16[128,512]{1,0:T(8,128)(2,1)S(1)}, u32[]{:S(2)}, u32[]{:S(2)}) collective-permute-start(bf16[128,512]{1,0:T(8,128)(2,1)S(1)} %get-tuple-element.60.refs_1_), channel_id=1, source_target_pairs={{0,4},{4,8},{8,12},{12,14},{14,10},{10,6},{6,2},{2,0},{1,5},{5,9},... | collective-permute-start | bytes 393224 | tf_op jit(solution)/shard_map/ppermute | solution.py:276
  12.8 1.9 %collective-permute-start.3 = (bf16[128,512]{1,0:T(8,128)(2,1)S(1)}, bf16[128,512]{1,0:T(8,128)(2,1)S(1)}, u32[]{:S(2)}, u32[]{:S(2)}) collective-permute-start(bf16[128,512]{1,0:T(8,128)(2,1)S(1)} %get-tuple-element.61.refs_2_), channel_id=1, source_target_pairs={{0,4},{4,8},{8,12},{12,14},{14,10},{10,6},{6,2},{2,0},{1,5},{5,9},... | collective-permute-start | bytes 393224 | tf_op jit(solution)/shard_map/ppermute | solution.py:276
  16.3 2.1 %collective-permute-start.6 = (bf16[128,512]{1,0:T(8,128)(2,1)S(1)}, bf16[128,512]{1,0:T(8,128)(2,1)S(1)}, u32[]{:S(2)}, u32[]{:S(2)}) collective-permute-start(bf16[128,512]{1,0:T(8,128)(2,1)S(1)} %collective-permute-done.2.refs_1_), channel_id=1, source_target_pairs={{0,4},{4,8},{8,12},{12,14},{14,10},{10,6},{6,2},{2,0},{1,5},{5,9},... | collective-permute-start | bytes 393224 | tf_op jit(solution)/shard_map/ppermute | solution.py:276
  19.3 1.9 %collective-permute-start.7 = (bf16[128,512]{1,0:T(8,128)(2,1)S(1)}, bf16[128,512]{1,0:T(8,128)(2,1)S(1)}, u32[]{:S(2)}, u32[]{:S(2)}) collective-permute-start(bf16[128,512]{1,0:T(8,128)(2,1)S(1)} %collective-permute-done.3.refs_2_), channel_id=1, source_target_pairs={{0,4},{4,8},{8,12},{12,14},{14,10},{10,6},{6,2},{2,0},{1,5},{5,9},... | collective-permute-start | bytes 393224 | tf_op jit(solution)/shard_map/ppermute | solution.py:276
  22.2 1.8 %collective-permute-start.10 = (bf16[128,512]{1,0:T(8,128)(2,1)S(1)}, bf16[128,512]{1,0:T(8,128)(2,1)S(1)}, u32[]{:S(2)}, u32[]{:S(2)}) collective-permute-start(bf16[128,512]{1,0:T(8,128)(2,1)S(1)} %collective-permute-done.6.refs_1_), channel_id=1, source_target_pairs={{0,4},{4,8},{8,12},{12,14},{14,10},{10,6},{6,2},{2,0},{1,5},{5,9},... | collective-permute-start | bytes 393224 | tf_op jit(solution)/shard_map/ppermute | solution.py:281
  25.1 1.5 %collective-permute-done.8.refs_3_ = bf16[128,512]{1,0:T(8,128)(2,1)S(1)} collective-permute-done((bf16[128,512]{1,0:T(8,128)(2,1)S(1)}, bf16[128,512]{1,0:T(8,128)(2,1)S(1)}, u32[]{:S(2)}, u32[]{:S(2)}) %collective-permute-start.8) | collective-permute-done | bytes 131104 | tf_op jit(solution)/shard_map/ppermute | solution.py:277
  27.6 1.9 %collective-permute-start.12 = (bf16[128,512]{1,0:T(8,128)(2,1)S(1)}, bf16[128,512]{1,0:T(8,128)(2,1)S(1)}, u32[]{:S(2)}, u32[]{:S(2)}) collective-permute-start(bf16[128,512]{1,0:T(8,128)(2,1)S(1)} %shard_map.99.refs_2_), channel_id=1, source_target_pairs={{0,4},{4,8},{8,12},{12,14},{14,10},{10,6},{6,2},{2,0},{1,5},{5,9},... | collective-permute-start | bytes 393224 | tf_op jit(solution)/shard_map/ppermute | solution.py:268
  30.1 1.8 %collective-permute-start.13 = (bf16[128,512]{1,0:T(8,128)(2,1)S(1)}, bf16[128,512]{1,0:T(8,128)(2,1)S(1)}, u32[]{:S(2)}, u32[]{:S(2)}) collective-permute-start(bf16[128,512]{1,0:T(8,128)(2,1)S(1)} %shard_map.100.refs_3_), channel_id=1, source_target_pairs={{0,4},{4,8},{8,12},{12,14},{14,10},{10,6},{6,2},{2,0},{1,5},{5,9},... | collective-permute-start | bytes 393224 | tf_op jit(solution)/shard_map/ppermute | solution.py:268
  33.2 2.0 %collective-permute-start.16 = (bf16[128,512]{1,0:T(8,128)(2,1)S(1)}, bf16[128,512]{1,0:T(8,128)(2,1)S(1)}, u32[]{:S(2)}, u32[]{:S(2)}) collective-permute-start(bf16[128,512]{1,0:T(8,128)(2,1)S(1)} %collective-permute-done.12.refs_1_), channel_id=1, source_target_pairs={{0,4},{4,8},{8,12},{12,14},{14,10},{10,6},{6,2},{2,0},{1,5},{5,9},... | collective-permute-start | bytes 393224 | tf_op jit(solution)/shard_map/ppermute | solution.py:276
  36.5 1.8 %collective-permute-start.17 = (bf16[128,512]{1,0:T(8,128)(2,1)S(1)}, bf16[128,512]{1,0:T(8,128)(2,1)S(1)}, u32[]{:S(2)}, u32[]{:S(2)}) collective-permute-start(bf16[128,512]{1,0:T(8,128)(2,1)S(1)} %collective-permute-done.13.refs_2_), channel_id=1, source_target_pairs={{0,4},{4,8},{8,12},{12,14},{14,10},{10,6},{6,2},{2,0},{1,5},{5,9},... | collective-permute-start | bytes 393224 | tf_op jit(solution)/shard_map/ppermute | solution.py:276
  40.3 2.0 %collective-permute-start.20 = (bf16[128,512]{1,0:T(8,128)(2,1)S(1)}, bf16[128,512]{1,0:T(8,128)(2,1)S(1)}, u32[]{:S(2)}, u32[]{:S(2)}) collective-permute-start(bf16[128,512]{1,0:T(8,128)(2,1)S(1)} %collective-permute-done.16.refs_1_), channel_id=1, source_target_pairs={{0,4},{4,8},{8,12},{12,14},{14,10},{10,6},{6,2},{2,0},{1,5},{5,9},... | collective-permute-start | bytes 393224 | tf_op jit(solution)/shard_map/ppermute | solution.py:276
  42.4 1.9 %collective-permute-start.21 = (bf16[128,512]{1,0:T(8,128)(2,1)S(1)}, bf16[128,512]{1,0:T(8,128)(2,1)S(1)}, u32[]{:S(2)}, u32[]{:S(2)}) collective-permute-start(bf16[128,512]{1,0:T(8,128)(2,1)S(1)} %collective-permute-done.17.refs_2_), channel_id=1, source_target_pairs={{0,4},{4,8},{8,12},{12,14},{14,10},{10,6},{6,2},{2,0},{1,5},{5,9},... | collective-permute-start | bytes 393224 | tf_op jit(solution)/shard_map/ppermute | solution.py:276
  45.4 2.0 %collective-permute-start.24 = (bf16[128,512]{1,0:T(8,128)(2,1)S(1)}, bf16[128,512]{1,0:T(8,128)(2,1)S(1)}, u32[]{:S(2)}, u32[]{:S(2)}) collective-permute-start(bf16[128,512]{1,0:T(8,128)(2,1)S(1)} %collective-permute-done.20.refs_1_), channel_id=1, source_target_pairs={{0,4},{4,8},{8,12},{12,14},{14,10},{10,6},{6,2},{2,0},{1,5},{5,9},... | collective-permute-start | bytes 393224 | tf_op jit(solution)/shard_map/ppermute | solution.py:281
  52.7 2.2 %collective-permute-start.26 = (bf16[128,512]{1,0:T(8,128)(2,1)S(1)}, bf16[128,512]{1,0:T(8,128)(2,1)S(1)}, u32[]{:S(2)}, u32[]{:S(2)}) collective-permute-start(bf16[128,512]{1,0:T(8,128)(2,1)S(1)} %get-tuple-element.76.refs_0_), channel_id=1, source_target_pairs={{0,4},{4,8},{8,12},{12,14},{14,10},{10,6},{6,2},{2,0},{1,5},{5,9},... | collective-permute-start | bytes 393224 | tf_op jit(solution)/shard_map/ppermute | solution.py:268
  56.1 2.0 %collective-permute-start.27 = (bf16[128,512]{1,0:T(8,128)(2,1)S(1)}, bf16[128,512]{1,0:T(8,128)(2,1)S(1)}, u32[]{:S(2)}, u32[]{:S(2)}) collective-permute-start(bf16[128,512]{1,0:T(8,128)(2,1)S(1)} %get-tuple-element.77.refs_1_), channel_id=1, source_target_pairs={{0,4},{4,8},{8,12},{12,14},{14,10},{10,6},{6,2},{2,0},{1,5},{5,9},... | collective-permute-start | bytes 393224 | tf_op jit(solution)/shard_map/ppermute | solution.py:268
  59.1 2.1 %collective-permute-start.30 = (bf16[128,512]{1,0:T(8,128)(2,1)S(1)}, bf16[128,512]{1,0:T(8,128)(2,1)S(1)}, u32[]{:S(2)}, u32[]{:S(2)}) collective-permute-start(bf16[128,512]{1,0:T(8,128)(2,1)S(1)} %collective-permute-done.26.refs_1_), channel_id=1, source_target_pairs={{0,4},{4,8},{8,12},{12,14},{14,10},{10,6},{6,2},{2,0},{1,5},{5,9},... | collective-permute-start | bytes 393224 | tf_op jit(solution)/shard_map/ppermute | solution.py:276
  62.0 2.1 %collective-permute-start.31 = (bf16[128,512]{1,0:T(8,128)(2,1)S(1)}, bf16[128,512]{1,0:T(8,128)(2,1)S(1)}, u32[]{:S(2)}, u32[]{:S(2)}) collective-permute-start(bf16[128,512]{1,0:T(8,128)(2,1)S(1)} %collective-permute-done.27.refs_2_), channel_id=1, source_target_pairs={{0,4},{4,8},{8,12},{12,14},{14,10},{10,6},{6,2},{2,0},{1,5},{5,9},... | collective-permute-start | bytes 393224 | tf_op jit(solution)/shard_map/ppermute | solution.py:276
  65.4 2.0 %collective-permute-start.34 = (bf16[128,512]{1,0:T(8,128)(2,1)S(1)}, bf16[128,512]{1,0:T(8,128)(2,1)S(1)}, u32[]{:S(2)}, u32[]{:S(2)}) collective-permute-start(bf16[128,512]{1,0:T(8,128)(2,1)S(1)} %collective-permute-done.30.refs_1_), channel_id=1, source_target_pairs={{0,4},{4,8},{8,12},{12,14},{14,10},{10,6},{6,2},{2,0},{1,5},{5,9},... | collective-permute-start | bytes 393224 | tf_op jit(solution)/shard_map/ppermute | solution.py:276
  67.6 2.0 %collective-permute-start.35 = (bf16[128,512]{1,0:T(8,128)(2,1)S(1)}, bf16[128,512]{1,0:T(8,128)(2,1)S(1)}, u32[]{:S(2)}, u32[]{:S(2)}) collective-permute-start(bf16[128,512]{1,0:T(8,128)(2,1)S(1)} %collective-permute-done.31.refs_2_), channel_id=1, source_target_pairs={{0,4},{4,8},{8,12},{12,14},{14,10},{10,6},{6,2},{2,0},{1,5},{5,9},... | collective-permute-start | bytes 393224 | tf_op jit(solution)/shard_map/ppermute | solution.py:276
  69.6 1.6 %collective-permute-done.34.refs_1_ = bf16[128,512]{1,0:T(8,128)(2,1)S(1)} collective-permute-done((bf16[128,512]{1,0:T(8,128)(2,1)S(1)}, bf16[128,512]{1,0:T(8,128)(2,1)S(1)}, u32[]{:S(2)}, u32[]{:S(2)}) %collective-permute-start.34) | collective-permute-done | bytes 131104 | tf_op jit(solution)/shard_map/ppermute | solution.py:276
  71.3 2.5 %collective-permute-start.38 = (bf16[128,512]{1,0:T(8,128)(2,1)S(1)}, bf16[128,512]{1,0:T(8,128)(2,1)S(1)}, u32[]{:S(2)}, u32[]{:S(2)}) collective-permute-start(bf16[128,512]{1,0:T(8,128)(2,1)S(1)} %collective-permute-done.34.refs_1_), channel_id=1, source_target_pairs={{0,4},{4,8},{8,12},{12,14},{14,10},{10,6},{6,2},{2,0},{1,5},{5,9},... | collective-permute-start | bytes 393224 | tf_op jit(solution)/shard_map/ppermute | solution.py:281
  74.3 2.3 %collective-permute-done.36.refs_3_ = bf16[128,512]{1,0:T(8,128)(2,1)S(1)} collective-permute-done((bf16[128,512]{1,0:T(8,128)(2,1)S(1)}, bf16[128,512]{1,0:T(8,128)(2,1)S(1)}, u32[]{:S(2)}, u32[]{:S(2)}) %collective-permute-start.36) | collective-permute-done | bytes 131104 | tf_op jit(solution)/shard_map/ppermute | solution.py:277
  77.7 2.3 %collective-permute-start.40 = (bf16[128,512]{1,0:T(8,128)(2,1)S(1)}, bf16[128,512]{1,0:T(8,128)(2,1)S(1)}, u32[]{:S(2)}, u32[]{:S(2)}) collective-permute-start(bf16[128,512]{1,0:T(8,128)(2,1)S(1)} %shard_map.111.refs_2_), channel_id=1, source_target_pairs={{0,4},{4,8},{8,12},{12,14},{14,10},{10,6},{6,2},{2,0},{1,5},{5,9},... | collective-permute-start | bytes 393224 | tf_op jit(solution)/shard_map/ppermute | solution.py:268
  80.5 1.9 %collective-permute-start.41 = (bf16[128,512]{1,0:T(8,128)(2,1)S(1)}, bf16[128,512]{1,0:T(8,128)(2,1)S(1)}, u32[]{:S(2)}, u32[]{:S(2)}) collective-permute-start(bf16[128,512]{1,0:T(8,128)(2,1)S(1)} %shard_map.112.refs_3_), channel_id=1, source_target_pairs={{0,4},{4,8},{8,12},{12,14},{14,10},{10,6},{6,2},{2,0},{1,5},{5,9},... | collective-permute-start | bytes 393224 | tf_op jit(solution)/shard_map/ppermute | solution.py:268
  84.0 2.3 %collective-permute-start.44 = (bf16[128,512]{1,0:T(8,128)(2,1)S(1)}, bf16[128,512]{1,0:T(8,128)(2,1)S(1)}, u32[]{:S(2)}, u32[]{:S(2)}) collective-permute-start(bf16[128,512]{1,0:T(8,128)(2,1)S(1)} %collective-permute-done.40.refs_1_), channel_id=1, source_target_pairs={{0,4},{4,8},{8,12},{12,14},{14,10},{10,6},{6,2},{2,0},{1,5},{5,9},... | collective-permute-start | bytes 393224 | tf_op jit(solution)/shard_map/ppermute | solution.py:276
  86.9 2.2 %collective-permute-start.45 = (bf16[128,512]{1,0:T(8,128)(2,1)S(1)}, bf16[128,512]{1,0:T(8,128)(2,1)S(1)}, u32[]{:S(2)}, u32[]{:S(2)}) collective-permute-start(bf16[128,512]{1,0:T(8,128)(2,1)S(1)} %collective-permute-done.41.refs_2_), channel_id=1, source_target_pairs={{0,4},{4,8},{8,12},{12,14},{14,10},{10,6},{6,2},{2,0},{1,5},{5,9},... | collective-permute-start | bytes 393224 | tf_op jit(solution)/shard_map/ppermute | solution.py:276
  90.4 2.0 %collective-permute-start.48 = (bf16[128,512]{1,0:T(8,128)(2,1)S(1)}, bf16[128,512]{1,0:T(8,128)(2,1)S(1)}, u32[]{:S(2)}, u32[]{:S(2)}) collective-permute-start(bf16[128,512]{1,0:T(8,128)(2,1)S(1)} %collective-permute-done.44.refs_1_), channel_id=1, source_target_pairs={{0,4},{4,8},{8,12},{12,14},{14,10},{10,6},{6,2},{2,0},{1,5},{5,9},... | collective-permute-start | bytes 393224 | tf_op jit(solution)/shard_map/ppermute | solution.py:276
  92.5 2.3 %collective-permute-start.49 = (bf16[128,512]{1,0:T(8,128)(2,1)S(1)}, bf16[128,512]{1,0:T(8,128)(2,1)S(1)}, u32[]{:S(2)}, u32[]{:S(2)}) collective-permute-start(bf16[128,512]{1,0:T(8,128)(2,1)S(1)} %collective-permute-done.45.refs_2_), channel_id=1, source_target_pairs={{0,4},{4,8},{8,12},{12,14},{14,10},{10,6},{6,2},{2,0},{1,5},{5,9},... | collective-permute-start | bytes 393224 | tf_op jit(solution)/shard_map/ppermute | solution.py:276
  94.8 1.8 %collective-permute-done.48.refs_1_ = bf16[128,512]{1,0:T(8,128)(2,1)S(1)} collective-permute-done((bf16[128,512]{1,0:T(8,128)(2,1)S(1)}, bf16[128,512]{1,0:T(8,128)(2,1)S(1)}, u32[]{:S(2)}, u32[]{:S(2)}) %collective-permute-start.48) | collective-permute-done | bytes 131104 | tf_op jit(solution)/shard_map/ppermute | solution.py:276
  96.5 2.3 %collective-permute-start.52 = (bf16[128,512]{1,0:T(8,128)(2,1)S(1)}, bf16[128,512]{1,0:T(8,128)(2,1)S(1)}, u32[]{:S(2)}, u32[]{:S(2)}) collective-permute-start(bf16[128,512]{1,0:T(8,128)(2,1)S(1)} %collective-permute-done.48.refs_1_), channel_id=1, source_target_pairs={{0,4},{4,8},{8,12},{12,14},{14,10},{10,6},{6,2},{2,0},{1,5},{5,9},... | collective-permute-start | bytes 393224 | tf_op jit(solution)/shard_map/ppermute | solution.py:281
  104.0 1.6 %collective-permute-start.54 = (bf16[128,512]{1,0:T(8,128)(2,1)S(1)}, bf16[128,512]{1,0:T(8,128)(2,1)S(1)}, u32[]{:S(2)}, u32[]{:S(2)}) collective-permute-start(bf16[128,512]{1,0:T(8,128)(2,1)S(1)} %get-tuple-element.95.refs_0_), channel_id=1, source_target_pairs={{0,4},{4,8},{8,12},{12,14},{14,10},{10,6},{6,2},{2,0},{1,5},{5,9},... | collective-permute-start | bytes 393224 | tf_op jit(solution)/shard_map/ppermute | solution.py:268
  107.3 1.6 %collective-permute-start.55 = (bf16[128,512]{1,0:T(8,128)(2,1)S(1)}, bf16[128,512]{1,0:T(8,128)(2,1)S(1)}, u32[]{:S(2)}, u32[]{:S(2)}) collective-permute-start(bf16[128,512]{1,0:T(8,128)(2,1)S(1)} %get-tuple-element.97.refs_1_), channel_id=1, source_target_pairs={{0,4},{4,8},{8,12},{12,14},{14,10},{10,6},{6,2},{2,0},{1,5},{5,9},... | collective-permute-start | bytes 393224 | tf_op jit(solution)/shard_map/ppermute | solution.py:268
  109.6 1.7 %collective-permute-start.58 = (bf16[128,512]{1,0:T(8,128)(2,1)S(1)}, bf16[128,512]{1,0:T(8,128)(2,1)S(1)}, u32[]{:S(2)}, u32[]{:S(2)}) collective-permute-start(bf16[128,512]{1,0:T(8,128)(2,1)S(1)} %collective-permute-done.54.refs_1_), channel_id=1, source_target_pairs={{0,4},{4,8},{8,12},{12,14},{14,10},{10,6},{6,2},{2,0},{1,5},{5,9},... | collective-permute-start | bytes 393224 | tf_op jit(solution)/shard_map/ppermute | solution.py:276
  116.1 1.5 %collective-permute-start.62 = (bf16[128,512]{1,0:T(8,128)(2,1)S(1)}, bf16[128,512]{1,0:T(8,128)(2,1)S(1)}, u32[]{:S(2)}, u32[]{:S(2)}) collective-permute-start(bf16[128,512]{1,0:T(8,128)(2,1)S(1)} %collective-permute-done.58.refs_1_), channel_id=1, source_target_pairs={{0,4},{4,8},{8,12},{12,14},{14,10},{10,6},{6,2},{2,0},{1,5},{5,9},... | collective-permute-start | bytes 393224 | tf_op jit(solution)/shard_map/ppermute | solution.py:276
  118.7 1.7 %collective-permute-start.63 = (bf16[128,512]{1,0:T(8,128)(2,1)S(1)}, bf16[128,512]{1,0:T(8,128)(2,1)S(1)}, u32[]{:S(2)}, u32[]{:S(2)}) collective-permute-start(bf16[128,512]{1,0:T(8,128)(2,1)S(1)} %collective-permute-done.59.refs_2_), channel_id=1, source_target_pairs={{0,4},{4,8},{8,12},{12,14},{14,10},{10,6},{6,2},{2,0},{1,5},{5,9},... | collective-permute-start | bytes 393224 | tf_op jit(solution)/shard_map/ppermute | solution.py:276
  122.3 1.7 %collective-permute-start.66 = (bf16[128,512]{1,0:T(8,128)(2,1)S(1)}, bf16[128,512]{1,0:T(8,128)(2,1)S(1)}, u32[]{:S(2)}, u32[]{:S(2)}) collective-permute-start(bf16[128,512]{1,0:T(8,128)(2,1)S(1)} %collective-permute-done.62.refs_1_), channel_id=1, source_target_pairs={{0,4},{4,8},{8,12},{12,14},{14,10},{10,6},{6,2},{2,0},{1,5},{5,9},... | collective-permute-start | bytes 393224 | tf_op jit(solution)/shard_map/ppermute | solution.py:281
  124.9 1.9 %collective-permute-done.64.refs_3_ = bf16[128,512]{1,0:T(8,128)(2,1)S(1)} collective-permute-done((bf16[128,512]{1,0:T(8,128)(2,1)S(1)}, bf16[128,512]{1,0:T(8,128)(2,1)S(1)}, u32[]{:S(2)}, u32[]{:S(2)}) %collective-permute-start.64) | collective-permute-done | bytes 131104 | tf_op jit(solution)/shard_map/ppermute | solution.py:277
  128.5 1.6 %collective-permute-start.68 = (bf16[128,512]{1,0:T(8,128)(2,1)S(1)}, bf16[128,512]{1,0:T(8,128)(2,1)S(1)}, u32[]{:S(2)}, u32[]{:S(2)}) collective-permute-start(bf16[128,512]{1,0:T(8,128)(2,1)S(1)} %shard_map.123.refs_2_), channel_id=1, source_target_pairs={{0,4},{4,8},{8,12},{12,14},{14,10},{10,6},{6,2},{2,0},{1,5},{5,9},... | collective-permute-start | bytes 393224 | tf_op jit(solution)/shard_map/ppermute | solution.py:268
  131.0 1.5 %collective-permute-start.69 = (bf16[128,512]{1,0:T(8,128)(2,1)S(1)}, bf16[128,512]{1,0:T(8,128)(2,1)S(1)}, u32[]{:S(2)}, u32[]{:S(2)}) collective-permute-start(bf16[128,512]{1,0:T(8,128)(2,1)S(1)} %shard_map.124.refs_3_), channel_id=1, source_target_pairs={{0,4},{4,8},{8,12},{12,14},{14,10},{10,6},{6,2},{2,0},{1,5},{5,9},... | collective-permute-start | bytes 393224 | tf_op jit(solution)/shard_map/ppermute | solution.py:268
  134.0 1.6 %collective-permute-start.72 = (bf16[128,512]{1,0:T(8,128)(2,1)S(1)}, bf16[128,512]{1,0:T(8,128)(2,1)S(1)}, u32[]{:S(2)}, u32[]{:S(2)}) collective-permute-start(bf16[128,512]{1,0:T(8,128)(2,1)S(1)} %collective-permute-done.68.refs_1_), channel_id=1, source_target_pairs={{0,4},{4,8},{8,12},{12,14},{14,10},{10,6},{6,2},{2,0},{1,5},{5,9},... | collective-permute-start | bytes 393224 | tf_op jit(solution)/shard_map/ppermute | solution.py:276
  136.1 1.5 %collective-permute-start.73 = (bf16[128,512]{1,0:T(8,128)(2,1)S(1)}, bf16[128,512]{1,0:T(8,128)(2,1)S(1)}, u32[]{:S(2)}, u32[]{:S(2)}) collective-permute-start(bf16[128,512]{1,0:T(8,128)(2,1)S(1)} %collective-permute-done.69.refs_2_), channel_id=1, source_target_pairs={{0,4},{4,8},{8,12},{12,14},{14,10},{10,6},{6,2},{2,0},{1,5},{5,9},... | collective-permute-start | bytes 393224 | tf_op jit(solution)/shard_map/ppermute | solution.py:276
  139.4 1.6 %collective-permute-start.76 = (bf16[128,512]{1,0:T(8,128)(2,1)S(1)}, bf16[128,512]{1,0:T(8,128)(2,1)S(1)}, u32[]{:S(2)}, u32[]{:S(2)}) collective-permute-start(bf16[128,512]{1,0:T(8,128)(2,1)S(1)} %collective-permute-done.72.refs_1_), channel_id=1, source_target_pairs={{0,4},{4,8},{8,12},{12,14},{14,10},{10,6},{6,2},{2,0},{1,5},{5,9},... | collective-permute-start | bytes 393224 | tf_op jit(solution)/shard_map/ppermute | solution.py:276
  141.4 1.5 %collective-permute-start.77 = (bf16[128,512]{1,0:T(8,128)(2,1)S(1)}, bf16[128,512]{1,0:T(8,128)(2,1)S(1)}, u32[]{:S(2)}, u32[]{:S(2)}) collective-permute-start(bf16[128,512]{1,0:T(8,128)(2,1)S(1)} %collective-permute-done.73.refs_2_), channel_id=1, source_target_pairs={{0,4},{4,8},{8,12},{12,14},{14,10},{10,6},{6,2},{2,0},{1,5},{5,9},... | collective-permute-start | bytes 393224 | tf_op jit(solution)/shard_map/ppermute | solution.py:276
  144.4 1.5 %collective-permute-start.81 = (bf16[128,512]{1,0:T(8,128)(2,1)S(1)}, bf16[128,512]{1,0:T(8,128)(2,1)S(1)}, u32[]{:S(2)}, u32[]{:S(2)}) collective-permute-start(bf16[128,512]{1,0:T(8,128)(2,1)S(1)} %collective-permute-done.76.refs_1_), channel_id=1, source_target_pairs={{0,4},{4,8},{8,12},{12,14},{14,10},{10,6},{6,2},{2,0},{1,5},{5,9},... | collective-permute-start | bytes 393224 | tf_op jit(solution)/shard_map/ppermute | solution.py:281
  150.9 1.9 %shard_map.130 = (bf16[256,512]{1,0:T(8,128)(2,1)}, f32[256,512]{1,0:T(8,128)}) custom-call(s32[1]{0:T(128)} %bitcast.me_ref, bf16[4096,2048]{1,0:T(8,128)(2,1)S(1)} %bitcast.3, f32[256,2048]{1,0:T(8,128)S(1)} %shard_map.128.total_ref, f32[1,2048]{1,0:T(1,128)S(1)} %bitcast.9, f32[128,512]{1,0:T(8,128)S(1)} %get-tuple-element.114.cell_ref, ...), custom_call_target="tpu_custom_call" | custom-call | tf_op jit(solution)/shard_map/pallas_call | solution.py:140
  (182 shorter events, 58.8 us)
Async XLA Ops:
  0.6 9.5 %collective-permute-start = (bf16[256,512]{1,0:T(8,128)(2,1)}, bf16[256,512]{1,0:T(8,128)(2,1)S(1)}, u32[]{:S(2)}, u32[]{:S(2)}) collective-permute-start(bf16[256,512]{1,0:T(8,128)(2,1)} %refs_0_.1), channel_id=1, source_target_pairs={{0,4},{4,8},{8,12},{12,14},{14,10},{10,6},{6,2},{2,0},{1,5},{5,9},... | collective-permute-start | bytes 786440 | tf_op jit(solution)/shard_map/ppermute | solution.py:268
  3.7 8.3 %collective-permute-start.1 = (bf16[256,512]{1,0:T(8,128)(2,1)}, bf16[256,512]{1,0:T(8,128)(2,1)S(1)}, u32[]{:S(2)}, u32[]{:S(2)}) collective-permute-start(bf16[256,512]{1,0:T(8,128)(2,1)} %refs_0_.1), channel_id=1, source_target_pairs={{4,0},{8,4},{12,8},{14,12},{10,14},{6,10},{2,6},{0,2},{5,1},{9,5},... | collective-permute-start | bytes 786440 | tf_op jit(solution)/shard_map/ppermute | solution.py:269
  10.2 6.1 %collective-permute-start.2 = (bf16[128,512]{1,0:T(8,128)(2,1)S(1)}, bf16[128,512]{1,0:T(8,128)(2,1)S(1)}, u32[]{:S(2)}, u32[]{:S(2)}) collective-permute-start(bf16[128,512]{1,0:T(8,128)(2,1)S(1)} %get-tuple-element.60.refs_1_), channel_id=1, source_target_pairs={{0,4},{4,8},{8,12},{12,14},{14,10},{10,6},{6,2},{2,0},{1,5},{5,9},... | collective-permute-start | bytes 393224 | tf_op jit(solution)/shard_map/ppermute | solution.py:276
  12.1 6.4 %collective-permute-start.5 = (bf16[128,512]{1,0:T(8,128)(2,1)S(1)}, bf16[128,512]{1,0:T(8,128)(2,1)S(1)}, u32[]{:S(2)}, u32[]{:S(2)}) collective-permute-start(bf16[128,512]{1,0:T(8,128)(2,1)S(1)} %get-tuple-element.63.refs_4_), channel_id=1, source_target_pairs={{4,0},{8,4},{12,8},{14,12},{10,14},{6,10},{2,6},{0,2},{5,1},{9,5},... | collective-permute-start | bytes 393224 | tf_op jit(solution)/shard_map/ppermute | solution.py:277
  12.8 6.5 %collective-permute-start.3 = (bf16[128,512]{1,0:T(8,128)(2,1)S(1)}, bf16[128,512]{1,0:T(8,128)(2,1)S(1)}, u32[]{:S(2)}, u32[]{:S(2)}) collective-permute-start(bf16[128,512]{1,0:T(8,128)(2,1)S(1)} %get-tuple-element.61.refs_2_), channel_id=1, source_target_pairs={{0,4},{4,8},{8,12},{12,14},{14,10},{10,6},{6,2},{2,0},{1,5},{5,9},... | collective-permute-start | bytes 393224 | tf_op jit(solution)/shard_map/ppermute | solution.py:276
  14.7 6.5 %collective-permute-start.4 = (bf16[128,512]{1,0:T(8,128)(2,1)S(1)}, bf16[128,512]{1,0:T(8,128)(2,1)S(1)}, u32[]{:S(2)}, u32[]{:S(2)}) collective-permute-start(bf16[128,512]{1,0:T(8,128)(2,1)S(1)} %get-tuple-element.62.refs_3_), channel_id=1, source_target_pairs={{4,0},{8,4},{12,8},{14,12},{10,14},{6,10},{2,6},{0,2},{5,1},{9,5},... | collective-permute-start | bytes 393224 | tf_op jit(solution)/shard_map/ppermute | solution.py:277
  16.3 6.0 %collective-permute-start.6 = (bf16[128,512]{1,0:T(8,128)(2,1)S(1)}, bf16[128,512]{1,0:T(8,128)(2,1)S(1)}, u32[]{:S(2)}, u32[]{:S(2)}) collective-permute-start(bf16[128,512]{1,0:T(8,128)(2,1)S(1)} %collective-permute-done.2.refs_1_), channel_id=1, source_target_pairs={{0,4},{4,8},{8,12},{12,14},{14,10},{10,6},{6,2},{2,0},{1,5},{5,9},... | collective-permute-start | bytes 393224 | tf_op jit(solution)/shard_map/ppermute | solution.py:276
  29.8 6.4 %collective-permute-start.15 = (bf16[128,512]{1,0:T(8,128)(2,1)S(1)}, bf16[128,512]{1,0:T(8,128)(2,1)S(1)}, u32[]{:S(2)}, u32[]{:S(2)}) collective-permute-start(bf16[128,512]{1,0:T(8,128)(2,1)S(1)} %shard_map.100.refs_3_), channel_id=1, source_target_pairs={{4,0},{8,4},{12,8},{14,12},{10,14},{6,10},{2,6},{0,2},{5,1},{9,5},... | collective-permute-start | bytes 393224 | tf_op jit(solution)/shard_map/ppermute | solution.py:269
  30.1 6.4 %collective-permute-start.13 = (bf16[128,512]{1,0:T(8,128)(2,1)S(1)}, bf16[128,512]{1,0:T(8,128)(2,1)S(1)}, u32[]{:S(2)}, u32[]{:S(2)}) collective-permute-start(bf16[128,512]{1,0:T(8,128)(2,1)S(1)} %shard_map.100.refs_3_), channel_id=1, source_target_pairs={{0,4},{4,8},{8,12},{12,14},{14,10},{10,6},{6,2},{2,0},{1,5},{5,9},... | collective-permute-start | bytes 393224 | tf_op jit(solution)/shard_map/ppermute | solution.py:268
  31.9 7.1 %collective-permute-start.14 = (bf16[128,512]{1,0:T(8,128)(2,1)S(1)}, bf16[128,512]{1,0:T(8,128)(2,1)S(1)}, u32[]{:S(2)}, u32[]{:S(2)}) collective-permute-start(bf16[128,512]{1,0:T(8,128)(2,1)S(1)} %shard_map.99.refs_2_), channel_id=1, source_target_pairs={{4,0},{8,4},{12,8},{14,12},{10,14},{6,10},{2,6},{0,2},{5,1},{9,5},... | collective-permute-start | bytes 393224 | tf_op jit(solution)/shard_map/ppermute | solution.py:269
  33.2 7.2 %collective-permute-start.16 = (bf16[128,512]{1,0:T(8,128)(2,1)S(1)}, bf16[128,512]{1,0:T(8,128)(2,1)S(1)}, u32[]{:S(2)}, u32[]{:S(2)}) collective-permute-start(bf16[128,512]{1,0:T(8,128)(2,1)S(1)} %collective-permute-done.12.refs_1_), channel_id=1, source_target_pairs={{0,4},{4,8},{8,12},{12,14},{14,10},{10,6},{6,2},{2,0},{1,5},{5,9},... | collective-permute-start | bytes 393224 | tf_op jit(solution)/shard_map/ppermute | solution.py:276
  36.2 6.2 %collective-permute-start.19 = (bf16[128,512]{1,0:T(8,128)(2,1)S(1)}, bf16[128,512]{1,0:T(8,128)(2,1)S(1)}, u32[]{:S(2)}, u32[]{:S(2)}) collective-permute-start(bf16[128,512]{1,0:T(8,128)(2,1)S(1)} %collective-permute-done.15.refs_4_), channel_id=1, source_target_pairs={{4,0},{8,4},{12,8},{14,12},{10,14},{6,10},{2,6},{0,2},{5,1},{9,5},... | collective-permute-start | bytes 393224 | tf_op jit(solution)/shard_map/ppermute | solution.py:277
  36.5 5.9 %collective-permute-start.17 = (bf16[128,512]{1,0:T(8,128)(2,1)S(1)}, bf16[128,512]{1,0:T(8,128)(2,1)S(1)}, u32[]{:S(2)}, u32[]{:S(2)}) collective-permute-start(bf16[128,512]{1,0:T(8,128)(2,1)S(1)} %collective-permute-done.13.refs_2_), channel_id=1, source_target_pairs={{0,4},{4,8},{8,12},{12,14},{14,10},{10,6},{6,2},{2,0},{1,5},{5,9},... | collective-permute-start | bytes 393224 | tf_op jit(solution)/shard_map/ppermute | solution.py:276
  39.0 6.3 %collective-permute-start.18 = (bf16[128,512]{1,0:T(8,128)(2,1)S(1)}, bf16[128,512]{1,0:T(8,128)(2,1)S(1)}, u32[]{:S(2)}, u32[]{:S(2)}) collective-permute-start(bf16[128,512]{1,0:T(8,128)(2,1)S(1)} %collective-permute-done.14.refs_3_), channel_id=1, source_target_pairs={{4,0},{8,4},{12,8},{14,12},{10,14},{6,10},{2,6},{0,2},{5,1},{9,5},... | collective-permute-start | bytes 393224 | tf_op jit(solution)/shard_map/ppermute | solution.py:277
  42.4 6.8 %collective-permute-start.21 = (bf16[128,512]{1,0:T(8,128)(2,1)S(1)}, bf16[128,512]{1,0:T(8,128)(2,1)S(1)}, u32[]{:S(2)}, u32[]{:S(2)}) collective-permute-start(bf16[128,512]{1,0:T(8,128)(2,1)S(1)} %collective-permute-done.17.refs_2_), channel_id=1, source_target_pairs={{0,4},{4,8},{8,12},{12,14},{14,10},{10,6},{6,2},{2,0},{1,5},{5,9},... | collective-permute-start | bytes 393224 | tf_op jit(solution)/shard_map/ppermute | solution.py:276
  45.4 6.2 %collective-permute-start.24 = (bf16[128,512]{1,0:T(8,128)(2,1)S(1)}, bf16[128,512]{1,0:T(8,128)(2,1)S(1)}, u32[]{:S(2)}, u32[]{:S(2)}) collective-permute-start(bf16[128,512]{1,0:T(8,128)(2,1)S(1)} %collective-permute-done.20.refs_1_), channel_id=1, source_target_pairs={{0,4},{4,8},{8,12},{12,14},{14,10},{10,6},{6,2},{2,0},{1,5},{5,9},... | collective-permute-start | bytes 393224 | tf_op jit(solution)/shard_map/ppermute | solution.py:281
  47.5 7.4 %collective-permute-start.25 = (bf16[128,512]{1,0:T(8,128)(2,1)S(1)}, bf16[128,512]{1,0:T(8,128)(2,1)S(1)}, u32[]{:S(2)}, u32[]{:S(2)}) collective-permute-start(bf16[128,512]{1,0:T(8,128)(2,1)S(1)} %collective-permute-done.23.refs_4_), channel_id=1, source_target_pairs={{4,0},{8,4},{12,8},{14,12},{10,14},{6,10},{2,6},{0,2},{5,1},{9,5},... | collective-permute-start | bytes 393224 | tf_op jit(solution)/shard_map/ppermute | solution.py:279
  52.7 6.4 %collective-permute-start.26 = (bf16[128,512]{1,0:T(8,128)(2,1)S(1)}, bf16[128,512]{1,0:T(8,128)(2,1)S(1)}, u32[]{:S(2)}, u32[]{:S(2)}) collective-permute-start(bf16[128,512]{1,0:T(8,128)(2,1)S(1)} %get-tuple-element.76.refs_0_), channel_id=1, source_target_pairs={{0,4},{4,8},{8,12},{12,14},{14,10},{10,6},{6,2},{2,0},{1,5},{5,9},... | collective-permute-start | bytes 393224 | tf_op jit(solution)/shard_map/ppermute | solution.py:268
  56.1 5.9 %collective-permute-start.27 = (bf16[128,512]{1,0:T(8,128)(2,1)S(1)}, bf16[128,512]{1,0:T(8,128)(2,1)S(1)}, u32[]{:S(2)}, u32[]{:S(2)}) collective-permute-start(bf16[128,512]{1,0:T(8,128)(2,1)S(1)} %get-tuple-element.77.refs_1_), channel_id=1, source_target_pairs={{0,4},{4,8},{8,12},{12,14},{14,10},{10,6},{6,2},{2,0},{1,5},{5,9},... | collective-permute-start | bytes 393224 | tf_op jit(solution)/shard_map/ppermute | solution.py:268
  58.1 6.4 %collective-permute-start.28 = (bf16[128,512]{1,0:T(8,128)(2,1)S(1)}, bf16[128,512]{1,0:T(8,128)(2,1)S(1)}, u32[]{:S(2)}, u32[]{:S(2)}) collective-permute-start(bf16[128,512]{1,0:T(8,128)(2,1)S(1)} %get-tuple-element.76.refs_0_), channel_id=1, source_target_pairs={{4,0},{8,4},{12,8},{14,12},{10,14},{6,10},{2,6},{0,2},{5,1},{9,5},... | collective-permute-start | bytes 393224 | tf_op jit(solution)/shard_map/ppermute | solution.py:269
  59.1 6.3 %collective-permute-start.30 = (bf16[128,512]{1,0:T(8,128)(2,1)S(1)}, bf16[128,512]{1,0:T(8,128)(2,1)S(1)}, u32[]{:S(2)}, u32[]{:S(2)}) collective-permute-start(bf16[128,512]{1,0:T(8,128)(2,1)S(1)} %collective-permute-done.26.refs_1_), channel_id=1, source_target_pairs={{0,4},{4,8},{8,12},{12,14},{14,10},{10,6},{6,2},{2,0},{1,5},{5,9},... | collective-permute-start | bytes 393224 | tf_op jit(solution)/shard_map/ppermute | solution.py:276
  61.7 5.9 %collective-permute-start.33 = (bf16[128,512]{1,0:T(8,128)(2,1)S(1)}, bf16[128,512]{1,0:T(8,128)(2,1)S(1)}, u32[]{:S(2)}, u32[]{:S(2)}) collective-permute-start(bf16[128,512]{1,0:T(8,128)(2,1)S(1)} %collective-permute-done.29.refs_4_), channel_id=1, source_target_pairs={{4,0},{8,4},{12,8},{14,12},{10,14},{6,10},{2,6},{0,2},{5,1},{9,5},... | collective-permute-start | bytes 393224 | tf_op jit(solution)/shard_map/ppermute | solution.py:277
  67.6 6.2 %collective-permute-start.37 = (bf16[128,512]{1,0:T(8,128)(2,1)S(1)}, bf16[128,512]{1,0:T(8,128)(2,1)S(1)}, u32[]{:S(2)}, u32[]{:S(2)}) collective-permute-start(bf16[128,512]{1,0:T(8,128)(2,1)S(1)} %collective-permute-done.33.refs_4_), channel_id=1, source_target_pairs={{4,0},{8,4},{12,8},{14,12},{10,14},{6,10},{2,6},{0,2},{5,1},{9,5},... | collective-permute-start | bytes 393224 | tf_op jit(solution)/shard_map/ppermute | solution.py:277
  67.6 6.7 %collective-permute-start.35 = (bf16[128,512]{1,0:T(8,128)(2,1)S(1)}, bf16[128,512]{1,0:T(8,128)(2,1)S(1)}, u32[]{:S(2)}, u32[]{:S(2)}) collective-permute-start(bf16[128,512]{1,0:T(8,128)(2,1)S(1)} %collective-permute-done.31.refs_2_), channel_id=1, source_target_pairs={{0,4},{4,8},{8,12},{12,14},{14,10},{10,6},{6,2},{2,0},{1,5},{5,9},... | collective-permute-start | bytes 393224 | tf_op jit(solution)/shard_map/ppermute | solution.py:276
  69.6 7.0 %collective-permute-start.36 = (bf16[128,512]{1,0:T(8,128)(2,1)S(1)}, bf16[128,512]{1,0:T(8,128)(2,1)S(1)}, u32[]{:S(2)}, u32[]{:S(2)}) collective-permute-start(bf16[128,512]{1,0:T(8,128)(2,1)S(1)} %collective-permute-done.32.refs_3_), channel_id=1, source_target_pairs={{4,0},{8,4},{12,8},{14,12},{10,14},{6,10},{2,6},{0,2},{5,1},{9,5},... | collective-permute-start | bytes 393224 | tf_op jit(solution)/shard_map/ppermute | solution.py:277
  71.3 6.1 %collective-permute-start.38 = (bf16[128,512]{1,0:T(8,128)(2,1)S(1)}, bf16[128,512]{1,0:T(8,128)(2,1)S(1)}, u32[]{:S(2)}, u32[]{:S(2)}) collective-permute-start(bf16[128,512]{1,0:T(8,128)(2,1)S(1)} %collective-permute-done.34.refs_1_), channel_id=1, source_target_pairs={{0,4},{4,8},{8,12},{12,14},{14,10},{10,6},{6,2},{2,0},{1,5},{5,9},... | collective-permute-start | bytes 393224 | tf_op jit(solution)/shard_map/ppermute | solution.py:281
  73.8 6.2 %collective-permute-start.39 = (bf16[128,512]{1,0:T(8,128)(2,1)S(1)}, bf16[128,512]{1,0:T(8,128)(2,1)S(1)}, u32[]{:S(2)}, u32[]{:S(2)}) collective-permute-start(bf16[128,512]{1,0:T(8,128)(2,1)S(1)} %collective-permute-done.37.refs_4_), channel_id=1, source_target_pairs={{4,0},{8,4},{12,8},{14,12},{10,14},{6,10},{2,6},{0,2},{5,1},{9,5},... | collective-permute-start | bytes 393224 | tf_op jit(solution)/shard_map/ppermute | solution.py:279
  77.7 6.4 %collective-permute-start.40 = (bf16[128,512]{1,0:T(8,128)(2,1)S(1)}, bf16[128,512]{1,0:T(8,128)(2,1)S(1)}, u32[]{:S(2)}, u32[]{:S(2)}) collective-permute-start(bf16[128,512]{1,0:T(8,128)(2,1)S(1)} %shard_map.111.refs_2_), channel_id=1, source_target_pairs={{0,4},{4,8},{8,12},{12,14},{14,10},{10,6},{6,2},{2,0},{1,5},{5,9},... | collective-permute-start | bytes 393224 | tf_op jit(solution)/shard_map/ppermute | solution.py:268
  80.3 6.2 %collective-permute-start.43 = (bf16[128,512]{1,0:T(8,128)(2,1)S(1)}, bf16[128,512]{1,0:T(8,128)(2,1)S(1)}, u32[]{:S(2)}, u32[]{:S(2)}) collective-permute-start(bf16[128,512]{1,0:T(8,128)(2,1)S(1)} %shard_map.112.refs_3_), channel_id=1, source_target_pairs={{4,0},{8,4},{12,8},{14,12},{10,14},{6,10},{2,6},{0,2},{5,1},{9,5},... | collective-permute-start | bytes 393224 | tf_op jit(solution)/shard_map/ppermute | solution.py:269
  80.5 6.4 %collective-permute-start.41 = (bf16[128,512]{1,0:T(8,128)(2,1)S(1)}, bf16[128,512]{1,0:T(8,128)(2,1)S(1)}, u32[]{:S(2)}, u32[]{:S(2)}) collective-permute-start(bf16[128,512]{1,0:T(8,128)(2,1)S(1)} %shard_map.112.refs_3_), channel_id=1, source_target_pairs={{0,4},{4,8},{8,12},{12,14},{14,10},{10,6},{6,2},{2,0},{1,5},{5,9},... | collective-permute-start | bytes 393224 | tf_op jit(solution)/shard_map/ppermute | solution.py:268
  82.4 6.7 %collective-permute-start.42 = (bf16[128,512]{1,0:T(8,128)(2,1)S(1)}, bf16[128,512]{1,0:T(8,128)(2,1)S(1)}, u32[]{:S(2)}, u32[]{:S(2)}) collective-permute-start(bf16[128,512]{1,0:T(8,128)(2,1)S(1)} %shard_map.111.refs_2_), channel_id=1, source_target_pairs={{4,0},{8,4},{12,8},{14,12},{10,14},{6,10},{2,6},{0,2},{5,1},{9,5},... | collective-permute-start | bytes 393224 | tf_op jit(solution)/shard_map/ppermute | solution.py:269
  84.0 6.4 %collective-permute-start.44 = (bf16[128,512]{1,0:T(8,128)(2,1)S(1)}, bf16[128,512]{1,0:T(8,128)(2,1)S(1)}, u32[]{:S(2)}, u32[]{:S(2)}) collective-permute-start(bf16[128,512]{1,0:T(8,128)(2,1)S(1)} %collective-permute-done.40.refs_1_), channel_id=1, source_target_pairs={{0,4},{4,8},{8,12},{12,14},{14,10},{10,6},{6,2},{2,0},{1,5},{5,9},... | collective-permute-start | bytes 393224 | tf_op jit(solution)/shard_map/ppermute | solution.py:276
  86.5 5.9 %collective-permute-start.47 = (bf16[128,512]{1,0:T(8,128)(2,1)S(1)}, bf16[128,512]{1,0:T(8,128)(2,1)S(1)}, u32[]{:S(2)}, u32[]{:S(2)}) collective-permute-start(bf16[128,512]{1,0:T(8,128)(2,1)S(1)} %collective-permute-done.43.refs_4_), channel_id=1, source_target_pairs={{4,0},{8,4},{12,8},{14,12},{10,14},{6,10},{2,6},{0,2},{5,1},{9,5},... | collective-permute-start | bytes 393224 | tf_op jit(solution)/shard_map/ppermute | solution.py:277
  90.4 6.1 %collective-permute-start.48 = (bf16[128,512]{1,0:T(8,128)(2,1)S(1)}, bf16[128,512]{1,0:T(8,128)(2,1)S(1)}, u32[]{:S(2)}, u32[]{:S(2)}) collective-permute-start(bf16[128,512]{1,0:T(8,128)(2,1)S(1)} %collective-permute-done.44.refs_1_), channel_id=1, source_target_pairs={{0,4},{4,8},{8,12},{12,14},{14,10},{10,6},{6,2},{2,0},{1,5},{5,9},... | collective-permute-start | bytes 393224 | tf_op jit(solution)/shard_map/ppermute | solution.py:276
  92.5 6.4 %collective-permute-start.51 = (bf16[128,512]{1,0:T(8,128)(2,1)S(1)}, bf16[128,512]{1,0:T(8,128)(2,1)S(1)}, u32[]{:S(2)}, u32[]{:S(2)}) collective-permute-start(bf16[128,512]{1,0:T(8,128)(2,1)S(1)} %collective-permute-done.47.refs_4_), channel_id=1, source_target_pairs={{4,0},{8,4},{12,8},{14,12},{10,14},{6,10},{2,6},{0,2},{5,1},{9,5},... | collective-permute-start | bytes 393224 | tf_op jit(solution)/shard_map/ppermute | solution.py:277
  92.5 7.6 %collective-permute-start.49 = (bf16[128,512]{1,0:T(8,128)(2,1)S(1)}, bf16[128,512]{1,0:T(8,128)(2,1)S(1)}, u32[]{:S(2)}, u32[]{:S(2)}) collective-permute-start(bf16[128,512]{1,0:T(8,128)(2,1)S(1)} %collective-permute-done.45.refs_2_), channel_id=1, source_target_pairs={{0,4},{4,8},{8,12},{12,14},{14,10},{10,6},{6,2},{2,0},{1,5},{5,9},... | collective-permute-start | bytes 393224 | tf_op jit(solution)/shard_map/ppermute | solution.py:276
  94.8 6.6 %collective-permute-start.50 = (bf16[128,512]{1,0:T(8,128)(2,1)S(1)}, bf16[128,512]{1,0:T(8,128)(2,1)S(1)}, u32[]{:S(2)}, u32[]{:S(2)}) collective-permute-start(bf16[128,512]{1,0:T(8,128)(2,1)S(1)} %collective-permute-done.46.refs_3_), channel_id=1, source_target_pairs={{4,0},{8,4},{12,8},{14,12},{10,14},{6,10},{2,6},{0,2},{5,1},{9,5},... | collective-permute-start | bytes 393224 | tf_op jit(solution)/shard_map/ppermute | solution.py:277
  96.5 6.4 %collective-permute-start.52 = (bf16[128,512]{1,0:T(8,128)(2,1)S(1)}, bf16[128,512]{1,0:T(8,128)(2,1)S(1)}, u32[]{:S(2)}, u32[]{:S(2)}) collective-permute-start(bf16[128,512]{1,0:T(8,128)(2,1)S(1)} %collective-permute-done.48.refs_1_), channel_id=1, source_target_pairs={{0,4},{4,8},{8,12},{12,14},{14,10},{10,6},{6,2},{2,0},{1,5},{5,9},... | collective-permute-start | bytes 393224 | tf_op jit(solution)/shard_map/ppermute | solution.py:281
  98.8 6.8 %collective-permute-start.53 = (bf16[128,512]{1,0:T(8,128)(2,1)S(1)}, bf16[128,512]{1,0:T(8,128)(2,1)S(1)}, u32[]{:S(2)}, u32[]{:S(2)}) collective-permute-start(bf16[128,512]{1,0:T(8,128)(2,1)S(1)} %collective-permute-done.51.refs_4_), channel_id=1, source_target_pairs={{4,0},{8,4},{12,8},{14,12},{10,14},{6,10},{2,6},{0,2},{5,1},{9,5},... | collective-permute-start | bytes 393224 | tf_op jit(solution)/shard_map/ppermute | solution.py:279
  109.6 6.4 %collective-permute-start.58 = (bf16[128,512]{1,0:T(8,128)(2,1)S(1)}, bf16[128,512]{1,0:T(8,128)(2,1)S(1)}, u32[]{:S(2)}, u32[]{:S(2)}) collective-permute-start(bf16[128,512]{1,0:T(8,128)(2,1)S(1)} %collective-permute-done.54.refs_1_), channel_id=1, source_target_pairs={{0,4},{4,8},{8,12},{12,14},{14,10},{10,6},{6,2},{2,0},{1,5},{5,9},... | collective-permute-start | bytes 393224 | tf_op jit(solution)/shard_map/ppermute | solution.py:276
  111.8 6.4 %collective-permute-start.61 = (bf16[128,512]{1,0:T(8,128)(2,1)S(1)}, bf16[128,512]{1,0:T(8,128)(2,1)S(1)}, u32[]{:S(2)}, u32[]{:S(2)}) collective-permute-start(bf16[128,512]{1,0:T(8,128)(2,1)S(1)} %collective-permute-done.57.refs_4_), channel_id=1, source_target_pairs={{4,0},{8,4},{12,8},{14,12},{10,14},{6,10},{2,6},{0,2},{5,1},{9,5},... | collective-permute-start | bytes 393224 | tf_op jit(solution)/shard_map/ppermute | solution.py:277
  112.6 6.2 %collective-permute-start.59 = (bf16[128,512]{1,0:T(8,128)(2,1)S(1)}, bf16[128,512]{1,0:T(8,128)(2,1)S(1)}, u32[]{:S(2)}, u32[]{:S(2)}) collective-permute-start(bf16[128,512]{1,0:T(8,128)(2,1)S(1)} %collective-permute-done.55.refs_2_), channel_id=1, source_target_pairs={{0,4},{4,8},{8,12},{12,14},{14,10},{10,6},{6,2},{2,0},{1,5},{5,9},... | collective-permute-start | bytes 393224 | tf_op jit(solution)/shard_map/ppermute | solution.py:276
  113.8 7.1 %collective-permute-start.60 = (bf16[128,512]{1,0:T(8,128)(2,1)S(1)}, bf16[128,512]{1,0:T(8,128)(2,1)S(1)}, u32[]{:S(2)}, u32[]{:S(2)}) collective-permute-start(bf16[128,512]{1,0:T(8,128)(2,1)S(1)} %collective-permute-done.56.refs_3_), channel_id=1, source_target_pairs={{4,0},{8,4},{12,8},{14,12},{10,14},{6,10},{2,6},{0,2},{5,1},{9,5},... | collective-permute-start | bytes 393224 | tf_op jit(solution)/shard_map/ppermute | solution.py:277
  116.1 6.2 %collective-permute-start.62 = (bf16[128,512]{1,0:T(8,128)(2,1)S(1)}, bf16[128,512]{1,0:T(8,128)(2,1)S(1)}, u32[]{:S(2)}, u32[]{:S(2)}) collective-permute-start(bf16[128,512]{1,0:T(8,128)(2,1)S(1)} %collective-permute-done.58.refs_1_), channel_id=1, source_target_pairs={{0,4},{4,8},{8,12},{12,14},{14,10},{10,6},{6,2},{2,0},{1,5},{5,9},... | collective-permute-start | bytes 393224 | tf_op jit(solution)/shard_map/ppermute | solution.py:276
  118.7 6.1 %collective-permute-start.63 = (bf16[128,512]{1,0:T(8,128)(2,1)S(1)}, bf16[128,512]{1,0:T(8,128)(2,1)S(1)}, u32[]{:S(2)}, u32[]{:S(2)}) collective-permute-start(bf16[128,512]{1,0:T(8,128)(2,1)S(1)} %collective-permute-done.59.refs_2_), channel_id=1, source_target_pairs={{0,4},{4,8},{8,12},{12,14},{14,10},{10,6},{6,2},{2,0},{1,5},{5,9},... | collective-permute-start | bytes 393224 | tf_op jit(solution)/shard_map/ppermute | solution.py:276
  121.0 5.8 %collective-permute-start.64 = (bf16[128,512]{1,0:T(8,128)(2,1)S(1)}, bf16[128,512]{1,0:T(8,128)(2,1)S(1)}, u32[]{:S(2)}, u32[]{:S(2)}) collective-permute-start(bf16[128,512]{1,0:T(8,128)(2,1)S(1)} %collective-permute-done.60.refs_3_), channel_id=1, source_target_pairs={{4,0},{8,4},{12,8},{14,12},{10,14},{6,10},{2,6},{0,2},{5,1},{9,5},... | collective-permute-start | bytes 393224 | tf_op jit(solution)/shard_map/ppermute | solution.py:277
  123.9 6.1 %collective-permute-start.67 = (bf16[128,512]{1,0:T(8,128)(2,1)S(1)}, bf16[128,512]{1,0:T(8,128)(2,1)S(1)}, u32[]{:S(2)}, u32[]{:S(2)}) collective-permute-start(bf16[128,512]{1,0:T(8,128)(2,1)S(1)} %collective-permute-done.65.refs_4_), channel_id=1, source_target_pairs={{4,0},{8,4},{12,8},{14,12},{10,14},{6,10},{2,6},{0,2},{5,1},{9,5},... | collective-permute-start | bytes 393224 | tf_op jit(solution)/shard_map/ppermute | solution.py:279
  141.4 6.2 %collective-permute-start.77 = (bf16[128,512]{1,0:T(8,128)(2,1)S(1)}, bf16[128,512]{1,0:T(8,128)(2,1)S(1)}, u32[]{:S(2)}, u32[]{:S(2)}) collective-permute-start(bf16[128,512]{1,0:T(8,128)(2,1)S(1)} %collective-permute-done.73.refs_2_), channel_id=1, source_target_pairs={{0,4},{4,8},{8,12},{12,14},{14,10},{10,6},{6,2},{2,0},{1,5},{5,9},... | collective-permute-start | bytes 393224 | tf_op jit(solution)/shard_map/ppermute | solution.py:276
  (46 other events, 268.7 us)
